TPU v7x, 128 devices: a whole 4x4x4 slice. The times are simulated.
128 devices in a mesh: band: 2 (over x_hi), dom: 64 (over z, y, x_lo, core).
Axes of the slice: x: 4 (x_hi: 2, x_lo: 2; x = x_hi * 2 + x_lo), y: 4, z: 4, core: 2. Of those that a mesh axis runs over, the one named last changes fastest.
Arguments:
- orbitals: float32 [16, 64, 8, 3072], P('band', 'dom'), may hold values from -6 to 6
- occupation: float32 [16], P('band'), may hold values from 0.2 to 2
- potential: float32 [64, 8, 3072], P('dom'), may hold values from -4 to 1
- projectors: float32 [64, 4, 448, 128], P('dom'), may hold values from -0.2 to 0.2
- energies: float32 [64, 4, 128], P('dom'), may hold values from -10 to 10
- piece_column: int32 [64, 448], P('dom'), may hold values from 0 to 127
- piece_shift: int32 [64, 448], P('dom'), may hold values from 0 to 64
- piece_owner: int32 [64, 448], P('dom'), may hold values from 0 to 8
- piece_atom: int32 [64, 448], P('dom'), may hold values from 0 to 127
- lower_edge: float32 [1], replicated, may hold values from -1 to 1
- upper_edge: float32 [1], replicated, may hold values from 80 to 100
Outputs:
- filtered: float32 [16, 64, 8, 3072], P('band', 'dom')
- density: float32 [64, 8, 3072], P('dom', None, 'band')
All inputs are finite; a program needn't handle non-finite values.
Results may differ from a plain program's by a relative error of at most 0.00012.
Values sent between devices are 32-bit elements; how exact they have to be, the bound alone decides.
No kernel may reach another device: no remote copies, remote signals or barrier semaphores. Data moves between devices by JAX's collectives and lax.ppermute only.
A program may use at most 128 MiB of HBM per device.

v0:
```python
import functools

import jax
import jax.numpy as jnp
import numpy as np
from jax import lax
from jax.experimental import pallas as pl
from jax.experimental.pallas import tpu as pltpu
from jax.sharding import PartitionSpec as P

NZ = 192
HALO = 6
DEG = 4
CX = 8
CY = 16
WX = 2 * CX
COLS = WX * CY
ORB = 4
NPJ = 4
PIECES = 448
ALL = 2 * PIECES
PTS = 128
SLOTS = 128
ROWS = ORB * NPJ
PACKED = 144
TAIL = NZ - PACKED
LANES = 128
EDGE = HALO * 16
OWN = 512
ROOM = 58
CODES = 12
TABLE = CODES * ROWS
THIRD = TABLE // 3
HALF = 2 * THIRD
NOTE = TABLE + NZ

WEIGHTS = (
    -5369.0 / 1800.0,
    12.0 / 7.0,
    -15.0 / 56.0,
    10.0 / 189.0,
    -1.0 / 112.0,
    2.0 / 1925.0,
    -1.0 / 16632.0,
)
KINETIC = -0.5 / 0.16
F32 = jnp.float32
BF16 = jnp.bfloat16


def coupling(steps):
    reach = np.abs(steps)
    near = (reach >= 1) & (reach <= HALO)
    table = np.array(WEIGHTS) * KINETIC
    return np.where(near, table[np.minimum(reach, HALO)], 0.0)


def stencil_matrices():
    col = np.arange(COLS)
    x, y = col // CY, col % CY
    same_x = x[:, None] == x[None, :]
    same_y = y[:, None] == y[None, :]
    own = np.where(same_y, coupling(x[None, :] - x[:, None]), 0.0)
    own = own + np.where(same_x, coupling(y[None, :] - y[:, None]), 0.0)
    lane = np.arange(LANES)
    used = (lane < EDGE)[:, None]
    parts = []
    for start in (-HALO, WX):
        hx, hy = start + lane // CY, lane % CY
        parts.append(np.where(used & (hy[:, None] == y[None, :]), coupling(x[None, :] - hx[:, None]), 0.0))
    for start in (-HALO, CY):
        hy, hx = start + lane // WX, lane % WX
        parts.append(np.where(used & (hx[:, None] == x[None, :]), coupling(y[None, :] - hy[:, None]), 0.0))
    halo = np.concatenate(parts, axis=0)
    depth = np.arange(NZ)
    apart = (depth[None, :] - depth[:, None] + NZ // 2) % NZ - NZ // 2
    ring = coupling(apart)
    picks = []
    for start in (0, CY - HALO):
        hy, hx = start + lane // WX, lane % WX
        picks.append(np.where(used.T & (col[:, None] == (hx * CY + hy)[None, :]), 1.0, 0.0))
    edge = np.concatenate(picks, axis=1)
    return own, halo, ring, edge


def two_parts(matrix):
    high = np.asarray(matrix, np.float32).astype(jnp.bfloat16)
    low = (np.asarray(matrix, np.float64) - high.astype(np.float64)).astype(np.float32).astype(jnp.bfloat16)
    return high, low


def split(value):
    high = value.astype(BF16)
    low = (value - high.astype(F32)).astype(BF16)
    return high, low


def mul(left, right):
    return jnp.dot(left, right, preferred_element_type=F32)


def mul_t(left, right):
    return lax.dot_general(left, right, (((1,), (1,)), ((), ())), preferred_element_type=F32)


def pack_edge(value):
    main = value[:PACKED]
    lane = lax.broadcasted_iota(jnp.int32, (TAIL, LANES), 1)
    rows = []
    for k in range(3):
        tail = pltpu.roll(value[PACKED:], (EDGE - 32 * k) % LANES, 1)
        rows.append(jnp.where(lane < EDGE, main[k * TAIL : (k + 1) * TAIL], tail))
    return jnp.concatenate(rows, axis=0)


def unpack_edge(value):
    lane = lax.broadcasted_iota(jnp.int32, (TAIL, LANES), 1)
    tail = jnp.zeros((TAIL, LANES), F32)
    for k in range(3):
        moved = pltpu.roll(value[k * TAIL : (k + 1) * TAIL], (32 * k - EDGE) % LANES, 1)
        tail = jnp.where((lane >= 32 * k) & (lane < 32 * k + 32), moved, tail)
    return jnp.concatenate([value, tail], axis=0)


def each(count, step):
    def run(k, carry):
        step(k)
        return carry

    lax.fori_loop(0, count, run, 0)


def emit_edges(field, below_inner, edge_ref, xl_ref, xh_ref, inner_ref, outer_ref):
    def step(o):
        value = field[o]
        high, low = split(value)
        picked = mul(high, edge_ref[...]) + mul(low, edge_ref[...])
        xl_ref[o] = pack_edge(value[:, :LANES])
        xh_ref[o] = pack_edge(pltpu.roll(value[:, LANES:], LANES - 32, 1))
        bottom, top = pack_edge(picked[:, :LANES]), pack_edge(picked[:, LANES:])
        inner_ref[o] = jnp.where(below_inner, bottom, top)
        outer_ref[o] = jnp.where(below_inner, top, bottom)

    each(ORB, step)


def to_columns(source, near, far):
    for y in range(CY):
        at = y * NZ
        line = source(at)
        near[pl.ds(y, CX, stride=CY), :] = line[:, :LANES]
        tail = line[:, LANES:]
        far[pl.ds(y, CX, stride=CY), :] = jnp.concatenate([tail, jnp.zeros((CX, 2 * LANES - NZ), F32)], axis=1)
    return jnp.concatenate([jnp.transpose(near[...]), jnp.transpose(far[...])[: NZ - LANES]], axis=0)


def from_columns(value, near, far):
    near[...] = jnp.transpose(value[:LANES])
    far[...] = jnp.transpose(jnp.concatenate([value[LANES:], jnp.zeros((2 * LANES - NZ, LANES), F32)], axis=0))
    for y in range(0, CY, 2):
        lines = []
        for at in (y, y + 1):
            lines.append(near[pl.ds(at, CX, stride=CY), :])
            lines.append(far[pl.ds(at, CX, stride=CY), :][:, : NZ - LANES])
        yield y * NZ, jnp.concatenate(lines, axis=1)


def flag(params, row):
    return params[row : row + 1, :] == 1.0


def begin_kernel(
    place, upper_edge, lower_edge, weights, column_in, shift_in, owner_in, atom_in, raw_in, proj_in, pot_in, energy_in,
    keep, params, ints, table, local, note,
    column, shift, owner, atom, raw, proj, potential, energy, turned, tables, both, placed, partial, near, far, sems,
):
    pairs = (
        (raw_in, raw), (column_in, column), (shift_in, shift), (owner_in, owner),
        (atom_in, atom), (proj_in, proj), (pot_in, potential), (energy_in, energy),
    )
    copies = [pltpu.make_async_copy(source, target, sems.at[k]) for k, (source, target) in enumerate(pairs)]
    for copy in copies:
        copy.start()
    side, core = place[0], place[1]
    upper = jnp.full((1, LANES), side, jnp.int32) == 1
    params[0:1] = jnp.full((1, LANES), side, jnp.int32).astype(F32)
    params[1:2] = jnp.full((1, LANES), core, jnp.int32).astype(F32)
    top = jnp.full((1, LANES), upper_edge[0], F32)
    bottom = jnp.full((1, LANES), lower_edge[0], F32)
    half_width = (top - bottom) / 2.0
    params[2:3] = (top + bottom) / 2.0
    params[3:4] = 1.0 / half_width
    params[4:5] = 2.0 / half_width
    params[5:6] = jnp.full((1, LANES), place[2], jnp.int32).astype(F32)
    params[6:8] = jnp.zeros((2, LANES), F32)
    for o in range(ORB):
        params[8 + o : 9 + o] = jnp.full((1, LANES), weights[side * ORB + o], F32)
    params[8 + ORB :] = jnp.zeros((8 - ORB, LANES), F32)
    sub = jnp.full((1, PIECES), side, jnp.int32)
    for copy in copies[:5]:
        copy.wait()
    step_x = (owner[...] >= 3).astype(jnp.int32) + (owner[...] >= 6).astype(jnp.int32)
    row = owner[...] - 3 * step_x
    lines = [
        sub * LANES + column[...],
        shift[...],
        row * 4 + sub + step_x,
        atom[...],
        column[...],
    ]
    gap = jnp.full((1, OWN - PIECES), -1, jnp.int32)
    for k, line in enumerate(lines):
        ints[k : k + 1] = jnp.concatenate([line, gap], axis=1)
    ints[len(lines) :] = jnp.zeros((8 - len(lines), OWN), jnp.int32)
    def turn(o):
        def kept(at):
            return jnp.where(upper[:, :1], raw[ORB + o, :, at : at + NZ], raw[o, :, at : at + NZ])

        def sent(at):
            return jnp.where(upper[:, :1], raw[o, :, at : at + NZ], raw[ORB + o, :, at : at + NZ])

        turned[o] = to_columns(kept, near, far)
        turned[ORB + o] = to_columns(sent, near, far)
        keep[o] = turned[o]

    each(ORB, turn)
    for copy in copies[5:]:
        copy.wait()
    first_tables(ints, turned, tables, both, proj, placed, partial)
    table[...] = tables[0]
    note[:TABLE] = tables[1]
    lines = to_columns(lambda at: potential[:, at : at + NZ], near, far)
    local[...] = lines
    note[TABLE:NOTE] = lines
    note[NOTE : NOTE + NPJ] = energy[...]
    note[NOTE + NPJ : NOTE + 8] = jnp.zeros((4, LANES), F32)
    numbers = ints[:4].astype(F32)
    for k in range(OWN // LANES):
        note[NOTE + 8 + 4 * k : NOTE + 12 + 4 * k] = numbers[:, k * LANES : (k + 1) * LANES]


def start_kernel(params, keep, came, edge, field, xl, xh, inner, outer, near, far):
    upper = flag(params, 0)

    def step(o):
        turned = to_columns(lambda at: came[o, :, at : at + NZ], near, far)
        kept = keep[o]
        field[o, :, :LANES] = jnp.where(upper, turned, kept)
        field[o, :, LANES:] = jnp.where(upper, kept, turned)

    each(ORB, step)
    emit_edges(field, flag(params, 1), edge, xl, xh, inner, outer)


def gate_kernel(came, note_came, proj, out):
    pass


def prepare_kernel(ints, note_came, own, came, placed, index):
    lines = [note_came[NOTE + 8 + 4 * k : NOTE + 12 + 4 * k] for k in range(OWN // LANES)]
    other = jnp.concatenate(lines, axis=1)[:, :PIECES].astype(jnp.int32)
    index[...] = jnp.concatenate([ints[:4, :PIECES], other], axis=1)

    def step(j):
        both = jnp.concatenate([own[j], came[j]], axis=0)
        for k in range(ALL // LANES):
            at = slice(k * LANES, (k + 1) * LANES)
            placed[j, :, at] = shifted(both[at], ints_row(index, at))

    each(NPJ, step)


def ints_row(index, at):
    return index[1:2, at]


def column_hot(index, at, wide):
    where = lax.broadcasted_iota(jnp.int32, (COLS, wide), 0) == index[0:1, pl.ds(at, wide)]
    return where.astype(F32).astype(BF16)


def chunks(step):
    each(ALL // 256, lambda k: step(pl.multiple_of(k * 256, 256), 256))
    step(ALL - LANES, LANES)


def atom_hot(index):
    codes = index[3:4, :]
    return (lax.broadcasted_iota(jnp.int32, (SLOTS, codes.shape[1]), 0) == codes).astype(F32).astype(BF16)


def shifted(block, shift):
    block = jnp.concatenate([jnp.transpose(block), jnp.zeros((NZ - PTS, LANES), F32)], axis=0)
    for bit in (64, 32, 16, 8, 4, 2, 1):
        block = jnp.where((shift & bit) != 0, pltpu.roll(block, bit, 0), block)
    return block


def gather_table(index, spread):
    codes = index[2:3, :]
    rows = jnp.concatenate([jnp.where(codes == code, spread, 0.0) for code in range(CODES)], axis=0)
    high, low = split(rows)
    atoms = atom_hot(index)
    return mul_t(high, atoms) + mul_t(low, atoms)


def project(both, hot, placed, partial, at, wide):
    picked = mul(both, jnp.concatenate([hot, hot], axis=0))
    for j in range(NPJ):
        values = placed[j, :, pl.ds(at, wide)]
        for o in range(ORB):
            term = picked[o * NZ : (o + 1) * NZ] * values
            row = o * NPJ + j
            partial[row : row + 1, pl.ds(at, wide)] = jnp.sum(term, axis=0, keepdims=True)


def first_tables(index, turned, tables, both, proj, placed, partial):
    blocks = OWN // LANES

    def place(j):
        for k in range(blocks):
            block = proj[j, k * LANES : min((k + 1) * LANES, PIECES)]
            if k == blocks - 1:
                block = jnp.concatenate([block, jnp.zeros((OWN - PIECES, LANES), F32)], axis=0)
            placed[j, :, k * LANES : (k + 1) * LANES] = shifted(block, index[1:2, k * LANES : (k + 1) * LANES])

    each(NPJ, place)

    def table(s):
        for o in range(ORB):
            both[o * NZ : (o + 1) * NZ, :] = jnp.concatenate(split(turned[s * ORB + o]), axis=1)

        def chunk(k):
            at = pl.multiple_of(k * 256, 256)
            where = lax.broadcasted_iota(jnp.int32, (LANES, 256), 0) == index[4:5, pl.ds(at, 256)]
            project(both[...], where.astype(F32).astype(BF16), placed, partial, at, 256)

        each(OWN // 256, chunk)
        tables[s] = gather_table(index, partial[...])

    each(2, table)


def table_kernel(index, field, placed, table, partial, both):
    def gather(o):
        rows = pl.ds(pl.multiple_of(o * NZ, NZ), NZ)
        both[rows, :] = jnp.concatenate(split(field[o]), axis=1)

    each(ORB, gather)
    chunks(lambda at, wide: project(both[...], column_hot(index, at, wide), placed, partial, at, wide))
    table[...] = gather_table(index, partial[...])


def pair_sum(second, table, came):
    gap = jnp.zeros((THIRD, LANES), F32)
    up = table[THIRD:] + jnp.concatenate([came[HALF:], gap], axis=0)
    down = table[:HALF] + jnp.concatenate([gap, came[:THIRD]], axis=0)
    return jnp.where(second, up, down)


def join_table_kernel(params, table, local, note_came, field, out, pot):
    out[...] = table[...] + note_came[:TABLE]
    upper = flag(params, 0)
    there = note_came[TABLE:NOTE]
    pot[:, :LANES] = jnp.where(upper, there, local[...])
    pot[:, LANES:] = jnp.where(upper, local[...], there)


def first_pair_kernel(params, table, came, energy, note_came, half):
    half[:HALF] = pair_sum(flag(params, 1), table[...], came[...])
    upper = flag(params, 0)
    there = note_came[NOTE : NOTE + NPJ]
    half[HALF : HALF + NPJ] = jnp.where(upper, there, energy[...])
    half[HALF + NPJ :] = jnp.where(upper, energy[...], there)


def pair_kernel(params, table, came, half):
    half[...] = pair_sum(flag(params, 1), table[...], came[...])


def sum_kernel(mine, came, acc, low, high, acc_out):
    total = mine[:HALF] + came[:HALF]
    step = 2 * ROWS
    for q in range(2):
        low[q * step : (q + 1) * step] = total[2 * q * step : (2 * q + 1) * step]
        high[q * step : (q + 1) * step] = total[(2 * q + 1) * step : (2 * q + 2) * step]


def first_sum_kernel(params, mine, came, acc, low, high, acc_out):
    sum_kernel(mine, came, acc, low, high, acc_out)
    second = flag(params, 1)
    for sub, out in ((0, low), (1, high)):
        at = HALF + sub * NPJ
        here, there = mine[at : at + NPJ], came[at : at + NPJ]
        out[THIRD : THIRD + NPJ] = jnp.where(second, here, there)
        out[THIRD + NPJ :] = jnp.where(second, there, here)


def spread_energy(low, high, below, above, energy):
    for q in range(2):
        at = slice(THIRD + q * NPJ, THIRD + (q + 1) * NPJ)
        for r, source in enumerate((below, low, high, above)):
            row = (q * 4 + r) * ROWS
            energy[row : row + ROWS] = jnp.concatenate([source[at]] * ORB, axis=0)


def scale_of(first, params):
    row = 3 if first else 4
    return params[row : row + 1, 0:1]


def total_kernel(first, params, low, high, below, above, acc, energy, out, acc_out, energy_out=None):
    if first:
        spread_energy(low, high, below, above, energy_out)
        energy = energy_out
    step = 2 * ROWS
    scale = params[3 if first else 4 : 4 if first else 5, :]
    for q in range(2):
        at = slice(q * step, (q + 1) * step)
        row = 2 * q * step
        out[row : row + step] = (low[at] + below[at]) * energy[row : row + step] * scale
        row = row + step
        out[row : row + step] = (high[at] + above[at]) * energy[row : row + step] * scale


def first_total_kernel(params, low, high, below, above, acc, out, energy, acc_out):
    total_kernel(True, params, low, high, below, above, acc, None, out, acc_out, energy)


def later_total_kernel(params, low, high, below, above, energy, acc, out, acc_out):
    total_kernel(False, params, low, high, below, above, acc, energy, out, acc_out)


def local_kernel(first, params, half, field, before, pot, own_w, ring_w, out):
    center = params[2:3, 0:1]
    scale = scale_of(first, params)
    diagonal = pot[...] + (3.0 * WEIGHTS[0] * KINETIC - center)

    def step(o):
        value = field[o]
        high, low = split(value)
        across = mul(jnp.concatenate([high, low, high], axis=1), own_w[...])
        along = mul(ring_w[...], jnp.concatenate([high, low, high], axis=0))
        total = scale * (across + along + diagonal * value)
        out[o] = total if first else total - before[o]

    each(ORB, step)


def halo_kernel(first, params, inner, outer, xl, xh, acc, halo_w, out):
    scale = scale_of(first, params)
    below_inner = flag(params, 1)

    def step(o):
        inside, outside = unpack_edge(inner[o]), unpack_edge(outer[o])
        bottom = jnp.where(below_inner, inside, outside)
        top = jnp.where(below_inner, outside, inside)
        line = jnp.concatenate([unpack_edge(xl[o]), unpack_edge(xh[o]), bottom, top], axis=1)
        high, low = split(line)
        out[o] = acc[o] + scale * mul(jnp.concatenate([high, low, high], axis=1), halo_w[...])

    each(ORB, step)


def update_kernel(last, params, index, acc, mine, came, placed, *rest):
    if last:
        kept, sent, field, coef_rows, near_sums, near, far = rest
    else:
        edge, field, xl, xh, inner, outer, coef_rows, near_sums = rest
    second = flag(params, 1)
    total = jnp.concatenate(
        [jnp.where(second, came[THIRD:], mine[...][:THIRD]), jnp.where(second, mine[...][:THIRD], mine[...][THIRD:]),
         jnp.where(second, mine[...][THIRD:], came[:THIRD])], axis=0
    )
    atoms = atom_hot(index)
    spread = mul(jnp.concatenate(split(total), axis=1), jnp.concatenate([atoms, atoms], axis=0))
    codes = index[2:3, :]
    coefs = jnp.zeros((ROWS, ALL), F32)
    for code in range(CODES):
        coefs = jnp.where(codes == code, spread[code * ROWS : (code + 1) * ROWS], coefs)
    near_sums[...] = jnp.zeros((ORB * NZ, COLS), F32)
    coef_rows[...] = coefs

    def chunk(at, wide):
        hot = column_hot(index, at, wide)
        lines = []
        for o in range(ORB):
            rows = coef_rows[o * NPJ : (o + 1) * NPJ, pl.ds(at, wide)]
            line = rows[0:1] * placed[0, :, pl.ds(at, wide)]
            for j in range(1, NPJ):
                line = line + rows[j : j + 1] * placed[j, :, pl.ds(at, wide)]
            lines.append(jnp.concatenate(split(line), axis=1))
        near_sums[...] += mul_t(jnp.concatenate(lines, axis=0), jnp.concatenate([hot, hot], axis=1))

    chunks(chunk)

    def finish(o):
        rows = pl.ds(pl.multiple_of(o * NZ, NZ), NZ)
        field[o] = acc[o] + near_sums[rows, :]

    each(ORB, finish)
    if not last:
        emit_edges(field, second, edge, xl, xh, inner, outer)
        return
    upper = flag(params, 0)

    def emit(o):
        left, right = field[o, :, :LANES], field[o, :, LANES:]
        for spot, pair in from_columns(jnp.where(upper, left, right), near, far):
            sent[o, :, spot : spot + 2 * NZ] = pair
        for spot, pair in from_columns(jnp.where(upper, right, left), near, far):
            kept[o, :, spot : spot + 2 * NZ] = pair

    each(ORB, emit)


def join_kernel(params, came, b, c, d, mine, a, out, density):
    upper = params[0:1, 0:1] == 1.0
    density[...] = a[...] + b[...] + c[...] + d[...]

    def step(o):
        out[o] = jnp.where(upper, came[o], mine[o])
        out[ORB + o] = jnp.where(upper, mine[o], came[o])

    each(ORB, step)


def density_kernel(params, field, quarter, across_x, across_band, across_both, plane, near, far):
    dens = jnp.zeros((NZ, COLS), F32)
    for o in range(ORB):
        dens = dens + params[8 + o : 9 + o, 0:1] * field[o] * field[o]
    left, right = dens[:, :LANES], dens[:, LANES:]
    upper = flag(params, 0)
    second = params[5:6, 0:1] == 1.0
    span = CY * NZ // 2
    for value, same, opposite in (
        (jnp.where(upper, right, left), quarter, across_band),
        (jnp.where(upper, left, right), across_x, across_both),
    ):
        for spot, pair in from_columns(value, near, far):
            plane[:, spot : spot + 2 * NZ] = pair
        same[...] = jnp.where(second, plane[:, span:], plane[:, :span])
        opposite[...] = jnp.where(second, plane[:, :span], plane[:, span:])


VM = pl.BlockSpec(memory_space=pltpu.VMEM)
ANY = pl.BlockSpec(memory_space=pl.ANY)
SM = pl.BlockSpec(memory_space=pltpu.SMEM)
HB = pl.BlockSpec(memory_space=pltpu.HBM)


def call(kernel, in_specs, shapes, args, scratch=(), flops=10**8, name=None, passed=0, room=48):
    single = isinstance(shapes, tuple)
    outs = [shapes] if single else list(shapes)
    outs = [shape if isinstance(shape[0], tuple) else (shape, F32) for shape in outs]
    plain = len(outs) - passed
    result = pl.pallas_call(
        kernel,
        out_shape=[jax.ShapeDtypeStruct(*out) for out in outs],
        in_specs=in_specs,
        out_specs=[VM] * plain + [ANY] * passed,
        scratch_shapes=list(scratch),
        input_output_aliases={len(args) - passed + k: plain + k for k in range(passed)},
        compiler_params=pltpu.CompilerParams(vmem_limit_bytes=room * 1024 * 1024),
        cost_estimate=pl.CostEstimate(flops=flops, bytes_accessed=4 * 10**6, transcendentals=0),
        name=name,
    )(*args)
    return result[0] if single else result


def send(value, pairs):
    return lax.ppermute(value, "dom", pairs)


def along_z(step):
    return [(d, (d + 16 * step) % 64) for d in range(64)]


def outward(d):
    y = d % 8
    return d // 8 * 8 + ((y - 1) % 8 if y % 2 == 0 else (y + 1) % 8)


SWAP = [(d, d ^ 8) for d in range(64)]
CORES = [(d, d ^ 1) for d in range(64)]
OUTER = [(d, outward(d)) for d in range(64)]


def body(
    orbitals,
    occupation,
    potential,
    projectors,
    energies,
    piece_column,
    piece_shift,
    piece_owner,
    piece_atom,
    lower_edge,
    upper_edge,
):
    own_m, halo_m, ring_m, edge_m = stencil_matrices()
    a, b = two_parts(own_m)
    own_w = jnp.asarray(np.concatenate([a, a, b], axis=0))
    a, b = two_parts(halo_m)
    halo_w = jnp.asarray(np.concatenate([a, a, b], axis=0))
    a, b = two_parts(ring_m)
    ring_w = jnp.asarray(np.concatenate([a, a, b], axis=1))
    edge_w = jnp.asarray(edge_m.astype(np.float32).astype(jnp.bfloat16))

    here = lax.axis_index("dom")
    side = (here // 8 % 2).astype(jnp.int32)
    core = (here % 2).astype(jnp.int32)
    place = jnp.stack([side, core, lax.axis_index("band").astype(jnp.int32)])
    packed = (ORB, PACKED, LANES)
    grid = (ORB, NZ, COLS)
    stage = [pltpu.VMEM((LANES, LANES), F32)] * 2

    raw = orbitals[:, 0]
    came = send(lax.dynamic_slice_in_dim(raw, (1 - side) * ORB, ORB, 0), SWAP)
    line = pltpu.VMEM((1, PIECES), jnp.int32)
    keep, params, ints, own_table, local, note = call(
        begin_kernel,
        [SM] * 4 + [HB] * 8,
        [
            (ORB, NZ, LANES),
            (16, LANES),
            ((8, OWN), jnp.int32),
            (TABLE, LANES),
            (NZ, LANES),
            (NOTE + 24, LANES),
        ],
        (
            place, upper_edge, lower_edge, occupation, piece_column, piece_shift, piece_owner, piece_atom,
            raw, projectors[0], potential[0], energies[0],
        ),
        [
            line, line, line, line,
            pltpu.VMEM((2 * ORB, CX, CY * NZ), F32),
            pltpu.VMEM((NPJ, PIECES, LANES), F32),
            pltpu.VMEM((CX, CY * NZ), F32),
            pltpu.VMEM((NPJ, LANES), F32),
            pltpu.VMEM((2 * ORB, NZ, LANES), F32),
            pltpu.VMEM((2, TABLE, LANES), F32),
            pltpu.VMEM((ORB * NZ, 2 * LANES), BF16),
            pltpu.VMEM((NPJ, NZ, OWN), F32),
            pltpu.VMEM((ROWS, OWN), F32),
            *stage,
            pltpu.SemaphoreType.DMA((8,)),
        ],
        name="begin",
        room=ROOM,
    )
    note_came = send(note, SWAP)
    proj = call(gate_kernel, [ANY] * 3, [(NPJ, PIECES, LANES)], (came, note_came, projectors[0]), flops=10**6, name="gate", passed=1)
    proj_came = send(proj[0], SWAP)
    field, xl, xh, inner, outer = call(
        start_kernel,
        [VM] * 4,
        [grid] + [packed] * 4,
        (params, keep, came, edge_w),
        stage,
        name="start",
    )
    table, pot = call(
        join_table_kernel,
        [VM] * 4 + [ANY],
        [(TABLE, LANES), (NZ, COLS)],
        (params, own_table, local, note_came, field),
        flops=10**6,
        name="join_table",
    )
    placed, index = call(
        prepare_kernel,
        [VM] * 4,
        [(NPJ, NZ, ALL), ((4, ALL), jnp.int32)],
        (ints, note_came, projectors[0], proj_came),
        name="prepare",
    )

    sums_room = [pltpu.VMEM((ROWS, ALL), F32), pltpu.VMEM((ORB * NZ, COLS), F32)]
    before = field
    for level in range(DEG):
        first, last = level == 0, level == DEG - 1
        if not first:
            table = call(
                table_kernel,
                [VM] * 3,
                (TABLE, LANES),
                (index, field, placed),
                [pltpu.VMEM((ROWS, ALL), F32), pltpu.VMEM((ORB * NZ, 2 * COLS), BF16)],
                name="table",
            )
        inner_came = send(inner, CORES)
        table_came = send(table, CORES)
        if first:
            half = call(
                first_pair_kernel,
                [VM] * 5,
                (HALF + 8, LANES),
                (params, table, table_came, energies[0], note_came),
                flops=10**6,
                name="pair",
            )
        else:
            half = call(pair_kernel, [VM] * 3, (HALF, LANES), (params, table, table_came), flops=10**6, name="pair")
        half_came = send(half, OUTER)
        xl_came = send(xh, along_z(1))
        xh_came = send(xl, along_z(-1))
        outer_came = send(outer, OUTER)
        acc = call(
            functools.partial(local_kernel, first),
            [VM, ANY] + [VM] * 5,
            grid,
            (params, half, field, before, pot, own_w, ring_w),
            name="local",
        )
        size = (THIRD + 8, LANES) if first else (THIRD, LANES)
        low, high, acc = call(
            first_sum_kernel if first else sum_kernel,
            [VM] * (3 if first else 2) + [ANY],
            [size, size, grid],
            ((params,) if first else ()) + (half, half_came, acc),
            flops=10**6,
            name="sums",
            passed=1,
        )
        below = send(high, along_z(1))
        above = send(low, along_z(-1))
        acc = call(
            functools.partial(halo_kernel, first),
            [VM] * 7,
            grid,
            (params, inner_came, outer_came, xl_came, xh_came, acc, halo_w),
            name="halo",
        )
        if first:
            total, energy, acc = call(
                first_total_kernel,
                [VM] * 5 + [ANY],
                [(HALF, LANES), (HALF, LANES), grid],
                (params, low, high, below, above, acc),
                flops=10**6,
                name="totals",
                passed=1,
            )
        else:
            total, acc = call(
                later_total_kernel,
                [VM] * 6 + [ANY],
                [(HALF, LANES), grid],
                (params, low, high, below, above, energy, acc),
                flops=10**6,
                name="totals",
                passed=1,
            )
        total_came = send(total, CORES)
        args = (params, index, acc, total, total_came, placed)
        if not last:
            before, (field, xl, xh, inner, outer) = field, call(
                functools.partial(update_kernel, last),
                [VM] * 7,
                [grid] + [packed] * 4,
                args + (edge_w,),
                sums_room,
                name="update",
            )
        else:
            flat = (ORB, CX, CY * NZ)
            mine, other, result = call(
                functools.partial(update_kernel, last),
                [VM] * 6,
                [flat, flat, grid],
                args,
                sums_room + stage,
                name="finish",
            )
    part = (CX, CY * NZ // 2)
    quarter, across_x, across_band, across_both = call(
        density_kernel,
        [VM] * 2,
        [part] * 4,
        (params, result),
        [pltpu.VMEM((CX, CY * NZ), F32)] + stage,
        name="density",
    )
    swapped = send(other, SWAP)
    both = [(d, d ^ 72) for d in range(128)]
    filtered, density = call(
        join_kernel,
        [VM] * 7,
        [(2 * ORB, CX, CY * NZ), part],
        (
            params,
            swapped,
            send(across_x, SWAP),
            lax.ppermute(across_band, "band", [(0, 1), (1, 0)]),
            lax.ppermute(across_both, ("band", "dom"), both),
            mine,
            quarter,
        ),
        name="join",
    )
    return filtered[:, None], density[None]


def solution(mesh):
    in_specs = (
        P("band", "dom", None, None),
        P("band"),
        P("dom", None, None),
        P("dom", None, None, None),
        P("dom", None, None),
        P("dom", None),
        P("dom", None),
        P("dom", None),
        P("dom", None),
        P(),
        P(),
    )
    out_specs = (P("band", "dom", None, None), P("dom", None, "band"))
    return jax.shard_map(body, mesh=mesh, in_specs=in_specs, out_specs=out_specs, check_vma=False)
```

profile of v0, /device:TPU:0, one launch (start us, length us, event | category | flops | bytes accessed | tf_op | source)
XLA Modules:
  0.0 143.4 jit_solution(974222378250056827)
XLA Ops:
  1.8 3.4 %collective-permute-start.1 = (f32[4,8,3072]{2,1,0:T(8,128)S(1)}, f32[4,8,3072]{2,1,0:T(8,128)S(1)}, u32[]{:S(2)}, u32[]{:S(2)}) collective-permute-start(f32[4,8,3072]{2,1,0:T(8,128)S(1)} %dynamic-slice_bitcast_fusion), channel_id=1, source_target_pairs={{0,8},{1,9},{2,10},{3,11},{4,12},{5,13},{6,14},{7,15},{8,0},{9,1},... | collective-permute-start | bytes 1179656 | tf_op jit(solution)/shard_map/ppermute | solution.py:572
  7.1 7.5 %begin.1 = (f32[4,192,128]{2,1,0:T(8,128)}, f32[16,128]{1,0:T(8,128)}, s32[8,512]{1,0:T(8,128)}, f32[192,128]{1,0:T(8,128)}, f32[192,128]{1,0:T(8,128)}, /*index=5*/f32[408,128]{1,0:T(8,128)}) custom-call(s32[3]{0:T(128)} %pad_add_fusion.place, f32[1]{0:T(128)S(6)} %copy.37.upper_edge, f32[1]{0:T(128)S(6)} %copy.36.lower_edge, f32[8]{0:T(128)} %weights.1, ...), custom_call_target="tpu_custom_call" | custom-call | flops 100000000 | bytes 4000000 | tf_op jit(solution)/shard_map/begin/pallas_call | solution.py:557
  15.1 8.0 %collective-permute-done.note_came = f32[408,128]{1,0:T(8,128)S(1)} collective-permute-done((f32[408,128]{1,0:T(8,128)}, f32[408,128]{1,0:T(8,128)S(1)}, u32[]{:S(2)}, u32[]{:S(2)}) %collective-permute-start) | collective-permute-done | bytes 208928 | tf_op jit(solution)/shard_map/ppermute | solution.py:572
  23.4 2.0 %start.1 = (f32[4,192,256]{2,1,0:T(8,128)S(1)}, f32[4,144,128]{2,1,0:T(8,128)S(1)}, f32[4,144,128]{2,1,0:T(8,128)S(1)}, f32[4,144,128]{2,1,0:T(8,128)S(1)}, f32[4,144,128]{2,1,0:T(8,128)S(1)}) custom-call(f32[16,128]{1,0:T(8,128)S(1)} %copy-done.3, f32[4,192,128]{2,1,0:T(8,128)S(1)} %copy-done.6, f32[4,8,3072]{2,1,0:T(8,128)S(1)} %collective-permute-done.1.came, ...), custom_call_target="tpu_custom_call" | custom-call | flops 100000000 | bytes 4000000 | tf_op jit(solution)/shard_map/start/pallas_call | solution.py:557
  25.6 1.3 collective-permute-done.3.came
  26.9 2.4 %collective-permute-start.4 = (f32[136,128]{1,0:T(8,128)S(1)}, f32[136,128]{1,0:T(8,128)S(1)}, u32[]{:S(2)}, u32[]{:S(2)}) collective-permute-start(f32[136,128]{1,0:T(8,128)S(1)} %pair.4.half.mine), channel_id=1, source_target_pairs={{0,7},{1,2},{2,1},{3,4},{4,3},{5,6},{6,5},{7,0},{8,15},{9,10},{10,... | collective-permute-start | bytes 208904 | tf_op jit(solution)/shard_map/ppermute | solution.py:572
  29.9 1.9 %collective-permute-start.9 = (f32[4,144,128]{2,1,0:T(8,128)S(1)}, f32[4,144,128]{2,1,0:T(8,128)S(1)}, u32[]{:S(2)}, u32[]{:S(2)}) collective-permute-start(f32[4,144,128]{2,1,0:T(8,128)S(1)} %get-tuple-element.76), channel_id=1, source_target_pairs={{0,16},{1,17},{2,18},{3,19},{4,20},{5,21},{6,22},{7,23},{8,24},{9,... | collective-permute-start | bytes 884744 | tf_op jit(solution)/shard_map/ppermute | solution.py:572
  31.9 4.1 %collective-permute-start.10 = (f32[4,144,128]{2,1,0:T(8,128)S(1)}, f32[4,144,128]{2,1,0:T(8,128)S(1)}, u32[]{:S(2)}, u32[]{:S(2)}) collective-permute-start(f32[4,144,128]{2,1,0:T(8,128)S(1)} %get-tuple-element.77), channel_id=1, source_target_pairs={{0,48},{1,49},{2,50},{3,51},{4,52},{5,53},{6,54},{7,55},{8,56},{9,... | collective-permute-start | bytes 884744 | tf_op jit(solution)/shard_map/ppermute | solution.py:572
  36.0 1.4 local.4.acc
  37.9 1.3 collective-permute-done.8.outer
  39.2 1.9 %collective-permute-start.5 = (f32[72,128]{1,0:T(8,128)S(1)}, f32[72,128]{1,0:T(8,128)S(1)}, u32[]{:S(2)}, u32[]{:S(2)}) collective-permute-start(f32[72,128]{1,0:T(8,128)S(1)} %get-tuple-element.73.high), channel_id=1, source_target_pairs={{0,16},{1,17},{2,18},{3,19},{4,20},{5,21},{6,22},{7,23},{8,24},{9,... | collective-permute-start | bytes 110600 | tf_op jit(solution)/shard_map/ppermute | solution.py:572
  42.2 1.6 %halo.4.acc = f32[4,192,256]{2,1,0:T(8,128)S(1)} custom-call(f32[16,128]{1,0:T(8,128)S(1)} %copy-done.3, f32[4,144,128]{2,1,0:T(8,128)S(1)} %collective-permute-done.7.inner, f32[4,144,128]{2,1,0:T(8,128)S(1)} %collective-permute-done.8.outer, f32[4,144,128]{2,1,0:T(8,128)S(1)} %collective-permute-done.9.xl, f32[4,144,128]{2,1,0:T(8,128)S(1)} %collective-permute-done.10.xh, ...), custom_call_target="tpu_custom_call" | custom-call | flops 100000000 | bytes 4000000 | tf_op jit(solution)/shard_map/halo/pallas_call | solution.py:557
  43.8 1.4 %collective-permute-done.5.below = f32[72,128]{1,0:T(8,128)S(1)} collective-permute-done((f32[72,128]{1,0:T(8,128)S(1)}, f32[72,128]{1,0:T(8,128)S(1)}, u32[]{:S(2)}, u32[]{:S(2)}) %collective-permute-start.5) | collective-permute-done | bytes 36896 | tf_op jit(solution)/shard_map/ppermute | solution.py:572
  45.3 4.0 %collective-permute-done.2.came = f32[4,448,128]{2,1,0:T(8,128)S(1)} collective-permute-done((f32[4,448,128]{2,1,0:T(8,128)S(1)}, f32[4,448,128]{2,1,0:T(8,128)S(1)}, u32[]{:S(2)}, u32[]{:S(2)}) %collective-permute-start.2) | collective-permute-done | bytes 917536 | tf_op jit(solution)/shard_map/ppermute | solution.py:572
  49.4 2.0 %prepare.1 = (f32[4,192,896]{2,1,0:T(8,128)S(1)}, s32[4,896]{1,0:T(4,128)S(1)}) custom-call(s32[8,512]{1,0:T(8,128)S(1)} %copy-done.9, f32[408,128]{1,0:T(8,128)S(1)} %collective-permute-done.note_came, f32[4,448,128]{2,1,0:T(8,128)S(1)} %bitcast.15, f32[4,448,128]{2,1,0:T(8,128)S(1)} %collective-permute-done.2.came), custom_call_target="tpu_custom_call" | custom-call | flops 100000000 | bytes 4000000 | tf_op jit(solution)/shard_map/prepare/pallas_call | solution.py:557
  51.4 3.4 %update.3 = (f32[4,192,256]{2,1,0:T(8,128)S(1)}, f32[4,144,128]{2,1,0:T(8,128)S(1)}, f32[4,144,128]{2,1,0:T(8,128)S(1)}, f32[4,144,128]{2,1,0:T(8,128)S(1)}, f32[4,144,128]{2,1,0:T(8,128)S(1)}) custom-call(f32[16,128]{1,0:T(8,128)S(1)} %copy-done.3, s32[4,896]{1,0:T(4,128)S(1)} %get-tuple-element.65.index, f32[4,192,256]{2,1,0:T(8,128)S(1)} %get-tuple-element.79.acc, ...), custom_call_target="tpu_custom_call" | custom-call | flops 100000000 | bytes 4000000 | tf_op jit(solution)/shard_map/update/pallas_call | solution.py:557
  54.8 1.7 %collective-permute-start.17 = (f32[4,144,128]{2,1,0:T(8,128)S(1)}, f32[4,144,128]{2,1,0:T(8,128)S(1)}, u32[]{:S(2)}, u32[]{:S(2)}) collective-permute-start(f32[4,144,128]{2,1,0:T(8,128)S(1)} %get-tuple-element.87), channel_id=1, source_target_pairs={{0,7},{1,2},{2,1},{3,4},{4,3},{5,6},{6,5},{7,0},{8,15},{9,10},{10,... | collective-permute-start | bytes 884744 | tf_op jit(solution)/shard_map/ppermute | solution.py:572
  56.5 1.9 %collective-permute-start.18 = (f32[4,144,128]{2,1,0:T(8,128)S(1)}, f32[4,144,128]{2,1,0:T(8,128)S(1)}, u32[]{:S(2)}, u32[]{:S(2)}) collective-permute-start(f32[4,144,128]{2,1,0:T(8,128)S(1)} %get-tuple-element.88), channel_id=1, source_target_pairs={{0,16},{1,17},{2,18},{3,19},{4,20},{5,21},{6,22},{7,23},{8,24},{9,... | collective-permute-start | bytes 884744 | tf_op jit(solution)/shard_map/ppermute | solution.py:572
  58.5 2.1 %collective-permute-start.19 = (f32[4,144,128]{2,1,0:T(8,128)S(1)}, f32[4,144,128]{2,1,0:T(8,128)S(1)}, u32[]{:S(2)}, u32[]{:S(2)}) collective-permute-start(f32[4,144,128]{2,1,0:T(8,128)S(1)} %get-tuple-element.89), channel_id=1, source_target_pairs={{0,48},{1,49},{2,50},{3,51},{4,52},{5,53},{6,54},{7,55},{8,56},{9,... | collective-permute-start | bytes 884744 | tf_op jit(solution)/shard_map/ppermute | solution.py:572
  60.6 2.3 %table.3 = f32[192,128]{1,0:T(8,128)S(1)} custom-call(s32[4,896]{1,0:T(4,128)S(1)} %get-tuple-element.65.index, f32[4,192,256]{2,1,0:T(8,128)S(1)} %get-tuple-element.82.field.before, f32[4,192,896]{2,1,0:T(8,128)S(1)} %get-tuple-element.81.placed), custom_call_target="tpu_custom_call" | custom-call | flops 100000000 | bytes 4000000 | tf_op jit(solution)/shard_map/table/pallas_call | solution.py:557
  63.0 1.3 collective-permute-done.12.came
  65.1 1.4 local.5.acc
  66.5 3.0 %collective-permute-done.13.came = f32[128,128]{1,0:T(8,128)S(1)} collective-permute-done((f32[128,128]{1,0:T(8,128)S(1)}, f32[128,128]{1,0:T(8,128)S(1)}, u32[]{:S(2)}, u32[]{:S(2)}) %collective-permute-start.13) | collective-permute-done | bytes 65568 | tf_op jit(solution)/shard_map/ppermute | solution.py:572
  69.5 2.1 %collective-permute-start.15 = (f32[64,128]{1,0:T(8,128)S(1)}, f32[64,128]{1,0:T(8,128)S(1)}, u32[]{:S(2)}, u32[]{:S(2)}) collective-permute-start(f32[64,128]{1,0:T(8,128)S(1)} %get-tuple-element.83.low), channel_id=1, source_target_pairs={{0,48},{1,49},{2,50},{3,51},{4,52},{5,53},{6,54},{7,55},{8,56},{9,... | collective-permute-start | bytes 98312 | tf_op jit(solution)/shard_map/ppermute | solution.py:572
  71.7 1.6 %halo.5.acc = f32[4,192,256]{2,1,0:T(8,128)S(1)} custom-call(f32[16,128]{1,0:T(8,128)S(1)} %copy-done.3, f32[4,144,128]{2,1,0:T(8,128)S(1)} %collective-permute-done.16.inner, f32[4,144,128]{2,1,0:T(8,128)S(1)} %collective-permute-done.17.outer, f32[4,144,128]{2,1,0:T(8,128)S(1)} %collective-permute-done.18.xl, ...), custom_call_target="tpu_custom_call" | custom-call | flops 100000000 | bytes 4000000 | tf_op jit(solution)/shard_map/halo/pallas_call | solution.py:557
  73.5 3.3 %collective-permute-done.14.below = f32[64,128]{1,0:T(8,128)S(1)} collective-permute-done((f32[64,128]{1,0:T(8,128)S(1)}, f32[64,128]{1,0:T(8,128)S(1)}, u32[]{:S(2)}, u32[]{:S(2)}) %collective-permute-start.14) | collective-permute-done | bytes 32800 | tf_op jit(solution)/shard_map/ppermute | solution.py:572
  78.1 3.4 %update.4 = (f32[4,192,256]{2,1,0:T(8,128)S(1)}, f32[4,144,128]{2,1,0:T(8,128)S(1)}, f32[4,144,128]{2,1,0:T(8,128)S(1)}, f32[4,144,128]{2,1,0:T(8,128)S(1)}, f32[4,144,128]{2,1,0:T(8,128)S(1)}) custom-call(f32[16,128]{1,0:T(8,128)S(1)} %copy-done.3, s32[4,896]{1,0:T(4,128)S(1)} %get-tuple-element.65.index, f32[4,192,256]{2,1,0:T(8,128)S(1)} %get-tuple-element.91.acc, ...), custom_call_target="tpu_custom_call" | custom-call | flops 100000000 | bytes 4000000 | tf_op jit(solution)/shard_map/update/pallas_call | solution.py:557
  81.8 3.2 %collective-permute-start.28 = (f32[4,144,128]{2,1,0:T(8,128)S(1)}, f32[4,144,128]{2,1,0:T(8,128)S(1)}, u32[]{:S(2)}, u32[]{:S(2)}) collective-permute-start(f32[4,144,128]{2,1,0:T(8,128)S(1)} %get-tuple-element.99), channel_id=1, source_target_pairs={{0,48},{1,49},{2,50},{3,51},{4,52},{5,53},{6,54},{7,55},{8,56},{9,... | collective-permute-start | bytes 884744 | tf_op jit(solution)/shard_map/ppermute | solution.py:572
  85.0 2.3 %table.4 = f32[192,128]{1,0:T(8,128)S(1)} custom-call(s32[4,896]{1,0:T(4,128)S(1)} %get-tuple-element.65.index, f32[4,192,256]{2,1,0:T(8,128)S(1)} %get-tuple-element.93.field.before, f32[4,192,896]{2,1,0:T(8,128)S(1)} %get-tuple-element.81.placed), custom_call_target="tpu_custom_call" | custom-call | flops 100000000 | bytes 4000000 | tf_op jit(solution)/shard_map/table/pallas_call | solution.py:557
  88.7 2.3 %collective-permute-start.22 = (f32[128,128]{1,0:T(8,128)S(1)}, f32[128,128]{1,0:T(8,128)S(1)}, u32[]{:S(2)}, u32[]{:S(2)}) collective-permute-start(f32[128,128]{1,0:T(8,128)S(1)} %pair.6.half.mine), channel_id=1, source_target_pairs={{0,7},{1,2},{2,1},{3,4},{4,3},{5,6},{6,5},{7,0},{8,15},{9,10},{10,... | collective-permute-start | bytes 196616 | tf_op jit(solution)/shard_map/ppermute | solution.py:572
  91.0 1.4 local.6.acc
  92.4 1.5 %collective-permute-done.22.came = f32[128,128]{1,0:T(8,128)S(1)} collective-permute-done((f32[128,128]{1,0:T(8,128)S(1)}, f32[128,128]{1,0:T(8,128)S(1)}, u32[]{:S(2)}, u32[]{:S(2)}) %collective-permute-start.22) | collective-permute-done | bytes 65568 | tf_op jit(solution)/shard_map/ppermute | solution.py:572
  94.1 2.0 %collective-permute-start.23 = (f32[64,128]{1,0:T(8,128)S(1)}, f32[64,128]{1,0:T(8,128)S(1)}, u32[]{:S(2)}, u32[]{:S(2)}) collective-permute-start(f32[64,128]{1,0:T(8,128)S(1)} %get-tuple-element.95.high), channel_id=1, source_target_pairs={{0,16},{1,17},{2,18},{3,19},{4,20},{5,21},{6,22},{7,23},{8,24},{9,... | collective-permute-start | bytes 98312 | tf_op jit(solution)/shard_map/ppermute | solution.py:572
  96.1 1.6 %halo.6.acc = f32[4,192,256]{2,1,0:T(8,128)S(1)} custom-call(f32[16,128]{1,0:T(8,128)S(1)} %copy-done.3, f32[4,144,128]{2,1,0:T(8,128)S(1)} %collective-permute-done.25.inner, f32[4,144,128]{2,1,0:T(8,128)S(1)} %collective-permute-done.26.outer, f32[4,144,128]{2,1,0:T(8,128)S(1)} %collective-permute-done.27.xl, ...), custom_call_target="tpu_custom_call" | custom-call | flops 100000000 | bytes 4000000 | tf_op jit(solution)/shard_map/halo/pallas_call | solution.py:557
  98.0 1.3 collective-permute-done.23.below
  100.6 3.3 %update.5 = (f32[4,192,256]{2,1,0:T(8,128)S(1)}, f32[4,144,128]{2,1,0:T(8,128)S(1)}, f32[4,144,128]{2,1,0:T(8,128)S(1)}, f32[4,144,128]{2,1,0:T(8,128)S(1)}, f32[4,144,128]{2,1,0:T(8,128)S(1)}) custom-call(f32[16,128]{1,0:T(8,128)S(1)} %copy-done.3, s32[4,896]{1,0:T(4,128)S(1)} %get-tuple-element.65.index, f32[4,192,256]{2,1,0:T(8,128)S(1)} %get-tuple-element.101.acc, ...), custom_call_target="tpu_custom_call" | custom-call | flops 100000000 | bytes 4000000 | tf_op jit(solution)/shard_map/update/pallas_call | solution.py:557
  106.0 2.6 %collective-permute-start.37 = (f32[4,144,128]{2,1,0:T(8,128)S(1)}, f32[4,144,128]{2,1,0:T(8,128)S(1)}, u32[]{:S(2)}, u32[]{:S(2)}) collective-permute-start(f32[4,144,128]{2,1,0:T(8,128)S(1)} %get-tuple-element.109), channel_id=1, source_target_pairs={{0,48},{1,49},{2,50},{3,51},{4,52},{5,53},{6,54},{7,55},{8,56},{9,... | collective-permute-start | bytes 884744 | tf_op jit(solution)/shard_map/ppermute | solution.py:572
  108.6 2.3 %table.5 = f32[192,128]{1,0:T(8,128)S(1)} custom-call(s32[4,896]{1,0:T(4,128)S(1)} %get-tuple-element.65.index, f32[4,192,256]{2,1,0:T(8,128)S(1)} %get-tuple-element.103.field, f32[4,192,896]{2,1,0:T(8,128)S(1)} %get-tuple-element.81.placed), custom_call_target="tpu_custom_call" | custom-call | flops 100000000 | bytes 4000000 | tf_op jit(solution)/shard_map/table/pallas_call | solution.py:557
  113.6 1.4 local.7.acc
  115.0 2.4 %collective-permute-done.31.came = f32[128,128]{1,0:T(8,128)S(1)} collective-permute-done((f32[128,128]{1,0:T(8,128)S(1)}, f32[128,128]{1,0:T(8,128)S(1)}, u32[]{:S(2)}, u32[]{:S(2)}) %collective-permute-start.31) | collective-permute-done | bytes 65568 | tf_op jit(solution)/shard_map/ppermute | solution.py:572
  117.6 2.0 %collective-permute-start.32 = (f32[64,128]{1,0:T(8,128)S(1)}, f32[64,128]{1,0:T(8,128)S(1)}, u32[]{:S(2)}, u32[]{:S(2)}) collective-permute-start(f32[64,128]{1,0:T(8,128)S(1)} %get-tuple-element.105.high), channel_id=1, source_target_pairs={{0,16},{1,17},{2,18},{3,19},{4,20},{5,21},{6,22},{7,23},{8,24},{9,... | collective-permute-start | bytes 98312 | tf_op jit(solution)/shard_map/ppermute | solution.py:572
  119.6 1.6 %halo.7.acc = f32[4,192,256]{2,1,0:T(8,128)S(1)} custom-call(f32[16,128]{1,0:T(8,128)S(1)} %copy-done.3, f32[4,144,128]{2,1,0:T(8,128)S(1)} %collective-permute-done.34.inner, f32[4,144,128]{2,1,0:T(8,128)S(1)} %collective-permute-done.35.outer, f32[4,144,128]{2,1,0:T(8,128)S(1)} %collective-permute-done.36.xl, ...), custom_call_target="tpu_custom_call" | custom-call | flops 100000000 | bytes 4000000 | tf_op jit(solution)/shard_map/halo/pallas_call | solution.py:557
  121.5 1.3 collective-permute-done.32.below
  124.3 3.1 %finish.1 = (f32[4,8,3072]{2,1,0:T(8,128)S(1)}, f32[4,8,3072]{2,1,0:T(8,128)S(1)}, f32[4,192,256]{2,1,0:T(8,128)S(1)}) custom-call(f32[16,128]{1,0:T(8,128)S(1)} %copy-done.3, s32[4,896]{1,0:T(4,128)S(1)} %get-tuple-element.65.index, f32[4,192,256]{2,1,0:T(8,128)S(1)} %get-tuple-element.111.acc, f32[128,128]{1,0:T(8,128)S(1)} %get-tuple-element.112.mine, ...), custom_call_target="tpu_custom_call" | custom-call | flops 100000000 | bytes 4000000 | tf_op jit(solution)/shard_map/finish/pallas_call | solution.py:557
  128.8 2.6 %collective-permute-start.40 = (f32[8,1536]{1,0:T(8,128)S(1)}, f32[8,1536]{1,0:T(8,128)S(1)}, u32[]{:S(2)}, u32[]{:S(2)}) collective-permute-start(f32[8,1536]{1,0:T(8,128)S(1)} %get-tuple-element.115), channel_id=1, source_target_pairs={{0,8},{1,9},{2,10},{3,11},{4,12},{5,13},{6,14},{7,15},{8,0},{9,1},... | collective-permute-start | bytes 147464 | tf_op jit(solution)/shard_map/ppermute | solution.py:572
  131.4 2.6 %collective-permute-start.41 = (f32[8,1536]{1,0:T(8,128)S(1)}, f32[8,1536]{1,0:T(8,128)S(1)}, u32[]{:S(2)}, u32[]{:S(2)}) collective-permute-start(f32[8,1536]{1,0:T(8,128)S(1)} %get-tuple-element.116), channel_id=1, source_target_pairs={{0,64},{64,0},{1,65},{65,1},{2,66},{66,2},{3,67},{67,3},{4,68},{68... | collective-permute-start | bytes 147464 | tf_op jit(solution)/shard_map/ppermute | solution.py:797
  134.1 1.3 collective-permute-start.42
  135.4 6.9 %collective-permute-done.40.b = f32[8,1536]{1,0:T(8,128)S(1)} collective-permute-done((f32[8,1536]{1,0:T(8,128)S(1)}, f32[8,1536]{1,0:T(8,128)S(1)}, u32[]{:S(2)}, u32[]{:S(2)}) %collective-permute-start.40) | collective-permute-done | bytes 49184 | tf_op jit(solution)/shard_map/ppermute | solution.py:572
  (97 shorter events, 20.0 us)
Async XLA Ops:
  0.6 14.3 %copy-start.1 = (f32[1,4,448,128]{3,2,1,0:T(8,128)S(1)}, f32[1,4,448,128]{3,2,1,0:T(8,128)}, u32[]{:S(2)}) copy-start(f32[1,4,448,128]{3,2,1,0:T(8,128)} %param.18) | copy-start | bytes 2752516
  1.8 21.3 %collective-permute-start.1 = (f32[4,8,3072]{2,1,0:T(8,128)S(1)}, f32[4,8,3072]{2,1,0:T(8,128)S(1)}, u32[]{:S(2)}, u32[]{:S(2)}) collective-permute-start(f32[4,8,3072]{2,1,0:T(8,128)S(1)} %dynamic-slice_bitcast_fusion), channel_id=1, source_target_pairs={{0,8},{1,9},{2,10},{3,11},{4,12},{5,13},{6,14},{7,15},{8,0},{9,1},... | collective-permute-start | bytes 1179656 | tf_op jit(solution)/shard_map/ppermute | solution.py:572
  7.1 16.3 %copy-start.5 = (bf16[256,256]{1,0:T(8,128)(2,1)S(1)}, bf16[256,256]{1,0:T(8,128)(2,1)}, u32[]{:S(2)}) copy-start(bf16[256,256]{1,0:T(8,128)(2,1)} %constant.57.clone.edge.rest_0_) | copy-start | bytes 393220
  14.6 8.4 %collective-permute-start = (f32[408,128]{1,0:T(8,128)}, f32[408,128]{1,0:T(8,128)S(1)}, u32[]{:S(2)}, u32[]{:S(2)}) collective-permute-start(f32[408,128]{1,0:T(8,128)} %get-tuple-element.64), channel_id=1, source_target_pairs={{0,8},{1,9},{2,10},{3,11},{4,12},{5,13},{6,14},{7,15},{8,0},{9,1},... | collective-permute-start | bytes 626696 | tf_op jit(solution)/shard_map/ppermute | solution.py:572
  15.0 21.0 %copy-start.2 = (bf16[768,256]{1,0:T(8,128)(2,1)S(1)}, bf16[768,256]{1,0:T(8,128)(2,1)}, u32[]{:S(2)}) copy-start(bf16[768,256]{1,0:T(8,128)(2,1)} %constant.54.clone.own_w) | copy-start | bytes 1179652
  15.0 21.0 %copy-start.4 = (bf16[192,576]{1,0:T(8,128)(2,1)S(1)}, bf16[192,576]{1,0:T(8,128)(2,1)}, u32[]{:S(2)}) copy-start(bf16[192,576]{1,0:T(8,128)(2,1)} %constant.56.clone.ring_w) | copy-start | bytes 663556
  23.0 26.3 %collective-permute-start.2 = (f32[4,448,128]{2,1,0:T(8,128)S(1)}, f32[4,448,128]{2,1,0:T(8,128)S(1)}, u32[]{:S(2)}, u32[]{:S(2)}) collective-permute-start(f32[4,448,128]{2,1,0:T(8,128)S(1)} %gate.1), channel_id=1, source_target_pairs={{0,8},{1,9},{2,10},{3,11},{4,12},{5,13},{6,14},{7,15},{8,0},{9,1},... | collective-permute-start | bytes 2752520 | tf_op jit(solution)/shard_map/ppermute | solution.py:572
  25.4 16.7 %copy-start = (bf16[1536,256]{1,0:T(8,128)(2,1)S(1)}, bf16[1536,256]{1,0:T(8,128)(2,1)}, u32[]{:S(2)}) copy-start(bf16[1536,256]{1,0:T(8,128)(2,1)} %constant.55.clone.halo_w) | copy-start | bytes 2359300
  25.5 1.4 collective-permute-start.3
  26.9 5.1 %collective-permute-start.4 = (f32[136,128]{1,0:T(8,128)S(1)}, f32[136,128]{1,0:T(8,128)S(1)}, u32[]{:S(2)}, u32[]{:S(2)}) collective-permute-start(f32[136,128]{1,0:T(8,128)S(1)} %pair.4.half.mine), channel_id=1, source_target_pairs={{0,7},{1,2},{2,1},{3,4},{4,3},{5,6},{6,5},{7,0},{8,15},{9,10},{10,... | collective-permute-start | bytes 208904 | tf_op jit(solution)/shard_map/ppermute | solution.py:572
  29.2 8.2 %collective-permute-start.7 = (f32[4,144,128]{2,1,0:T(8,128)S(1)}, f32[4,144,128]{2,1,0:T(8,128)S(1)}, u32[]{:S(2)}, u32[]{:S(2)}) collective-permute-start(f32[4,144,128]{2,1,0:T(8,128)S(1)} %get-tuple-element.74), channel_id=1, source_target_pairs={{0,1},{1,0},{2,3},{3,2},{4,5},{5,4},{6,7},{7,6},{8,9},{9,8},{10,11... | collective-permute-start | bytes 884744 | tf_op jit(solution)/shard_map/ppermute | solution.py:572
  29.2 10.0 %collective-permute-start.8 = (f32[4,144,128]{2,1,0:T(8,128)S(1)}, f32[4,144,128]{2,1,0:T(8,128)S(1)}, u32[]{:S(2)}, u32[]{:S(2)}) collective-permute-start(f32[4,144,128]{2,1,0:T(8,128)S(1)} %get-tuple-element.75), channel_id=1, source_target_pairs={{0,7},{1,2},{2,1},{3,4},{4,3},{5,6},{6,5},{7,0},{8,15},{9,10},{10,... | collective-permute-start | bytes 884744 | tf_op jit(solution)/shard_map/ppermute | solution.py:572
  29.9 11.6 %collective-permute-start.9 = (f32[4,144,128]{2,1,0:T(8,128)S(1)}, f32[4,144,128]{2,1,0:T(8,128)S(1)}, u32[]{:S(2)}, u32[]{:S(2)}) collective-permute-start(f32[4,144,128]{2,1,0:T(8,128)S(1)} %get-tuple-element.76), channel_id=1, source_target_pairs={{0,16},{1,17},{2,18},{3,19},{4,20},{5,21},{6,22},{7,23},{8,24},{9,... | collective-permute-start | bytes 884744 | tf_op jit(solution)/shard_map/ppermute | solution.py:572
  31.9 10.2 %collective-permute-start.10 = (f32[4,144,128]{2,1,0:T(8,128)S(1)}, f32[4,144,128]{2,1,0:T(8,128)S(1)}, u32[]{:S(2)}, u32[]{:S(2)}) collective-permute-start(f32[4,144,128]{2,1,0:T(8,128)S(1)} %get-tuple-element.77), channel_id=1, source_target_pairs={{0,48},{1,49},{2,50},{3,51},{4,52},{5,53},{6,54},{7,55},{8,56},{9,... | collective-permute-start | bytes 884744 | tf_op jit(solution)/shard_map/ppermute | solution.py:572
  37.5 6.3 %collective-permute-start.6 = (f32[72,128]{1,0:T(8,128)S(1)}, f32[72,128]{1,0:T(8,128)S(1)}, u32[]{:S(2)}, u32[]{:S(2)}) collective-permute-start(f32[72,128]{1,0:T(8,128)S(1)} %get-tuple-element.72.low), channel_id=1, source_target_pairs={{0,48},{1,49},{2,50},{3,51},{4,52},{5,53},{6,54},{7,55},{8,56},{9,... | collective-permute-start | bytes 110600 | tf_op jit(solution)/shard_map/ppermute | solution.py:572
  39.2 6.0 %collective-permute-start.5 = (f32[72,128]{1,0:T(8,128)S(1)}, f32[72,128]{1,0:T(8,128)S(1)}, u32[]{:S(2)}, u32[]{:S(2)}) collective-permute-start(f32[72,128]{1,0:T(8,128)S(1)} %get-tuple-element.73.high), channel_id=1, source_target_pairs={{0,16},{1,17},{2,18},{3,19},{4,20},{5,21},{6,22},{7,23},{8,24},{9,... | collective-permute-start | bytes 110600 | tf_op jit(solution)/shard_map/ppermute | solution.py:572
  45.2 6.1 %collective-permute-start.11 = (f32[128,128]{1,0:T(8,128)S(1)}, f32[128,128]{1,0:T(8,128)S(1)}, u32[]{:S(2)}, u32[]{:S(2)}) collective-permute-start(f32[128,128]{1,0:T(8,128)S(1)} %get-tuple-element.80.mine), channel_id=1, source_target_pairs={{0,1},{1,0},{2,3},{3,2},{4,5},{5,4},{6,7},{7,6},{8,9},{9,8},{10,11... | collective-permute-start | bytes 196616 | tf_op jit(solution)/shard_map/ppermute | solution.py:572
  54.7 16.9 %collective-permute-start.16 = (f32[4,144,128]{2,1,0:T(8,128)S(1)}, f32[4,144,128]{2,1,0:T(8,128)S(1)}, u32[]{:S(2)}, u32[]{:S(2)}) collective-permute-start(f32[4,144,128]{2,1,0:T(8,128)S(1)} %get-tuple-element.86), channel_id=1, source_target_pairs={{0,1},{1,0},{2,3},{3,2},{4,5},{5,4},{6,7},{7,6},{8,9},{9,8},{10,11... | collective-permute-start | bytes 884744 | tf_op jit(solution)/shard_map/ppermute | solution.py:572
  54.8 16.8 %collective-permute-start.17 = (f32[4,144,128]{2,1,0:T(8,128)S(1)}, f32[4,144,128]{2,1,0:T(8,128)S(1)}, u32[]{:S(2)}, u32[]{:S(2)}) collective-permute-start(f32[4,144,128]{2,1,0:T(8,128)S(1)} %get-tuple-element.87), channel_id=1, source_target_pairs={{0,7},{1,2},{2,1},{3,4},{4,3},{5,6},{6,5},{7,0},{8,15},{9,10},{10,... | collective-permute-start | bytes 884744 | tf_op jit(solution)/shard_map/ppermute | solution.py:572
  56.5 15.1 %collective-permute-start.18 = (f32[4,144,128]{2,1,0:T(8,128)S(1)}, f32[4,144,128]{2,1,0:T(8,128)S(1)}, u32[]{:S(2)}, u32[]{:S(2)}) collective-permute-start(f32[4,144,128]{2,1,0:T(8,128)S(1)} %get-tuple-element.88), channel_id=1, source_target_pairs={{0,16},{1,17},{2,18},{3,19},{4,20},{5,21},{6,22},{7,23},{8,24},{9,... | collective-permute-start | bytes 884744 | tf_op jit(solution)/shard_map/ppermute | solution.py:572
  58.5 13.2 %collective-permute-start.19 = (f32[4,144,128]{2,1,0:T(8,128)S(1)}, f32[4,144,128]{2,1,0:T(8,128)S(1)}, u32[]{:S(2)}, u32[]{:S(2)}) collective-permute-start(f32[4,144,128]{2,1,0:T(8,128)S(1)} %get-tuple-element.89), channel_id=1, source_target_pairs={{0,48},{1,49},{2,50},{3,51},{4,52},{5,53},{6,54},{7,55},{8,56},{9,... | collective-permute-start | bytes 884744 | tf_op jit(solution)/shard_map/ppermute | solution.py:572
  62.9 1.4 collective-permute-start.12
  64.3 5.2 %collective-permute-start.13 = (f32[128,128]{1,0:T(8,128)S(1)}, f32[128,128]{1,0:T(8,128)S(1)}, u32[]{:S(2)}, u32[]{:S(2)}) collective-permute-start(f32[128,128]{1,0:T(8,128)S(1)} %pair.5.half.mine), channel_id=1, source_target_pairs={{0,7},{1,2},{2,1},{3,4},{4,3},{5,6},{6,5},{7,0},{8,15},{9,10},{10,... | collective-permute-start | bytes 196616 | tf_op jit(solution)/shard_map/ppermute | solution.py:572
  69.5 4.0 %collective-permute-start.15 = (f32[64,128]{1,0:T(8,128)S(1)}, f32[64,128]{1,0:T(8,128)S(1)}, u32[]{:S(2)}, u32[]{:S(2)}) collective-permute-start(f32[64,128]{1,0:T(8,128)S(1)} %get-tuple-element.83.low), channel_id=1, source_target_pairs={{0,48},{1,49},{2,50},{3,51},{4,52},{5,53},{6,54},{7,55},{8,56},{9,... | collective-permute-start | bytes 98312 | tf_op jit(solution)/shard_map/ppermute | solution.py:572
  71.6 5.1 %collective-permute-start.14 = (f32[64,128]{1,0:T(8,128)S(1)}, f32[64,128]{1,0:T(8,128)S(1)}, u32[]{:S(2)}, u32[]{:S(2)}) collective-permute-start(f32[64,128]{1,0:T(8,128)S(1)} %get-tuple-element.84.high), channel_id=1, source_target_pairs={{0,16},{1,17},{2,18},{3,19},{4,20},{5,21},{6,22},{7,23},{8,24},{9,... | collective-permute-start | bytes 98312 | tf_op jit(solution)/shard_map/ppermute | solution.py:572
  76.8 1.3 collective-permute-start.20
  81.5 12.6 %collective-permute-start.25 = (f32[4,144,128]{2,1,0:T(8,128)S(1)}, f32[4,144,128]{2,1,0:T(8,128)S(1)}, u32[]{:S(2)}, u32[]{:S(2)}) collective-permute-start(f32[4,144,128]{2,1,0:T(8,128)S(1)} %get-tuple-element.96), channel_id=1, source_target_pairs={{0,1},{1,0},{2,3},{3,2},{4,5},{5,4},{6,7},{7,6},{8,9},{9,8},{10,11... | collective-permute-start | bytes 884744 | tf_op jit(solution)/shard_map/ppermute | solution.py:572
  81.7 14.4 %collective-permute-start.26 = (f32[4,144,128]{2,1,0:T(8,128)S(1)}, f32[4,144,128]{2,1,0:T(8,128)S(1)}, u32[]{:S(2)}, u32[]{:S(2)}) collective-permute-start(f32[4,144,128]{2,1,0:T(8,128)S(1)} %get-tuple-element.97), channel_id=1, source_target_pairs={{0,7},{1,2},{2,1},{3,4},{4,3},{5,6},{6,5},{7,0},{8,15},{9,10},{10,... | collective-permute-start | bytes 884744 | tf_op jit(solution)/shard_map/ppermute | solution.py:572
  81.7 14.4 %collective-permute-start.27 = (f32[4,144,128]{2,1,0:T(8,128)S(1)}, f32[4,144,128]{2,1,0:T(8,128)S(1)}, u32[]{:S(2)}, u32[]{:S(2)}) collective-permute-start(f32[4,144,128]{2,1,0:T(8,128)S(1)} %get-tuple-element.98), channel_id=1, source_target_pairs={{0,16},{1,17},{2,18},{3,19},{4,20},{5,21},{6,22},{7,23},{8,24},{9,... | collective-permute-start | bytes 884744 | tf_op jit(solution)/shard_map/ppermute | solution.py:572
  81.8 14.3 %collective-permute-start.28 = (f32[4,144,128]{2,1,0:T(8,128)S(1)}, f32[4,144,128]{2,1,0:T(8,128)S(1)}, u32[]{:S(2)}, u32[]{:S(2)}) collective-permute-start(f32[4,144,128]{2,1,0:T(8,128)S(1)} %get-tuple-element.99), channel_id=1, source_target_pairs={{0,48},{1,49},{2,50},{3,51},{4,52},{5,53},{6,54},{7,55},{8,56},{9,... | collective-permute-start | bytes 884744 | tf_op jit(solution)/shard_map/ppermute | solution.py:572
  87.3 1.4 collective-permute-start.21
  88.7 5.3 %collective-permute-start.22 = (f32[128,128]{1,0:T(8,128)S(1)}, f32[128,128]{1,0:T(8,128)S(1)}, u32[]{:S(2)}, u32[]{:S(2)}) collective-permute-start(f32[128,128]{1,0:T(8,128)S(1)} %pair.6.half.mine), channel_id=1, source_target_pairs={{0,7},{1,2},{2,1},{3,4},{4,3},{5,6},{6,5},{7,0},{8,15},{9,10},{10,... | collective-permute-start | bytes 196616 | tf_op jit(solution)/shard_map/ppermute | solution.py:572
  94.0 4.0 %collective-permute-start.24 = (f32[64,128]{1,0:T(8,128)S(1)}, f32[64,128]{1,0:T(8,128)S(1)}, u32[]{:S(2)}, u32[]{:S(2)}) collective-permute-start(f32[64,128]{1,0:T(8,128)S(1)} %get-tuple-element.94.low), channel_id=1, source_target_pairs={{0,48},{1,49},{2,50},{3,51},{4,52},{5,53},{6,54},{7,55},{8,56},{9,... | collective-permute-start | bytes 98312 | tf_op jit(solution)/shard_map/ppermute | solution.py:572
  94.1 5.2 %collective-permute-start.23 = (f32[64,128]{1,0:T(8,128)S(1)}, f32[64,128]{1,0:T(8,128)S(1)}, u32[]{:S(2)}, u32[]{:S(2)}) collective-permute-start(f32[64,128]{1,0:T(8,128)S(1)} %get-tuple-element.95.high), channel_id=1, source_target_pairs={{0,16},{1,17},{2,18},{3,19},{4,20},{5,21},{6,22},{7,23},{8,24},{9,... | collective-permute-start | bytes 98312 | tf_op jit(solution)/shard_map/ppermute | solution.py:572
  99.3 1.3 collective-permute-start.29
  104.0 13.6 %collective-permute-start.34 = (f32[4,144,128]{2,1,0:T(8,128)S(1)}, f32[4,144,128]{2,1,0:T(8,128)S(1)}, u32[]{:S(2)}, u32[]{:S(2)}) collective-permute-start(f32[4,144,128]{2,1,0:T(8,128)S(1)} %get-tuple-element.106), channel_id=1, source_target_pairs={{0,1},{1,0},{2,3},{3,2},{4,5},{5,4},{6,7},{7,6},{8,9},{9,8},{10,11... | collective-permute-start | bytes 884744 | tf_op jit(solution)/shard_map/ppermute | solution.py:572
  104.2 15.4 %collective-permute-start.35 = (f32[4,144,128]{2,1,0:T(8,128)S(1)}, f32[4,144,128]{2,1,0:T(8,128)S(1)}, u32[]{:S(2)}, u32[]{:S(2)}) collective-permute-start(f32[4,144,128]{2,1,0:T(8,128)S(1)} %get-tuple-element.107), channel_id=1, source_target_pairs={{0,7},{1,2},{2,1},{3,4},{4,3},{5,6},{6,5},{7,0},{8,15},{9,10},{10,... | collective-permute-start | bytes 884744 | tf_op jit(solution)/shard_map/ppermute | solution.py:572
  105.4 14.2 %collective-permute-start.36 = (f32[4,144,128]{2,1,0:T(8,128)S(1)}, f32[4,144,128]{2,1,0:T(8,128)S(1)}, u32[]{:S(2)}, u32[]{:S(2)}) collective-permute-start(f32[4,144,128]{2,1,0:T(8,128)S(1)} %get-tuple-element.108), channel_id=1, source_target_pairs={{0,16},{1,17},{2,18},{3,19},{4,20},{5,21},{6,22},{7,23},{8,24},{9,... | collective-permute-start | bytes 884744 | tf_op jit(solution)/shard_map/ppermute | solution.py:572
  106.0 13.6 %collective-permute-start.37 = (f32[4,144,128]{2,1,0:T(8,128)S(1)}, f32[4,144,128]{2,1,0:T(8,128)S(1)}, u32[]{:S(2)}, u32[]{:S(2)}) collective-permute-start(f32[4,144,128]{2,1,0:T(8,128)S(1)} %get-tuple-element.109), channel_id=1, source_target_pairs={{0,48},{1,49},{2,50},{3,51},{4,52},{5,53},{6,54},{7,55},{8,56},{9,... | collective-permute-start | bytes 884744 | tf_op jit(solution)/shard_map/ppermute | solution.py:572
  111.0 1.4 collective-permute-start.30
  112.4 5.1 %collective-permute-start.31 = (f32[128,128]{1,0:T(8,128)S(1)}, f32[128,128]{1,0:T(8,128)S(1)}, u32[]{:S(2)}, u32[]{:S(2)}) collective-permute-start(f32[128,128]{1,0:T(8,128)S(1)} %pair.7.half.mine), channel_id=1, source_target_pairs={{0,7},{1,2},{2,1},{3,4},{4,3},{5,6},{6,5},{7,0},{8,15},{9,10},{10,... | collective-permute-start | bytes 196616 | tf_op jit(solution)/shard_map/ppermute | solution.py:572
  117.5 4.0 %collective-permute-start.33 = (f32[64,128]{1,0:T(8,128)S(1)}, f32[64,128]{1,0:T(8,128)S(1)}, u32[]{:S(2)}, u32[]{:S(2)}) collective-permute-start(f32[64,128]{1,0:T(8,128)S(1)} %get-tuple-element.104.low), channel_id=1, source_target_pairs={{0,48},{1,49},{2,50},{3,51},{4,52},{5,53},{6,54},{7,55},{8,56},{9,... | collective-permute-start | bytes 98312 | tf_op jit(solution)/shard_map/ppermute | solution.py:572
  117.6 5.2 %collective-permute-start.32 = (f32[64,128]{1,0:T(8,128)S(1)}, f32[64,128]{1,0:T(8,128)S(1)}, u32[]{:S(2)}, u32[]{:S(2)}) collective-permute-start(f32[64,128]{1,0:T(8,128)S(1)} %get-tuple-element.105.high), channel_id=1, source_target_pairs={{0,16},{1,17},{2,18},{3,19},{4,20},{5,21},{6,22},{7,23},{8,24},{9,... | collective-permute-start | bytes 98312 | tf_op jit(solution)/shard_map/ppermute | solution.py:572
  122.8 1.6 %collective-permute-start.38 = (f32[128,128]{1,0:T(8,128)S(1)}, f32[128,128]{1,0:T(8,128)S(1)}, u32[]{:S(2)}, u32[]{:S(2)}) collective-permute-start(f32[128,128]{1,0:T(8,128)S(1)} %get-tuple-element.112.mine), channel_id=1, source_target_pairs={{0,1},{1,0},{2,3},{3,2},{4,5},{5,4},{6,7},{7,6},{8,9},{9,8},{10,11... | collective-permute-start | bytes 196616 | tf_op jit(solution)/shard_map/ppermute | solution.py:572
  127.4 14.9 %collective-permute-start.39 = (f32[4,8,3072]{2,1,0:T(8,128)S(1)}, f32[4,8,3072]{2,1,0:T(8,128)S(1)}, u32[]{:S(2)}, u32[]{:S(2)}) collective-permute-start(f32[4,8,3072]{2,1,0:T(8,128)S(1)} %get-tuple-element.113), channel_id=1, source_target_pairs={{0,8},{1,9},{2,10},{3,11},{4,12},{5,13},{6,14},{7,15},{8,0},{9,1},... | collective-permute-start | bytes 1179656 | tf_op jit(solution)/shard_map/ppermute | solution.py:572
  128.8 13.5 %collective-permute-start.40 = (f32[8,1536]{1,0:T(8,128)S(1)}, f32[8,1536]{1,0:T(8,128)S(1)}, u32[]{:S(2)}, u32[]{:S(2)}) collective-permute-start(f32[8,1536]{1,0:T(8,128)S(1)} %get-tuple-element.115), channel_id=1, source_target_pairs={{0,8},{1,9},{2,10},{3,11},{4,12},{5,13},{6,14},{7,15},{8,0},{9,1},... | collective-permute-start | bytes 147464 | tf_op jit(solution)/shard_map/ppermute | solution.py:572
  131.4 10.9 %collective-permute-start.41 = (f32[8,1536]{1,0:T(8,128)S(1)}, f32[8,1536]{1,0:T(8,128)S(1)}, u32[]{:S(2)}, u32[]{:S(2)}) collective-permute-start(f32[8,1536]{1,0:T(8,128)S(1)} %get-tuple-element.116), channel_id=1, source_target_pairs={{0,64},{64,0},{1,65},{65,1},{2,66},{66,2},{3,67},{67,3},{4,68},{68... | collective-permute-start | bytes 147464 | tf_op jit(solution)/shard_map/ppermute | solution.py:797
  134.1 8.2 %collective-permute-start.42 = (f32[8,1536]{1,0:T(8,128)S(1)}, f32[8,1536]{1,0:T(8,128)S(1)}, u32[]{:S(2)}, u32[]{:S(2)}) collective-permute-start(f32[8,1536]{1,0:T(8,128)S(1)} %get-tuple-element.117), channel_id=1, source_target_pairs={{0,72},{1,73},{2,74},{3,75},{4,76},{5,77},{6,78},{7,79},{8,64},{9,... | collective-permute-start | bytes 147464 | tf_op jit(solution)/shard_map/ppermute | solution.py:798
  (6 other events, 63.4 us)
where the time goes:
time: 144 us; the launch traced here: 143 us
  starting transfers between devices  48.5 us (34%)
  waiting for transfers between devices  45.4 us (32%)
  Pallas kernels  45.2 us (31%)
  between operations  2.46 us (2%)
    ppermute x41, waiting for transfers between devices, send(): return lax.ppermute(value, 'dom', pairs)  45.4 us
    pallas_call x34, Pallas kernels, call(): pl.pallas_call(kernel, out_shape=[jax.ShapeDtypeStruct(*out) for out in o...  45.2 us
    ppermute x41, starting transfers between devices, send(): return lax.ppermute(value, 'dom', pairs)  44.6 us
  transfers between devices with their start and end apart: 43, of which 24 were waited for; matrix products, arithmetic and copies ran while one was open for 0% of the time, Pallas kernels for 22%

commit v1 on v0

--- a/solution.py
+++ b/solution.py
@@ -28,6 +28,8 @@
 EDGE = HALO * 16
 OWN = 512
 ROOM = 58
+LOOP_A = False
+LOOP_B = False
 CODES = 12
 TABLE = CODES * ROWS
 THIRD = TABLE // 3
@@ -103,6 +105,10 @@
     return lax.dot_general(left, right, (((1,), (1,)), ((), ())), preferred_element_type=F32)
 
 
+def three(high, low, parts):
+    return mul(high, parts[0]) + mul(low, parts[0]) + mul(high, parts[1])
+
+
 def pack_edge(value):
     main = value[:PACKED]
     lane = lax.broadcasted_iota(jnp.int32, (TAIL, LANES), 1)
@@ -122,7 +128,12 @@
     return jnp.concatenate([value, tail], axis=0)
 
 
-def each(count, step):
+def each(count, step, loop=True):
+    if not loop:
+        for k in range(count):
+            step(k)
+        return
+
     def run(k, carry):
         step(k)
         return carry
@@ -141,7 +152,7 @@
         inner_ref[o] = jnp.where(below_inner, bottom, top)
         outer_ref[o] = jnp.where(below_inner, top, bottom)
 
-    each(ORB, step)
+    each(ORB, step, LOOP_B)
 
 
 def to_columns(source, near, far):
@@ -280,7 +291,7 @@
 
 
 def chunks(step):
-    each(ALL // 256, lambda k: step(pl.multiple_of(k * 256, 256), 256))
+    each(ALL // 256, lambda k: step(k * 256, 256), LOOP_A)
     step(ALL - LANES, LANES)
 
 
@@ -343,10 +354,10 @@
 
 def table_kernel(index, field, placed, table, partial, both):
     def gather(o):
-        rows = pl.ds(pl.multiple_of(o * NZ, NZ), NZ)
+        rows = pl.ds(o * NZ, NZ)
         both[rows, :] = jnp.concatenate(split(field[o]), axis=1)
 
-    each(ORB, gather)
+    each(ORB, gather, LOOP_B)
     chunks(lambda at, wide: project(both[...], column_hot(index, at, wide), placed, partial, at, wide))
     table[...] = gather_table(index, partial[...])
 
@@ -439,8 +450,8 @@
     def step(o):
         value = field[o]
         high, low = split(value)
-        across = mul(jnp.concatenate([high, low, high], axis=1), own_w[...])
-        along = mul(ring_w[...], jnp.concatenate([high, low, high], axis=0))
+        across = three(high, low, own_w)
+        along = mul(ring_w[0], high) + mul(ring_w[0], low) + mul(ring_w[1], high)
         total = scale * (across + along + diagonal * value)
         out[o] = total if first else total - before[o]
 
@@ -457,7 +468,7 @@
         top = jnp.where(below_inner, outside, inside)
         line = jnp.concatenate([unpack_edge(xl[o]), unpack_edge(xh[o]), bottom, top], axis=1)
         high, low = split(line)
-        out[o] = acc[o] + scale * mul(jnp.concatenate([high, low, high], axis=1), halo_w[...])
+        out[o] = acc[o] + scale * three(high, low, halo_w)
 
     each(ORB, step)
 
@@ -495,10 +506,10 @@
     chunks(chunk)
 
     def finish(o):
-        rows = pl.ds(pl.multiple_of(o * NZ, NZ), NZ)
+        rows = pl.ds(o * NZ, NZ)
         field[o] = acc[o] + near_sums[rows, :]
 
-    each(ORB, finish)
+    each(ORB, finish, LOOP_B)
     if not last:
         emit_edges(field, second, edge, xl, xh, inner, outer)
         return
@@ -600,12 +611,9 @@
     upper_edge,
 ):
     own_m, halo_m, ring_m, edge_m = stencil_matrices()
-    a, b = two_parts(own_m)
-    own_w = jnp.asarray(np.concatenate([a, a, b], axis=0))
-    a, b = two_parts(halo_m)
-    halo_w = jnp.asarray(np.concatenate([a, a, b], axis=0))
-    a, b = two_parts(ring_m)
-    ring_w = jnp.asarray(np.concatenate([a, a, b], axis=1))
+    own_w = jnp.asarray(np.stack(two_parts(own_m)))
+    halo_w = jnp.asarray(np.stack(two_parts(halo_m)))
+    ring_w = jnp.asarray(np.stack(two_parts(ring_m)))
     edge_w = jnp.asarray(edge_m.astype(np.float32).astype(jnp.bfloat16))
 
     here = lax.axis_index("dom")

time: 144 us -> 139 us (0.965)
  Pallas kernels: 45.2 us -> 40.5 us
    pallas_call x34, Pallas kernels: 45.2 us -> 40.5 us  [call(): pl.pallas_call(kernel, out_shape=[jax.ShapeDtypeStruct(*out) for out in o...]
  transfers between devices with their start and end apart: 43 -> 43, of which waited for: 24 -> 24; matrix products, arithmetic and copies ran while one was open for 0% -> 0% of each run, Pallas kernels for 22% -> 21%
where the time goes in v1:
time: 139 us
  starting transfers between devices  48.7 us (35%)
  waiting for transfers between devices  45.6 us (33%)
  Pallas kernels  40.5 us (29%)
  between operations  2.45 us (2%)
    ppermute x41, waiting for transfers between devices, send(): return lax.ppermute(value, 'dom', pairs)  45.6 us
    ppermute x41, starting transfers between devices, send(): return lax.ppermute(value, 'dom', pairs)  44.7 us
    pallas_call x34, Pallas kernels, call(): pl.pallas_call(kernel, out_shape=[jax.ShapeDtypeStruct(*out) for out in o...  40.5 us
  transfers between devices with their start and end apart: 43, of which 24 were waited for; matrix products, arithmetic and copies ran while one was open for 0% of the time, Pallas kernels for 21%

profile of v1, /device:TPU:0, one launch (start us, length us, event | category | flops | bytes accessed | tf_op | source)
XLA Modules:
  0.0 139.0 jit_solution(3188720286679528213)
XLA Ops:
  1.8 3.4 %collective-permute-start.1 = (f32[4,8,3072]{2,1,0:T(8,128)S(1)}, f32[4,8,3072]{2,1,0:T(8,128)S(1)}, u32[]{:S(2)}, u32[]{:S(2)}) collective-permute-start(f32[4,8,3072]{2,1,0:T(8,128)S(1)} %dynamic-slice_bitcast_fusion), channel_id=1, source_target_pairs={{0,8},{1,9},{2,10},{3,11},{4,12},{5,13},{6,14},{7,15},{8,0},{9,1},... | collective-permute-start | bytes 1179656 | tf_op jit(solution)/shard_map/ppermute | solution.py:583
  7.1 7.5 %begin.1 = (f32[4,192,128]{2,1,0:T(8,128)}, f32[16,128]{1,0:T(8,128)}, s32[8,512]{1,0:T(8,128)}, f32[192,128]{1,0:T(8,128)}, f32[192,128]{1,0:T(8,128)}, /*index=5*/f32[408,128]{1,0:T(8,128)}) custom-call(s32[3]{0:T(128)} %pad_add_fusion.place, f32[1]{0:T(128)S(6)} %copy.37.upper_edge, f32[1]{0:T(128)S(6)} %copy.36.lower_edge, f32[8]{0:T(128)} %weights.1, ...), custom_call_target="tpu_custom_call" | custom-call | flops 100000000 | bytes 4000000 | tf_op jit(solution)/shard_map/begin/pallas_call | solution.py:568
  15.1 8.0 %collective-permute-done.note_came = f32[408,128]{1,0:T(8,128)S(1)} collective-permute-done((f32[408,128]{1,0:T(8,128)}, f32[408,128]{1,0:T(8,128)S(1)}, u32[]{:S(2)}, u32[]{:S(2)}) %collective-permute-start) | collective-permute-done | bytes 208928 | tf_op jit(solution)/shard_map/ppermute | solution.py:583
  23.4 1.4 %start.1 = (f32[4,192,256]{2,1,0:T(8,128)S(1)}, f32[4,144,128]{2,1,0:T(8,128)S(1)}, f32[4,144,128]{2,1,0:T(8,128)S(1)}, f32[4,144,128]{2,1,0:T(8,128)S(1)}, f32[4,144,128]{2,1,0:T(8,128)S(1)}) custom-call(f32[16,128]{1,0:T(8,128)S(1)} %copy-done.2, f32[4,192,128]{2,1,0:T(8,128)S(1)} %copy-done.6, f32[4,8,3072]{2,1,0:T(8,128)S(1)} %collective-permute-done.1.came, ...), custom_call_target="tpu_custom_call" | custom-call | flops 100000000 | bytes 4000000 | tf_op jit(solution)/shard_map/start/pallas_call | solution.py:568
  24.9 1.3 collective-permute-done.3.came
  26.3 2.4 %collective-permute-start.4 = (f32[136,128]{1,0:T(8,128)S(1)}, f32[136,128]{1,0:T(8,128)S(1)}, u32[]{:S(2)}, u32[]{:S(2)}) collective-permute-start(f32[136,128]{1,0:T(8,128)S(1)} %pair.4.half.mine), channel_id=1, source_target_pairs={{0,7},{1,2},{2,1},{3,4},{4,3},{5,6},{6,5},{7,0},{8,15},{9,10},{10,... | collective-permute-start | bytes 208904 | tf_op jit(solution)/shard_map/ppermute | solution.py:583
  29.3 1.9 %collective-permute-start.9 = (f32[4,144,128]{2,1,0:T(8,128)S(1)}, f32[4,144,128]{2,1,0:T(8,128)S(1)}, u32[]{:S(2)}, u32[]{:S(2)}) collective-permute-start(f32[4,144,128]{2,1,0:T(8,128)S(1)} %get-tuple-element.76), channel_id=1, source_target_pairs={{0,16},{1,17},{2,18},{3,19},{4,20},{5,21},{6,22},{7,23},{8,24},{9,... | collective-permute-start | bytes 884744 | tf_op jit(solution)/shard_map/ppermute | solution.py:583
  31.3 4.1 %collective-permute-start.10 = (f32[4,144,128]{2,1,0:T(8,128)S(1)}, f32[4,144,128]{2,1,0:T(8,128)S(1)}, u32[]{:S(2)}, u32[]{:S(2)}) collective-permute-start(f32[4,144,128]{2,1,0:T(8,128)S(1)} %get-tuple-element.77), channel_id=1, source_target_pairs={{0,48},{1,49},{2,50},{3,51},{4,52},{5,53},{6,54},{7,55},{8,56},{9,... | collective-permute-start | bytes 884744 | tf_op jit(solution)/shard_map/ppermute | solution.py:583
  35.4 1.4 %local.4.acc = f32[4,192,256]{2,1,0:T(8,128)S(1)} custom-call(f32[16,128]{1,0:T(8,128)S(1)} %copy-done.2, f32[136,128]{1,0:T(8,128)S(1)} %pair.4.half.mine, f32[4,192,256]{2,1,0:T(8,128)S(1)} %get-tuple-element.69.field.before, f32[4,192,256]{2,1,0:T(8,128)S(1)} %get-tuple-element.69.field.before, f32[192,256]{1,0:T(8,128)S(1)} %get-tuple-element.71.pot, ...), custom_call_target="tpu_custom_call" | custom-call | flops 100000000 | bytes 4000000 | tf_op jit(solution)/shard_map/local/pallas_call | solution.py:568
  38.6 1.9 %collective-permute-start.5 = (f32[72,128]{1,0:T(8,128)S(1)}, f32[72,128]{1,0:T(8,128)S(1)}, u32[]{:S(2)}, u32[]{:S(2)}) collective-permute-start(f32[72,128]{1,0:T(8,128)S(1)} %get-tuple-element.73.high), channel_id=1, source_target_pairs={{0,16},{1,17},{2,18},{3,19},{4,20},{5,21},{6,22},{7,23},{8,24},{9,... | collective-permute-start | bytes 110600 | tf_op jit(solution)/shard_map/ppermute | solution.py:583
  41.5 1.6 %halo.4.acc = f32[4,192,256]{2,1,0:T(8,128)S(1)} custom-call(f32[16,128]{1,0:T(8,128)S(1)} %copy-done.2, f32[4,144,128]{2,1,0:T(8,128)S(1)} %collective-permute-done.7.inner, f32[4,144,128]{2,1,0:T(8,128)S(1)} %collective-permute-done.8.outer, f32[4,144,128]{2,1,0:T(8,128)S(1)} %collective-permute-done.9.xl, f32[4,144,128]{2,1,0:T(8,128)S(1)} %collective-permute-done.10.xh, ...), custom_call_target="tpu_custom_call" | custom-call | flops 100000000 | bytes 4000000 | tf_op jit(solution)/shard_map/halo/pallas_call | solution.py:568
  43.2 1.4 %collective-permute-done.5.below = f32[72,128]{1,0:T(8,128)S(1)} collective-permute-done((f32[72,128]{1,0:T(8,128)S(1)}, f32[72,128]{1,0:T(8,128)S(1)}, u32[]{:S(2)}, u32[]{:S(2)}) %collective-permute-start.5) | collective-permute-done | bytes 36896 | tf_op jit(solution)/shard_map/ppermute | solution.py:583
  44.7 4.6 %collective-permute-done.2.came = f32[4,448,128]{2,1,0:T(8,128)S(1)} collective-permute-done((f32[4,448,128]{2,1,0:T(8,128)S(1)}, f32[4,448,128]{2,1,0:T(8,128)S(1)}, u32[]{:S(2)}, u32[]{:S(2)}) %collective-permute-start.2) | collective-permute-done | bytes 917536 | tf_op jit(solution)/shard_map/ppermute | solution.py:583
  49.4 2.0 %prepare.1 = (f32[4,192,896]{2,1,0:T(8,128)S(1)}, s32[4,896]{1,0:T(4,128)S(1)}) custom-call(s32[8,512]{1,0:T(8,128)S(1)} %copy-done.9, f32[408,128]{1,0:T(8,128)S(1)} %collective-permute-done.note_came, f32[4,448,128]{2,1,0:T(8,128)S(1)} %bitcast.15, f32[4,448,128]{2,1,0:T(8,128)S(1)} %collective-permute-done.2.came), custom_call_target="tpu_custom_call" | custom-call | flops 100000000 | bytes 4000000 | tf_op jit(solution)/shard_map/prepare/pallas_call | solution.py:568
  51.4 2.4 %update.3 = (f32[4,192,256]{2,1,0:T(8,128)S(1)}, f32[4,144,128]{2,1,0:T(8,128)S(1)}, f32[4,144,128]{2,1,0:T(8,128)S(1)}, f32[4,144,128]{2,1,0:T(8,128)S(1)}, f32[4,144,128]{2,1,0:T(8,128)S(1)}) custom-call(f32[16,128]{1,0:T(8,128)S(1)} %copy-done.2, s32[4,896]{1,0:T(4,128)S(1)} %get-tuple-element.65.index, f32[4,192,256]{2,1,0:T(8,128)S(1)} %get-tuple-element.79.acc, ...), custom_call_target="tpu_custom_call" | custom-call | flops 100000000 | bytes 4000000 | tf_op jit(solution)/shard_map/update/pallas_call | solution.py:568
  53.9 1.7 %collective-permute-start.17 = (f32[4,144,128]{2,1,0:T(8,128)S(1)}, f32[4,144,128]{2,1,0:T(8,128)S(1)}, u32[]{:S(2)}, u32[]{:S(2)}) collective-permute-start(f32[4,144,128]{2,1,0:T(8,128)S(1)} %get-tuple-element.87), channel_id=1, source_target_pairs={{0,7},{1,2},{2,1},{3,4},{4,3},{5,6},{6,5},{7,0},{8,15},{9,10},{10,... | collective-permute-start | bytes 884744 | tf_op jit(solution)/shard_map/ppermute | solution.py:583
  55.6 1.9 %collective-permute-start.18 = (f32[4,144,128]{2,1,0:T(8,128)S(1)}, f32[4,144,128]{2,1,0:T(8,128)S(1)}, u32[]{:S(2)}, u32[]{:S(2)}) collective-permute-start(f32[4,144,128]{2,1,0:T(8,128)S(1)} %get-tuple-element.88), channel_id=1, source_target_pairs={{0,16},{1,17},{2,18},{3,19},{4,20},{5,21},{6,22},{7,23},{8,24},{9,... | collective-permute-start | bytes 884744 | tf_op jit(solution)/shard_map/ppermute | solution.py:583
  57.5 2.1 %collective-permute-start.19 = (f32[4,144,128]{2,1,0:T(8,128)S(1)}, f32[4,144,128]{2,1,0:T(8,128)S(1)}, u32[]{:S(2)}, u32[]{:S(2)}) collective-permute-start(f32[4,144,128]{2,1,0:T(8,128)S(1)} %get-tuple-element.89), channel_id=1, source_target_pairs={{0,48},{1,49},{2,50},{3,51},{4,52},{5,53},{6,54},{7,55},{8,56},{9,... | collective-permute-start | bytes 884744 | tf_op jit(solution)/shard_map/ppermute | solution.py:583
  59.7 1.9 %table.3 = f32[192,128]{1,0:T(8,128)S(1)} custom-call(s32[4,896]{1,0:T(4,128)S(1)} %get-tuple-element.65.index, f32[4,192,256]{2,1,0:T(8,128)S(1)} %get-tuple-element.82.field.before, f32[4,192,896]{2,1,0:T(8,128)S(1)} %get-tuple-element.81.placed), custom_call_target="tpu_custom_call" | custom-call | flops 100000000 | bytes 4000000 | tf_op jit(solution)/shard_map/table/pallas_call | solution.py:568
  61.7 1.3 collective-permute-done.12.came
  63.8 1.4 %local.5.acc = f32[4,192,256]{2,1,0:T(8,128)S(1)} custom-call(f32[16,128]{1,0:T(8,128)S(1)} %copy-done.2, f32[128,128]{1,0:T(8,128)S(1)} %pair.5.half.mine, f32[4,192,256]{2,1,0:T(8,128)S(1)} %get-tuple-element.82.field.before, f32[4,192,256]{2,1,0:T(8,128)S(1)} %get-tuple-element.69.field.before, f32[192,256]{1,0:T(8,128)S(1)} %get-tuple-element.71.pot, ...), custom_call_target="tpu_custom_call" | custom-call | flops 100000000 | bytes 4000000 | tf_op jit(solution)/shard_map/local/pallas_call | solution.py:568
  65.2 3.0 %collective-permute-done.13.came = f32[128,128]{1,0:T(8,128)S(1)} collective-permute-done((f32[128,128]{1,0:T(8,128)S(1)}, f32[128,128]{1,0:T(8,128)S(1)}, u32[]{:S(2)}, u32[]{:S(2)}) %collective-permute-start.13) | collective-permute-done | bytes 65568 | tf_op jit(solution)/shard_map/ppermute | solution.py:583
  68.2 2.1 %collective-permute-start.15 = (f32[64,128]{1,0:T(8,128)S(1)}, f32[64,128]{1,0:T(8,128)S(1)}, u32[]{:S(2)}, u32[]{:S(2)}) collective-permute-start(f32[64,128]{1,0:T(8,128)S(1)} %get-tuple-element.83.low), channel_id=1, source_target_pairs={{0,48},{1,49},{2,50},{3,51},{4,52},{5,53},{6,54},{7,55},{8,56},{9,... | collective-permute-start | bytes 98312 | tf_op jit(solution)/shard_map/ppermute | solution.py:583
  70.3 1.6 %halo.5.acc = f32[4,192,256]{2,1,0:T(8,128)S(1)} custom-call(f32[16,128]{1,0:T(8,128)S(1)} %copy-done.2, f32[4,144,128]{2,1,0:T(8,128)S(1)} %collective-permute-done.16.inner, f32[4,144,128]{2,1,0:T(8,128)S(1)} %collective-permute-done.17.outer, f32[4,144,128]{2,1,0:T(8,128)S(1)} %collective-permute-done.18.xl, ...), custom_call_target="tpu_custom_call" | custom-call | flops 100000000 | bytes 4000000 | tf_op jit(solution)/shard_map/halo/pallas_call | solution.py:568
  72.2 3.2 %collective-permute-done.14.below = f32[64,128]{1,0:T(8,128)S(1)} collective-permute-done((f32[64,128]{1,0:T(8,128)S(1)}, f32[64,128]{1,0:T(8,128)S(1)}, u32[]{:S(2)}, u32[]{:S(2)}) %collective-permute-start.14) | collective-permute-done | bytes 32800 | tf_op jit(solution)/shard_map/ppermute | solution.py:583
  76.8 2.4 %update.4 = (f32[4,192,256]{2,1,0:T(8,128)S(1)}, f32[4,144,128]{2,1,0:T(8,128)S(1)}, f32[4,144,128]{2,1,0:T(8,128)S(1)}, f32[4,144,128]{2,1,0:T(8,128)S(1)}, f32[4,144,128]{2,1,0:T(8,128)S(1)}) custom-call(f32[16,128]{1,0:T(8,128)S(1)} %copy-done.2, s32[4,896]{1,0:T(4,128)S(1)} %get-tuple-element.65.index, f32[4,192,256]{2,1,0:T(8,128)S(1)} %get-tuple-element.91.acc, ...), custom_call_target="tpu_custom_call" | custom-call | flops 100000000 | bytes 4000000 | tf_op jit(solution)/shard_map/update/pallas_call | solution.py:568
  79.4 3.2 %collective-permute-start.28 = (f32[4,144,128]{2,1,0:T(8,128)S(1)}, f32[4,144,128]{2,1,0:T(8,128)S(1)}, u32[]{:S(2)}, u32[]{:S(2)}) collective-permute-start(f32[4,144,128]{2,1,0:T(8,128)S(1)} %get-tuple-element.99), channel_id=1, source_target_pairs={{0,48},{1,49},{2,50},{3,51},{4,52},{5,53},{6,54},{7,55},{8,56},{9,... | collective-permute-start | bytes 884744 | tf_op jit(solution)/shard_map/ppermute | solution.py:583
  82.7 1.9 %table.4 = f32[192,128]{1,0:T(8,128)S(1)} custom-call(s32[4,896]{1,0:T(4,128)S(1)} %get-tuple-element.65.index, f32[4,192,256]{2,1,0:T(8,128)S(1)} %get-tuple-element.93.field.before, f32[4,192,896]{2,1,0:T(8,128)S(1)} %get-tuple-element.81.placed), custom_call_target="tpu_custom_call" | custom-call | flops 100000000 | bytes 4000000 | tf_op jit(solution)/shard_map/table/pallas_call | solution.py:568
  84.7 1.3 collective-permute-done.21.came
  86.0 2.3 %collective-permute-start.22 = (f32[128,128]{1,0:T(8,128)S(1)}, f32[128,128]{1,0:T(8,128)S(1)}, u32[]{:S(2)}, u32[]{:S(2)}) collective-permute-start(f32[128,128]{1,0:T(8,128)S(1)} %pair.6.half.mine), channel_id=1, source_target_pairs={{0,7},{1,2},{2,1},{3,4},{4,3},{5,6},{6,5},{7,0},{8,15},{9,10},{10,... | collective-permute-start | bytes 196616 | tf_op jit(solution)/shard_map/ppermute | solution.py:583
  88.3 1.4 local.6.acc
  89.7 1.5 %collective-permute-done.22.came = f32[128,128]{1,0:T(8,128)S(1)} collective-permute-done((f32[128,128]{1,0:T(8,128)S(1)}, f32[128,128]{1,0:T(8,128)S(1)}, u32[]{:S(2)}, u32[]{:S(2)}) %collective-permute-start.22) | collective-permute-done | bytes 65568 | tf_op jit(solution)/shard_map/ppermute | solution.py:583
  91.3 2.0 %collective-permute-start.23 = (f32[64,128]{1,0:T(8,128)S(1)}, f32[64,128]{1,0:T(8,128)S(1)}, u32[]{:S(2)}, u32[]{:S(2)}) collective-permute-start(f32[64,128]{1,0:T(8,128)S(1)} %get-tuple-element.95.high), channel_id=1, source_target_pairs={{0,16},{1,17},{2,18},{3,19},{4,20},{5,21},{6,22},{7,23},{8,24},{9,... | collective-permute-start | bytes 98312 | tf_op jit(solution)/shard_map/ppermute | solution.py:583
  93.3 1.6 %halo.6.acc = f32[4,192,256]{2,1,0:T(8,128)S(1)} custom-call(f32[16,128]{1,0:T(8,128)S(1)} %copy-done.2, f32[4,144,128]{2,1,0:T(8,128)S(1)} %collective-permute-done.25.inner, f32[4,144,128]{2,1,0:T(8,128)S(1)} %collective-permute-done.26.outer, f32[4,144,128]{2,1,0:T(8,128)S(1)} %collective-permute-done.27.xl, ...), custom_call_target="tpu_custom_call" | custom-call | flops 100000000 | bytes 4000000 | tf_op jit(solution)/shard_map/halo/pallas_call | solution.py:568
  95.2 1.3 collective-permute-done.23.below
  98.1 2.4 %update.5 = (f32[4,192,256]{2,1,0:T(8,128)S(1)}, f32[4,144,128]{2,1,0:T(8,128)S(1)}, f32[4,144,128]{2,1,0:T(8,128)S(1)}, f32[4,144,128]{2,1,0:T(8,128)S(1)}, f32[4,144,128]{2,1,0:T(8,128)S(1)}) custom-call(f32[16,128]{1,0:T(8,128)S(1)} %copy-done.2, s32[4,896]{1,0:T(4,128)S(1)} %get-tuple-element.65.index, f32[4,192,256]{2,1,0:T(8,128)S(1)} %get-tuple-element.101.acc, ...), custom_call_target="tpu_custom_call" | custom-call | flops 100000000 | bytes 4000000 | tf_op jit(solution)/shard_map/update/pallas_call | solution.py:568
  102.6 2.6 %collective-permute-start.37 = (f32[4,144,128]{2,1,0:T(8,128)S(1)}, f32[4,144,128]{2,1,0:T(8,128)S(1)}, u32[]{:S(2)}, u32[]{:S(2)}) collective-permute-start(f32[4,144,128]{2,1,0:T(8,128)S(1)} %get-tuple-element.109), channel_id=1, source_target_pairs={{0,48},{1,49},{2,50},{3,51},{4,52},{5,53},{6,54},{7,55},{8,56},{9,... | collective-permute-start | bytes 884744 | tf_op jit(solution)/shard_map/ppermute | solution.py:583
  105.2 1.9 %table.5 = f32[192,128]{1,0:T(8,128)S(1)} custom-call(s32[4,896]{1,0:T(4,128)S(1)} %get-tuple-element.65.index, f32[4,192,256]{2,1,0:T(8,128)S(1)} %get-tuple-element.103.field, f32[4,192,896]{2,1,0:T(8,128)S(1)} %get-tuple-element.81.placed), custom_call_target="tpu_custom_call" | custom-call | flops 100000000 | bytes 4000000 | tf_op jit(solution)/shard_map/table/pallas_call | solution.py:568
  109.8 1.4 %local.7.acc = f32[4,192,256]{2,1,0:T(8,128)S(1)} custom-call(f32[16,128]{1,0:T(8,128)S(1)} %copy-done.2, f32[128,128]{1,0:T(8,128)S(1)} %pair.7.half.mine, f32[4,192,256]{2,1,0:T(8,128)S(1)} %get-tuple-element.103.field, f32[4,192,256]{2,1,0:T(8,128)S(1)} %get-tuple-element.93.field.before, f32[192,256]{1,0:T(8,128)S(1)} %get-tuple-element.71.pot, ...), custom_call_target="tpu_custom_call" | custom-call | flops 100000000 | bytes 4000000 | tf_op jit(solution)/shard_map/local/pallas_call | solution.py:568
  111.2 2.4 %collective-permute-done.31.came = f32[128,128]{1,0:T(8,128)S(1)} collective-permute-done((f32[128,128]{1,0:T(8,128)S(1)}, f32[128,128]{1,0:T(8,128)S(1)}, u32[]{:S(2)}, u32[]{:S(2)}) %collective-permute-start.31) | collective-permute-done | bytes 65568 | tf_op jit(solution)/shard_map/ppermute | solution.py:583
  113.7 2.0 %collective-permute-start.32 = (f32[64,128]{1,0:T(8,128)S(1)}, f32[64,128]{1,0:T(8,128)S(1)}, u32[]{:S(2)}, u32[]{:S(2)}) collective-permute-start(f32[64,128]{1,0:T(8,128)S(1)} %get-tuple-element.105.high), channel_id=1, source_target_pairs={{0,16},{1,17},{2,18},{3,19},{4,20},{5,21},{6,22},{7,23},{8,24},{9,... | collective-permute-start | bytes 98312 | tf_op jit(solution)/shard_map/ppermute | solution.py:583
  115.7 1.6 %halo.7.acc = f32[4,192,256]{2,1,0:T(8,128)S(1)} custom-call(f32[16,128]{1,0:T(8,128)S(1)} %copy-done.2, f32[4,144,128]{2,1,0:T(8,128)S(1)} %collective-permute-done.34.inner, f32[4,144,128]{2,1,0:T(8,128)S(1)} %collective-permute-done.35.outer, f32[4,144,128]{2,1,0:T(8,128)S(1)} %collective-permute-done.36.xl, ...), custom_call_target="tpu_custom_call" | custom-call | flops 100000000 | bytes 4000000 | tf_op jit(solution)/shard_map/halo/pallas_call | solution.py:568
  117.6 1.3 collective-permute-done.32.below
  120.2 2.8 %finish.1 = (f32[4,8,3072]{2,1,0:T(8,128)S(1)}, f32[4,8,3072]{2,1,0:T(8,128)S(1)}, f32[4,192,256]{2,1,0:T(8,128)S(1)}) custom-call(f32[16,128]{1,0:T(8,128)S(1)} %copy-done.2, s32[4,896]{1,0:T(4,128)S(1)} %get-tuple-element.65.index, f32[4,192,256]{2,1,0:T(8,128)S(1)} %get-tuple-element.111.acc, f32[128,128]{1,0:T(8,128)S(1)} %get-tuple-element.112.mine, ...), custom_call_target="tpu_custom_call" | custom-call | flops 100000000 | bytes 4000000 | tf_op jit(solution)/shard_map/finish/pallas_call | solution.py:568
  124.4 2.6 %collective-permute-start.40 = (f32[8,1536]{1,0:T(8,128)S(1)}, f32[8,1536]{1,0:T(8,128)S(1)}, u32[]{:S(2)}, u32[]{:S(2)}) collective-permute-start(f32[8,1536]{1,0:T(8,128)S(1)} %get-tuple-element.115), channel_id=1, source_target_pairs={{0,8},{1,9},{2,10},{3,11},{4,12},{5,13},{6,14},{7,15},{8,0},{9,1},... | collective-permute-start | bytes 147464 | tf_op jit(solution)/shard_map/ppermute | solution.py:583
  127.0 2.6 %collective-permute-start.41 = (f32[8,1536]{1,0:T(8,128)S(1)}, f32[8,1536]{1,0:T(8,128)S(1)}, u32[]{:S(2)}, u32[]{:S(2)}) collective-permute-start(f32[8,1536]{1,0:T(8,128)S(1)} %get-tuple-element.116), channel_id=1, source_target_pairs={{0,64},{64,0},{1,65},{65,1},{2,66},{66,2},{3,67},{67,3},{4,68},{68... | collective-permute-start | bytes 147464 | tf_op jit(solution)/shard_map/ppermute | solution.py:805
  129.7 1.3 collective-permute-start.42
  131.0 6.9 %collective-permute-done.40.b = f32[8,1536]{1,0:T(8,128)S(1)} collective-permute-done((f32[8,1536]{1,0:T(8,128)S(1)}, f32[8,1536]{1,0:T(8,128)S(1)}, u32[]{:S(2)}, u32[]{:S(2)}) %collective-permute-start.40) | collective-permute-done | bytes 49184 | tf_op jit(solution)/shard_map/ppermute | solution.py:583
  (97 shorter events, 19.9 us)
Async XLA Ops:
  0.6 14.3 %copy-start.1 = (f32[1,4,448,128]{3,2,1,0:T(8,128)S(1)}, f32[1,4,448,128]{3,2,1,0:T(8,128)}, u32[]{:S(2)}) copy-start(f32[1,4,448,128]{3,2,1,0:T(8,128)} %param.18) | copy-start | bytes 2752516
  1.8 21.3 %collective-permute-start.1 = (f32[4,8,3072]{2,1,0:T(8,128)S(1)}, f32[4,8,3072]{2,1,0:T(8,128)S(1)}, u32[]{:S(2)}, u32[]{:S(2)}) collective-permute-start(f32[4,8,3072]{2,1,0:T(8,128)S(1)} %dynamic-slice_bitcast_fusion), channel_id=1, source_target_pairs={{0,8},{1,9},{2,10},{3,11},{4,12},{5,13},{6,14},{7,15},{8,0},{9,1},... | collective-permute-start | bytes 1179656 | tf_op jit(solution)/shard_map/ppermute | solution.py:583
  7.1 16.3 %copy-start.5 = (bf16[256,256]{1,0:T(8,128)(2,1)S(1)}, bf16[256,256]{1,0:T(8,128)(2,1)}, u32[]{:S(2)}) copy-start(bf16[256,256]{1,0:T(8,128)(2,1)} %constant.57.clone.edge.rest_0_) | copy-start | bytes 393220
  14.6 8.4 %collective-permute-start = (f32[408,128]{1,0:T(8,128)}, f32[408,128]{1,0:T(8,128)S(1)}, u32[]{:S(2)}, u32[]{:S(2)}) collective-permute-start(f32[408,128]{1,0:T(8,128)} %get-tuple-element.64), channel_id=1, source_target_pairs={{0,8},{1,9},{2,10},{3,11},{4,12},{5,13},{6,14},{7,15},{8,0},{9,1},... | collective-permute-start | bytes 626696 | tf_op jit(solution)/shard_map/ppermute | solution.py:583
  15.0 20.4 %copy-start.3 = (bf16[2,256,256]{2,1,0:T(8,128)(2,1)S(1)}, bf16[2,256,256]{2,1,0:T(8,128)(2,1)}, u32[]{:S(2)}) copy-start(bf16[2,256,256]{2,1,0:T(8,128)(2,1)} %constant.54.clone.own_w) | copy-start | bytes 786436
  15.0 20.4 %copy-start.4 = (bf16[2,192,192]{2,1,0:T(8,128)(2,1)S(1)}, bf16[2,192,192]{2,1,0:T(8,128)(2,1)}, u32[]{:S(2)}) copy-start(bf16[2,192,192]{2,1,0:T(8,128)(2,1)} %constant.56.clone.ring_w) | copy-start | bytes 442372
  23.0 26.3 %collective-permute-start.2 = (f32[4,448,128]{2,1,0:T(8,128)S(1)}, f32[4,448,128]{2,1,0:T(8,128)S(1)}, u32[]{:S(2)}, u32[]{:S(2)}) collective-permute-start(f32[4,448,128]{2,1,0:T(8,128)S(1)} %gate.1), channel_id=1, source_target_pairs={{0,8},{1,9},{2,10},{3,11},{4,12},{5,13},{6,14},{7,15},{8,0},{9,1},... | collective-permute-start | bytes 2752520 | tf_op jit(solution)/shard_map/ppermute | solution.py:583
  24.8 16.7 %copy-start = (bf16[2,512,256]{2,1,0:T(8,128)(2,1)S(1)}, bf16[2,512,256]{2,1,0:T(8,128)(2,1)}, u32[]{:S(2)}) copy-start(bf16[2,512,256]{2,1,0:T(8,128)(2,1)} %constant.55.clone.halo_w) | copy-start | bytes 1572868
  24.9 1.4 collective-permute-start.3
  26.3 5.1 %collective-permute-start.4 = (f32[136,128]{1,0:T(8,128)S(1)}, f32[136,128]{1,0:T(8,128)S(1)}, u32[]{:S(2)}, u32[]{:S(2)}) collective-permute-start(f32[136,128]{1,0:T(8,128)S(1)} %pair.4.half.mine), channel_id=1, source_target_pairs={{0,7},{1,2},{2,1},{3,4},{4,3},{5,6},{6,5},{7,0},{8,15},{9,10},{10,... | collective-permute-start | bytes 208904 | tf_op jit(solution)/shard_map/ppermute | solution.py:583
  28.6 8.3 %collective-permute-start.7 = (f32[4,144,128]{2,1,0:T(8,128)S(1)}, f32[4,144,128]{2,1,0:T(8,128)S(1)}, u32[]{:S(2)}, u32[]{:S(2)}) collective-permute-start(f32[4,144,128]{2,1,0:T(8,128)S(1)} %get-tuple-element.74), channel_id=1, source_target_pairs={{0,1},{1,0},{2,3},{3,2},{4,5},{5,4},{6,7},{7,6},{8,9},{9,8},{10,11... | collective-permute-start | bytes 884744 | tf_op jit(solution)/shard_map/ppermute | solution.py:583
  28.6 10.0 %collective-permute-start.8 = (f32[4,144,128]{2,1,0:T(8,128)S(1)}, f32[4,144,128]{2,1,0:T(8,128)S(1)}, u32[]{:S(2)}, u32[]{:S(2)}) collective-permute-start(f32[4,144,128]{2,1,0:T(8,128)S(1)} %get-tuple-element.75), channel_id=1, source_target_pairs={{0,7},{1,2},{2,1},{3,4},{4,3},{5,6},{6,5},{7,0},{8,15},{9,10},{10,... | collective-permute-start | bytes 884744 | tf_op jit(solution)/shard_map/ppermute | solution.py:583
  29.3 11.6 %collective-permute-start.9 = (f32[4,144,128]{2,1,0:T(8,128)S(1)}, f32[4,144,128]{2,1,0:T(8,128)S(1)}, u32[]{:S(2)}, u32[]{:S(2)}) collective-permute-start(f32[4,144,128]{2,1,0:T(8,128)S(1)} %get-tuple-element.76), channel_id=1, source_target_pairs={{0,16},{1,17},{2,18},{3,19},{4,20},{5,21},{6,22},{7,23},{8,24},{9,... | collective-permute-start | bytes 884744 | tf_op jit(solution)/shard_map/ppermute | solution.py:583
  31.3 10.2 %collective-permute-start.10 = (f32[4,144,128]{2,1,0:T(8,128)S(1)}, f32[4,144,128]{2,1,0:T(8,128)S(1)}, u32[]{:S(2)}, u32[]{:S(2)}) collective-permute-start(f32[4,144,128]{2,1,0:T(8,128)S(1)} %get-tuple-element.77), channel_id=1, source_target_pairs={{0,48},{1,49},{2,50},{3,51},{4,52},{5,53},{6,54},{7,55},{8,56},{9,... | collective-permute-start | bytes 884744 | tf_op jit(solution)/shard_map/ppermute | solution.py:583
  36.9 6.3 %collective-permute-start.6 = (f32[72,128]{1,0:T(8,128)S(1)}, f32[72,128]{1,0:T(8,128)S(1)}, u32[]{:S(2)}, u32[]{:S(2)}) collective-permute-start(f32[72,128]{1,0:T(8,128)S(1)} %get-tuple-element.72.low), channel_id=1, source_target_pairs={{0,48},{1,49},{2,50},{3,51},{4,52},{5,53},{6,54},{7,55},{8,56},{9,... | collective-permute-start | bytes 110600 | tf_op jit(solution)/shard_map/ppermute | solution.py:583
  38.6 6.0 %collective-permute-start.5 = (f32[72,128]{1,0:T(8,128)S(1)}, f32[72,128]{1,0:T(8,128)S(1)}, u32[]{:S(2)}, u32[]{:S(2)}) collective-permute-start(f32[72,128]{1,0:T(8,128)S(1)} %get-tuple-element.73.high), channel_id=1, source_target_pairs={{0,16},{1,17},{2,18},{3,19},{4,20},{5,21},{6,22},{7,23},{8,24},{9,... | collective-permute-start | bytes 110600 | tf_op jit(solution)/shard_map/ppermute | solution.py:583
  44.6 6.7 %collective-permute-start.11 = (f32[128,128]{1,0:T(8,128)S(1)}, f32[128,128]{1,0:T(8,128)S(1)}, u32[]{:S(2)}, u32[]{:S(2)}) collective-permute-start(f32[128,128]{1,0:T(8,128)S(1)} %get-tuple-element.80.mine), channel_id=1, source_target_pairs={{0,1},{1,0},{2,3},{3,2},{4,5},{5,4},{6,7},{7,6},{8,9},{9,8},{10,11... | collective-permute-start | bytes 196616 | tf_op jit(solution)/shard_map/ppermute | solution.py:583
  53.8 16.5 %collective-permute-start.16 = (f32[4,144,128]{2,1,0:T(8,128)S(1)}, f32[4,144,128]{2,1,0:T(8,128)S(1)}, u32[]{:S(2)}, u32[]{:S(2)}) collective-permute-start(f32[4,144,128]{2,1,0:T(8,128)S(1)} %get-tuple-element.86), channel_id=1, source_target_pairs={{0,1},{1,0},{2,3},{3,2},{4,5},{5,4},{6,7},{7,6},{8,9},{9,8},{10,11... | collective-permute-start | bytes 884744 | tf_op jit(solution)/shard_map/ppermute | solution.py:583
  53.9 16.4 %collective-permute-start.17 = (f32[4,144,128]{2,1,0:T(8,128)S(1)}, f32[4,144,128]{2,1,0:T(8,128)S(1)}, u32[]{:S(2)}, u32[]{:S(2)}) collective-permute-start(f32[4,144,128]{2,1,0:T(8,128)S(1)} %get-tuple-element.87), channel_id=1, source_target_pairs={{0,7},{1,2},{2,1},{3,4},{4,3},{5,6},{6,5},{7,0},{8,15},{9,10},{10,... | collective-permute-start | bytes 884744 | tf_op jit(solution)/shard_map/ppermute | solution.py:583
  55.6 14.7 %collective-permute-start.18 = (f32[4,144,128]{2,1,0:T(8,128)S(1)}, f32[4,144,128]{2,1,0:T(8,128)S(1)}, u32[]{:S(2)}, u32[]{:S(2)}) collective-permute-start(f32[4,144,128]{2,1,0:T(8,128)S(1)} %get-tuple-element.88), channel_id=1, source_target_pairs={{0,16},{1,17},{2,18},{3,19},{4,20},{5,21},{6,22},{7,23},{8,24},{9,... | collective-permute-start | bytes 884744 | tf_op jit(solution)/shard_map/ppermute | solution.py:583
  57.5 12.8 %collective-permute-start.19 = (f32[4,144,128]{2,1,0:T(8,128)S(1)}, f32[4,144,128]{2,1,0:T(8,128)S(1)}, u32[]{:S(2)}, u32[]{:S(2)}) collective-permute-start(f32[4,144,128]{2,1,0:T(8,128)S(1)} %get-tuple-element.89), channel_id=1, source_target_pairs={{0,48},{1,49},{2,50},{3,51},{4,52},{5,53},{6,54},{7,55},{8,56},{9,... | collective-permute-start | bytes 884744 | tf_op jit(solution)/shard_map/ppermute | solution.py:583
  61.6 1.4 collective-permute-start.12
  63.0 5.2 %collective-permute-start.13 = (f32[128,128]{1,0:T(8,128)S(1)}, f32[128,128]{1,0:T(8,128)S(1)}, u32[]{:S(2)}, u32[]{:S(2)}) collective-permute-start(f32[128,128]{1,0:T(8,128)S(1)} %pair.5.half.mine), channel_id=1, source_target_pairs={{0,7},{1,2},{2,1},{3,4},{4,3},{5,6},{6,5},{7,0},{8,15},{9,10},{10,... | collective-permute-start | bytes 196616 | tf_op jit(solution)/shard_map/ppermute | solution.py:583
  68.2 4.0 %collective-permute-start.15 = (f32[64,128]{1,0:T(8,128)S(1)}, f32[64,128]{1,0:T(8,128)S(1)}, u32[]{:S(2)}, u32[]{:S(2)}) collective-permute-start(f32[64,128]{1,0:T(8,128)S(1)} %get-tuple-element.83.low), channel_id=1, source_target_pairs={{0,48},{1,49},{2,50},{3,51},{4,52},{5,53},{6,54},{7,55},{8,56},{9,... | collective-permute-start | bytes 98312 | tf_op jit(solution)/shard_map/ppermute | solution.py:583
  70.3 5.1 %collective-permute-start.14 = (f32[64,128]{1,0:T(8,128)S(1)}, f32[64,128]{1,0:T(8,128)S(1)}, u32[]{:S(2)}, u32[]{:S(2)}) collective-permute-start(f32[64,128]{1,0:T(8,128)S(1)} %get-tuple-element.84.high), channel_id=1, source_target_pairs={{0,16},{1,17},{2,18},{3,19},{4,20},{5,21},{6,22},{7,23},{8,24},{9,... | collective-permute-start | bytes 98312 | tf_op jit(solution)/shard_map/ppermute | solution.py:583
  75.4 1.3 collective-permute-start.20
  79.2 12.1 %collective-permute-start.25 = (f32[4,144,128]{2,1,0:T(8,128)S(1)}, f32[4,144,128]{2,1,0:T(8,128)S(1)}, u32[]{:S(2)}, u32[]{:S(2)}) collective-permute-start(f32[4,144,128]{2,1,0:T(8,128)S(1)} %get-tuple-element.96), channel_id=1, source_target_pairs={{0,1},{1,0},{2,3},{3,2},{4,5},{5,4},{6,7},{7,6},{8,9},{9,8},{10,11... | collective-permute-start | bytes 884744 | tf_op jit(solution)/shard_map/ppermute | solution.py:583
  79.4 13.9 %collective-permute-start.26 = (f32[4,144,128]{2,1,0:T(8,128)S(1)}, f32[4,144,128]{2,1,0:T(8,128)S(1)}, u32[]{:S(2)}, u32[]{:S(2)}) collective-permute-start(f32[4,144,128]{2,1,0:T(8,128)S(1)} %get-tuple-element.97), channel_id=1, source_target_pairs={{0,7},{1,2},{2,1},{3,4},{4,3},{5,6},{6,5},{7,0},{8,15},{9,10},{10,... | collective-permute-start | bytes 884744 | tf_op jit(solution)/shard_map/ppermute | solution.py:583
  79.4 13.9 %collective-permute-start.27 = (f32[4,144,128]{2,1,0:T(8,128)S(1)}, f32[4,144,128]{2,1,0:T(8,128)S(1)}, u32[]{:S(2)}, u32[]{:S(2)}) collective-permute-start(f32[4,144,128]{2,1,0:T(8,128)S(1)} %get-tuple-element.98), channel_id=1, source_target_pairs={{0,16},{1,17},{2,18},{3,19},{4,20},{5,21},{6,22},{7,23},{8,24},{9,... | collective-permute-start | bytes 884744 | tf_op jit(solution)/shard_map/ppermute | solution.py:583
  79.4 13.9 %collective-permute-start.28 = (f32[4,144,128]{2,1,0:T(8,128)S(1)}, f32[4,144,128]{2,1,0:T(8,128)S(1)}, u32[]{:S(2)}, u32[]{:S(2)}) collective-permute-start(f32[4,144,128]{2,1,0:T(8,128)S(1)} %get-tuple-element.99), channel_id=1, source_target_pairs={{0,48},{1,49},{2,50},{3,51},{4,52},{5,53},{6,54},{7,55},{8,56},{9,... | collective-permute-start | bytes 884744 | tf_op jit(solution)/shard_map/ppermute | solution.py:583
  84.6 1.4 collective-permute-start.21
  86.0 5.2 %collective-permute-start.22 = (f32[128,128]{1,0:T(8,128)S(1)}, f32[128,128]{1,0:T(8,128)S(1)}, u32[]{:S(2)}, u32[]{:S(2)}) collective-permute-start(f32[128,128]{1,0:T(8,128)S(1)} %pair.6.half.mine), channel_id=1, source_target_pairs={{0,7},{1,2},{2,1},{3,4},{4,3},{5,6},{6,5},{7,0},{8,15},{9,10},{10,... | collective-permute-start | bytes 196616 | tf_op jit(solution)/shard_map/ppermute | solution.py:583
  91.2 4.0 %collective-permute-start.24 = (f32[64,128]{1,0:T(8,128)S(1)}, f32[64,128]{1,0:T(8,128)S(1)}, u32[]{:S(2)}, u32[]{:S(2)}) collective-permute-start(f32[64,128]{1,0:T(8,128)S(1)} %get-tuple-element.94.low), channel_id=1, source_target_pairs={{0,48},{1,49},{2,50},{3,51},{4,52},{5,53},{6,54},{7,55},{8,56},{9,... | collective-permute-start | bytes 98312 | tf_op jit(solution)/shard_map/ppermute | solution.py:583
  91.3 5.2 %collective-permute-start.23 = (f32[64,128]{1,0:T(8,128)S(1)}, f32[64,128]{1,0:T(8,128)S(1)}, u32[]{:S(2)}, u32[]{:S(2)}) collective-permute-start(f32[64,128]{1,0:T(8,128)S(1)} %get-tuple-element.95.high), channel_id=1, source_target_pairs={{0,16},{1,17},{2,18},{3,19},{4,20},{5,21},{6,22},{7,23},{8,24},{9,... | collective-permute-start | bytes 98312 | tf_op jit(solution)/shard_map/ppermute | solution.py:583
  96.5 1.6 %collective-permute-start.29 = (f32[128,128]{1,0:T(8,128)S(1)}, f32[128,128]{1,0:T(8,128)S(1)}, u32[]{:S(2)}, u32[]{:S(2)}) collective-permute-start(f32[128,128]{1,0:T(8,128)S(1)} %get-tuple-element.102.mine), channel_id=1, source_target_pairs={{0,1},{1,0},{2,3},{3,2},{4,5},{5,4},{6,7},{7,6},{8,9},{9,8},{10,11... | collective-permute-start | bytes 196616 | tf_op jit(solution)/shard_map/ppermute | solution.py:583
  100.5 13.2 %collective-permute-start.34 = (f32[4,144,128]{2,1,0:T(8,128)S(1)}, f32[4,144,128]{2,1,0:T(8,128)S(1)}, u32[]{:S(2)}, u32[]{:S(2)}) collective-permute-start(f32[4,144,128]{2,1,0:T(8,128)S(1)} %get-tuple-element.106), channel_id=1, source_target_pairs={{0,1},{1,0},{2,3},{3,2},{4,5},{5,4},{6,7},{7,6},{8,9},{9,8},{10,11... | collective-permute-start | bytes 884744 | tf_op jit(solution)/shard_map/ppermute | solution.py:583
  100.7 14.9 %collective-permute-start.35 = (f32[4,144,128]{2,1,0:T(8,128)S(1)}, f32[4,144,128]{2,1,0:T(8,128)S(1)}, u32[]{:S(2)}, u32[]{:S(2)}) collective-permute-start(f32[4,144,128]{2,1,0:T(8,128)S(1)} %get-tuple-element.107), channel_id=1, source_target_pairs={{0,7},{1,2},{2,1},{3,4},{4,3},{5,6},{6,5},{7,0},{8,15},{9,10},{10,... | collective-permute-start | bytes 884744 | tf_op jit(solution)/shard_map/ppermute | solution.py:583
  102.0 13.7 %collective-permute-start.36 = (f32[4,144,128]{2,1,0:T(8,128)S(1)}, f32[4,144,128]{2,1,0:T(8,128)S(1)}, u32[]{:S(2)}, u32[]{:S(2)}) collective-permute-start(f32[4,144,128]{2,1,0:T(8,128)S(1)} %get-tuple-element.108), channel_id=1, source_target_pairs={{0,16},{1,17},{2,18},{3,19},{4,20},{5,21},{6,22},{7,23},{8,24},{9,... | collective-permute-start | bytes 884744 | tf_op jit(solution)/shard_map/ppermute | solution.py:583
  102.6 13.1 %collective-permute-start.37 = (f32[4,144,128]{2,1,0:T(8,128)S(1)}, f32[4,144,128]{2,1,0:T(8,128)S(1)}, u32[]{:S(2)}, u32[]{:S(2)}) collective-permute-start(f32[4,144,128]{2,1,0:T(8,128)S(1)} %get-tuple-element.109), channel_id=1, source_target_pairs={{0,48},{1,49},{2,50},{3,51},{4,52},{5,53},{6,54},{7,55},{8,56},{9,... | collective-permute-start | bytes 884744 | tf_op jit(solution)/shard_map/ppermute | solution.py:583
  107.1 1.4 collective-permute-start.30
  108.5 5.0 %collective-permute-start.31 = (f32[128,128]{1,0:T(8,128)S(1)}, f32[128,128]{1,0:T(8,128)S(1)}, u32[]{:S(2)}, u32[]{:S(2)}) collective-permute-start(f32[128,128]{1,0:T(8,128)S(1)} %pair.7.half.mine), channel_id=1, source_target_pairs={{0,7},{1,2},{2,1},{3,4},{4,3},{5,6},{6,5},{7,0},{8,15},{9,10},{10,... | collective-permute-start | bytes 196616 | tf_op jit(solution)/shard_map/ppermute | solution.py:583
  113.6 4.0 %collective-permute-start.33 = (f32[64,128]{1,0:T(8,128)S(1)}, f32[64,128]{1,0:T(8,128)S(1)}, u32[]{:S(2)}, u32[]{:S(2)}) collective-permute-start(f32[64,128]{1,0:T(8,128)S(1)} %get-tuple-element.104.low), channel_id=1, source_target_pairs={{0,48},{1,49},{2,50},{3,51},{4,52},{5,53},{6,54},{7,55},{8,56},{9,... | collective-permute-start | bytes 98312 | tf_op jit(solution)/shard_map/ppermute | solution.py:583
  113.7 5.2 %collective-permute-start.32 = (f32[64,128]{1,0:T(8,128)S(1)}, f32[64,128]{1,0:T(8,128)S(1)}, u32[]{:S(2)}, u32[]{:S(2)}) collective-permute-start(f32[64,128]{1,0:T(8,128)S(1)} %get-tuple-element.105.high), channel_id=1, source_target_pairs={{0,16},{1,17},{2,18},{3,19},{4,20},{5,21},{6,22},{7,23},{8,24},{9,... | collective-permute-start | bytes 98312 | tf_op jit(solution)/shard_map/ppermute | solution.py:583
  118.9 1.3 collective-permute-start.38
  123.0 14.9 %collective-permute-start.39 = (f32[4,8,3072]{2,1,0:T(8,128)S(1)}, f32[4,8,3072]{2,1,0:T(8,128)S(1)}, u32[]{:S(2)}, u32[]{:S(2)}) collective-permute-start(f32[4,8,3072]{2,1,0:T(8,128)S(1)} %get-tuple-element.113), channel_id=1, source_target_pairs={{0,8},{1,9},{2,10},{3,11},{4,12},{5,13},{6,14},{7,15},{8,0},{9,1},... | collective-permute-start | bytes 1179656 | tf_op jit(solution)/shard_map/ppermute | solution.py:583
  124.4 13.5 %collective-permute-start.40 = (f32[8,1536]{1,0:T(8,128)S(1)}, f32[8,1536]{1,0:T(8,128)S(1)}, u32[]{:S(2)}, u32[]{:S(2)}) collective-permute-start(f32[8,1536]{1,0:T(8,128)S(1)} %get-tuple-element.115), channel_id=1, source_target_pairs={{0,8},{1,9},{2,10},{3,11},{4,12},{5,13},{6,14},{7,15},{8,0},{9,1},... | collective-permute-start | bytes 147464 | tf_op jit(solution)/shard_map/ppermute | solution.py:583
  127.0 10.9 %collective-permute-start.41 = (f32[8,1536]{1,0:T(8,128)S(1)}, f32[8,1536]{1,0:T(8,128)S(1)}, u32[]{:S(2)}, u32[]{:S(2)}) collective-permute-start(f32[8,1536]{1,0:T(8,128)S(1)} %get-tuple-element.116), channel_id=1, source_target_pairs={{0,64},{64,0},{1,65},{65,1},{2,66},{66,2},{3,67},{67,3},{4,68},{68... | collective-permute-start | bytes 147464 | tf_op jit(solution)/shard_map/ppermute | solution.py:805
  129.7 8.2 %collective-permute-start.42 = (f32[8,1536]{1,0:T(8,128)S(1)}, f32[8,1536]{1,0:T(8,128)S(1)}, u32[]{:S(2)}, u32[]{:S(2)}) collective-permute-start(f32[8,1536]{1,0:T(8,128)S(1)} %get-tuple-element.117), channel_id=1, source_target_pairs={{0,72},{1,73},{2,74},{3,75},{4,76},{5,77},{6,78},{7,79},{8,64},{9,... | collective-permute-start | bytes 147464 | tf_op jit(solution)/shard_map/ppermute | solution.py:806
  (6 other events, 62.1 us)

commit v2 on v1

--- a/solution.py
+++ b/solution.py
@@ -34,7 +34,7 @@
 TABLE = CODES * ROWS
 THIRD = TABLE // 3
 HALF = 2 * THIRD
-NOTE = TABLE + NZ
+NOTE = TABLE
 
 WEIGHTS = (
     -5369.0 / 1800.0,
@@ -181,13 +181,13 @@
 
 
 def begin_kernel(
-    place, upper_edge, lower_edge, weights, column_in, shift_in, owner_in, atom_in, raw_in, proj_in, pot_in, energy_in,
-    keep, params, ints, table, local, note,
-    column, shift, owner, atom, raw, proj, potential, energy, turned, tables, both, placed, partial, near, far, sems,
+    place, upper_edge, lower_edge, weights, column_in, shift_in, owner_in, atom_in, raw_in, proj_in, energy_in,
+    keep, params, ints, table, note,
+    column, shift, owner, atom, raw, proj, energy, turned, tables, both, placed, partial, near, far, sems,
 ):
     pairs = (
         (raw_in, raw), (column_in, column), (shift_in, shift), (owner_in, owner),
-        (atom_in, atom), (proj_in, proj), (pot_in, potential), (energy_in, energy),
+        (atom_in, atom), (proj_in, proj), (energy_in, energy),
     )
     copies = [pltpu.make_async_copy(source, target, sems.at[k]) for k, (source, target) in enumerate(pairs)]
     for copy in copies:
@@ -240,9 +240,6 @@
     first_tables(ints, turned, tables, both, proj, placed, partial)
     table[...] = tables[0]
     note[:TABLE] = tables[1]
-    lines = to_columns(lambda at: potential[:, at : at + NZ], near, far)
-    local[...] = lines
-    note[TABLE:NOTE] = lines
     note[NOTE : NOTE + NPJ] = energy[...]
     note[NOTE + NPJ : NOTE + 8] = jnp.zeros((4, LANES), F32)
     numbers = ints[:4].astype(F32)
@@ -250,8 +247,12 @@
         note[NOTE + 8 + 4 * k : NOTE + 12 + 4 * k] = numbers[:, k * LANES : (k + 1) * LANES]
 
 
-def start_kernel(params, keep, came, edge, field, xl, xh, inner, outer, near, far):
+def start_kernel(params, keep, came, potential, edge, field, pot, xl, xh, inner, outer, near, far):
     upper = flag(params, 0)
+    here = to_columns(lambda at: potential[0, :, at : at + NZ], near, far)
+    there = to_columns(lambda at: came[ORB, :, at : at + NZ], near, far)
+    pot[:, :LANES] = jnp.where(upper, there, here)
+    pot[:, LANES:] = jnp.where(upper, here, there)
 
     def step(o):
         turned = to_columns(lambda at: came[o, :, at : at + NZ], near, far)
@@ -317,12 +318,17 @@
 
 def project(both, hot, placed, partial, at, wide):
     picked = mul(both, jnp.concatenate([hot, hot], axis=0))
-    for j in range(NPJ):
-        values = placed[j, :, pl.ds(at, wide)]
-        for o in range(ORB):
-            term = picked[o * NZ : (o + 1) * NZ] * values
-            row = o * NPJ + j
-            partial[row : row + 1, pl.ds(at, wide)] = jnp.sum(term, axis=0, keepdims=True)
+    sums = [None] * ROWS
+    for z in range(0, NZ, 8):
+        lines = [picked[o * NZ + z : o * NZ + z + 8] for o in range(ORB)]
+        for j in range(NPJ):
+            values = placed[j, z : z + 8, pl.ds(at, wide)]
+            for o in range(ORB):
+                term = lines[o] * values
+                row = o * NPJ + j
+                sums[row] = term if z == 0 else sums[row] + term
+    for row in range(ROWS):
+        partial[row : row + 1, pl.ds(at, wide)] = jnp.sum(sums[row], axis=0, keepdims=True)
 
 
 def first_tables(index, turned, tables, both, proj, placed, partial):
@@ -342,11 +348,11 @@
             both[o * NZ : (o + 1) * NZ, :] = jnp.concatenate(split(turned[s * ORB + o]), axis=1)
 
         def chunk(k):
-            at = pl.multiple_of(k * 256, 256)
+            at = k * 256
             where = lax.broadcasted_iota(jnp.int32, (LANES, 256), 0) == index[4:5, pl.ds(at, 256)]
             project(both[...], where.astype(F32).astype(BF16), placed, partial, at, 256)
 
-        each(OWN // 256, chunk)
+        each(OWN // 256, chunk, False)
         tables[s] = gather_table(index, partial[...])
 
     each(2, table)
@@ -369,12 +375,8 @@
     return jnp.where(second, up, down)
 
 
-def join_table_kernel(params, table, local, note_came, field, out, pot):
+def join_table_kernel(table, note_came, field, out):
     out[...] = table[...] + note_came[:TABLE]
-    upper = flag(params, 0)
-    there = note_came[TABLE:NOTE]
-    pot[:, :LANES] = jnp.where(upper, there, local[...])
-    pot[:, LANES:] = jnp.where(upper, local[...], there)
 
 
 def first_pair_kernel(params, table, came, energy, note_came, half):
@@ -625,28 +627,27 @@
     stage = [pltpu.VMEM((LANES, LANES), F32)] * 2
 
     raw = orbitals[:, 0]
-    came = send(lax.dynamic_slice_in_dim(raw, (1 - side) * ORB, ORB, 0), SWAP)
+    going = lax.dynamic_slice_in_dim(raw, (1 - side) * ORB, ORB, 0)
+    came = send(jnp.concatenate([going, potential], axis=0), SWAP)
     line = pltpu.VMEM((1, PIECES), jnp.int32)
-    keep, params, ints, own_table, local, note = call(
+    keep, params, ints, own_table, note = call(
         begin_kernel,
-        [SM] * 4 + [HB] * 8,
+        [SM] * 4 + [HB] * 7,
         [
             (ORB, NZ, LANES),
             (16, LANES),
             ((8, OWN), jnp.int32),
             (TABLE, LANES),
-            (NZ, LANES),
             (NOTE + 24, LANES),
         ],
         (
             place, upper_edge, lower_edge, occupation, piece_column, piece_shift, piece_owner, piece_atom,
-            raw, projectors[0], potential[0], energies[0],
+            raw, projectors[0], energies[0],
         ),
         [
             line, line, line, line,
             pltpu.VMEM((2 * ORB, CX, CY * NZ), F32),
             pltpu.VMEM((NPJ, PIECES, LANES), F32),
-            pltpu.VMEM((CX, CY * NZ), F32),
             pltpu.VMEM((NPJ, LANES), F32),
             pltpu.VMEM((2 * ORB, NZ, LANES), F32),
             pltpu.VMEM((2, TABLE, LANES), F32),
@@ -654,7 +655,7 @@
             pltpu.VMEM((NPJ, NZ, OWN), F32),
             pltpu.VMEM((ROWS, OWN), F32),
             *stage,
-            pltpu.SemaphoreType.DMA((8,)),
+            pltpu.SemaphoreType.DMA((7,)),
         ],
         name="begin",
         room=ROOM,
@@ -662,21 +663,16 @@
     note_came = send(note, SWAP)
     proj = call(gate_kernel, [ANY] * 3, [(NPJ, PIECES, LANES)], (came, note_came, projectors[0]), flops=10**6, name="gate", passed=1)
     proj_came = send(proj[0], SWAP)
-    field, xl, xh, inner, outer = call(
+    field, pot, xl, xh, inner, outer = call(
         start_kernel,
-        [VM] * 4,
-        [grid] + [packed] * 4,
-        (params, keep, came, edge_w),
+        [VM] * 5,
+        [grid, (NZ, COLS)] + [packed] * 4,
+        (params, keep, came, potential, edge_w),
         stage,
         name="start",
     )
-    table, pot = call(
-        join_table_kernel,
-        [VM] * 4 + [ANY],
-        [(TABLE, LANES), (NZ, COLS)],
-        (params, own_table, local, note_came, field),
-        flops=10**6,
-        name="join_table",
+    table = call(
+        join_table_kernel, [VM] * 2 + [ANY], (TABLE, LANES), (own_table, note_came, field), flops=10**6, name="join_table"
     )
     placed, index = call(
         prepare_kernel,

time: 139 us -> 138 us (level)
  waiting for transfers between devices: 45.6 us -> 41.3 us
  starting transfers between devices: 48.7 us -> 50.5 us
    ppermute x41, waiting for transfers between devices: 45.6 us -> 41.3 us  [send(): return lax.ppermute(value, 'dom', pairs)]
  transfers between devices with their start and end apart: 43 -> 43, of which waited for: 24 -> 24; matrix products, arithmetic and copies ran while one was open for 0% -> 1% of each run, Pallas kernels for 21% -> 21%
where the time goes in v2:
time: 138 us; the launch traced here: 137 us
  starting transfers between devices  50.5 us (37%)
  waiting for transfers between devices  41.3 us (30%)
  Pallas kernels  40.3 us (29%)
  between operations  2.44 us (2%)
  other arithmetic  1.59 us (1%)
    ppermute x41, starting transfers between devices, send(): return lax.ppermute(value, 'dom', pairs)  45.2 us
    ppermute x41, waiting for transfers between devices, send(): return lax.ppermute(value, 'dom', pairs)  41.3 us
    pallas_call x34, Pallas kernels, call(): pl.pallas_call(kernel, out_shape=[jax.ShapeDtypeStruct(*out) for out in o...  40.3 us
  transfers between devices with their start and end apart: 43, of which 24 were waited for; matrix products, arithmetic and copies ran while one was open for 1% of the time, Pallas kernels for 21%

profile of v2, /device:TPU:0, one launch (start us, length us, event | category | flops | bytes accessed | tf_op | source)
XLA Modules:
  0.0 137.4 jit_solution(17336643241803133729)
XLA Ops:
  2.7 3.4 %collective-permute-start.1 = (f32[5,8,3072]{2,1,0:T(8,128)S(1)}, f32[5,8,3072]{2,1,0:T(8,128)S(1)}, u32[]{:S(2)}, u32[]{:S(2)}) collective-permute-start(f32[5,8,3072]{2,1,0:T(8,128)S(1)} %pad_maximum_fusion), channel_id=1, source_target_pairs={{0,8},{1,9},{2,10},{3,11},{4,12},{5,13},{6,14},{7,15},{8,0},{9,1},... | collective-permute-start | bytes 1474568 | tf_op jit(solution)/shard_map/ppermute | solution.py:585
  8.0 7.1 %begin.1 = (f32[4,192,128]{2,1,0:T(8,128)}, f32[16,128]{1,0:T(8,128)}, s32[8,512]{1,0:T(8,128)}, f32[192,128]{1,0:T(8,128)}, f32[216,128]{1,0:T(8,128)}) custom-call(s32[3]{0:T(128)} %pad_add_fusion.place, f32[1]{0:T(128)S(6)} %copy.37.upper_edge, f32[1]{0:T(128)S(6)} %copy.36.lower_edge, f32[8]{0:T(128)} %weights.1, s32[1,448]{1,0:T(1,128)} %column_in.1, ...), custom_call_target="tpu_custom_call" | custom-call | flops 100000000 | bytes 4000000 | tf_op jit(solution)/shard_map/begin/pallas_call | solution.py:570
  15.6 6.1 %collective-permute-done.note_came = f32[216,128]{1,0:T(8,128)S(1)} collective-permute-done((f32[216,128]{1,0:T(8,128)}, f32[216,128]{1,0:T(8,128)S(1)}, u32[]{:S(2)}, u32[]{:S(2)}) %collective-permute-start) | collective-permute-done | bytes 110624 | tf_op jit(solution)/shard_map/ppermute | solution.py:585
  22.9 1.7 %start.1 = (f32[4,192,256]{2,1,0:T(8,128)S(1)}, f32[192,256]{1,0:T(8,128)S(1)}, f32[4,144,128]{2,1,0:T(8,128)S(1)}, f32[4,144,128]{2,1,0:T(8,128)S(1)}, f32[4,14...) custom-call(f32[16,128]{1,0:T(8,128)S(1)} %copy-done.2, f32[4,192,128]{2,1,0:T(8,128)S(1)} %copy-done.6, ...), custom_call_target="tpu_custom_call" | custom-call | flops 100000000 | bytes 4000000 | tf_op jit(solution)/shard_map/start/pallas_call | solution.py:570
  24.8 1.3 collective-permute-done.3.came
  26.1 1.5 %collective-permute-start.4 = (f32[136,128]{1,0:T(8,128)S(1)}, f32[136,128]{1,0:T(8,128)S(1)}, u32[]{:S(2)}, u32[]{:S(2)}) collective-permute-start(f32[136,128]{1,0:T(8,128)S(1)} %pair.4.half.mine), channel_id=1, source_target_pairs={{0,7},{1,2},{2,1},{3,4},{4,3},{5,6},{6,5},{7,0},{8,15},{9,10},{10,... | collective-permute-start | bytes 208904 | tf_op jit(solution)/shard_map/ppermute | solution.py:585
  28.8 1.9 %collective-permute-start.9 = (f32[4,144,128]{2,1,0:T(8,128)S(1)}, f32[4,144,128]{2,1,0:T(8,128)S(1)}, u32[]{:S(2)}, u32[]{:S(2)}) collective-permute-start(f32[4,144,128]{2,1,0:T(8,128)S(1)} %get-tuple-element.72), channel_id=1, source_target_pairs={{0,16},{1,17},{2,18},{3,19},{4,20},{5,21},{6,22},{7,23},{8,24},{9,... | collective-permute-start | bytes 884744 | tf_op jit(solution)/shard_map/ppermute | solution.py:585
  31.1 4.0 %collective-permute-start.10 = (f32[4,144,128]{2,1,0:T(8,128)S(1)}, f32[4,144,128]{2,1,0:T(8,128)S(1)}, u32[]{:S(2)}, u32[]{:S(2)}) collective-permute-start(f32[4,144,128]{2,1,0:T(8,128)S(1)} %get-tuple-element.73), channel_id=1, source_target_pairs={{0,48},{1,49},{2,50},{3,51},{4,52},{5,53},{6,54},{7,55},{8,56},{9,... | collective-permute-start | bytes 884744 | tf_op jit(solution)/shard_map/ppermute | solution.py:585
  35.2 1.4 %local.4.acc = f32[4,192,256]{2,1,0:T(8,128)S(1)} custom-call(f32[16,128]{1,0:T(8,128)S(1)} %copy-done.2, f32[136,128]{1,0:T(8,128)S(1)} %pair.4.half.mine, f32[4,192,256]{2,1,0:T(8,128)S(1)} %get-tuple-element.66.field.before, f32[4,192,256]{2,1,0:T(8,128)S(1)} %get-tuple-element.66.field.before, f32[192,256]{1,0:T(8,128)S(1)} %get-tuple-element.67.pot, ...), custom_call_target="tpu_custom_call" | custom-call | flops 100000000 | bytes 4000000 | tf_op jit(solution)/shard_map/local/pallas_call | solution.py:570
  37.6 1.9 %collective-permute-start.5 = (f32[72,128]{1,0:T(8,128)S(1)}, f32[72,128]{1,0:T(8,128)S(1)}, u32[]{:S(2)}, u32[]{:S(2)}) collective-permute-start(f32[72,128]{1,0:T(8,128)S(1)} %get-tuple-element.69.high), channel_id=1, source_target_pairs={{0,16},{1,17},{2,18},{3,19},{4,20},{5,21},{6,22},{7,23},{8,24},{9,... | collective-permute-start | bytes 110600 | tf_op jit(solution)/shard_map/ppermute | solution.py:585
  39.8 2.0 %collective-permute-done.10.xh = f32[4,144,128]{2,1,0:T(8,128)S(1)} collective-permute-done((f32[4,144,128]{2,1,0:T(8,128)S(1)}, f32[4,144,128]{2,1,0:T(8,128)S(1)}, u32[]{:S(2)}, u32[]{:S(2)}) %collective-permute-start.10) | collective-permute-done | bytes 294944 | tf_op jit(solution)/shard_map/ppermute | solution.py:585
  41.8 1.6 %halo.4.acc = f32[4,192,256]{2,1,0:T(8,128)S(1)} custom-call(f32[16,128]{1,0:T(8,128)S(1)} %copy-done.2, f32[4,144,128]{2,1,0:T(8,128)S(1)} %collective-permute-done.7.inner, f32[4,144,128]{2,1,0:T(8,128)S(1)} %collective-permute-done.8.outer, f32[4,144,128]{2,1,0:T(8,128)S(1)} %collective-permute-done.9.xl, f32[4,144,128]{2,1,0:T(8,128)S(1)} %collective-permute-done.10.xh, ...), custom_call_target="tpu_custom_call" | custom-call | flops 100000000 | bytes 4000000 | tf_op jit(solution)/shard_map/halo/pallas_call | solution.py:570
  43.7 4.1 %collective-permute-done.2.came = f32[4,448,128]{2,1,0:T(8,128)S(1)} collective-permute-done((f32[4,448,128]{2,1,0:T(8,128)S(1)}, f32[4,448,128]{2,1,0:T(8,128)S(1)}, u32[]{:S(2)}, u32[]{:S(2)}) %collective-permute-start.2) | collective-permute-done | bytes 917536 | tf_op jit(solution)/shard_map/ppermute | solution.py:585
  47.8 2.0 %prepare.1 = (f32[4,192,896]{2,1,0:T(8,128)S(1)}, s32[4,896]{1,0:T(4,128)S(1)}) custom-call(s32[8,512]{1,0:T(8,128)S(1)} %copy-done.9, f32[216,128]{1,0:T(8,128)S(1)} %collective-permute-done.note_came, f32[4,448,128]{2,1,0:T(8,128)S(1)} %bitcast.14, f32[4,448,128]{2,1,0:T(8,128)S(1)} %collective-permute-done.2.came), custom_call_target="tpu_custom_call" | custom-call | flops 100000000 | bytes 4000000 | tf_op jit(solution)/shard_map/prepare/pallas_call | solution.py:570
  49.8 2.4 %update.3 = (f32[4,192,256]{2,1,0:T(8,128)S(1)}, f32[4,144,128]{2,1,0:T(8,128)S(1)}, f32[4,144,128]{2,1,0:T(8,128)S(1)}, f32[4,144,128]{2,1,0:T(8,128)S(1)}, f32[4,144,128]{2,1,0:T(8,128)S(1)}) custom-call(f32[16,128]{1,0:T(8,128)S(1)} %copy-done.2, s32[4,896]{1,0:T(4,128)S(1)} %get-tuple-element.63.index, f32[4,192,256]{2,1,0:T(8,128)S(1)} %get-tuple-element.75.acc, ...), custom_call_target="tpu_custom_call" | custom-call | flops 100000000 | bytes 4000000 | tf_op jit(solution)/shard_map/update/pallas_call | solution.py:570
  52.3 1.7 %collective-permute-start.17 = (f32[4,144,128]{2,1,0:T(8,128)S(1)}, f32[4,144,128]{2,1,0:T(8,128)S(1)}, u32[]{:S(2)}, u32[]{:S(2)}) collective-permute-start(f32[4,144,128]{2,1,0:T(8,128)S(1)} %get-tuple-element.83), channel_id=1, source_target_pairs={{0,7},{1,2},{2,1},{3,4},{4,3},{5,6},{6,5},{7,0},{8,15},{9,10},{10,... | collective-permute-start | bytes 884744 | tf_op jit(solution)/shard_map/ppermute | solution.py:585
  54.0 1.9 %collective-permute-start.18 = (f32[4,144,128]{2,1,0:T(8,128)S(1)}, f32[4,144,128]{2,1,0:T(8,128)S(1)}, u32[]{:S(2)}, u32[]{:S(2)}) collective-permute-start(f32[4,144,128]{2,1,0:T(8,128)S(1)} %get-tuple-element.84), channel_id=1, source_target_pairs={{0,16},{1,17},{2,18},{3,19},{4,20},{5,21},{6,22},{7,23},{8,24},{9,... | collective-permute-start | bytes 884744 | tf_op jit(solution)/shard_map/ppermute | solution.py:585
  55.9 2.1 %collective-permute-start.19 = (f32[4,144,128]{2,1,0:T(8,128)S(1)}, f32[4,144,128]{2,1,0:T(8,128)S(1)}, u32[]{:S(2)}, u32[]{:S(2)}) collective-permute-start(f32[4,144,128]{2,1,0:T(8,128)S(1)} %get-tuple-element.85), channel_id=1, source_target_pairs={{0,48},{1,49},{2,50},{3,51},{4,52},{5,53},{6,54},{7,55},{8,56},{9,... | collective-permute-start | bytes 884744 | tf_op jit(solution)/shard_map/ppermute | solution.py:585
  58.1 1.9 %table.3 = f32[192,128]{1,0:T(8,128)S(1)} custom-call(s32[4,896]{1,0:T(4,128)S(1)} %get-tuple-element.63.index, f32[4,192,256]{2,1,0:T(8,128)S(1)} %get-tuple-element.78.field.before, f32[4,192,896]{2,1,0:T(8,128)S(1)} %get-tuple-element.77.placed), custom_call_target="tpu_custom_call" | custom-call | flops 100000000 | bytes 4000000 | tf_op jit(solution)/shard_map/table/pallas_call | solution.py:570
  60.1 1.3 collective-permute-done.12.came
  62.2 1.4 %local.5.acc = f32[4,192,256]{2,1,0:T(8,128)S(1)} custom-call(f32[16,128]{1,0:T(8,128)S(1)} %copy-done.2, f32[128,128]{1,0:T(8,128)S(1)} %pair.5.half.mine, f32[4,192,256]{2,1,0:T(8,128)S(1)} %get-tuple-element.78.field.before, f32[4,192,256]{2,1,0:T(8,128)S(1)} %get-tuple-element.66.field.before, f32[192,256]{1,0:T(8,128)S(1)} %get-tuple-element.67.pot, ...), custom_call_target="tpu_custom_call" | custom-call | flops 100000000 | bytes 4000000 | tf_op jit(solution)/shard_map/local/pallas_call | solution.py:570
  63.6 3.0 %collective-permute-done.13.came = f32[128,128]{1,0:T(8,128)S(1)} collective-permute-done((f32[128,128]{1,0:T(8,128)S(1)}, f32[128,128]{1,0:T(8,128)S(1)}, u32[]{:S(2)}, u32[]{:S(2)}) %collective-permute-start.13) | collective-permute-done | bytes 65568 | tf_op jit(solution)/shard_map/ppermute | solution.py:585
  66.6 2.1 %collective-permute-start.15 = (f32[64,128]{1,0:T(8,128)S(1)}, f32[64,128]{1,0:T(8,128)S(1)}, u32[]{:S(2)}, u32[]{:S(2)}) collective-permute-start(f32[64,128]{1,0:T(8,128)S(1)} %get-tuple-element.79.low), channel_id=1, source_target_pairs={{0,48},{1,49},{2,50},{3,51},{4,52},{5,53},{6,54},{7,55},{8,56},{9,... | collective-permute-start | bytes 98312 | tf_op jit(solution)/shard_map/ppermute | solution.py:585
  68.7 1.6 %halo.5.acc = f32[4,192,256]{2,1,0:T(8,128)S(1)} custom-call(f32[16,128]{1,0:T(8,128)S(1)} %copy-done.2, f32[4,144,128]{2,1,0:T(8,128)S(1)} %collective-permute-done.16.inner, f32[4,144,128]{2,1,0:T(8,128)S(1)} %collective-permute-done.17.outer, f32[4,144,128]{2,1,0:T(8,128)S(1)} %collective-permute-done.18.xl, ...), custom_call_target="tpu_custom_call" | custom-call | flops 100000000 | bytes 4000000 | tf_op jit(solution)/shard_map/halo/pallas_call | solution.py:570
  70.5 3.2 %collective-permute-done.14.below = f32[64,128]{1,0:T(8,128)S(1)} collective-permute-done((f32[64,128]{1,0:T(8,128)S(1)}, f32[64,128]{1,0:T(8,128)S(1)}, u32[]{:S(2)}, u32[]{:S(2)}) %collective-permute-start.14) | collective-permute-done | bytes 32800 | tf_op jit(solution)/shard_map/ppermute | solution.py:585
  75.1 2.4 %update.4 = (f32[4,192,256]{2,1,0:T(8,128)S(1)}, f32[4,144,128]{2,1,0:T(8,128)S(1)}, f32[4,144,128]{2,1,0:T(8,128)S(1)}, f32[4,144,128]{2,1,0:T(8,128)S(1)}, f32[4,144,128]{2,1,0:T(8,128)S(1)}) custom-call(f32[16,128]{1,0:T(8,128)S(1)} %copy-done.2, s32[4,896]{1,0:T(4,128)S(1)} %get-tuple-element.63.index, f32[4,192,256]{2,1,0:T(8,128)S(1)} %get-tuple-element.87.acc, ...), custom_call_target="tpu_custom_call" | custom-call | flops 100000000 | bytes 4000000 | tf_op jit(solution)/shard_map/update/pallas_call | solution.py:570
  77.8 3.2 %collective-permute-start.28 = (f32[4,144,128]{2,1,0:T(8,128)S(1)}, f32[4,144,128]{2,1,0:T(8,128)S(1)}, u32[]{:S(2)}, u32[]{:S(2)}) collective-permute-start(f32[4,144,128]{2,1,0:T(8,128)S(1)} %get-tuple-element.95), channel_id=1, source_target_pairs={{0,48},{1,49},{2,50},{3,51},{4,52},{5,53},{6,54},{7,55},{8,56},{9,... | collective-permute-start | bytes 884744 | tf_op jit(solution)/shard_map/ppermute | solution.py:585
  81.1 1.9 %table.4 = f32[192,128]{1,0:T(8,128)S(1)} custom-call(s32[4,896]{1,0:T(4,128)S(1)} %get-tuple-element.63.index, f32[4,192,256]{2,1,0:T(8,128)S(1)} %get-tuple-element.89.field.before, f32[4,192,896]{2,1,0:T(8,128)S(1)} %get-tuple-element.77.placed), custom_call_target="tpu_custom_call" | custom-call | flops 100000000 | bytes 4000000 | tf_op jit(solution)/shard_map/table/pallas_call | solution.py:570
  84.4 2.3 %collective-permute-start.22 = (f32[128,128]{1,0:T(8,128)S(1)}, f32[128,128]{1,0:T(8,128)S(1)}, u32[]{:S(2)}, u32[]{:S(2)}) collective-permute-start(f32[128,128]{1,0:T(8,128)S(1)} %pair.6.half.mine), channel_id=1, source_target_pairs={{0,7},{1,2},{2,1},{3,4},{4,3},{5,6},{6,5},{7,0},{8,15},{9,10},{10,... | collective-permute-start | bytes 196616 | tf_op jit(solution)/shard_map/ppermute | solution.py:585
  86.7 1.4 %local.6.acc = f32[4,192,256]{2,1,0:T(8,128)S(1)} custom-call(f32[16,128]{1,0:T(8,128)S(1)} %copy-done.2, f32[128,128]{1,0:T(8,128)S(1)} %pair.6.half.mine, f32[4,192,256]{2,1,0:T(8,128)S(1)} %get-tuple-element.89.field.before, f32[4,192,256]{2,1,0:T(8,128)S(1)} %get-tuple-element.78.field.before, f32[192,256]{1,0:T(8,128)S(1)} %get-tuple-element.67.pot, ...), custom_call_target="tpu_custom_call" | custom-call | flops 100000000 | bytes 4000000 | tf_op jit(solution)/shard_map/local/pallas_call | solution.py:570
  88.1 1.5 %collective-permute-done.22.came = f32[128,128]{1,0:T(8,128)S(1)} collective-permute-done((f32[128,128]{1,0:T(8,128)S(1)}, f32[128,128]{1,0:T(8,128)S(1)}, u32[]{:S(2)}, u32[]{:S(2)}) %collective-permute-start.22) | collective-permute-done | bytes 65568 | tf_op jit(solution)/shard_map/ppermute | solution.py:585
  89.7 2.0 %collective-permute-start.23 = (f32[64,128]{1,0:T(8,128)S(1)}, f32[64,128]{1,0:T(8,128)S(1)}, u32[]{:S(2)}, u32[]{:S(2)}) collective-permute-start(f32[64,128]{1,0:T(8,128)S(1)} %get-tuple-element.91.high), channel_id=1, source_target_pairs={{0,16},{1,17},{2,18},{3,19},{4,20},{5,21},{6,22},{7,23},{8,24},{9,... | collective-permute-start | bytes 98312 | tf_op jit(solution)/shard_map/ppermute | solution.py:585
  91.7 1.6 %halo.6.acc = f32[4,192,256]{2,1,0:T(8,128)S(1)} custom-call(f32[16,128]{1,0:T(8,128)S(1)} %copy-done.2, f32[4,144,128]{2,1,0:T(8,128)S(1)} %collective-permute-done.25.inner, f32[4,144,128]{2,1,0:T(8,128)S(1)} %collective-permute-done.26.outer, f32[4,144,128]{2,1,0:T(8,128)S(1)} %collective-permute-done.27.xl, ...), custom_call_target="tpu_custom_call" | custom-call | flops 100000000 | bytes 4000000 | tf_op jit(solution)/shard_map/halo/pallas_call | solution.py:570
  93.6 1.3 collective-permute-done.23.below
  96.5 2.4 %update.5 = (f32[4,192,256]{2,1,0:T(8,128)S(1)}, f32[4,144,128]{2,1,0:T(8,128)S(1)}, f32[4,144,128]{2,1,0:T(8,128)S(1)}, f32[4,144,128]{2,1,0:T(8,128)S(1)}, f32[4,144,128]{2,1,0:T(8,128)S(1)}) custom-call(f32[16,128]{1,0:T(8,128)S(1)} %copy-done.2, s32[4,896]{1,0:T(4,128)S(1)} %get-tuple-element.63.index, f32[4,192,256]{2,1,0:T(8,128)S(1)} %get-tuple-element.97.acc, ...), custom_call_target="tpu_custom_call" | custom-call | flops 100000000 | bytes 4000000 | tf_op jit(solution)/shard_map/update/pallas_call | solution.py:570
  99.1 1.4 %collective-permute-start.35 = (f32[4,144,128]{2,1,0:T(8,128)S(1)}, f32[4,144,128]{2,1,0:T(8,128)S(1)}, u32[]{:S(2)}, u32[]{:S(2)}) collective-permute-start(f32[4,144,128]{2,1,0:T(8,128)S(1)} %get-tuple-element.103), channel_id=1, source_target_pairs={{0,7},{1,2},{2,1},{3,4},{4,3},{5,6},{6,5},{7,0},{8,15},{9,10},{10,... | collective-permute-start | bytes 884744 | tf_op jit(solution)/shard_map/ppermute | solution.py:585
  101.0 2.7 %collective-permute-start.37 = (f32[4,144,128]{2,1,0:T(8,128)S(1)}, f32[4,144,128]{2,1,0:T(8,128)S(1)}, u32[]{:S(2)}, u32[]{:S(2)}) collective-permute-start(f32[4,144,128]{2,1,0:T(8,128)S(1)} %get-tuple-element.105), channel_id=1, source_target_pairs={{0,48},{1,49},{2,50},{3,51},{4,52},{5,53},{6,54},{7,55},{8,56},{9,... | collective-permute-start | bytes 884744 | tf_op jit(solution)/shard_map/ppermute | solution.py:585
  103.8 1.9 %table.5 = f32[192,128]{1,0:T(8,128)S(1)} custom-call(s32[4,896]{1,0:T(4,128)S(1)} %get-tuple-element.63.index, f32[4,192,256]{2,1,0:T(8,128)S(1)} %get-tuple-element.99.field, f32[4,192,896]{2,1,0:T(8,128)S(1)} %get-tuple-element.77.placed), custom_call_target="tpu_custom_call" | custom-call | flops 100000000 | bytes 4000000 | tf_op jit(solution)/shard_map/table/pallas_call | solution.py:570
  108.2 1.4 %local.7.acc = f32[4,192,256]{2,1,0:T(8,128)S(1)} custom-call(f32[16,128]{1,0:T(8,128)S(1)} %copy-done.2, f32[128,128]{1,0:T(8,128)S(1)} %pair.7.half.mine, f32[4,192,256]{2,1,0:T(8,128)S(1)} %get-tuple-element.99.field, f32[4,192,256]{2,1,0:T(8,128)S(1)} %get-tuple-element.89.field.before, f32[192,256]{1,0:T(8,128)S(1)} %get-tuple-element.67.pot, ...), custom_call_target="tpu_custom_call" | custom-call | flops 100000000 | bytes 4000000 | tf_op jit(solution)/shard_map/local/pallas_call | solution.py:570
  109.6 2.3 %collective-permute-done.31.came = f32[128,128]{1,0:T(8,128)S(1)} collective-permute-done((f32[128,128]{1,0:T(8,128)S(1)}, f32[128,128]{1,0:T(8,128)S(1)}, u32[]{:S(2)}, u32[]{:S(2)}) %collective-permute-start.31) | collective-permute-done | bytes 65568 | tf_op jit(solution)/shard_map/ppermute | solution.py:585
  112.0 2.0 %collective-permute-start.32 = (f32[64,128]{1,0:T(8,128)S(1)}, f32[64,128]{1,0:T(8,128)S(1)}, u32[]{:S(2)}, u32[]{:S(2)}) collective-permute-start(f32[64,128]{1,0:T(8,128)S(1)} %get-tuple-element.101.high), channel_id=1, source_target_pairs={{0,16},{1,17},{2,18},{3,19},{4,20},{5,21},{6,22},{7,23},{8,24},{9,... | collective-permute-start | bytes 98312 | tf_op jit(solution)/shard_map/ppermute | solution.py:585
  114.0 1.6 %halo.7.acc = f32[4,192,256]{2,1,0:T(8,128)S(1)} custom-call(f32[16,128]{1,0:T(8,128)S(1)} %copy-done.2, f32[4,144,128]{2,1,0:T(8,128)S(1)} %collective-permute-done.34.inner, f32[4,144,128]{2,1,0:T(8,128)S(1)} %collective-permute-done.35.outer, f32[4,144,128]{2,1,0:T(8,128)S(1)} %collective-permute-done.36.xl, ...), custom_call_target="tpu_custom_call" | custom-call | flops 100000000 | bytes 4000000 | tf_op jit(solution)/shard_map/halo/pallas_call | solution.py:570
  115.9 1.3 collective-permute-done.32.below
  118.6 2.8 %finish.1 = (f32[4,8,3072]{2,1,0:T(8,128)S(1)}, f32[4,8,3072]{2,1,0:T(8,128)S(1)}, f32[4,192,256]{2,1,0:T(8,128)S(1)}) custom-call(f32[16,128]{1,0:T(8,128)S(1)} %copy-done.2, s32[4,896]{1,0:T(4,128)S(1)} %get-tuple-element.63.index, f32[4,192,256]{2,1,0:T(8,128)S(1)} %get-tuple-element.107.acc, f32[128,128]{1,0:T(8,128)S(1)} %get-tuple-element.108.mine, ...), custom_call_target="tpu_custom_call" | custom-call | flops 100000000 | bytes 4000000 | tf_op jit(solution)/shard_map/finish/pallas_call | solution.py:570
  121.4 2.4 %collective-permute-start.39 = (f32[4,8,3072]{2,1,0:T(8,128)S(1)}, f32[4,8,3072]{2,1,0:T(8,128)S(1)}, u32[]{:S(2)}, u32[]{:S(2)}) collective-permute-start(f32[4,8,3072]{2,1,0:T(8,128)S(1)} %get-tuple-element.109), channel_id=1, source_target_pairs={{0,8},{1,9},{2,10},{3,11},{4,12},{5,13},{6,14},{7,15},{8,0},{9,1},... | collective-permute-start | bytes 1179656 | tf_op jit(solution)/shard_map/ppermute | solution.py:585
  125.4 2.7 %collective-permute-start.41 = (f32[8,1536]{1,0:T(8,128)S(1)}, f32[8,1536]{1,0:T(8,128)S(1)}, u32[]{:S(2)}, u32[]{:S(2)}) collective-permute-start(f32[8,1536]{1,0:T(8,128)S(1)} %get-tuple-element.112), channel_id=1, source_target_pairs={{0,64},{64,0},{1,65},{65,1},{2,66},{66,2},{3,67},{67,3},{4,68},{68... | collective-permute-start | bytes 147464 | tf_op jit(solution)/shard_map/ppermute | solution.py:801
  128.1 2.6 %collective-permute-start.42 = (f32[8,1536]{1,0:T(8,128)S(1)}, f32[8,1536]{1,0:T(8,128)S(1)}, u32[]{:S(2)}, u32[]{:S(2)}) collective-permute-start(f32[8,1536]{1,0:T(8,128)S(1)} %get-tuple-element.113), channel_id=1, source_target_pairs={{0,72},{1,73},{2,74},{3,75},{4,76},{5,77},{6,78},{7,79},{8,64},{9,... | collective-permute-start | bytes 147464 | tf_op jit(solution)/shard_map/ppermute | solution.py:802
  130.7 5.6 %collective-permute-done.40.b = f32[8,1536]{1,0:T(8,128)S(1)} collective-permute-done((f32[8,1536]{1,0:T(8,128)S(1)}, f32[8,1536]{1,0:T(8,128)S(1)}, u32[]{:S(2)}, u32[]{:S(2)}) %collective-permute-start.40) | collective-permute-done | bytes 49184 | tf_op jit(solution)/shard_map/ppermute | solution.py:585
  (98 shorter events, 21.3 us)
Async XLA Ops:
  2.7 19.0 %collective-permute-start.1 = (f32[5,8,3072]{2,1,0:T(8,128)S(1)}, f32[5,8,3072]{2,1,0:T(8,128)S(1)}, u32[]{:S(2)}, u32[]{:S(2)}) collective-permute-start(f32[5,8,3072]{2,1,0:T(8,128)S(1)} %pad_maximum_fusion), channel_id=1, source_target_pairs={{0,8},{1,9},{2,10},{3,11},{4,12},{5,13},{6,14},{7,15},{8,0},{9,1},... | collective-permute-start | bytes 1474568 | tf_op jit(solution)/shard_map/ppermute | solution.py:585
  8.0 14.9 %copy-start.5 = (bf16[256,256]{1,0:T(8,128)(2,1)S(1)}, bf16[256,256]{1,0:T(8,128)(2,1)}, u32[]{:S(2)}) copy-start(bf16[256,256]{1,0:T(8,128)(2,1)} %constant.57.clone.edge.rest_0_) | copy-start | bytes 393220
  8.0 14.9 %copy-start.7 = (f32[1,8,3072]{2,1,0:T(8,128)S(1)}, f32[1,8,3072]{2,1,0:T(8,128)}, u32[]{:S(2)}) copy-start(f32[1,8,3072]{2,1,0:T(8,128)} %potential.1) | copy-start | bytes 294916
  15.2 6.5 %collective-permute-start = (f32[216,128]{1,0:T(8,128)}, f32[216,128]{1,0:T(8,128)S(1)}, u32[]{:S(2)}, u32[]{:S(2)}) collective-permute-start(f32[216,128]{1,0:T(8,128)} %get-tuple-element.62), channel_id=1, source_target_pairs={{0,8},{1,9},{2,10},{3,11},{4,12},{5,13},{6,14},{7,15},{8,0},{9,1},... | collective-permute-start | bytes 331784 | tf_op jit(solution)/shard_map/ppermute | solution.py:585
  15.6 19.6 %copy-start.3 = (bf16[2,256,256]{2,1,0:T(8,128)(2,1)S(1)}, bf16[2,256,256]{2,1,0:T(8,128)(2,1)}, u32[]{:S(2)}) copy-start(bf16[2,256,256]{2,1,0:T(8,128)(2,1)} %constant.54.clone.own_w) | copy-start | bytes 786436
  15.6 19.6 %copy-start.4 = (bf16[2,192,192]{2,1,0:T(8,128)(2,1)S(1)}, bf16[2,192,192]{2,1,0:T(8,128)(2,1)}, u32[]{:S(2)}) copy-start(bf16[2,192,192]{2,1,0:T(8,128)(2,1)} %constant.56.clone.ring_w) | copy-start | bytes 442372
  21.7 26.1 %collective-permute-start.2 = (f32[4,448,128]{2,1,0:T(8,128)S(1)}, f32[4,448,128]{2,1,0:T(8,128)S(1)}, u32[]{:S(2)}, u32[]{:S(2)}) collective-permute-start(f32[4,448,128]{2,1,0:T(8,128)S(1)} %gate.1), channel_id=1, source_target_pairs={{0,8},{1,9},{2,10},{3,11},{4,12},{5,13},{6,14},{7,15},{8,0},{9,1},... | collective-permute-start | bytes 2752520 | tf_op jit(solution)/shard_map/ppermute | solution.py:585
  24.6 17.1 %copy-start = (bf16[2,512,256]{2,1,0:T(8,128)(2,1)S(1)}, bf16[2,512,256]{2,1,0:T(8,128)(2,1)}, u32[]{:S(2)}) copy-start(bf16[2,512,256]{2,1,0:T(8,128)(2,1)} %constant.55.clone.halo_w) | copy-start | bytes 1572868
  24.7 1.4 %collective-permute-start.3 = (f32[192,128]{1,0:T(8,128)S(1)}, f32[192,128]{1,0:T(8,128)S(1)}, u32[]{:S(2)}, u32[]{:S(2)}) collective-permute-start(f32[192,128]{1,0:T(8,128)S(1)} %join_table.1.table), channel_id=1, source_target_pairs={{0,1},{1,0},{2,3},{3,2},{4,5},{5,4},{6,7},{7,6},{8,9},{9,8},{10,11... | collective-permute-start | bytes 294920 | tf_op jit(solution)/shard_map/ppermute | solution.py:585
  26.1 5.0 %collective-permute-start.4 = (f32[136,128]{1,0:T(8,128)S(1)}, f32[136,128]{1,0:T(8,128)S(1)}, u32[]{:S(2)}, u32[]{:S(2)}) collective-permute-start(f32[136,128]{1,0:T(8,128)S(1)} %pair.4.half.mine), channel_id=1, source_target_pairs={{0,7},{1,2},{2,1},{3,4},{4,3},{5,6},{6,5},{7,0},{8,15},{9,10},{10,... | collective-permute-start | bytes 208904 | tf_op jit(solution)/shard_map/ppermute | solution.py:585
  27.5 9.1 %collective-permute-start.7 = (f32[4,144,128]{2,1,0:T(8,128)S(1)}, f32[4,144,128]{2,1,0:T(8,128)S(1)}, u32[]{:S(2)}, u32[]{:S(2)}) collective-permute-start(f32[4,144,128]{2,1,0:T(8,128)S(1)} %get-tuple-element.70), channel_id=1, source_target_pairs={{0,1},{1,0},{2,3},{3,2},{4,5},{5,4},{6,7},{7,6},{8,9},{9,8},{10,11... | collective-permute-start | bytes 884744 | tf_op jit(solution)/shard_map/ppermute | solution.py:585
  27.8 9.9 %collective-permute-start.8 = (f32[4,144,128]{2,1,0:T(8,128)S(1)}, f32[4,144,128]{2,1,0:T(8,128)S(1)}, u32[]{:S(2)}, u32[]{:S(2)}) collective-permute-start(f32[4,144,128]{2,1,0:T(8,128)S(1)} %get-tuple-element.71), channel_id=1, source_target_pairs={{0,7},{1,2},{2,1},{3,4},{4,3},{5,6},{6,5},{7,0},{8,15},{9,10},{10,... | collective-permute-start | bytes 884744 | tf_op jit(solution)/shard_map/ppermute | solution.py:585
  28.8 11.0 %collective-permute-start.9 = (f32[4,144,128]{2,1,0:T(8,128)S(1)}, f32[4,144,128]{2,1,0:T(8,128)S(1)}, u32[]{:S(2)}, u32[]{:S(2)}) collective-permute-start(f32[4,144,128]{2,1,0:T(8,128)S(1)} %get-tuple-element.72), channel_id=1, source_target_pairs={{0,16},{1,17},{2,18},{3,19},{4,20},{5,21},{6,22},{7,23},{8,24},{9,... | collective-permute-start | bytes 884744 | tf_op jit(solution)/shard_map/ppermute | solution.py:585
  31.1 10.6 %collective-permute-start.10 = (f32[4,144,128]{2,1,0:T(8,128)S(1)}, f32[4,144,128]{2,1,0:T(8,128)S(1)}, u32[]{:S(2)}, u32[]{:S(2)}) collective-permute-start(f32[4,144,128]{2,1,0:T(8,128)S(1)} %get-tuple-element.73), channel_id=1, source_target_pairs={{0,48},{1,49},{2,50},{3,51},{4,52},{5,53},{6,54},{7,55},{8,56},{9,... | collective-permute-start | bytes 884744 | tf_op jit(solution)/shard_map/ppermute | solution.py:585
  36.6 6.8 %collective-permute-start.6 = (f32[72,128]{1,0:T(8,128)S(1)}, f32[72,128]{1,0:T(8,128)S(1)}, u32[]{:S(2)}, u32[]{:S(2)}) collective-permute-start(f32[72,128]{1,0:T(8,128)S(1)} %get-tuple-element.68.low), channel_id=1, source_target_pairs={{0,48},{1,49},{2,50},{3,51},{4,52},{5,53},{6,54},{7,55},{8,56},{9,... | collective-permute-start | bytes 110600 | tf_op jit(solution)/shard_map/ppermute | solution.py:585
  37.6 6.0 %collective-permute-start.5 = (f32[72,128]{1,0:T(8,128)S(1)}, f32[72,128]{1,0:T(8,128)S(1)}, u32[]{:S(2)}, u32[]{:S(2)}) collective-permute-start(f32[72,128]{1,0:T(8,128)S(1)} %get-tuple-element.69.high), channel_id=1, source_target_pairs={{0,16},{1,17},{2,18},{3,19},{4,20},{5,21},{6,22},{7,23},{8,24},{9,... | collective-permute-start | bytes 110600 | tf_op jit(solution)/shard_map/ppermute | solution.py:585
  43.6 6.2 %collective-permute-start.11 = (f32[128,128]{1,0:T(8,128)S(1)}, f32[128,128]{1,0:T(8,128)S(1)}, u32[]{:S(2)}, u32[]{:S(2)}) collective-permute-start(f32[128,128]{1,0:T(8,128)S(1)} %get-tuple-element.76.mine), channel_id=1, source_target_pairs={{0,1},{1,0},{2,3},{3,2},{4,5},{5,4},{6,7},{7,6},{8,9},{9,8},{10,11... | collective-permute-start | bytes 196616 | tf_op jit(solution)/shard_map/ppermute | solution.py:585
  52.2 16.4 %collective-permute-start.16 = (f32[4,144,128]{2,1,0:T(8,128)S(1)}, f32[4,144,128]{2,1,0:T(8,128)S(1)}, u32[]{:S(2)}, u32[]{:S(2)}) collective-permute-start(f32[4,144,128]{2,1,0:T(8,128)S(1)} %get-tuple-element.82), channel_id=1, source_target_pairs={{0,1},{1,0},{2,3},{3,2},{4,5},{5,4},{6,7},{7,6},{8,9},{9,8},{10,11... | collective-permute-start | bytes 884744 | tf_op jit(solution)/shard_map/ppermute | solution.py:585
  52.3 16.3 %collective-permute-start.17 = (f32[4,144,128]{2,1,0:T(8,128)S(1)}, f32[4,144,128]{2,1,0:T(8,128)S(1)}, u32[]{:S(2)}, u32[]{:S(2)}) collective-permute-start(f32[4,144,128]{2,1,0:T(8,128)S(1)} %get-tuple-element.83), channel_id=1, source_target_pairs={{0,7},{1,2},{2,1},{3,4},{4,3},{5,6},{6,5},{7,0},{8,15},{9,10},{10,... | collective-permute-start | bytes 884744 | tf_op jit(solution)/shard_map/ppermute | solution.py:585
  54.0 14.6 %collective-permute-start.18 = (f32[4,144,128]{2,1,0:T(8,128)S(1)}, f32[4,144,128]{2,1,0:T(8,128)S(1)}, u32[]{:S(2)}, u32[]{:S(2)}) collective-permute-start(f32[4,144,128]{2,1,0:T(8,128)S(1)} %get-tuple-element.84), channel_id=1, source_target_pairs={{0,16},{1,17},{2,18},{3,19},{4,20},{5,21},{6,22},{7,23},{8,24},{9,... | collective-permute-start | bytes 884744 | tf_op jit(solution)/shard_map/ppermute | solution.py:585
  55.9 12.7 %collective-permute-start.19 = (f32[4,144,128]{2,1,0:T(8,128)S(1)}, f32[4,144,128]{2,1,0:T(8,128)S(1)}, u32[]{:S(2)}, u32[]{:S(2)}) collective-permute-start(f32[4,144,128]{2,1,0:T(8,128)S(1)} %get-tuple-element.85), channel_id=1, source_target_pairs={{0,48},{1,49},{2,50},{3,51},{4,52},{5,53},{6,54},{7,55},{8,56},{9,... | collective-permute-start | bytes 884744 | tf_op jit(solution)/shard_map/ppermute | solution.py:585
  60.0 1.4 %collective-permute-start.12 = (f32[192,128]{1,0:T(8,128)S(1)}, f32[192,128]{1,0:T(8,128)S(1)}, u32[]{:S(2)}, u32[]{:S(2)}) collective-permute-start(f32[192,128]{1,0:T(8,128)S(1)} %table.3), channel_id=1, source_target_pairs={{0,1},{1,0},{2,3},{3,2},{4,5},{5,4},{6,7},{7,6},{8,9},{9,8},{10,11... | collective-permute-start | bytes 294920 | tf_op jit(solution)/shard_map/ppermute | solution.py:585
  61.4 5.2 %collective-permute-start.13 = (f32[128,128]{1,0:T(8,128)S(1)}, f32[128,128]{1,0:T(8,128)S(1)}, u32[]{:S(2)}, u32[]{:S(2)}) collective-permute-start(f32[128,128]{1,0:T(8,128)S(1)} %pair.5.half.mine), channel_id=1, source_target_pairs={{0,7},{1,2},{2,1},{3,4},{4,3},{5,6},{6,5},{7,0},{8,15},{9,10},{10,... | collective-permute-start | bytes 196616 | tf_op jit(solution)/shard_map/ppermute | solution.py:585
  66.6 4.0 %collective-permute-start.15 = (f32[64,128]{1,0:T(8,128)S(1)}, f32[64,128]{1,0:T(8,128)S(1)}, u32[]{:S(2)}, u32[]{:S(2)}) collective-permute-start(f32[64,128]{1,0:T(8,128)S(1)} %get-tuple-element.79.low), channel_id=1, source_target_pairs={{0,48},{1,49},{2,50},{3,51},{4,52},{5,53},{6,54},{7,55},{8,56},{9,... | collective-permute-start | bytes 98312 | tf_op jit(solution)/shard_map/ppermute | solution.py:585
  68.7 5.1 %collective-permute-start.14 = (f32[64,128]{1,0:T(8,128)S(1)}, f32[64,128]{1,0:T(8,128)S(1)}, u32[]{:S(2)}, u32[]{:S(2)}) collective-permute-start(f32[64,128]{1,0:T(8,128)S(1)} %get-tuple-element.80.high), channel_id=1, source_target_pairs={{0,16},{1,17},{2,18},{3,19},{4,20},{5,21},{6,22},{7,23},{8,24},{9,... | collective-permute-start | bytes 98312 | tf_op jit(solution)/shard_map/ppermute | solution.py:585
  73.8 1.3 collective-permute-start.20
  77.6 12.1 %collective-permute-start.25 = (f32[4,144,128]{2,1,0:T(8,128)S(1)}, f32[4,144,128]{2,1,0:T(8,128)S(1)}, u32[]{:S(2)}, u32[]{:S(2)}) collective-permute-start(f32[4,144,128]{2,1,0:T(8,128)S(1)} %get-tuple-element.92), channel_id=1, source_target_pairs={{0,1},{1,0},{2,3},{3,2},{4,5},{5,4},{6,7},{7,6},{8,9},{9,8},{10,11... | collective-permute-start | bytes 884744 | tf_op jit(solution)/shard_map/ppermute | solution.py:585
  77.8 13.9 %collective-permute-start.26 = (f32[4,144,128]{2,1,0:T(8,128)S(1)}, f32[4,144,128]{2,1,0:T(8,128)S(1)}, u32[]{:S(2)}, u32[]{:S(2)}) collective-permute-start(f32[4,144,128]{2,1,0:T(8,128)S(1)} %get-tuple-element.93), channel_id=1, source_target_pairs={{0,7},{1,2},{2,1},{3,4},{4,3},{5,6},{6,5},{7,0},{8,15},{9,10},{10,... | collective-permute-start | bytes 884744 | tf_op jit(solution)/shard_map/ppermute | solution.py:585
  77.8 13.9 %collective-permute-start.27 = (f32[4,144,128]{2,1,0:T(8,128)S(1)}, f32[4,144,128]{2,1,0:T(8,128)S(1)}, u32[]{:S(2)}, u32[]{:S(2)}) collective-permute-start(f32[4,144,128]{2,1,0:T(8,128)S(1)} %get-tuple-element.94), channel_id=1, source_target_pairs={{0,16},{1,17},{2,18},{3,19},{4,20},{5,21},{6,22},{7,23},{8,24},{9,... | collective-permute-start | bytes 884744 | tf_op jit(solution)/shard_map/ppermute | solution.py:585
  77.8 13.9 %collective-permute-start.28 = (f32[4,144,128]{2,1,0:T(8,128)S(1)}, f32[4,144,128]{2,1,0:T(8,128)S(1)}, u32[]{:S(2)}, u32[]{:S(2)}) collective-permute-start(f32[4,144,128]{2,1,0:T(8,128)S(1)} %get-tuple-element.95), channel_id=1, source_target_pairs={{0,48},{1,49},{2,50},{3,51},{4,52},{5,53},{6,54},{7,55},{8,56},{9,... | collective-permute-start | bytes 884744 | tf_op jit(solution)/shard_map/ppermute | solution.py:585
  83.0 1.4 %collective-permute-start.21 = (f32[192,128]{1,0:T(8,128)S(1)}, f32[192,128]{1,0:T(8,128)S(1)}, u32[]{:S(2)}, u32[]{:S(2)}) collective-permute-start(f32[192,128]{1,0:T(8,128)S(1)} %table.4), channel_id=1, source_target_pairs={{0,1},{1,0},{2,3},{3,2},{4,5},{5,4},{6,7},{7,6},{8,9},{9,8},{10,11... | collective-permute-start | bytes 294920 | tf_op jit(solution)/shard_map/ppermute | solution.py:585
  84.4 5.2 %collective-permute-start.22 = (f32[128,128]{1,0:T(8,128)S(1)}, f32[128,128]{1,0:T(8,128)S(1)}, u32[]{:S(2)}, u32[]{:S(2)}) collective-permute-start(f32[128,128]{1,0:T(8,128)S(1)} %pair.6.half.mine), channel_id=1, source_target_pairs={{0,7},{1,2},{2,1},{3,4},{4,3},{5,6},{6,5},{7,0},{8,15},{9,10},{10,... | collective-permute-start | bytes 196616 | tf_op jit(solution)/shard_map/ppermute | solution.py:585
  89.6 4.0 %collective-permute-start.24 = (f32[64,128]{1,0:T(8,128)S(1)}, f32[64,128]{1,0:T(8,128)S(1)}, u32[]{:S(2)}, u32[]{:S(2)}) collective-permute-start(f32[64,128]{1,0:T(8,128)S(1)} %get-tuple-element.90.low), channel_id=1, source_target_pairs={{0,48},{1,49},{2,50},{3,51},{4,52},{5,53},{6,54},{7,55},{8,56},{9,... | collective-permute-start | bytes 98312 | tf_op jit(solution)/shard_map/ppermute | solution.py:585
  89.7 5.2 %collective-permute-start.23 = (f32[64,128]{1,0:T(8,128)S(1)}, f32[64,128]{1,0:T(8,128)S(1)}, u32[]{:S(2)}, u32[]{:S(2)}) collective-permute-start(f32[64,128]{1,0:T(8,128)S(1)} %get-tuple-element.91.high), channel_id=1, source_target_pairs={{0,16},{1,17},{2,18},{3,19},{4,20},{5,21},{6,22},{7,23},{8,24},{9,... | collective-permute-start | bytes 98312 | tf_op jit(solution)/shard_map/ppermute | solution.py:585
  94.9 1.6 %collective-permute-start.29 = (f32[128,128]{1,0:T(8,128)S(1)}, f32[128,128]{1,0:T(8,128)S(1)}, u32[]{:S(2)}, u32[]{:S(2)}) collective-permute-start(f32[128,128]{1,0:T(8,128)S(1)} %get-tuple-element.98.mine), channel_id=1, source_target_pairs={{0,1},{1,0},{2,3},{3,2},{4,5},{5,4},{6,7},{7,6},{8,9},{9,8},{10,11... | collective-permute-start | bytes 196616 | tf_op jit(solution)/shard_map/ppermute | solution.py:585
  98.9 13.1 %collective-permute-start.34 = (f32[4,144,128]{2,1,0:T(8,128)S(1)}, f32[4,144,128]{2,1,0:T(8,128)S(1)}, u32[]{:S(2)}, u32[]{:S(2)}) collective-permute-start(f32[4,144,128]{2,1,0:T(8,128)S(1)} %get-tuple-element.102), channel_id=1, source_target_pairs={{0,1},{1,0},{2,3},{3,2},{4,5},{5,4},{6,7},{7,6},{8,9},{9,8},{10,11... | collective-permute-start | bytes 884744 | tf_op jit(solution)/shard_map/ppermute | solution.py:585
  99.1 14.9 %collective-permute-start.35 = (f32[4,144,128]{2,1,0:T(8,128)S(1)}, f32[4,144,128]{2,1,0:T(8,128)S(1)}, u32[]{:S(2)}, u32[]{:S(2)}) collective-permute-start(f32[4,144,128]{2,1,0:T(8,128)S(1)} %get-tuple-element.103), channel_id=1, source_target_pairs={{0,7},{1,2},{2,1},{3,4},{4,3},{5,6},{6,5},{7,0},{8,15},{9,10},{10,... | collective-permute-start | bytes 884744 | tf_op jit(solution)/shard_map/ppermute | solution.py:585
  100.5 13.5 %collective-permute-start.36 = (f32[4,144,128]{2,1,0:T(8,128)S(1)}, f32[4,144,128]{2,1,0:T(8,128)S(1)}, u32[]{:S(2)}, u32[]{:S(2)}) collective-permute-start(f32[4,144,128]{2,1,0:T(8,128)S(1)} %get-tuple-element.104), channel_id=1, source_target_pairs={{0,16},{1,17},{2,18},{3,19},{4,20},{5,21},{6,22},{7,23},{8,24},{9,... | collective-permute-start | bytes 884744 | tf_op jit(solution)/shard_map/ppermute | solution.py:585
  101.0 13.0 %collective-permute-start.37 = (f32[4,144,128]{2,1,0:T(8,128)S(1)}, f32[4,144,128]{2,1,0:T(8,128)S(1)}, u32[]{:S(2)}, u32[]{:S(2)}) collective-permute-start(f32[4,144,128]{2,1,0:T(8,128)S(1)} %get-tuple-element.105), channel_id=1, source_target_pairs={{0,48},{1,49},{2,50},{3,51},{4,52},{5,53},{6,54},{7,55},{8,56},{9,... | collective-permute-start | bytes 884744 | tf_op jit(solution)/shard_map/ppermute | solution.py:585
  105.7 1.4 %collective-permute-start.30 = (f32[192,128]{1,0:T(8,128)S(1)}, f32[192,128]{1,0:T(8,128)S(1)}, u32[]{:S(2)}, u32[]{:S(2)}) collective-permute-start(f32[192,128]{1,0:T(8,128)S(1)} %table.5), channel_id=1, source_target_pairs={{0,1},{1,0},{2,3},{3,2},{4,5},{5,4},{6,7},{7,6},{8,9},{9,8},{10,11... | collective-permute-start | bytes 294920 | tf_op jit(solution)/shard_map/ppermute | solution.py:585
  107.1 4.8 %collective-permute-start.31 = (f32[128,128]{1,0:T(8,128)S(1)}, f32[128,128]{1,0:T(8,128)S(1)}, u32[]{:S(2)}, u32[]{:S(2)}) collective-permute-start(f32[128,128]{1,0:T(8,128)S(1)} %pair.7.half.mine), channel_id=1, source_target_pairs={{0,7},{1,2},{2,1},{3,4},{4,3},{5,6},{6,5},{7,0},{8,15},{9,10},{10,... | collective-permute-start | bytes 196616 | tf_op jit(solution)/shard_map/ppermute | solution.py:585
  111.9 4.0 %collective-permute-start.33 = (f32[64,128]{1,0:T(8,128)S(1)}, f32[64,128]{1,0:T(8,128)S(1)}, u32[]{:S(2)}, u32[]{:S(2)}) collective-permute-start(f32[64,128]{1,0:T(8,128)S(1)} %get-tuple-element.100.low), channel_id=1, source_target_pairs={{0,48},{1,49},{2,50},{3,51},{4,52},{5,53},{6,54},{7,55},{8,56},{9,... | collective-permute-start | bytes 98312 | tf_op jit(solution)/shard_map/ppermute | solution.py:585
  112.0 5.2 %collective-permute-start.32 = (f32[64,128]{1,0:T(8,128)S(1)}, f32[64,128]{1,0:T(8,128)S(1)}, u32[]{:S(2)}, u32[]{:S(2)}) collective-permute-start(f32[64,128]{1,0:T(8,128)S(1)} %get-tuple-element.101.high), channel_id=1, source_target_pairs={{0,16},{1,17},{2,18},{3,19},{4,20},{5,21},{6,22},{7,23},{8,24},{9,... | collective-permute-start | bytes 98312 | tf_op jit(solution)/shard_map/ppermute | solution.py:585
  117.2 1.3 collective-permute-start.38
  121.4 14.9 %collective-permute-start.39 = (f32[4,8,3072]{2,1,0:T(8,128)S(1)}, f32[4,8,3072]{2,1,0:T(8,128)S(1)}, u32[]{:S(2)}, u32[]{:S(2)}) collective-permute-start(f32[4,8,3072]{2,1,0:T(8,128)S(1)} %get-tuple-element.109), channel_id=1, source_target_pairs={{0,8},{1,9},{2,10},{3,11},{4,12},{5,13},{6,14},{7,15},{8,0},{9,1},... | collective-permute-start | bytes 1179656 | tf_op jit(solution)/shard_map/ppermute | solution.py:585
  124.1 12.1 %collective-permute-start.40 = (f32[8,1536]{1,0:T(8,128)S(1)}, f32[8,1536]{1,0:T(8,128)S(1)}, u32[]{:S(2)}, u32[]{:S(2)}) collective-permute-start(f32[8,1536]{1,0:T(8,128)S(1)} %get-tuple-element.111), channel_id=1, source_target_pairs={{0,8},{1,9},{2,10},{3,11},{4,12},{5,13},{6,14},{7,15},{8,0},{9,1},... | collective-permute-start | bytes 147464 | tf_op jit(solution)/shard_map/ppermute | solution.py:585
  125.4 10.9 %collective-permute-start.41 = (f32[8,1536]{1,0:T(8,128)S(1)}, f32[8,1536]{1,0:T(8,128)S(1)}, u32[]{:S(2)}, u32[]{:S(2)}) collective-permute-start(f32[8,1536]{1,0:T(8,128)S(1)} %get-tuple-element.112), channel_id=1, source_target_pairs={{0,64},{64,0},{1,65},{65,1},{2,66},{66,2},{3,67},{67,3},{4,68},{68... | collective-permute-start | bytes 147464 | tf_op jit(solution)/shard_map/ppermute | solution.py:801
  128.1 8.1 %collective-permute-start.42 = (f32[8,1536]{1,0:T(8,128)S(1)}, f32[8,1536]{1,0:T(8,128)S(1)}, u32[]{:S(2)}, u32[]{:S(2)}) collective-permute-start(f32[8,1536]{1,0:T(8,128)S(1)} %get-tuple-element.113), channel_id=1, source_target_pairs={{0,72},{1,73},{2,74},{3,75},{4,76},{5,77},{6,78},{7,79},{8,64},{9,... | collective-permute-start | bytes 147464 | tf_op jit(solution)/shard_map/ppermute | solution.py:802
  (6 other events, 61.6 us)

commit v3 on v2

--- a/solution.py
+++ b/solution.py
@@ -28,8 +28,6 @@
 EDGE = HALO * 16
 OWN = 512
 ROOM = 58
-LOOP_A = False
-LOOP_B = False
 CODES = 12
 TABLE = CODES * ROWS
 THIRD = TABLE // 3
@@ -152,7 +150,7 @@
         inner_ref[o] = jnp.where(below_inner, bottom, top)
         outer_ref[o] = jnp.where(below_inner, top, bottom)
 
-    each(ORB, step, LOOP_B)
+    each(ORB, step, False)
 
 
 def to_columns(source, near, far):
@@ -181,17 +179,20 @@
 
 
 def begin_kernel(
-    place, upper_edge, lower_edge, weights, column_in, shift_in, owner_in, atom_in, raw_in, proj_in, energy_in,
+    place, upper_in, lower_in, weights_in, column_in, shift_in, owner_in, atom_in, raw_in, proj_in, energy_in,
     keep, params, ints, table, note,
-    column, shift, owner, atom, raw, proj, energy, turned, tables, both, placed, partial, near, far, sems,
+    column, shift, owner, atom, raw, proj, energy, turned, tables, both, placed, partial, near, far, upper_edge, lower_edge, weights, sems,
 ):
     pairs = (
         (raw_in, raw), (column_in, column), (shift_in, shift), (owner_in, owner),
-        (atom_in, atom), (proj_in, proj), (energy_in, energy),
+        (atom_in, atom), (upper_in, upper_edge), (lower_in, lower_edge), (weights_in, weights),
+        (proj_in, proj), (energy_in, energy),
     )
     copies = [pltpu.make_async_copy(source, target, sems.at[k]) for k, (source, target) in enumerate(pairs)]
     for copy in copies:
         copy.start()
+    for copy in copies[:8]:
+        copy.wait()
     side, core = place[0], place[1]
     upper = jnp.full((1, LANES), side, jnp.int32) == 1
     params[0:1] = jnp.full((1, LANES), side, jnp.int32).astype(F32)
@@ -208,8 +209,6 @@
         params[8 + o : 9 + o] = jnp.full((1, LANES), weights[side * ORB + o], F32)
     params[8 + ORB :] = jnp.zeros((8 - ORB, LANES), F32)
     sub = jnp.full((1, PIECES), side, jnp.int32)
-    for copy in copies[:5]:
-        copy.wait()
     step_x = (owner[...] >= 3).astype(jnp.int32) + (owner[...] >= 6).astype(jnp.int32)
     row = owner[...] - 3 * step_x
     lines = [
@@ -235,7 +234,7 @@
         keep[o] = turned[o]
 
     each(ORB, turn)
-    for copy in copies[5:]:
+    for copy in copies[8:]:
         copy.wait()
     first_tables(ints, turned, tables, both, proj, placed, partial)
     table[...] = tables[0]
@@ -260,7 +259,7 @@
         field[o, :, :LANES] = jnp.where(upper, turned, kept)
         field[o, :, LANES:] = jnp.where(upper, kept, turned)
 
-    each(ORB, step)
+    each(ORB, step, False)
     emit_edges(field, flag(params, 1), edge, xl, xh, inner, outer)
 
 
@@ -277,13 +276,9 @@
         both = jnp.concatenate([own[j], came[j]], axis=0)
         for k in range(ALL // LANES):
             at = slice(k * LANES, (k + 1) * LANES)
-            placed[j, :, at] = shifted(both[at], ints_row(index, at))
-
-    each(NPJ, step)
-
-
-def ints_row(index, at):
-    return index[1:2, at]
+            placed[j, :, at] = shifted(both[at], index[1:2, at])
+
+    each(NPJ, step, False)
 
 
 def column_hot(index, at, wide):
@@ -292,7 +287,7 @@
 
 
 def chunks(step):
-    each(ALL // 256, lambda k: step(k * 256, 256), LOOP_A)
+    each(ALL // 256, lambda k: step(k * 256, 256), False)
     step(ALL - LANES, LANES)
 
 
@@ -363,7 +358,7 @@
         rows = pl.ds(o * NZ, NZ)
         both[rows, :] = jnp.concatenate(split(field[o]), axis=1)
 
-    each(ORB, gather, LOOP_B)
+    each(ORB, gather, False)
     chunks(lambda at, wide: project(both[...], column_hot(index, at, wide), placed, partial, at, wide))
     table[...] = gather_table(index, partial[...])
 
@@ -477,9 +472,9 @@
 
 def update_kernel(last, params, index, acc, mine, came, placed, *rest):
     if last:
-        kept, sent, field, coef_rows, near_sums, near, far = rest
+        sent, field, coef_rows, near, far = rest
     else:
-        edge, field, xl, xh, inner, outer, coef_rows, near_sums = rest
+        edge, field, xl, xh, inner, outer, coef_rows = rest
     second = flag(params, 1)
     total = jnp.concatenate(
         [jnp.where(second, came[THIRD:], mine[...][:THIRD]), jnp.where(second, mine[...][:THIRD], mine[...][THIRD:]),
@@ -491,8 +486,8 @@
     coefs = jnp.zeros((ROWS, ALL), F32)
     for code in range(CODES):
         coefs = jnp.where(codes == code, spread[code * ROWS : (code + 1) * ROWS], coefs)
-    near_sums[...] = jnp.zeros((ORB * NZ, COLS), F32)
     coef_rows[...] = coefs
+    sums = []
 
     def chunk(at, wide):
         hot = column_hot(index, at, wide)
@@ -503,15 +498,15 @@
             for j in range(1, NPJ):
                 line = line + rows[j : j + 1] * placed[j, :, pl.ds(at, wide)]
             lines.append(jnp.concatenate(split(line), axis=1))
-        near_sums[...] += mul_t(jnp.concatenate(lines, axis=0), jnp.concatenate([hot, hot], axis=1))
+        term = mul_t(jnp.concatenate(lines, axis=0), jnp.concatenate([hot, hot], axis=1))
+        sums[:] = [sums[0] + term if sums else term]
 
     chunks(chunk)
 
     def finish(o):
-        rows = pl.ds(o * NZ, NZ)
-        field[o] = acc[o] + near_sums[rows, :]
-
-    each(ORB, finish, LOOP_B)
+        field[o] = acc[o] + sums[0][o * NZ : (o + 1) * NZ]
+
+    each(ORB, finish, False)
     if not last:
         emit_edges(field, second, edge, xl, xh, inner, outer)
         return
@@ -521,8 +516,6 @@
         left, right = field[o, :, :LANES], field[o, :, LANES:]
         for spot, pair in from_columns(jnp.where(upper, left, right), near, far):
             sent[o, :, spot : spot + 2 * NZ] = pair
-        for spot, pair in from_columns(jnp.where(upper, right, left), near, far):
-            kept[o, :, spot : spot + 2 * NZ] = pair
 
     each(ORB, emit)
 
@@ -538,7 +531,7 @@
     each(ORB, step)
 
 
-def density_kernel(params, field, quarter, across_x, across_band, across_both, plane, near, far):
+def density_kernel(params, field, kept, quarter, across_x, across_band, across_both, plane, near, far):
     dens = jnp.zeros((NZ, COLS), F32)
     for o in range(ORB):
         dens = dens + params[8 + o : 9 + o, 0:1] * field[o] * field[o]
@@ -554,6 +547,13 @@
             plane[:, spot : spot + 2 * NZ] = pair
         same[...] = jnp.where(second, plane[:, span:], plane[:, :span])
         opposite[...] = jnp.where(second, plane[:, :span], plane[:, span:])
+
+    def emit(o):
+        mine = jnp.where(upper, field[o, :, LANES:], field[o, :, :LANES])
+        for spot, pair in from_columns(mine, near, far):
+            kept[o, :, spot : spot + 2 * NZ] = pair
+
+    each(ORB, emit)
 
 
 VM = pl.BlockSpec(memory_space=pltpu.VMEM)
@@ -627,12 +627,12 @@
     stage = [pltpu.VMEM((LANES, LANES), F32)] * 2
 
     raw = orbitals[:, 0]
-    going = lax.dynamic_slice_in_dim(raw, (1 - side) * ORB, ORB, 0)
+    going = jnp.where(side == 0, raw[ORB:], raw[:ORB])
     came = send(jnp.concatenate([going, potential], axis=0), SWAP)
     line = pltpu.VMEM((1, PIECES), jnp.int32)
     keep, params, ints, own_table, note = call(
         begin_kernel,
-        [SM] * 4 + [HB] * 7,
+        [SM] + [HB] * 10,
         [
             (ORB, NZ, LANES),
             (16, LANES),
@@ -655,7 +655,10 @@
             pltpu.VMEM((NPJ, NZ, OWN), F32),
             pltpu.VMEM((ROWS, OWN), F32),
             *stage,
-            pltpu.SemaphoreType.DMA((7,)),
+            pltpu.SMEM((1,), F32),
+            pltpu.SMEM((1,), F32),
+            pltpu.SMEM((2 * ORB,), F32),
+            pltpu.SemaphoreType.DMA((10,)),
         ],
         name="begin",
         room=ROOM,
@@ -682,7 +685,7 @@
         name="prepare",
     )
 
-    sums_room = [pltpu.VMEM((ROWS, ALL), F32), pltpu.VMEM((ORB * NZ, COLS), F32)]
+    sums_room = [pltpu.VMEM((ROWS, ALL), F32)]
     before = field
     for level in range(DEG):
         first, last = level == 0, level == DEG - 1
@@ -771,19 +774,19 @@
             )
         else:
             flat = (ORB, CX, CY * NZ)
-            mine, other, result = call(
+            other, result = call(
                 functools.partial(update_kernel, last),
                 [VM] * 6,
-                [flat, flat, grid],
+                [flat, grid],
                 args,
                 sums_room + stage,
                 name="finish",
             )
     part = (CX, CY * NZ // 2)
-    quarter, across_x, across_band, across_both = call(
+    mine, quarter, across_x, across_band, across_both = call(
         density_kernel,
         [VM] * 2,
-        [part] * 4,
+        [flat] + [part] * 4,
         (params, result),
         [pltpu.VMEM((CX, CY * NZ), F32)] + stage,
         name="density",

time: 138 us -> 138 us (level)
  transfers between devices with their start and end apart: 43 -> 43, of which waited for: 24 -> 25; matrix products, arithmetic and copies ran while one was open for 1% -> 1% of each run, Pallas kernels for 21% -> 21%
where the time goes in v3:
time: 138 us
  starting transfers between devices  50.2 us (36%)
  waiting for transfers between devices  41.9 us (30%)
  Pallas kernels  40.1 us (29%)
  other arithmetic  2.82 us (2%)
  between operations  2.43 us (2%)
    ppermute x41, starting transfers between devices, send(): return lax.ppermute(value, 'dom', pairs)  45.1 us
    ppermute x41, waiting for transfers between devices, send(): return lax.ppermute(value, 'dom', pairs)  40.7 us
    pallas_call x34, Pallas kernels, call(): pl.pallas_call(kernel, out_shape=[jax.ShapeDtypeStruct(*out) for out in o...  40.1 us
  transfers between devices with their start and end apart: 43, of which 25 were waited for; matrix products, arithmetic and copies ran while one was open for 1% of the time, Pallas kernels for 21%

profile of v3, /device:TPU:0, one launch (start us, length us, event | category | flops | bytes accessed | tf_op | source)
XLA Modules:
  0.0 137.6 jit_solution(14257665110145777633)
XLA Ops:
  2.8 3.4 %collective-permute-start.1 = (f32[5,8,3072]{2,1,0:T(8,128)S(1)}, f32[5,8,3072]{2,1,0:T(8,128)S(1)}, u32[]{:S(2)}, u32[]{:S(2)}) collective-permute-start(f32[5,8,3072]{2,1,0:T(8,128)S(1)} %pad_maximum_fusion), channel_id=1, source_target_pairs={{0,8},{1,9},{2,10},{3,11},{4,12},{5,13},{6,14},{7,15},{8,0},{9,1},... | collective-permute-start | bytes 1474568 | tf_op jit(solution)/shard_map/ppermute | solution.py:585
  8.2 7.2 %begin.1 = (f32[4,192,128]{2,1,0:T(8,128)}, f32[16,128]{1,0:T(8,128)}, s32[8,512]{1,0:T(8,128)}, f32[192,128]{1,0:T(8,128)}, f32[216,128]{1,0:T(8,128)}) custom-call(s32[3]{0:T(128)} %pad_add_fusion.place, f32[1]{0:T(128)S(6)} %copy.39.upper_in, f32[1]{0:T(128)S(6)} %copy.38.lower_in, f32[8]{0:T(128)} %weights_in.1, s32[1,448]{1,0:T(1,128)} %column_in.1, ...), custom_call_target="tpu_custom_call" | custom-call | flops 100000000 | bytes 4000000 | tf_op jit(solution)/shard_map/begin/pallas_call | solution.py:570
  15.8 6.1 %collective-permute-done.note_came = f32[216,128]{1,0:T(8,128)S(1)} collective-permute-done((f32[216,128]{1,0:T(8,128)}, f32[216,128]{1,0:T(8,128)S(1)}, u32[]{:S(2)}, u32[]{:S(2)}) %collective-permute-start) | collective-permute-done | bytes 110624 | tf_op jit(solution)/shard_map/ppermute | solution.py:585
  24.4 1.3 collective-permute-done.3.came
  25.7 1.5 %collective-permute-start.4 = (f32[136,128]{1,0:T(8,128)S(1)}, f32[136,128]{1,0:T(8,128)S(1)}, u32[]{:S(2)}, u32[]{:S(2)}) collective-permute-start(f32[136,128]{1,0:T(8,128)S(1)} %pair.4.half.mine), channel_id=1, source_target_pairs={{0,7},{1,2},{2,1},{3,4},{4,3},{5,6},{6,5},{7,0},{8,15},{9,10},{10,... | collective-permute-start | bytes 208904 | tf_op jit(solution)/shard_map/ppermute | solution.py:585
  28.5 1.9 %collective-permute-start.9 = (f32[4,144,128]{2,1,0:T(8,128)S(1)}, f32[4,144,128]{2,1,0:T(8,128)S(1)}, u32[]{:S(2)}, u32[]{:S(2)}) collective-permute-start(f32[4,144,128]{2,1,0:T(8,128)S(1)} %get-tuple-element.72), channel_id=1, source_target_pairs={{0,16},{1,17},{2,18},{3,19},{4,20},{5,21},{6,22},{7,23},{8,24},{9,... | collective-permute-start | bytes 884744 | tf_op jit(solution)/shard_map/ppermute | solution.py:585
  31.0 3.9 %collective-permute-start.10 = (f32[4,144,128]{2,1,0:T(8,128)S(1)}, f32[4,144,128]{2,1,0:T(8,128)S(1)}, u32[]{:S(2)}, u32[]{:S(2)}) collective-permute-start(f32[4,144,128]{2,1,0:T(8,128)S(1)} %get-tuple-element.73), channel_id=1, source_target_pairs={{0,48},{1,49},{2,50},{3,51},{4,52},{5,53},{6,54},{7,55},{8,56},{9,... | collective-permute-start | bytes 884744 | tf_op jit(solution)/shard_map/ppermute | solution.py:585
  34.9 1.4 %local.4.acc = f32[4,192,256]{2,1,0:T(8,128)S(1)} custom-call(f32[16,128]{1,0:T(8,128)S(1)} %copy-done.2, f32[136,128]{1,0:T(8,128)S(1)} %pair.4.half.mine, f32[4,192,256]{2,1,0:T(8,128)S(1)} %get-tuple-element.66.field.before, f32[4,192,256]{2,1,0:T(8,128)S(1)} %get-tuple-element.66.field.before, f32[192,256]{1,0:T(8,128)S(1)} %get-tuple-element.67.pot, ...), custom_call_target="tpu_custom_call" | custom-call | flops 100000000 | bytes 4000000 | tf_op jit(solution)/shard_map/local/pallas_call | solution.py:570
  37.3 1.9 %collective-permute-start.5 = (f32[72,128]{1,0:T(8,128)S(1)}, f32[72,128]{1,0:T(8,128)S(1)}, u32[]{:S(2)}, u32[]{:S(2)}) collective-permute-start(f32[72,128]{1,0:T(8,128)S(1)} %get-tuple-element.69.high), channel_id=1, source_target_pairs={{0,16},{1,17},{2,18},{3,19},{4,20},{5,21},{6,22},{7,23},{8,24},{9,... | collective-permute-start | bytes 110600 | tf_op jit(solution)/shard_map/ppermute | solution.py:585
  39.5 2.0 %collective-permute-done.10.xh = f32[4,144,128]{2,1,0:T(8,128)S(1)} collective-permute-done((f32[4,144,128]{2,1,0:T(8,128)S(1)}, f32[4,144,128]{2,1,0:T(8,128)S(1)}, u32[]{:S(2)}, u32[]{:S(2)}) %collective-permute-start.10) | collective-permute-done | bytes 294944 | tf_op jit(solution)/shard_map/ppermute | solution.py:585
  41.5 1.6 %halo.4.acc = f32[4,192,256]{2,1,0:T(8,128)S(1)} custom-call(f32[16,128]{1,0:T(8,128)S(1)} %copy-done.2, f32[4,144,128]{2,1,0:T(8,128)S(1)} %collective-permute-done.7.inner, f32[4,144,128]{2,1,0:T(8,128)S(1)} %collective-permute-done.8.outer, f32[4,144,128]{2,1,0:T(8,128)S(1)} %collective-permute-done.9.xl, f32[4,144,128]{2,1,0:T(8,128)S(1)} %collective-permute-done.10.xh, ...), custom_call_target="tpu_custom_call" | custom-call | flops 100000000 | bytes 4000000 | tf_op jit(solution)/shard_map/halo/pallas_call | solution.py:570
  43.4 4.6 %collective-permute-done.2.came = f32[4,448,128]{2,1,0:T(8,128)S(1)} collective-permute-done((f32[4,448,128]{2,1,0:T(8,128)S(1)}, f32[4,448,128]{2,1,0:T(8,128)S(1)}, u32[]{:S(2)}, u32[]{:S(2)}) %collective-permute-start.2) | collective-permute-done | bytes 917536 | tf_op jit(solution)/shard_map/ppermute | solution.py:585
  48.0 1.7 %prepare.1 = (f32[4,192,896]{2,1,0:T(8,128)S(1)}, s32[4,896]{1,0:T(4,128)S(1)}) custom-call(s32[8,512]{1,0:T(8,128)S(1)} %copy-done.9, f32[216,128]{1,0:T(8,128)S(1)} %collective-permute-done.note_came, f32[4,448,128]{2,1,0:T(8,128)S(1)} %bitcast.15, f32[4,448,128]{2,1,0:T(8,128)S(1)} %collective-permute-done.2.came), custom_call_target="tpu_custom_call" | custom-call | flops 100000000 | bytes 4000000 | tf_op jit(solution)/shard_map/prepare/pallas_call | solution.py:570
  49.7 2.4 %update.3 = (f32[4,192,256]{2,1,0:T(8,128)S(1)}, f32[4,144,128]{2,1,0:T(8,128)S(1)}, f32[4,144,128]{2,1,0:T(8,128)S(1)}, f32[4,144,128]{2,1,0:T(8,128)S(1)}, f32[4,144,128]{2,1,0:T(8,128)S(1)}) custom-call(f32[16,128]{1,0:T(8,128)S(1)} %copy-done.2, s32[4,896]{1,0:T(4,128)S(1)} %get-tuple-element.63.index, f32[4,192,256]{2,1,0:T(8,128)S(1)} %get-tuple-element.75.acc, ...), custom_call_target="tpu_custom_call" | custom-call | flops 100000000 | bytes 4000000 | tf_op jit(solution)/shard_map/update/pallas_call | solution.py:570
  52.2 1.7 %collective-permute-start.17 = (f32[4,144,128]{2,1,0:T(8,128)S(1)}, f32[4,144,128]{2,1,0:T(8,128)S(1)}, u32[]{:S(2)}, u32[]{:S(2)}) collective-permute-start(f32[4,144,128]{2,1,0:T(8,128)S(1)} %get-tuple-element.83), channel_id=1, source_target_pairs={{0,7},{1,2},{2,1},{3,4},{4,3},{5,6},{6,5},{7,0},{8,15},{9,10},{10,... | collective-permute-start | bytes 884744 | tf_op jit(solution)/shard_map/ppermute | solution.py:585
  53.9 1.9 %collective-permute-start.18 = (f32[4,144,128]{2,1,0:T(8,128)S(1)}, f32[4,144,128]{2,1,0:T(8,128)S(1)}, u32[]{:S(2)}, u32[]{:S(2)}) collective-permute-start(f32[4,144,128]{2,1,0:T(8,128)S(1)} %get-tuple-element.84), channel_id=1, source_target_pairs={{0,16},{1,17},{2,18},{3,19},{4,20},{5,21},{6,22},{7,23},{8,24},{9,... | collective-permute-start | bytes 884744 | tf_op jit(solution)/shard_map/ppermute | solution.py:585
  55.8 2.1 %collective-permute-start.19 = (f32[4,144,128]{2,1,0:T(8,128)S(1)}, f32[4,144,128]{2,1,0:T(8,128)S(1)}, u32[]{:S(2)}, u32[]{:S(2)}) collective-permute-start(f32[4,144,128]{2,1,0:T(8,128)S(1)} %get-tuple-element.85), channel_id=1, source_target_pairs={{0,48},{1,49},{2,50},{3,51},{4,52},{5,53},{6,54},{7,55},{8,56},{9,... | collective-permute-start | bytes 884744 | tf_op jit(solution)/shard_map/ppermute | solution.py:585
  57.9 1.9 %table.3 = f32[192,128]{1,0:T(8,128)S(1)} custom-call(s32[4,896]{1,0:T(4,128)S(1)} %get-tuple-element.63.index, f32[4,192,256]{2,1,0:T(8,128)S(1)} %get-tuple-element.78.field.before, f32[4,192,896]{2,1,0:T(8,128)S(1)} %get-tuple-element.77.placed), custom_call_target="tpu_custom_call" | custom-call | flops 100000000 | bytes 4000000 | tf_op jit(solution)/shard_map/table/pallas_call | solution.py:570
  59.9 1.3 collective-permute-done.12.came
  62.1 1.4 %local.5.acc = f32[4,192,256]{2,1,0:T(8,128)S(1)} custom-call(f32[16,128]{1,0:T(8,128)S(1)} %copy-done.2, f32[128,128]{1,0:T(8,128)S(1)} %pair.5.half.mine, f32[4,192,256]{2,1,0:T(8,128)S(1)} %get-tuple-element.78.field.before, f32[4,192,256]{2,1,0:T(8,128)S(1)} %get-tuple-element.66.field.before, f32[192,256]{1,0:T(8,128)S(1)} %get-tuple-element.67.pot, ...), custom_call_target="tpu_custom_call" | custom-call | flops 100000000 | bytes 4000000 | tf_op jit(solution)/shard_map/local/pallas_call | solution.py:570
  63.5 2.9 %collective-permute-done.13.came = f32[128,128]{1,0:T(8,128)S(1)} collective-permute-done((f32[128,128]{1,0:T(8,128)S(1)}, f32[128,128]{1,0:T(8,128)S(1)}, u32[]{:S(2)}, u32[]{:S(2)}) %collective-permute-start.13) | collective-permute-done | bytes 65568 | tf_op jit(solution)/shard_map/ppermute | solution.py:585
  66.4 2.1 %collective-permute-start.15 = (f32[64,128]{1,0:T(8,128)S(1)}, f32[64,128]{1,0:T(8,128)S(1)}, u32[]{:S(2)}, u32[]{:S(2)}) collective-permute-start(f32[64,128]{1,0:T(8,128)S(1)} %get-tuple-element.79.low), channel_id=1, source_target_pairs={{0,48},{1,49},{2,50},{3,51},{4,52},{5,53},{6,54},{7,55},{8,56},{9,... | collective-permute-start | bytes 98312 | tf_op jit(solution)/shard_map/ppermute | solution.py:585
  68.5 1.6 %halo.5.acc = f32[4,192,256]{2,1,0:T(8,128)S(1)} custom-call(f32[16,128]{1,0:T(8,128)S(1)} %copy-done.2, f32[4,144,128]{2,1,0:T(8,128)S(1)} %collective-permute-done.16.inner, f32[4,144,128]{2,1,0:T(8,128)S(1)} %collective-permute-done.17.outer, f32[4,144,128]{2,1,0:T(8,128)S(1)} %collective-permute-done.18.xl, ...), custom_call_target="tpu_custom_call" | custom-call | flops 100000000 | bytes 4000000 | tf_op jit(solution)/shard_map/halo/pallas_call | solution.py:570
  70.4 3.2 %collective-permute-done.14.below = f32[64,128]{1,0:T(8,128)S(1)} collective-permute-done((f32[64,128]{1,0:T(8,128)S(1)}, f32[64,128]{1,0:T(8,128)S(1)}, u32[]{:S(2)}, u32[]{:S(2)}) %collective-permute-start.14) | collective-permute-done | bytes 32800 | tf_op jit(solution)/shard_map/ppermute | solution.py:585
  75.0 2.4 %update.4 = (f32[4,192,256]{2,1,0:T(8,128)S(1)}, f32[4,144,128]{2,1,0:T(8,128)S(1)}, f32[4,144,128]{2,1,0:T(8,128)S(1)}, f32[4,144,128]{2,1,0:T(8,128)S(1)}, f32[4,144,128]{2,1,0:T(8,128)S(1)}) custom-call(f32[16,128]{1,0:T(8,128)S(1)} %copy-done.2, s32[4,896]{1,0:T(4,128)S(1)} %get-tuple-element.63.index, f32[4,192,256]{2,1,0:T(8,128)S(1)} %get-tuple-element.87.acc, ...), custom_call_target="tpu_custom_call" | custom-call | flops 100000000 | bytes 4000000 | tf_op jit(solution)/shard_map/update/pallas_call | solution.py:570
  77.6 3.2 %collective-permute-start.28 = (f32[4,144,128]{2,1,0:T(8,128)S(1)}, f32[4,144,128]{2,1,0:T(8,128)S(1)}, u32[]{:S(2)}, u32[]{:S(2)}) collective-permute-start(f32[4,144,128]{2,1,0:T(8,128)S(1)} %get-tuple-element.95), channel_id=1, source_target_pairs={{0,48},{1,49},{2,50},{3,51},{4,52},{5,53},{6,54},{7,55},{8,56},{9,... | collective-permute-start | bytes 884744 | tf_op jit(solution)/shard_map/ppermute | solution.py:585
  80.9 1.9 %table.4 = f32[192,128]{1,0:T(8,128)S(1)} custom-call(s32[4,896]{1,0:T(4,128)S(1)} %get-tuple-element.63.index, f32[4,192,256]{2,1,0:T(8,128)S(1)} %get-tuple-element.89.field.before, f32[4,192,896]{2,1,0:T(8,128)S(1)} %get-tuple-element.77.placed), custom_call_target="tpu_custom_call" | custom-call | flops 100000000 | bytes 4000000 | tf_op jit(solution)/shard_map/table/pallas_call | solution.py:570
  84.2 2.4 %collective-permute-start.22 = (f32[128,128]{1,0:T(8,128)S(1)}, f32[128,128]{1,0:T(8,128)S(1)}, u32[]{:S(2)}, u32[]{:S(2)}) collective-permute-start(f32[128,128]{1,0:T(8,128)S(1)} %pair.6.half.mine), channel_id=1, source_target_pairs={{0,7},{1,2},{2,1},{3,4},{4,3},{5,6},{6,5},{7,0},{8,15},{9,10},{10,... | collective-permute-start | bytes 196616 | tf_op jit(solution)/shard_map/ppermute | solution.py:585
  86.5 1.4 %local.6.acc = f32[4,192,256]{2,1,0:T(8,128)S(1)} custom-call(f32[16,128]{1,0:T(8,128)S(1)} %copy-done.2, f32[128,128]{1,0:T(8,128)S(1)} %pair.6.half.mine, f32[4,192,256]{2,1,0:T(8,128)S(1)} %get-tuple-element.89.field.before, f32[4,192,256]{2,1,0:T(8,128)S(1)} %get-tuple-element.78.field.before, f32[192,256]{1,0:T(8,128)S(1)} %get-tuple-element.67.pot, ...), custom_call_target="tpu_custom_call" | custom-call | flops 100000000 | bytes 4000000 | tf_op jit(solution)/shard_map/local/pallas_call | solution.py:570
  87.9 1.4 %collective-permute-done.22.came = f32[128,128]{1,0:T(8,128)S(1)} collective-permute-done((f32[128,128]{1,0:T(8,128)S(1)}, f32[128,128]{1,0:T(8,128)S(1)}, u32[]{:S(2)}, u32[]{:S(2)}) %collective-permute-start.22) | collective-permute-done | bytes 65568 | tf_op jit(solution)/shard_map/ppermute | solution.py:585
  89.5 2.0 %collective-permute-start.23 = (f32[64,128]{1,0:T(8,128)S(1)}, f32[64,128]{1,0:T(8,128)S(1)}, u32[]{:S(2)}, u32[]{:S(2)}) collective-permute-start(f32[64,128]{1,0:T(8,128)S(1)} %get-tuple-element.91.high), channel_id=1, source_target_pairs={{0,16},{1,17},{2,18},{3,19},{4,20},{5,21},{6,22},{7,23},{8,24},{9,... | collective-permute-start | bytes 98312 | tf_op jit(solution)/shard_map/ppermute | solution.py:585
  91.5 1.6 %halo.6.acc = f32[4,192,256]{2,1,0:T(8,128)S(1)} custom-call(f32[16,128]{1,0:T(8,128)S(1)} %copy-done.2, f32[4,144,128]{2,1,0:T(8,128)S(1)} %collective-permute-done.25.inner, f32[4,144,128]{2,1,0:T(8,128)S(1)} %collective-permute-done.26.outer, f32[4,144,128]{2,1,0:T(8,128)S(1)} %collective-permute-done.27.xl, ...), custom_call_target="tpu_custom_call" | custom-call | flops 100000000 | bytes 4000000 | tf_op jit(solution)/shard_map/halo/pallas_call | solution.py:570
  93.4 1.3 collective-permute-done.23.below
  96.3 2.4 %update.5 = (f32[4,192,256]{2,1,0:T(8,128)S(1)}, f32[4,144,128]{2,1,0:T(8,128)S(1)}, f32[4,144,128]{2,1,0:T(8,128)S(1)}, f32[4,144,128]{2,1,0:T(8,128)S(1)}, f32[4,144,128]{2,1,0:T(8,128)S(1)}) custom-call(f32[16,128]{1,0:T(8,128)S(1)} %copy-done.2, s32[4,896]{1,0:T(4,128)S(1)} %get-tuple-element.63.index, f32[4,192,256]{2,1,0:T(8,128)S(1)} %get-tuple-element.97.acc, ...), custom_call_target="tpu_custom_call" | custom-call | flops 100000000 | bytes 4000000 | tf_op jit(solution)/shard_map/update/pallas_call | solution.py:570
  98.9 1.4 %collective-permute-start.35 = (f32[4,144,128]{2,1,0:T(8,128)S(1)}, f32[4,144,128]{2,1,0:T(8,128)S(1)}, u32[]{:S(2)}, u32[]{:S(2)}) collective-permute-start(f32[4,144,128]{2,1,0:T(8,128)S(1)} %get-tuple-element.103), channel_id=1, source_target_pairs={{0,7},{1,2},{2,1},{3,4},{4,3},{5,6},{6,5},{7,0},{8,15},{9,10},{10,... | collective-permute-start | bytes 884744 | tf_op jit(solution)/shard_map/ppermute | solution.py:585
  100.8 2.7 %collective-permute-start.37 = (f32[4,144,128]{2,1,0:T(8,128)S(1)}, f32[4,144,128]{2,1,0:T(8,128)S(1)}, u32[]{:S(2)}, u32[]{:S(2)}) collective-permute-start(f32[4,144,128]{2,1,0:T(8,128)S(1)} %get-tuple-element.105), channel_id=1, source_target_pairs={{0,48},{1,49},{2,50},{3,51},{4,52},{5,53},{6,54},{7,55},{8,56},{9,... | collective-permute-start | bytes 884744 | tf_op jit(solution)/shard_map/ppermute | solution.py:585
  103.6 1.9 %table.5 = f32[192,128]{1,0:T(8,128)S(1)} custom-call(s32[4,896]{1,0:T(4,128)S(1)} %get-tuple-element.63.index, f32[4,192,256]{2,1,0:T(8,128)S(1)} %get-tuple-element.99.field, f32[4,192,896]{2,1,0:T(8,128)S(1)} %get-tuple-element.77.placed), custom_call_target="tpu_custom_call" | custom-call | flops 100000000 | bytes 4000000 | tf_op jit(solution)/shard_map/table/pallas_call | solution.py:570
  108.0 1.4 %local.7.acc = f32[4,192,256]{2,1,0:T(8,128)S(1)} custom-call(f32[16,128]{1,0:T(8,128)S(1)} %copy-done.2, f32[128,128]{1,0:T(8,128)S(1)} %pair.7.half.mine, f32[4,192,256]{2,1,0:T(8,128)S(1)} %get-tuple-element.99.field, f32[4,192,256]{2,1,0:T(8,128)S(1)} %get-tuple-element.89.field.before, f32[192,256]{1,0:T(8,128)S(1)} %get-tuple-element.67.pot, ...), custom_call_target="tpu_custom_call" | custom-call | flops 100000000 | bytes 4000000 | tf_op jit(solution)/shard_map/local/pallas_call | solution.py:570
  109.4 2.3 %collective-permute-done.31.came = f32[128,128]{1,0:T(8,128)S(1)} collective-permute-done((f32[128,128]{1,0:T(8,128)S(1)}, f32[128,128]{1,0:T(8,128)S(1)}, u32[]{:S(2)}, u32[]{:S(2)}) %collective-permute-start.31) | collective-permute-done | bytes 65568 | tf_op jit(solution)/shard_map/ppermute | solution.py:585
  111.8 2.0 %collective-permute-start.32 = (f32[64,128]{1,0:T(8,128)S(1)}, f32[64,128]{1,0:T(8,128)S(1)}, u32[]{:S(2)}, u32[]{:S(2)}) collective-permute-start(f32[64,128]{1,0:T(8,128)S(1)} %get-tuple-element.101.high), channel_id=1, source_target_pairs={{0,16},{1,17},{2,18},{3,19},{4,20},{5,21},{6,22},{7,23},{8,24},{9,... | collective-permute-start | bytes 98312 | tf_op jit(solution)/shard_map/ppermute | solution.py:585
  113.8 1.6 %halo.7.acc = f32[4,192,256]{2,1,0:T(8,128)S(1)} custom-call(f32[16,128]{1,0:T(8,128)S(1)} %copy-done.2, f32[4,144,128]{2,1,0:T(8,128)S(1)} %collective-permute-done.34.inner, f32[4,144,128]{2,1,0:T(8,128)S(1)} %collective-permute-done.35.outer, f32[4,144,128]{2,1,0:T(8,128)S(1)} %collective-permute-done.36.xl, ...), custom_call_target="tpu_custom_call" | custom-call | flops 100000000 | bytes 4000000 | tf_op jit(solution)/shard_map/halo/pallas_call | solution.py:570
  115.7 1.3 collective-permute-done.32.below
  118.4 2.6 %finish.1 = (f32[4,8,3072]{2,1,0:T(8,128)S(1)}, f32[4,192,256]{2,1,0:T(8,128)S(1)}) custom-call(f32[16,128]{1,0:T(8,128)S(1)} %copy-done.2, s32[4,896]{1,0:T(4,128)S(1)} %get-tuple-element.63.index, f32[4,192,256]{2,1,0:T(8,128)S(1)} %get-tuple-element.107.acc, f32[128,128]{1,0:T(8,128)S(1)} %get-tuple-element.108.mine, ...), custom_call_target="tpu_custom_call" | custom-call | flops 100000000 | bytes 4000000 | tf_op jit(solution)/shard_map/finish/pallas_call | solution.py:570
  121.0 2.2 %collective-permute-start.39 = (f32[4,8,3072]{2,1,0:T(8,128)S(1)}, f32[4,8,3072]{2,1,0:T(8,128)S(1)}, u32[]{:S(2)}, u32[]{:S(2)}) collective-permute-start(f32[4,8,3072]{2,1,0:T(8,128)S(1)} %get-tuple-element.109), channel_id=1, source_target_pairs={{0,8},{1,9},{2,10},{3,11},{4,12},{5,13},{6,14},{7,15},{8,0},{9,1},... | collective-permute-start | bytes 1179656 | tf_op jit(solution)/shard_map/ppermute | solution.py:585
  124.3 1.5 %collective-permute-start.40 = (f32[8,1536]{1,0:T(8,128)S(1)}, f32[8,1536]{1,0:T(8,128)S(1)}, u32[]{:S(2)}, u32[]{:S(2)}) collective-permute-start(f32[8,1536]{1,0:T(8,128)S(1)} %get-tuple-element.111), channel_id=1, source_target_pairs={{0,8},{1,9},{2,10},{3,11},{4,12},{5,13},{6,14},{7,15},{8,0},{9,1},... | collective-permute-start | bytes 147464 | tf_op jit(solution)/shard_map/ppermute | solution.py:585
  125.8 2.7 %collective-permute-start.41 = (f32[8,1536]{1,0:T(8,128)S(1)}, f32[8,1536]{1,0:T(8,128)S(1)}, u32[]{:S(2)}, u32[]{:S(2)}) collective-permute-start(f32[8,1536]{1,0:T(8,128)S(1)} %get-tuple-element.112), channel_id=1, source_target_pairs={{0,64},{64,0},{1,65},{65,1},{2,66},{66,2},{3,67},{67,3},{4,68},{68... | collective-permute-start | bytes 147464 | tf_op jit(solution)/shard_map/ppermute | solution.py:804
  128.5 2.4 %collective-permute-start.42 = (f32[8,1536]{1,0:T(8,128)S(1)}, f32[8,1536]{1,0:T(8,128)S(1)}, u32[]{:S(2)}, u32[]{:S(2)}) collective-permute-start(f32[8,1536]{1,0:T(8,128)S(1)} %get-tuple-element.113), channel_id=1, source_target_pairs={{0,72},{1,73},{2,74},{3,75},{4,76},{5,77},{6,78},{7,79},{8,64},{9,... | collective-permute-start | bytes 147464 | tf_op jit(solution)/shard_map/ppermute | solution.py:805
  130.9 4.5 %collective-permute-done.40.b = f32[8,1536]{1,0:T(8,128)S(1)} collective-permute-done((f32[8,1536]{1,0:T(8,128)S(1)}, f32[8,1536]{1,0:T(8,128)S(1)}, u32[]{:S(2)}, u32[]{:S(2)}) %collective-permute-start.40) | collective-permute-done | bytes 49184 | tf_op jit(solution)/shard_map/ppermute | solution.py:585
  (98 shorter events, 23.3 us)
Async XLA Ops:
  0.6 15.1 %copy-start.1 = (f32[1,4,448,128]{3,2,1,0:T(8,128)S(1)}, f32[1,4,448,128]{3,2,1,0:T(8,128)}, u32[]{:S(2)}) copy-start(f32[1,4,448,128]{3,2,1,0:T(8,128)} %param.18) | copy-start | bytes 2752516
  2.8 19.1 %collective-permute-start.1 = (f32[5,8,3072]{2,1,0:T(8,128)S(1)}, f32[5,8,3072]{2,1,0:T(8,128)S(1)}, u32[]{:S(2)}, u32[]{:S(2)}) collective-permute-start(f32[5,8,3072]{2,1,0:T(8,128)S(1)} %pad_maximum_fusion), channel_id=1, source_target_pairs={{0,8},{1,9},{2,10},{3,11},{4,12},{5,13},{6,14},{7,15},{8,0},{9,1},... | collective-permute-start | bytes 1474568 | tf_op jit(solution)/shard_map/ppermute | solution.py:585
  8.2 14.9 %copy-start.7 = (f32[1,8,3072]{2,1,0:T(8,128)S(1)}, f32[1,8,3072]{2,1,0:T(8,128)}, u32[]{:S(2)}) copy-start(f32[1,8,3072]{2,1,0:T(8,128)} %potential.1) | copy-start | bytes 294916
  15.4 6.5 %collective-permute-start = (f32[216,128]{1,0:T(8,128)}, f32[216,128]{1,0:T(8,128)S(1)}, u32[]{:S(2)}, u32[]{:S(2)}) collective-permute-start(f32[216,128]{1,0:T(8,128)} %get-tuple-element.62), channel_id=1, source_target_pairs={{0,8},{1,9},{2,10},{3,11},{4,12},{5,13},{6,14},{7,15},{8,0},{9,1},... | collective-permute-start | bytes 331784 | tf_op jit(solution)/shard_map/ppermute | solution.py:585
  15.8 19.1 %copy-start.3 = (bf16[2,256,256]{2,1,0:T(8,128)(2,1)S(1)}, bf16[2,256,256]{2,1,0:T(8,128)(2,1)}, u32[]{:S(2)}) copy-start(bf16[2,256,256]{2,1,0:T(8,128)(2,1)} %constant.49.clone.own_w) | copy-start | bytes 786436
  15.8 19.1 %copy-start.4 = (bf16[2,192,192]{2,1,0:T(8,128)(2,1)S(1)}, bf16[2,192,192]{2,1,0:T(8,128)(2,1)}, u32[]{:S(2)}) copy-start(bf16[2,192,192]{2,1,0:T(8,128)(2,1)} %constant.51.clone.ring_w) | copy-start | bytes 442372
  21.9 26.1 %collective-permute-start.2 = (f32[4,448,128]{2,1,0:T(8,128)S(1)}, f32[4,448,128]{2,1,0:T(8,128)S(1)}, u32[]{:S(2)}, u32[]{:S(2)}) collective-permute-start(f32[4,448,128]{2,1,0:T(8,128)S(1)} %gate.1), channel_id=1, source_target_pairs={{0,8},{1,9},{2,10},{3,11},{4,12},{5,13},{6,14},{7,15},{8,0},{9,1},... | collective-permute-start | bytes 2752520 | tf_op jit(solution)/shard_map/ppermute | solution.py:585
  24.3 17.2 %copy-start = (bf16[2,512,256]{2,1,0:T(8,128)(2,1)S(1)}, bf16[2,512,256]{2,1,0:T(8,128)(2,1)}, u32[]{:S(2)}) copy-start(bf16[2,512,256]{2,1,0:T(8,128)(2,1)} %constant.50.clone.halo_w) | copy-start | bytes 1572868
  24.3 1.4 %collective-permute-start.3 = (f32[192,128]{1,0:T(8,128)S(1)}, f32[192,128]{1,0:T(8,128)S(1)}, u32[]{:S(2)}, u32[]{:S(2)}) collective-permute-start(f32[192,128]{1,0:T(8,128)S(1)} %join_table.1.table), channel_id=1, source_target_pairs={{0,1},{1,0},{2,3},{3,2},{4,5},{5,4},{6,7},{7,6},{8,9},{9,8},{10,11... | collective-permute-start | bytes 294920 | tf_op jit(solution)/shard_map/ppermute | solution.py:585
  25.7 5.2 %collective-permute-start.4 = (f32[136,128]{1,0:T(8,128)S(1)}, f32[136,128]{1,0:T(8,128)S(1)}, u32[]{:S(2)}, u32[]{:S(2)}) collective-permute-start(f32[136,128]{1,0:T(8,128)S(1)} %pair.4.half.mine), channel_id=1, source_target_pairs={{0,7},{1,2},{2,1},{3,4},{4,3},{5,6},{6,5},{7,0},{8,15},{9,10},{10,... | collective-permute-start | bytes 208904 | tf_op jit(solution)/shard_map/ppermute | solution.py:585
  27.3 9.1 %collective-permute-start.7 = (f32[4,144,128]{2,1,0:T(8,128)S(1)}, f32[4,144,128]{2,1,0:T(8,128)S(1)}, u32[]{:S(2)}, u32[]{:S(2)}) collective-permute-start(f32[4,144,128]{2,1,0:T(8,128)S(1)} %get-tuple-element.70), channel_id=1, source_target_pairs={{0,1},{1,0},{2,3},{3,2},{4,5},{5,4},{6,7},{7,6},{8,9},{9,8},{10,11... | collective-permute-start | bytes 884744 | tf_op jit(solution)/shard_map/ppermute | solution.py:585
  27.4 9.9 %collective-permute-start.8 = (f32[4,144,128]{2,1,0:T(8,128)S(1)}, f32[4,144,128]{2,1,0:T(8,128)S(1)}, u32[]{:S(2)}, u32[]{:S(2)}) collective-permute-start(f32[4,144,128]{2,1,0:T(8,128)S(1)} %get-tuple-element.71), channel_id=1, source_target_pairs={{0,7},{1,2},{2,1},{3,4},{4,3},{5,6},{6,5},{7,0},{8,15},{9,10},{10,... | collective-permute-start | bytes 884744 | tf_op jit(solution)/shard_map/ppermute | solution.py:585
  28.5 11.0 %collective-permute-start.9 = (f32[4,144,128]{2,1,0:T(8,128)S(1)}, f32[4,144,128]{2,1,0:T(8,128)S(1)}, u32[]{:S(2)}, u32[]{:S(2)}) collective-permute-start(f32[4,144,128]{2,1,0:T(8,128)S(1)} %get-tuple-element.72), channel_id=1, source_target_pairs={{0,16},{1,17},{2,18},{3,19},{4,20},{5,21},{6,22},{7,23},{8,24},{9,... | collective-permute-start | bytes 884744 | tf_op jit(solution)/shard_map/ppermute | solution.py:585
  31.0 10.5 %collective-permute-start.10 = (f32[4,144,128]{2,1,0:T(8,128)S(1)}, f32[4,144,128]{2,1,0:T(8,128)S(1)}, u32[]{:S(2)}, u32[]{:S(2)}) collective-permute-start(f32[4,144,128]{2,1,0:T(8,128)S(1)} %get-tuple-element.73), channel_id=1, source_target_pairs={{0,48},{1,49},{2,50},{3,51},{4,52},{5,53},{6,54},{7,55},{8,56},{9,... | collective-permute-start | bytes 884744 | tf_op jit(solution)/shard_map/ppermute | solution.py:585
  36.4 6.8 %collective-permute-start.6 = (f32[72,128]{1,0:T(8,128)S(1)}, f32[72,128]{1,0:T(8,128)S(1)}, u32[]{:S(2)}, u32[]{:S(2)}) collective-permute-start(f32[72,128]{1,0:T(8,128)S(1)} %get-tuple-element.68.low), channel_id=1, source_target_pairs={{0,48},{1,49},{2,50},{3,51},{4,52},{5,53},{6,54},{7,55},{8,56},{9,... | collective-permute-start | bytes 110600 | tf_op jit(solution)/shard_map/ppermute | solution.py:585
  37.3 6.0 %collective-permute-start.5 = (f32[72,128]{1,0:T(8,128)S(1)}, f32[72,128]{1,0:T(8,128)S(1)}, u32[]{:S(2)}, u32[]{:S(2)}) collective-permute-start(f32[72,128]{1,0:T(8,128)S(1)} %get-tuple-element.69.high), channel_id=1, source_target_pairs={{0,16},{1,17},{2,18},{3,19},{4,20},{5,21},{6,22},{7,23},{8,24},{9,... | collective-permute-start | bytes 110600 | tf_op jit(solution)/shard_map/ppermute | solution.py:585
  43.3 6.4 %collective-permute-start.11 = (f32[128,128]{1,0:T(8,128)S(1)}, f32[128,128]{1,0:T(8,128)S(1)}, u32[]{:S(2)}, u32[]{:S(2)}) collective-permute-start(f32[128,128]{1,0:T(8,128)S(1)} %get-tuple-element.76.mine), channel_id=1, source_target_pairs={{0,1},{1,0},{2,3},{3,2},{4,5},{5,4},{6,7},{7,6},{8,9},{9,8},{10,11... | collective-permute-start | bytes 196616 | tf_op jit(solution)/shard_map/ppermute | solution.py:585
  52.1 16.4 %collective-permute-start.16 = (f32[4,144,128]{2,1,0:T(8,128)S(1)}, f32[4,144,128]{2,1,0:T(8,128)S(1)}, u32[]{:S(2)}, u32[]{:S(2)}) collective-permute-start(f32[4,144,128]{2,1,0:T(8,128)S(1)} %get-tuple-element.82), channel_id=1, source_target_pairs={{0,1},{1,0},{2,3},{3,2},{4,5},{5,4},{6,7},{7,6},{8,9},{9,8},{10,11... | collective-permute-start | bytes 884744 | tf_op jit(solution)/shard_map/ppermute | solution.py:585
  52.2 16.3 %collective-permute-start.17 = (f32[4,144,128]{2,1,0:T(8,128)S(1)}, f32[4,144,128]{2,1,0:T(8,128)S(1)}, u32[]{:S(2)}, u32[]{:S(2)}) collective-permute-start(f32[4,144,128]{2,1,0:T(8,128)S(1)} %get-tuple-element.83), channel_id=1, source_target_pairs={{0,7},{1,2},{2,1},{3,4},{4,3},{5,6},{6,5},{7,0},{8,15},{9,10},{10,... | collective-permute-start | bytes 884744 | tf_op jit(solution)/shard_map/ppermute | solution.py:585
  53.9 14.6 %collective-permute-start.18 = (f32[4,144,128]{2,1,0:T(8,128)S(1)}, f32[4,144,128]{2,1,0:T(8,128)S(1)}, u32[]{:S(2)}, u32[]{:S(2)}) collective-permute-start(f32[4,144,128]{2,1,0:T(8,128)S(1)} %get-tuple-element.84), channel_id=1, source_target_pairs={{0,16},{1,17},{2,18},{3,19},{4,20},{5,21},{6,22},{7,23},{8,24},{9,... | collective-permute-start | bytes 884744 | tf_op jit(solution)/shard_map/ppermute | solution.py:585
  55.8 12.7 %collective-permute-start.19 = (f32[4,144,128]{2,1,0:T(8,128)S(1)}, f32[4,144,128]{2,1,0:T(8,128)S(1)}, u32[]{:S(2)}, u32[]{:S(2)}) collective-permute-start(f32[4,144,128]{2,1,0:T(8,128)S(1)} %get-tuple-element.85), channel_id=1, source_target_pairs={{0,48},{1,49},{2,50},{3,51},{4,52},{5,53},{6,54},{7,55},{8,56},{9,... | collective-permute-start | bytes 884744 | tf_op jit(solution)/shard_map/ppermute | solution.py:585
  59.8 1.4 %collective-permute-start.12 = (f32[192,128]{1,0:T(8,128)S(1)}, f32[192,128]{1,0:T(8,128)S(1)}, u32[]{:S(2)}, u32[]{:S(2)}) collective-permute-start(f32[192,128]{1,0:T(8,128)S(1)} %table.3), channel_id=1, source_target_pairs={{0,1},{1,0},{2,3},{3,2},{4,5},{5,4},{6,7},{7,6},{8,9},{9,8},{10,11... | collective-permute-start | bytes 294920 | tf_op jit(solution)/shard_map/ppermute | solution.py:585
  61.2 5.2 %collective-permute-start.13 = (f32[128,128]{1,0:T(8,128)S(1)}, f32[128,128]{1,0:T(8,128)S(1)}, u32[]{:S(2)}, u32[]{:S(2)}) collective-permute-start(f32[128,128]{1,0:T(8,128)S(1)} %pair.5.half.mine), channel_id=1, source_target_pairs={{0,7},{1,2},{2,1},{3,4},{4,3},{5,6},{6,5},{7,0},{8,15},{9,10},{10,... | collective-permute-start | bytes 196616 | tf_op jit(solution)/shard_map/ppermute | solution.py:585
  66.4 4.0 %collective-permute-start.15 = (f32[64,128]{1,0:T(8,128)S(1)}, f32[64,128]{1,0:T(8,128)S(1)}, u32[]{:S(2)}, u32[]{:S(2)}) collective-permute-start(f32[64,128]{1,0:T(8,128)S(1)} %get-tuple-element.79.low), channel_id=1, source_target_pairs={{0,48},{1,49},{2,50},{3,51},{4,52},{5,53},{6,54},{7,55},{8,56},{9,... | collective-permute-start | bytes 98312 | tf_op jit(solution)/shard_map/ppermute | solution.py:585
  68.5 5.1 %collective-permute-start.14 = (f32[64,128]{1,0:T(8,128)S(1)}, f32[64,128]{1,0:T(8,128)S(1)}, u32[]{:S(2)}, u32[]{:S(2)}) collective-permute-start(f32[64,128]{1,0:T(8,128)S(1)} %get-tuple-element.80.high), channel_id=1, source_target_pairs={{0,16},{1,17},{2,18},{3,19},{4,20},{5,21},{6,22},{7,23},{8,24},{9,... | collective-permute-start | bytes 98312 | tf_op jit(solution)/shard_map/ppermute | solution.py:585
  73.6 1.3 collective-permute-start.20
  77.4 12.1 %collective-permute-start.25 = (f32[4,144,128]{2,1,0:T(8,128)S(1)}, f32[4,144,128]{2,1,0:T(8,128)S(1)}, u32[]{:S(2)}, u32[]{:S(2)}) collective-permute-start(f32[4,144,128]{2,1,0:T(8,128)S(1)} %get-tuple-element.92), channel_id=1, source_target_pairs={{0,1},{1,0},{2,3},{3,2},{4,5},{5,4},{6,7},{7,6},{8,9},{9,8},{10,11... | collective-permute-start | bytes 884744 | tf_op jit(solution)/shard_map/ppermute | solution.py:585
  77.6 13.9 %collective-permute-start.26 = (f32[4,144,128]{2,1,0:T(8,128)S(1)}, f32[4,144,128]{2,1,0:T(8,128)S(1)}, u32[]{:S(2)}, u32[]{:S(2)}) collective-permute-start(f32[4,144,128]{2,1,0:T(8,128)S(1)} %get-tuple-element.93), channel_id=1, source_target_pairs={{0,7},{1,2},{2,1},{3,4},{4,3},{5,6},{6,5},{7,0},{8,15},{9,10},{10,... | collective-permute-start | bytes 884744 | tf_op jit(solution)/shard_map/ppermute | solution.py:585
  77.6 13.9 %collective-permute-start.27 = (f32[4,144,128]{2,1,0:T(8,128)S(1)}, f32[4,144,128]{2,1,0:T(8,128)S(1)}, u32[]{:S(2)}, u32[]{:S(2)}) collective-permute-start(f32[4,144,128]{2,1,0:T(8,128)S(1)} %get-tuple-element.94), channel_id=1, source_target_pairs={{0,16},{1,17},{2,18},{3,19},{4,20},{5,21},{6,22},{7,23},{8,24},{9,... | collective-permute-start | bytes 884744 | tf_op jit(solution)/shard_map/ppermute | solution.py:585
  77.6 13.9 %collective-permute-start.28 = (f32[4,144,128]{2,1,0:T(8,128)S(1)}, f32[4,144,128]{2,1,0:T(8,128)S(1)}, u32[]{:S(2)}, u32[]{:S(2)}) collective-permute-start(f32[4,144,128]{2,1,0:T(8,128)S(1)} %get-tuple-element.95), channel_id=1, source_target_pairs={{0,48},{1,49},{2,50},{3,51},{4,52},{5,53},{6,54},{7,55},{8,56},{9,... | collective-permute-start | bytes 884744 | tf_op jit(solution)/shard_map/ppermute | solution.py:585
  82.8 1.4 %collective-permute-start.21 = (f32[192,128]{1,0:T(8,128)S(1)}, f32[192,128]{1,0:T(8,128)S(1)}, u32[]{:S(2)}, u32[]{:S(2)}) collective-permute-start(f32[192,128]{1,0:T(8,128)S(1)} %table.4), channel_id=1, source_target_pairs={{0,1},{1,0},{2,3},{3,2},{4,5},{5,4},{6,7},{7,6},{8,9},{9,8},{10,11... | collective-permute-start | bytes 294920 | tf_op jit(solution)/shard_map/ppermute | solution.py:585
  84.2 5.2 %collective-permute-start.22 = (f32[128,128]{1,0:T(8,128)S(1)}, f32[128,128]{1,0:T(8,128)S(1)}, u32[]{:S(2)}, u32[]{:S(2)}) collective-permute-start(f32[128,128]{1,0:T(8,128)S(1)} %pair.6.half.mine), channel_id=1, source_target_pairs={{0,7},{1,2},{2,1},{3,4},{4,3},{5,6},{6,5},{7,0},{8,15},{9,10},{10,... | collective-permute-start | bytes 196616 | tf_op jit(solution)/shard_map/ppermute | solution.py:585
  89.4 4.0 %collective-permute-start.24 = (f32[64,128]{1,0:T(8,128)S(1)}, f32[64,128]{1,0:T(8,128)S(1)}, u32[]{:S(2)}, u32[]{:S(2)}) collective-permute-start(f32[64,128]{1,0:T(8,128)S(1)} %get-tuple-element.90.low), channel_id=1, source_target_pairs={{0,48},{1,49},{2,50},{3,51},{4,52},{5,53},{6,54},{7,55},{8,56},{9,... | collective-permute-start | bytes 98312 | tf_op jit(solution)/shard_map/ppermute | solution.py:585
  89.5 5.2 %collective-permute-start.23 = (f32[64,128]{1,0:T(8,128)S(1)}, f32[64,128]{1,0:T(8,128)S(1)}, u32[]{:S(2)}, u32[]{:S(2)}) collective-permute-start(f32[64,128]{1,0:T(8,128)S(1)} %get-tuple-element.91.high), channel_id=1, source_target_pairs={{0,16},{1,17},{2,18},{3,19},{4,20},{5,21},{6,22},{7,23},{8,24},{9,... | collective-permute-start | bytes 98312 | tf_op jit(solution)/shard_map/ppermute | solution.py:585
  94.7 1.6 %collective-permute-start.29 = (f32[128,128]{1,0:T(8,128)S(1)}, f32[128,128]{1,0:T(8,128)S(1)}, u32[]{:S(2)}, u32[]{:S(2)}) collective-permute-start(f32[128,128]{1,0:T(8,128)S(1)} %get-tuple-element.98.mine), channel_id=1, source_target_pairs={{0,1},{1,0},{2,3},{3,2},{4,5},{5,4},{6,7},{7,6},{8,9},{9,8},{10,11... | collective-permute-start | bytes 196616 | tf_op jit(solution)/shard_map/ppermute | solution.py:585
  98.7 13.2 %collective-permute-start.34 = (f32[4,144,128]{2,1,0:T(8,128)S(1)}, f32[4,144,128]{2,1,0:T(8,128)S(1)}, u32[]{:S(2)}, u32[]{:S(2)}) collective-permute-start(f32[4,144,128]{2,1,0:T(8,128)S(1)} %get-tuple-element.102), channel_id=1, source_target_pairs={{0,1},{1,0},{2,3},{3,2},{4,5},{5,4},{6,7},{7,6},{8,9},{9,8},{10,11... | collective-permute-start | bytes 884744 | tf_op jit(solution)/shard_map/ppermute | solution.py:585
  98.9 14.9 %collective-permute-start.35 = (f32[4,144,128]{2,1,0:T(8,128)S(1)}, f32[4,144,128]{2,1,0:T(8,128)S(1)}, u32[]{:S(2)}, u32[]{:S(2)}) collective-permute-start(f32[4,144,128]{2,1,0:T(8,128)S(1)} %get-tuple-element.103), channel_id=1, source_target_pairs={{0,7},{1,2},{2,1},{3,4},{4,3},{5,6},{6,5},{7,0},{8,15},{9,10},{10,... | collective-permute-start | bytes 884744 | tf_op jit(solution)/shard_map/ppermute | solution.py:585
  100.3 13.5 %collective-permute-start.36 = (f32[4,144,128]{2,1,0:T(8,128)S(1)}, f32[4,144,128]{2,1,0:T(8,128)S(1)}, u32[]{:S(2)}, u32[]{:S(2)}) collective-permute-start(f32[4,144,128]{2,1,0:T(8,128)S(1)} %get-tuple-element.104), channel_id=1, source_target_pairs={{0,16},{1,17},{2,18},{3,19},{4,20},{5,21},{6,22},{7,23},{8,24},{9,... | collective-permute-start | bytes 884744 | tf_op jit(solution)/shard_map/ppermute | solution.py:585
  100.8 13.0 %collective-permute-start.37 = (f32[4,144,128]{2,1,0:T(8,128)S(1)}, f32[4,144,128]{2,1,0:T(8,128)S(1)}, u32[]{:S(2)}, u32[]{:S(2)}) collective-permute-start(f32[4,144,128]{2,1,0:T(8,128)S(1)} %get-tuple-element.105), channel_id=1, source_target_pairs={{0,48},{1,49},{2,50},{3,51},{4,52},{5,53},{6,54},{7,55},{8,56},{9,... | collective-permute-start | bytes 884744 | tf_op jit(solution)/shard_map/ppermute | solution.py:585
  105.5 1.4 %collective-permute-start.30 = (f32[192,128]{1,0:T(8,128)S(1)}, f32[192,128]{1,0:T(8,128)S(1)}, u32[]{:S(2)}, u32[]{:S(2)}) collective-permute-start(f32[192,128]{1,0:T(8,128)S(1)} %table.5), channel_id=1, source_target_pairs={{0,1},{1,0},{2,3},{3,2},{4,5},{5,4},{6,7},{7,6},{8,9},{9,8},{10,11... | collective-permute-start | bytes 294920 | tf_op jit(solution)/shard_map/ppermute | solution.py:585
  106.9 4.8 %collective-permute-start.31 = (f32[128,128]{1,0:T(8,128)S(1)}, f32[128,128]{1,0:T(8,128)S(1)}, u32[]{:S(2)}, u32[]{:S(2)}) collective-permute-start(f32[128,128]{1,0:T(8,128)S(1)} %pair.7.half.mine), channel_id=1, source_target_pairs={{0,7},{1,2},{2,1},{3,4},{4,3},{5,6},{6,5},{7,0},{8,15},{9,10},{10,... | collective-permute-start | bytes 196616 | tf_op jit(solution)/shard_map/ppermute | solution.py:585
  111.7 4.0 %collective-permute-start.33 = (f32[64,128]{1,0:T(8,128)S(1)}, f32[64,128]{1,0:T(8,128)S(1)}, u32[]{:S(2)}, u32[]{:S(2)}) collective-permute-start(f32[64,128]{1,0:T(8,128)S(1)} %get-tuple-element.100.low), channel_id=1, source_target_pairs={{0,48},{1,49},{2,50},{3,51},{4,52},{5,53},{6,54},{7,55},{8,56},{9,... | collective-permute-start | bytes 98312 | tf_op jit(solution)/shard_map/ppermute | solution.py:585
  111.8 5.2 %collective-permute-start.32 = (f32[64,128]{1,0:T(8,128)S(1)}, f32[64,128]{1,0:T(8,128)S(1)}, u32[]{:S(2)}, u32[]{:S(2)}) collective-permute-start(f32[64,128]{1,0:T(8,128)S(1)} %get-tuple-element.101.high), channel_id=1, source_target_pairs={{0,16},{1,17},{2,18},{3,19},{4,20},{5,21},{6,22},{7,23},{8,24},{9,... | collective-permute-start | bytes 98312 | tf_op jit(solution)/shard_map/ppermute | solution.py:585
  117.0 1.3 collective-permute-start.38
  121.0 15.5 %collective-permute-start.39 = (f32[4,8,3072]{2,1,0:T(8,128)S(1)}, f32[4,8,3072]{2,1,0:T(8,128)S(1)}, u32[]{:S(2)}, u32[]{:S(2)}) collective-permute-start(f32[4,8,3072]{2,1,0:T(8,128)S(1)} %get-tuple-element.109), channel_id=1, source_target_pairs={{0,8},{1,9},{2,10},{3,11},{4,12},{5,13},{6,14},{7,15},{8,0},{9,1},... | collective-permute-start | bytes 1179656 | tf_op jit(solution)/shard_map/ppermute | solution.py:585
  124.3 11.0 %collective-permute-start.40 = (f32[8,1536]{1,0:T(8,128)S(1)}, f32[8,1536]{1,0:T(8,128)S(1)}, u32[]{:S(2)}, u32[]{:S(2)}) collective-permute-start(f32[8,1536]{1,0:T(8,128)S(1)} %get-tuple-element.111), channel_id=1, source_target_pairs={{0,8},{1,9},{2,10},{3,11},{4,12},{5,13},{6,14},{7,15},{8,0},{9,1},... | collective-permute-start | bytes 147464 | tf_op jit(solution)/shard_map/ppermute | solution.py:585
  125.8 9.6 %collective-permute-start.41 = (f32[8,1536]{1,0:T(8,128)S(1)}, f32[8,1536]{1,0:T(8,128)S(1)}, u32[]{:S(2)}, u32[]{:S(2)}) collective-permute-start(f32[8,1536]{1,0:T(8,128)S(1)} %get-tuple-element.112), channel_id=1, source_target_pairs={{0,64},{64,0},{1,65},{65,1},{2,66},{66,2},{3,67},{67,3},{4,68},{68... | collective-permute-start | bytes 147464 | tf_op jit(solution)/shard_map/ppermute | solution.py:804
  128.5 8.0 %collective-permute-start.42 = (f32[8,1536]{1,0:T(8,128)S(1)}, f32[8,1536]{1,0:T(8,128)S(1)}, u32[]{:S(2)}, u32[]{:S(2)}) collective-permute-start(f32[8,1536]{1,0:T(8,128)S(1)} %get-tuple-element.113), channel_id=1, source_target_pairs={{0,72},{1,73},{2,74},{3,75},{4,76},{5,77},{6,78},{7,79},{8,64},{9,... | collective-permute-start | bytes 147464 | tf_op jit(solution)/shard_map/ppermute | solution.py:805
  (6 other events, 60.9 us)

commit v4 on v3

--- a/solution.py
+++ b/solution.py
@@ -27,6 +27,7 @@
 LANES = 128
 EDGE = HALO * 16
 OWN = 512
+HEAD = 384
 ROOM = 58
 CODES = 12
 TABLE = CODES * ROWS
@@ -176,6 +177,16 @@
 
 def flag(params, row):
     return params[row : row + 1, :] == 1.0
+
+
+def pick_kernel(raw, potential, out, sems):
+    start = (1 - lax.axis_index("dom") // 8 % 2) * ORB
+    first = pltpu.make_async_copy(raw.at[pl.ds(start, ORB)], out.at[pl.ds(0, ORB)], sems.at[0])
+    second = pltpu.make_async_copy(potential, out.at[pl.ds(ORB, 1)], sems.at[1])
+    first.start()
+    second.start()
+    first.wait()
+    second.wait()
 
 
 def begin_kernel(
@@ -267,18 +278,23 @@
     pass
 
 
+def own_kernel(ints, own, note, placed):
+    for j in range(NPJ):
+        for k in range(HEAD // LANES):
+            at = slice(k * LANES, (k + 1) * LANES)
+            placed[j, :, at] = shifted(own[j, at], ints[1:2, at])
+
+
 def prepare_kernel(ints, note_came, own, came, placed, index):
     lines = [note_came[NOTE + 8 + 4 * k : NOTE + 12 + 4 * k] for k in range(OWN // LANES)]
     other = jnp.concatenate(lines, axis=1)[:, :PIECES].astype(jnp.int32)
     index[...] = jnp.concatenate([ints[:4, :PIECES], other], axis=1)
-
-    def step(j):
-        both = jnp.concatenate([own[j], came[j]], axis=0)
-        for k in range(ALL // LANES):
+    for j in range(NPJ):
+        both = jnp.concatenate([own[j, HEAD:], came[j]], axis=0)
+        for k in range((ALL - HEAD) // LANES):
             at = slice(k * LANES, (k + 1) * LANES)
-            placed[j, :, at] = shifted(both[at], index[1:2, at])
-
-    each(NPJ, step, False)
+            spot = slice(HEAD + k * LANES, HEAD + (k + 1) * LANES)
+            placed[j, :, at] = shifted(both[at], index[1:2, spot])
 
 
 def column_hot(index, at, wide):
@@ -286,9 +302,9 @@
     return where.astype(F32).astype(BF16)
 
 
-def chunks(step):
-    each(ALL // 256, lambda k: step(k * 256, 256), False)
-    step(ALL - LANES, LANES)
+def chunks(head, tail, step):
+    for source, at, base, wide in ((head, 0, 0, 256), (head, 256, 0, 128), (tail, 0, HEAD, 256), (tail, 256, HEAD, 256)):
+        step(source, at, base + at, wide)
 
 
 def atom_hot(index):
@@ -311,13 +327,13 @@
     return mul_t(high, atoms) + mul_t(low, atoms)
 
 
-def project(both, hot, placed, partial, at, wide):
+def project(both, hot, placed, partial, spot, at, wide):
     picked = mul(both, jnp.concatenate([hot, hot], axis=0))
     sums = [None] * ROWS
     for z in range(0, NZ, 8):
         lines = [picked[o * NZ + z : o * NZ + z + 8] for o in range(ORB)]
         for j in range(NPJ):
-            values = placed[j, z : z + 8, pl.ds(at, wide)]
+            values = placed[j, z : z + 8, pl.ds(spot, wide)]
             for o in range(ORB):
                 term = lines[o] * values
                 row = o * NPJ + j
@@ -345,7 +361,7 @@
         def chunk(k):
             at = k * 256
             where = lax.broadcasted_iota(jnp.int32, (LANES, 256), 0) == index[4:5, pl.ds(at, 256)]
-            project(both[...], where.astype(F32).astype(BF16), placed, partial, at, 256)
+            project(both[...], where.astype(F32).astype(BF16), placed, partial, at, at, 256)
 
         each(OWN // 256, chunk, False)
         tables[s] = gather_table(index, partial[...])
@@ -353,13 +369,16 @@
     each(2, table)
 
 
-def table_kernel(index, field, placed, table, partial, both):
+def table_kernel(index, field, head, tail, table, partial, both):
     def gather(o):
         rows = pl.ds(o * NZ, NZ)
         both[rows, :] = jnp.concatenate(split(field[o]), axis=1)
 
     each(ORB, gather, False)
-    chunks(lambda at, wide: project(both[...], column_hot(index, at, wide), placed, partial, at, wide))
+    def chunk(placed, spot, at, wide):
+        project(both[...], column_hot(index, at, wide), placed, partial, spot, at, wide)
+
+    chunks(head, tail, chunk)
     table[...] = gather_table(index, partial[...])
 
 
@@ -470,7 +489,7 @@
     each(ORB, step)
 
 
-def update_kernel(last, params, index, acc, mine, came, placed, *rest):
+def update_kernel(last, params, index, acc, mine, came, head, tail, *rest):
     if last:
         sent, field, coef_rows, near, far = rest
     else:
@@ -489,19 +508,19 @@
     coef_rows[...] = coefs
     sums = []
 
-    def chunk(at, wide):
+    def chunk(placed, spot, at, wide):
         hot = column_hot(index, at, wide)
         lines = []
         for o in range(ORB):
             rows = coef_rows[o * NPJ : (o + 1) * NPJ, pl.ds(at, wide)]
-            line = rows[0:1] * placed[0, :, pl.ds(at, wide)]
+            line = rows[0:1] * placed[0, :, pl.ds(spot, wide)]
             for j in range(1, NPJ):
-                line = line + rows[j : j + 1] * placed[j, :, pl.ds(at, wide)]
+                line = line + rows[j : j + 1] * placed[j, :, pl.ds(spot, wide)]
             lines.append(jnp.concatenate(split(line), axis=1))
         term = mul_t(jnp.concatenate(lines, axis=0), jnp.concatenate([hot, hot], axis=1))
         sums[:] = [sums[0] + term if sums else term]
 
-    chunks(chunk)
+    chunks(head, tail, chunk)
 
     def finish(o):
         field[o] = acc[o] + sums[0][o * NZ : (o + 1) * NZ]
@@ -520,9 +539,9 @@
     each(ORB, emit)
 
 
-def join_kernel(params, came, b, c, d, mine, a, out, density):
+def join_kernel(params, came, b, mine, a, out, density):
     upper = params[0:1, 0:1] == 1.0
-    density[...] = a[...] + b[...] + c[...] + d[...]
+    density[...] = a[...] + b[...]
 
     def step(o):
         out[o] = jnp.where(upper, came[o], mine[o])
@@ -531,7 +550,7 @@
     each(ORB, step)
 
 
-def density_kernel(params, field, kept, quarter, across_x, across_band, across_both, plane, near, far):
+def density_kernel(params, field, mine, across, plane, near, far):
     dens = jnp.zeros((NZ, COLS), F32)
     for o in range(ORB):
         dens = dens + params[8 + o : 9 + o, 0:1] * field[o] * field[o]
@@ -539,14 +558,15 @@
     upper = flag(params, 0)
     second = params[5:6, 0:1] == 1.0
     span = CY * NZ // 2
-    for value, same, opposite in (
-        (jnp.where(upper, right, left), quarter, across_band),
-        (jnp.where(upper, left, right), across_x, across_both),
-    ):
+    for k, value in enumerate((jnp.where(upper, right, left), jnp.where(upper, left, right))):
         for spot, pair in from_columns(value, near, far):
             plane[:, spot : spot + 2 * NZ] = pair
-        same[...] = jnp.where(second, plane[:, span:], plane[:, :span])
-        opposite[...] = jnp.where(second, plane[:, :span], plane[:, span:])
+        mine[k] = jnp.where(second, plane[:, span:], plane[:, :span])
+        across[k] = jnp.where(second, plane[:, :span], plane[:, span:])
+
+
+def keep_kernel(params, field, here, kept, near, far):
+    upper = flag(params, 0)
 
     def emit(o):
         mine = jnp.where(upper, field[o, :, LANES:], field[o, :, :LANES])
@@ -554,6 +574,11 @@
             kept[o, :, spot : spot + 2 * NZ] = pair
 
     each(ORB, emit)
+
+
+def band_kernel(here, came, quarter, going):
+    quarter[...] = here[0] + came[0]
+    going[...] = here[1] + came[1]
 
 
 VM = pl.BlockSpec(memory_space=pltpu.VMEM)
@@ -627,8 +652,16 @@
     stage = [pltpu.VMEM((LANES, LANES), F32)] * 2
 
     raw = orbitals[:, 0]
-    going = jnp.where(side == 0, raw[ORB:], raw[:ORB])
-    came = send(jnp.concatenate([going, potential], axis=0), SWAP)
+    message = call(
+        pick_kernel,
+        [HB] * 2,
+        (ORB + 1, CX, CY * NZ),
+        (raw, potential),
+        [pltpu.SemaphoreType.DMA((2,))],
+        flops=10**6,
+        name="pick",
+    )
+    came = send(message, SWAP)
     line = pltpu.VMEM((1, PIECES), jnp.int32)
     keep, params, ints, own_table, note = call(
         begin_kernel,
@@ -677,10 +710,11 @@
     table = call(
         join_table_kernel, [VM] * 2 + [ANY], (TABLE, LANES), (own_table, note_came, field), flops=10**6, name="join_table"
     )
-    placed, index = call(
+    head = call(own_kernel, [VM] * 2 + [ANY], (NPJ, NZ, HEAD), (ints, projectors[0], table), name="own")
+    tail, index = call(
         prepare_kernel,
         [VM] * 4,
-        [(NPJ, NZ, ALL), ((4, ALL), jnp.int32)],
+        [(NPJ, NZ, ALL - HEAD), ((4, ALL), jnp.int32)],
         (ints, note_came, projectors[0], proj_came),
         name="prepare",
     )
@@ -692,9 +726,9 @@
         if not first:
             table = call(
                 table_kernel,
-                [VM] * 3,
+                [VM] * 4,
                 (TABLE, LANES),
-                (index, field, placed),
+                (index, field, head, tail),
                 [pltpu.VMEM((ROWS, ALL), F32), pltpu.VMEM((ORB * NZ, 2 * COLS), BF16)],
                 name="table",
             )
@@ -762,11 +796,11 @@
                 passed=1,
             )
         total_came = send(total, CORES)
-        args = (params, index, acc, total, total_came, placed)
+        args = (params, index, acc, total, total_came, head, tail)
         if not last:
             before, (field, xl, xh, inner, outer) = field, call(
                 functools.partial(update_kernel, last),
-                [VM] * 7,
+                [VM] * 8,
                 [grid] + [packed] * 4,
                 args + (edge_w,),
                 sums_room,
@@ -776,36 +810,30 @@
             flat = (ORB, CX, CY * NZ)
             other, result = call(
                 functools.partial(update_kernel, last),
-                [VM] * 6,
+                [VM] * 7,
                 [flat, grid],
                 args,
                 sums_room + stage,
                 name="finish",
             )
     part = (CX, CY * NZ // 2)
-    mine, quarter, across_x, across_band, across_both = call(
+    here_parts, across = call(
         density_kernel,
         [VM] * 2,
-        [flat] + [part] * 4,
+        [(2,) + part] * 2,
         (params, result),
         [pltpu.VMEM((CX, CY * NZ), F32)] + stage,
         name="density",
     )
     swapped = send(other, SWAP)
-    both = [(d, d ^ 72) for d in range(128)]
+    across_came = lax.ppermute(across, "band", [(0, 1), (1, 0)])
+    mine = call(keep_kernel, [VM, VM, ANY], flat, (params, result, across), stage, name="keep")
+    quarter, going = call(band_kernel, [VM] * 2, [part] * 2, (here_parts, across_came), flops=10**6, name="band")
     filtered, density = call(
         join_kernel,
-        [VM] * 7,
+        [VM] * 5,
         [(2 * ORB, CX, CY * NZ), part],
-        (
-            params,
-            swapped,
-            send(across_x, SWAP),
-            lax.ppermute(across_band, "band", [(0, 1), (1, 0)]),
-            lax.ppermute(across_both, ("band", "dom"), both),
-            mine,
-            quarter,
-        ),
+        (params, swapped, send(going, SWAP), mine, quarter),
         name="join",
     )
     return filtered[:, None], density[None]

time: 138 us -> 137 us (level)
  other arithmetic: 2.82 us -> 0.65 us
  local copies, waits for them, and re-layouts: 0.12 us -> 2.13 us
  starting transfers between devices: 50.2 us -> 48.3 us
    ppermute x2 -> x1, starting transfers between devices: 5.09 us -> 2.79 us  [body(): across_came = lax.ppermute(across, 'band', [(0, 1), (1, 0)])]
    ppermute x2 -> x1, waiting for transfers between devices: 1.16 us -> 3.41 us  [body(): across_came = lax.ppermute(across, 'band', [(0, 1), (1, 0)])]
    unnamed x23 -> x27, local copies, waits for them, and re-layouts: 0.12 us -> 2.13 us
    ppermute x41, waiting for transfers between devices: 40.7 us -> 38.9 us  [send(): return lax.ppermute(value, 'dom', pairs)]
    pallas_call x34 -> x38, Pallas kernels: 40.1 us -> 40.6 us  [call(): pl.pallas_call(kernel, out_shape=[jax.ShapeDtypeStruct(*out) for out in o...]
  transfers between devices with their start and end apart: 43 -> 42, of which waited for: 25 -> 25; matrix products, arithmetic and copies ran while one was open for 1% -> 1% of each run, Pallas kernels for 21% -> 21%
where the time goes in v4:
time: 137 us; the launch traced here: 136 us
  starting transfers between devices  48.3 us (35%)
  waiting for transfers between devices  42.3 us (31%)
  Pallas kernels  40.6 us (30%)
  between operations  2.43 us (2%)
  local copies, waits for them, and re-layouts  2.13 us (2%)
    ppermute x41, starting transfers between devices, send(): return lax.ppermute(value, 'dom', pairs)  45.5 us
    pallas_call x38, Pallas kernels, call(): pl.pallas_call(kernel, out_shape=[jax.ShapeDtypeStruct(*out) for out in o...  40.6 us
    ppermute x41, waiting for transfers between devices, send(): return lax.ppermute(value, 'dom', pairs)  38.9 us
    ppermute x1, waiting for transfers between devices, body(): across_came = lax.ppermute(across, 'band', [(0, 1), (1, 0)])  3.41 us
    ppermute x1, starting transfers between devices, body(): across_came = lax.ppermute(across, 'band', [(0, 1), (1, 0)])  2.79 us
  transfers between devices with their start and end apart: 42, of which 25 were waited for; matrix products, arithmetic and copies ran while one was open for 1% of the time, Pallas kernels for 21%

profile of v4, /device:TPU:0, one launch (start us, length us, event | category | flops | bytes accessed | tf_op | source)
XLA Modules:
  0.0 136.4 jit_solution(13117177182915345965)
XLA Ops:
  3.0 3.4 %collective-permute-start.1 = (f32[5,8,3072]{2,1,0:T(8,128)S(1)}, f32[5,8,3072]{2,1,0:T(8,128)S(1)}, u32[]{:S(2)}, u32[]{:S(2)}) collective-permute-start(f32[5,8,3072]{2,1,0:T(8,128)S(1)} %pick.1), channel_id=1, source_target_pairs={{0,8},{1,9},{2,10},{3,11},{4,12},{5,13},{6,14},{7,15},{8,0},{9,1},... | collective-permute-start | bytes 1474568 | tf_op jit(solution)/shard_map/ppermute | solution.py:610
  8.3 7.0 %begin.1 = (f32[4,192,128]{2,1,0:T(8,128)}, f32[16,128]{1,0:T(8,128)}, s32[8,512]{1,0:T(8,128)}, f32[192,128]{1,0:T(8,128)}, f32[216,128]{1,0:T(8,128)}) custom-call(s32[3]{0:T(128)} %pad_add_fusion.place, f32[1]{0:T(128)S(6)} %copy.37.upper_in, f32[1]{0:T(128)S(6)} %copy.36.lower_in, f32[8]{0:T(128)} %weights_in.1, s32[1,448]{1,0:T(1,128)} %column_in.1, ...), custom_call_target="tpu_custom_call" | custom-call | flops 100000000 | bytes 4000000 | tf_op jit(solution)/shard_map/begin/pallas_call | solution.py:595
  15.8 6.1 %collective-permute-done.note_came = f32[216,128]{1,0:T(8,128)S(1)} collective-permute-done((f32[216,128]{1,0:T(8,128)}, f32[216,128]{1,0:T(8,128)S(1)}, u32[]{:S(2)}, u32[]{:S(2)}) %collective-permute-start) | collective-permute-done | bytes 110624 | tf_op jit(solution)/shard_map/ppermute | solution.py:610
  21.9 1.4 %collective-permute-start.2 = (f32[4,448,128]{2,1,0:T(8,128)S(1)}, f32[4,448,128]{2,1,0:T(8,128)S(1)}, u32[]{:S(2)}, u32[]{:S(2)}) collective-permute-start(f32[4,448,128]{2,1,0:T(8,128)S(1)} %gate.1), channel_id=1, source_target_pairs={{0,8},{1,9},{2,10},{3,11},{4,12},{5,13},{6,14},{7,15},{8,0},{9,1},... | collective-permute-start | bytes 2752520 | tf_op jit(solution)/shard_map/ppermute | solution.py:610
  24.7 1.3 collective-permute-done.3.came
  26.0 1.4 %collective-permute-start.4 = (f32[136,128]{1,0:T(8,128)S(1)}, f32[136,128]{1,0:T(8,128)S(1)}, u32[]{:S(2)}, u32[]{:S(2)}) collective-permute-start(f32[136,128]{1,0:T(8,128)S(1)} %pair.4.half.mine), channel_id=1, source_target_pairs={{0,7},{1,2},{2,1},{3,4},{4,3},{5,6},{6,5},{7,0},{8,15},{9,10},{10,... | collective-permute-start | bytes 208904 | tf_op jit(solution)/shard_map/ppermute | solution.py:610
  28.7 1.9 %collective-permute-start.9 = (f32[4,144,128]{2,1,0:T(8,128)S(1)}, f32[4,144,128]{2,1,0:T(8,128)S(1)}, u32[]{:S(2)}, u32[]{:S(2)}) collective-permute-start(f32[4,144,128]{2,1,0:T(8,128)S(1)} %get-tuple-element.71), channel_id=1, source_target_pairs={{0,16},{1,17},{2,18},{3,19},{4,20},{5,21},{6,22},{7,23},{8,24},{9,... | collective-permute-start | bytes 884744 | tf_op jit(solution)/shard_map/ppermute | solution.py:610
  31.0 4.0 %collective-permute-start.10 = (f32[4,144,128]{2,1,0:T(8,128)S(1)}, f32[4,144,128]{2,1,0:T(8,128)S(1)}, u32[]{:S(2)}, u32[]{:S(2)}) collective-permute-start(f32[4,144,128]{2,1,0:T(8,128)S(1)} %get-tuple-element.72), channel_id=1, source_target_pairs={{0,48},{1,49},{2,50},{3,51},{4,52},{5,53},{6,54},{7,55},{8,56},{9,... | collective-permute-start | bytes 884744 | tf_op jit(solution)/shard_map/ppermute | solution.py:610
  35.0 1.4 %local.4.acc = f32[4,192,256]{2,1,0:T(8,128)S(1)} custom-call(f32[16,128]{1,0:T(8,128)S(1)} %copy-done.2, f32[136,128]{1,0:T(8,128)S(1)} %pair.4.half.mine, f32[4,192,256]{2,1,0:T(8,128)S(1)} %get-tuple-element.65.field.before, f32[4,192,256]{2,1,0:T(8,128)S(1)} %get-tuple-element.65.field.before, f32[192,256]{1,0:T(8,128)S(1)} %get-tuple-element.66.pot, ...), custom_call_target="tpu_custom_call" | custom-call | flops 100000000 | bytes 4000000 | tf_op jit(solution)/shard_map/local/pallas_call | solution.py:595
  37.6 1.9 %collective-permute-start.5 = (f32[72,128]{1,0:T(8,128)S(1)}, f32[72,128]{1,0:T(8,128)S(1)}, u32[]{:S(2)}, u32[]{:S(2)}) collective-permute-start(f32[72,128]{1,0:T(8,128)S(1)} %get-tuple-element.68.high), channel_id=1, source_target_pairs={{0,16},{1,17},{2,18},{3,19},{4,20},{5,21},{6,22},{7,23},{8,24},{9,... | collective-permute-start | bytes 110600 | tf_op jit(solution)/shard_map/ppermute | solution.py:610
  39.6 2.0 %collective-permute-done.10.xh = f32[4,144,128]{2,1,0:T(8,128)S(1)} collective-permute-done((f32[4,144,128]{2,1,0:T(8,128)S(1)}, f32[4,144,128]{2,1,0:T(8,128)S(1)}, u32[]{:S(2)}, u32[]{:S(2)}) %collective-permute-start.10) | collective-permute-done | bytes 294944 | tf_op jit(solution)/shard_map/ppermute | solution.py:610
  41.6 1.6 %halo.4.acc = f32[4,192,256]{2,1,0:T(8,128)S(1)} custom-call(f32[16,128]{1,0:T(8,128)S(1)} %copy-done.2, f32[4,144,128]{2,1,0:T(8,128)S(1)} %collective-permute-done.7.inner, f32[4,144,128]{2,1,0:T(8,128)S(1)} %collective-permute-done.8.outer, f32[4,144,128]{2,1,0:T(8,128)S(1)} %collective-permute-done.9.xl, f32[4,144,128]{2,1,0:T(8,128)S(1)} %collective-permute-done.10.xh, ...), custom_call_target="tpu_custom_call" | custom-call | flops 100000000 | bytes 4000000 | tf_op jit(solution)/shard_map/halo/pallas_call | solution.py:595
  44.4 3.7 %collective-permute-done.2.came = f32[4,448,128]{2,1,0:T(8,128)S(1)} collective-permute-done((f32[4,448,128]{2,1,0:T(8,128)S(1)}, f32[4,448,128]{2,1,0:T(8,128)S(1)}, u32[]{:S(2)}, u32[]{:S(2)}) %collective-permute-start.2) | collective-permute-done | bytes 917536 | tf_op jit(solution)/shard_map/ppermute | solution.py:610
  49.1 2.4 %update.3 = (f32[4,192,256]{2,1,0:T(8,128)S(1)}, f32[4,144,128]{2,1,0:T(8,128)S(1)}, f32[4,144,128]{2,1,0:T(8,128)S(1)}, f32[4,144,128]{2,1,0:T(8,128)S(1)}, f32[4,144,128]{2,1,0:T(8,128)S(1)}) custom-call(f32[16,128]{1,0:T(8,128)S(1)} %copy-done.2, s32[4,896]{1,0:T(4,128)S(1)} %get-tuple-element.62.index, f32[4,192,256]{2,1,0:T(8,128)S(1)} %get-tuple-element.74.acc, ...), custom_call_target="tpu_custom_call" | custom-call | flops 100000000 | bytes 4000000 | tf_op jit(solution)/shard_map/update/pallas_call | solution.py:595
  51.6 1.7 %collective-permute-start.17 = (f32[4,144,128]{2,1,0:T(8,128)S(1)}, f32[4,144,128]{2,1,0:T(8,128)S(1)}, u32[]{:S(2)}, u32[]{:S(2)}) collective-permute-start(f32[4,144,128]{2,1,0:T(8,128)S(1)} %get-tuple-element.82), channel_id=1, source_target_pairs={{0,7},{1,2},{2,1},{3,4},{4,3},{5,6},{6,5},{7,0},{8,15},{9,10},{10,... | collective-permute-start | bytes 884744 | tf_op jit(solution)/shard_map/ppermute | solution.py:610
  53.3 1.9 %collective-permute-start.18 = (f32[4,144,128]{2,1,0:T(8,128)S(1)}, f32[4,144,128]{2,1,0:T(8,128)S(1)}, u32[]{:S(2)}, u32[]{:S(2)}) collective-permute-start(f32[4,144,128]{2,1,0:T(8,128)S(1)} %get-tuple-element.83), channel_id=1, source_target_pairs={{0,16},{1,17},{2,18},{3,19},{4,20},{5,21},{6,22},{7,23},{8,24},{9,... | collective-permute-start | bytes 884744 | tf_op jit(solution)/shard_map/ppermute | solution.py:610
  55.3 2.1 %collective-permute-start.19 = (f32[4,144,128]{2,1,0:T(8,128)S(1)}, f32[4,144,128]{2,1,0:T(8,128)S(1)}, u32[]{:S(2)}, u32[]{:S(2)}) collective-permute-start(f32[4,144,128]{2,1,0:T(8,128)S(1)} %get-tuple-element.84), channel_id=1, source_target_pairs={{0,48},{1,49},{2,50},{3,51},{4,52},{5,53},{6,54},{7,55},{8,56},{9,... | collective-permute-start | bytes 884744 | tf_op jit(solution)/shard_map/ppermute | solution.py:610
  57.4 1.9 %table.3 = f32[192,128]{1,0:T(8,128)S(1)} custom-call(s32[4,896]{1,0:T(4,128)S(1)} %get-tuple-element.62.index, f32[4,192,256]{2,1,0:T(8,128)S(1)} %get-tuple-element.77.field.before, f32[4,192,384]{2,1,0:T(8,128)S(1)} %own.1.head, f32[4,192,512]{2,1,0:T(8,128)S(1)} %get-tuple-element.76.tail), custom_call_target="tpu_custom_call" | custom-call | flops 100000000 | bytes 4000000 | tf_op jit(solution)/shard_map/table/pallas_call | solution.py:595
  59.4 1.3 collective-permute-done.12.came
  61.5 1.4 %local.5.acc = f32[4,192,256]{2,1,0:T(8,128)S(1)} custom-call(f32[16,128]{1,0:T(8,128)S(1)} %copy-done.2, f32[128,128]{1,0:T(8,128)S(1)} %pair.5.half.mine, f32[4,192,256]{2,1,0:T(8,128)S(1)} %get-tuple-element.77.field.before, f32[4,192,256]{2,1,0:T(8,128)S(1)} %get-tuple-element.65.field.before, f32[192,256]{1,0:T(8,128)S(1)} %get-tuple-element.66.pot, ...), custom_call_target="tpu_custom_call" | custom-call | flops 100000000 | bytes 4000000 | tf_op jit(solution)/shard_map/local/pallas_call | solution.py:595
  62.9 2.9 %collective-permute-done.13.came = f32[128,128]{1,0:T(8,128)S(1)} collective-permute-done((f32[128,128]{1,0:T(8,128)S(1)}, f32[128,128]{1,0:T(8,128)S(1)}, u32[]{:S(2)}, u32[]{:S(2)}) %collective-permute-start.13) | collective-permute-done | bytes 65568 | tf_op jit(solution)/shard_map/ppermute | solution.py:610
  65.8 2.1 %collective-permute-start.15 = (f32[64,128]{1,0:T(8,128)S(1)}, f32[64,128]{1,0:T(8,128)S(1)}, u32[]{:S(2)}, u32[]{:S(2)}) collective-permute-start(f32[64,128]{1,0:T(8,128)S(1)} %get-tuple-element.78.low), channel_id=1, source_target_pairs={{0,48},{1,49},{2,50},{3,51},{4,52},{5,53},{6,54},{7,55},{8,56},{9,... | collective-permute-start | bytes 98312 | tf_op jit(solution)/shard_map/ppermute | solution.py:610
  68.0 1.6 %halo.5.acc = f32[4,192,256]{2,1,0:T(8,128)S(1)} custom-call(f32[16,128]{1,0:T(8,128)S(1)} %copy-done.2, f32[4,144,128]{2,1,0:T(8,128)S(1)} %collective-permute-done.16.inner, f32[4,144,128]{2,1,0:T(8,128)S(1)} %collective-permute-done.17.outer, f32[4,144,128]{2,1,0:T(8,128)S(1)} %collective-permute-done.18.xl, ...), custom_call_target="tpu_custom_call" | custom-call | flops 100000000 | bytes 4000000 | tf_op jit(solution)/shard_map/halo/pallas_call | solution.py:595
  69.8 3.2 %collective-permute-done.14.below = f32[64,128]{1,0:T(8,128)S(1)} collective-permute-done((f32[64,128]{1,0:T(8,128)S(1)}, f32[64,128]{1,0:T(8,128)S(1)}, u32[]{:S(2)}, u32[]{:S(2)}) %collective-permute-start.14) | collective-permute-done | bytes 32800 | tf_op jit(solution)/shard_map/ppermute | solution.py:610
  74.4 2.4 %update.4 = (f32[4,192,256]{2,1,0:T(8,128)S(1)}, f32[4,144,128]{2,1,0:T(8,128)S(1)}, f32[4,144,128]{2,1,0:T(8,128)S(1)}, f32[4,144,128]{2,1,0:T(8,128)S(1)}, f32[4,144,128]{2,1,0:T(8,128)S(1)}) custom-call(f32[16,128]{1,0:T(8,128)S(1)} %copy-done.2, s32[4,896]{1,0:T(4,128)S(1)} %get-tuple-element.62.index, f32[4,192,256]{2,1,0:T(8,128)S(1)} %get-tuple-element.86.acc, ...), custom_call_target="tpu_custom_call" | custom-call | flops 100000000 | bytes 4000000 | tf_op jit(solution)/shard_map/update/pallas_call | solution.py:595
  77.1 3.2 %collective-permute-start.28 = (f32[4,144,128]{2,1,0:T(8,128)S(1)}, f32[4,144,128]{2,1,0:T(8,128)S(1)}, u32[]{:S(2)}, u32[]{:S(2)}) collective-permute-start(f32[4,144,128]{2,1,0:T(8,128)S(1)} %get-tuple-element.94), channel_id=1, source_target_pairs={{0,48},{1,49},{2,50},{3,51},{4,52},{5,53},{6,54},{7,55},{8,56},{9,... | collective-permute-start | bytes 884744 | tf_op jit(solution)/shard_map/ppermute | solution.py:610
  80.4 1.9 %table.4 = f32[192,128]{1,0:T(8,128)S(1)} custom-call(s32[4,896]{1,0:T(4,128)S(1)} %get-tuple-element.62.index, f32[4,192,256]{2,1,0:T(8,128)S(1)} %get-tuple-element.88.field.before, f32[4,192,384]{2,1,0:T(8,128)S(1)} %own.1.head, f32[4,192,512]{2,1,0:T(8,128)S(1)} %get-tuple-element.76.tail), custom_call_target="tpu_custom_call" | custom-call | flops 100000000 | bytes 4000000 | tf_op jit(solution)/shard_map/table/pallas_call | solution.py:595
  82.3 1.3 collective-permute-done.21.came
  83.7 2.4 %collective-permute-start.22 = (f32[128,128]{1,0:T(8,128)S(1)}, f32[128,128]{1,0:T(8,128)S(1)}, u32[]{:S(2)}, u32[]{:S(2)}) collective-permute-start(f32[128,128]{1,0:T(8,128)S(1)} %pair.6.half.mine), channel_id=1, source_target_pairs={{0,7},{1,2},{2,1},{3,4},{4,3},{5,6},{6,5},{7,0},{8,15},{9,10},{10,... | collective-permute-start | bytes 196616 | tf_op jit(solution)/shard_map/ppermute | solution.py:610
  86.0 1.4 %local.6.acc = f32[4,192,256]{2,1,0:T(8,128)S(1)} custom-call(f32[16,128]{1,0:T(8,128)S(1)} %copy-done.2, f32[128,128]{1,0:T(8,128)S(1)} %pair.6.half.mine, f32[4,192,256]{2,1,0:T(8,128)S(1)} %get-tuple-element.88.field.before, f32[4,192,256]{2,1,0:T(8,128)S(1)} %get-tuple-element.77.field.before, f32[192,256]{1,0:T(8,128)S(1)} %get-tuple-element.66.pot, ...), custom_call_target="tpu_custom_call" | custom-call | flops 100000000 | bytes 4000000 | tf_op jit(solution)/shard_map/local/pallas_call | solution.py:595
  87.4 1.4 %collective-permute-done.22.came = f32[128,128]{1,0:T(8,128)S(1)} collective-permute-done((f32[128,128]{1,0:T(8,128)S(1)}, f32[128,128]{1,0:T(8,128)S(1)}, u32[]{:S(2)}, u32[]{:S(2)}) %collective-permute-start.22) | collective-permute-done | bytes 65568 | tf_op jit(solution)/shard_map/ppermute | solution.py:610
  89.0 2.0 %collective-permute-start.23 = (f32[64,128]{1,0:T(8,128)S(1)}, f32[64,128]{1,0:T(8,128)S(1)}, u32[]{:S(2)}, u32[]{:S(2)}) collective-permute-start(f32[64,128]{1,0:T(8,128)S(1)} %get-tuple-element.90.high), channel_id=1, source_target_pairs={{0,16},{1,17},{2,18},{3,19},{4,20},{5,21},{6,22},{7,23},{8,24},{9,... | collective-permute-start | bytes 98312 | tf_op jit(solution)/shard_map/ppermute | solution.py:610
  91.0 1.6 %halo.6.acc = f32[4,192,256]{2,1,0:T(8,128)S(1)} custom-call(f32[16,128]{1,0:T(8,128)S(1)} %copy-done.2, f32[4,144,128]{2,1,0:T(8,128)S(1)} %collective-permute-done.25.inner, f32[4,144,128]{2,1,0:T(8,128)S(1)} %collective-permute-done.26.outer, f32[4,144,128]{2,1,0:T(8,128)S(1)} %collective-permute-done.27.xl, ...), custom_call_target="tpu_custom_call" | custom-call | flops 100000000 | bytes 4000000 | tf_op jit(solution)/shard_map/halo/pallas_call | solution.py:595
  92.8 1.3 collective-permute-done.23.below
  95.7 2.4 %update.5 = (f32[4,192,256]{2,1,0:T(8,128)S(1)}, f32[4,144,128]{2,1,0:T(8,128)S(1)}, f32[4,144,128]{2,1,0:T(8,128)S(1)}, f32[4,144,128]{2,1,0:T(8,128)S(1)}, f32[4,144,128]{2,1,0:T(8,128)S(1)}) custom-call(f32[16,128]{1,0:T(8,128)S(1)} %copy-done.2, s32[4,896]{1,0:T(4,128)S(1)} %get-tuple-element.62.index, f32[4,192,256]{2,1,0:T(8,128)S(1)} %get-tuple-element.96.acc, ...), custom_call_target="tpu_custom_call" | custom-call | flops 100000000 | bytes 4000000 | tf_op jit(solution)/shard_map/update/pallas_call | solution.py:595
  98.4 1.4 %collective-permute-start.35 = (f32[4,144,128]{2,1,0:T(8,128)S(1)}, f32[4,144,128]{2,1,0:T(8,128)S(1)}, u32[]{:S(2)}, u32[]{:S(2)}) collective-permute-start(f32[4,144,128]{2,1,0:T(8,128)S(1)} %get-tuple-element.102), channel_id=1, source_target_pairs={{0,7},{1,2},{2,1},{3,4},{4,3},{5,6},{6,5},{7,0},{8,15},{9,10},{10,... | collective-permute-start | bytes 884744 | tf_op jit(solution)/shard_map/ppermute | solution.py:610
  100.3 2.7 %collective-permute-start.37 = (f32[4,144,128]{2,1,0:T(8,128)S(1)}, f32[4,144,128]{2,1,0:T(8,128)S(1)}, u32[]{:S(2)}, u32[]{:S(2)}) collective-permute-start(f32[4,144,128]{2,1,0:T(8,128)S(1)} %get-tuple-element.104), channel_id=1, source_target_pairs={{0,48},{1,49},{2,50},{3,51},{4,52},{5,53},{6,54},{7,55},{8,56},{9,... | collective-permute-start | bytes 884744 | tf_op jit(solution)/shard_map/ppermute | solution.py:610
  103.0 1.9 %table.5 = f32[192,128]{1,0:T(8,128)S(1)} custom-call(s32[4,896]{1,0:T(4,128)S(1)} %get-tuple-element.62.index, f32[4,192,256]{2,1,0:T(8,128)S(1)} %get-tuple-element.98.field, f32[4,192,384]{2,1,0:T(8,128)S(1)} %own.1.head, f32[4,192,512]{2,1,0:T(8,128)S(1)} %get-tuple-element.76.tail), custom_call_target="tpu_custom_call" | custom-call | flops 100000000 | bytes 4000000 | tf_op jit(solution)/shard_map/table/pallas_call | solution.py:595
  107.5 1.4 %local.7.acc = f32[4,192,256]{2,1,0:T(8,128)S(1)} custom-call(f32[16,128]{1,0:T(8,128)S(1)} %copy-done.2, f32[128,128]{1,0:T(8,128)S(1)} %pair.7.half.mine, f32[4,192,256]{2,1,0:T(8,128)S(1)} %get-tuple-element.98.field, f32[4,192,256]{2,1,0:T(8,128)S(1)} %get-tuple-element.88.field.before, f32[192,256]{1,0:T(8,128)S(1)} %get-tuple-element.66.pot, ...), custom_call_target="tpu_custom_call" | custom-call | flops 100000000 | bytes 4000000 | tf_op jit(solution)/shard_map/local/pallas_call | solution.py:595
  108.9 2.3 %collective-permute-done.31.came = f32[128,128]{1,0:T(8,128)S(1)} collective-permute-done((f32[128,128]{1,0:T(8,128)S(1)}, f32[128,128]{1,0:T(8,128)S(1)}, u32[]{:S(2)}, u32[]{:S(2)}) %collective-permute-start.31) | collective-permute-done | bytes 65568 | tf_op jit(solution)/shard_map/ppermute | solution.py:610
  111.3 2.0 %collective-permute-start.32 = (f32[64,128]{1,0:T(8,128)S(1)}, f32[64,128]{1,0:T(8,128)S(1)}, u32[]{:S(2)}, u32[]{:S(2)}) collective-permute-start(f32[64,128]{1,0:T(8,128)S(1)} %get-tuple-element.100.high), channel_id=1, source_target_pairs={{0,16},{1,17},{2,18},{3,19},{4,20},{5,21},{6,22},{7,23},{8,24},{9,... | collective-permute-start | bytes 98312 | tf_op jit(solution)/shard_map/ppermute | solution.py:610
  113.3 1.6 %halo.7.acc = f32[4,192,256]{2,1,0:T(8,128)S(1)} custom-call(f32[16,128]{1,0:T(8,128)S(1)} %copy-done.2, f32[4,144,128]{2,1,0:T(8,128)S(1)} %collective-permute-done.34.inner, f32[4,144,128]{2,1,0:T(8,128)S(1)} %collective-permute-done.35.outer, f32[4,144,128]{2,1,0:T(8,128)S(1)} %collective-permute-done.36.xl, ...), custom_call_target="tpu_custom_call" | custom-call | flops 100000000 | bytes 4000000 | tf_op jit(solution)/shard_map/halo/pallas_call | solution.py:595
  115.2 1.3 collective-permute-done.32.below
  117.8 2.8 %finish.1 = (f32[4,8,3072]{2,1,0:T(8,128)S(1)}, f32[4,192,256]{2,1,0:T(8,128)S(1)}) custom-call(f32[16,128]{1,0:T(8,128)S(1)} %copy-done.2, s32[4,896]{1,0:T(4,128)S(1)} %get-tuple-element.62.index, f32[4,192,256]{2,1,0:T(8,128)S(1)} %get-tuple-element.106.acc, f32[128,128]{1,0:T(8,128)S(1)} %get-tuple-element.107.mine, ...), custom_call_target="tpu_custom_call" | custom-call | flops 100000000 | bytes 4000000 | tf_op jit(solution)/shard_map/finish/pallas_call | solution.py:595
  120.6 2.5 %collective-permute-start.39 = (f32[4,8,3072]{2,1,0:T(8,128)S(1)}, f32[4,8,3072]{2,1,0:T(8,128)S(1)}, u32[]{:S(2)}, u32[]{:S(2)}) collective-permute-start(f32[4,8,3072]{2,1,0:T(8,128)S(1)} %get-tuple-element.108), channel_id=1, source_target_pairs={{0,8},{1,9},{2,10},{3,11},{4,12},{5,13},{6,14},{7,15},{8,0},{9,1},... | collective-permute-start | bytes 1179656 | tf_op jit(solution)/shard_map/ppermute | solution.py:610
  123.4 2.8 %collective-permute-start.40 = (f32[2,8,1536]{2,1,0:T(8,128)S(1)}, f32[2,8,1536]{2,1,0:T(8,128)S(1)}, u32[]{:S(2)}, u32[]{:S(2)}) collective-permute-start(f32[2,8,1536]{2,1,0:T(8,128)S(1)} %get-tuple-element.111.here), channel_id=1, source_target_pairs={{0,64},{64,0},{1,65},{65,1},{2,66},{66,2},{3,67},{67,3},{4,68},{68... | collective-permute-start | bytes 294920 | tf_op jit(solution)/shard_map/ppermute | solution.py:829
  126.2 3.4 %collective-permute-done.40.came = f32[2,8,1536]{2,1,0:T(8,128)S(1)} collective-permute-done((f32[2,8,1536]{2,1,0:T(8,128)S(1)}, f32[2,8,1536]{2,1,0:T(8,128)S(1)}, u32[]{:S(2)}, u32[]{:S(2)}) %collective-permute-start.40) | collective-permute-done | bytes 98336 | tf_op jit(solution)/shard_map/ppermute | solution.py:829
  131.6 3.7 %collective-permute-done.41.b = f32[8,1536]{1,0:T(8,128)S(1)} collective-permute-done((f32[8,1536]{1,0:T(8,128)S(1)}, f32[8,1536]{1,0:T(8,128)S(1)}, u32[]{:S(2)}, u32[]{:S(2)}) %collective-permute-start.41) | collective-permute-done | bytes 49184 | tf_op jit(solution)/shard_map/ppermute | solution.py:610
  (102 shorter events, 22.9 us)
Async XLA Ops:
  2.7 13.0 %copy-start = (f32[1,4,448,128]{3,2,1,0:T(8,128)S(1)}, f32[1,4,448,128]{3,2,1,0:T(8,128)}, u32[]{:S(2)}) copy-start(f32[1,4,448,128]{3,2,1,0:T(8,128)} %param.18) | copy-start | bytes 2752516
  3.0 18.9 %collective-permute-start.1 = (f32[5,8,3072]{2,1,0:T(8,128)S(1)}, f32[5,8,3072]{2,1,0:T(8,128)S(1)}, u32[]{:S(2)}, u32[]{:S(2)}) collective-permute-start(f32[5,8,3072]{2,1,0:T(8,128)S(1)} %pick.1), channel_id=1, source_target_pairs={{0,8},{1,9},{2,10},{3,11},{4,12},{5,13},{6,14},{7,15},{8,0},{9,1},... | collective-permute-start | bytes 1474568 | tf_op jit(solution)/shard_map/ppermute | solution.py:610
  15.3 6.5 %collective-permute-start = (f32[216,128]{1,0:T(8,128)}, f32[216,128]{1,0:T(8,128)S(1)}, u32[]{:S(2)}, u32[]{:S(2)}) collective-permute-start(f32[216,128]{1,0:T(8,128)} %get-tuple-element.61), channel_id=1, source_target_pairs={{0,8},{1,9},{2,10},{3,11},{4,12},{5,13},{6,14},{7,15},{8,0},{9,1},... | collective-permute-start | bytes 331784 | tf_op jit(solution)/shard_map/ppermute | solution.py:610
  15.7 7.6 %copy-start.2 = (f32[16,128]{1,0:T(8,128)S(1)}, f32[16,128]{1,0:T(8,128)}, u32[]{:S(2)}) copy-start(f32[16,128]{1,0:T(8,128)} %get-tuple-element.59.params) | copy-start | bytes 24580
  15.8 7.5 %copy-start.6 = (bf16[256,256]{1,0:T(8,128)(2,1)S(1)}, bf16[256,256]{1,0:T(8,128)(2,1)}, u32[]{:S(2)}) copy-start(bf16[256,256]{1,0:T(8,128)(2,1)} %constant.51.clone.edge.rest_0_) | copy-start | bytes 393220
  15.8 8.8 %copy-start.10 = (f32[192,128]{1,0:T(8,128)S(1)}, f32[192,128]{1,0:T(8,128)}, u32[]{:S(2)}) copy-start(f32[192,128]{1,0:T(8,128)} %get-tuple-element.63.table) | copy-start | bytes 294916
  21.9 13.2 %copy-start.3 = (bf16[2,256,256]{2,1,0:T(8,128)(2,1)S(1)}, bf16[2,256,256]{2,1,0:T(8,128)(2,1)}, u32[]{:S(2)}) copy-start(bf16[2,256,256]{2,1,0:T(8,128)(2,1)} %constant.48.clone.own_w) | copy-start | bytes 786436
  21.9 13.2 %copy-start.4 = (bf16[2,192,192]{2,1,0:T(8,128)(2,1)S(1)}, bf16[2,192,192]{2,1,0:T(8,128)(2,1)}, u32[]{:S(2)}) copy-start(bf16[2,192,192]{2,1,0:T(8,128)(2,1)} %constant.50.clone.ring_w) | copy-start | bytes 442372
  21.9 26.2 %collective-permute-start.2 = (f32[4,448,128]{2,1,0:T(8,128)S(1)}, f32[4,448,128]{2,1,0:T(8,128)S(1)}, u32[]{:S(2)}, u32[]{:S(2)}) collective-permute-start(f32[4,448,128]{2,1,0:T(8,128)S(1)} %gate.1), channel_id=1, source_target_pairs={{0,8},{1,9},{2,10},{3,11},{4,12},{5,13},{6,14},{7,15},{8,0},{9,1},... | collective-permute-start | bytes 2752520 | tf_op jit(solution)/shard_map/ppermute | solution.py:610
  24.6 1.4 %collective-permute-start.3 = (f32[192,128]{1,0:T(8,128)S(1)}, f32[192,128]{1,0:T(8,128)S(1)}, u32[]{:S(2)}, u32[]{:S(2)}) collective-permute-start(f32[192,128]{1,0:T(8,128)S(1)} %join_table.1.table.note), channel_id=1, source_target_pairs={{0,1},{1,0},{2,3},{3,2},{4,5},{5,4},{6,7},{7,6},{8,9},{9,8},{10,11... | collective-permute-start | bytes 294920 | tf_op jit(solution)/shard_map/ppermute | solution.py:610
  26.0 5.0 %collective-permute-start.4 = (f32[136,128]{1,0:T(8,128)S(1)}, f32[136,128]{1,0:T(8,128)S(1)}, u32[]{:S(2)}, u32[]{:S(2)}) collective-permute-start(f32[136,128]{1,0:T(8,128)S(1)} %pair.4.half.mine), channel_id=1, source_target_pairs={{0,7},{1,2},{2,1},{3,4},{4,3},{5,6},{6,5},{7,0},{8,15},{9,10},{10,... | collective-permute-start | bytes 208904 | tf_op jit(solution)/shard_map/ppermute | solution.py:610
  27.4 9.1 %collective-permute-start.7 = (f32[4,144,128]{2,1,0:T(8,128)S(1)}, f32[4,144,128]{2,1,0:T(8,128)S(1)}, u32[]{:S(2)}, u32[]{:S(2)}) collective-permute-start(f32[4,144,128]{2,1,0:T(8,128)S(1)} %get-tuple-element.69), channel_id=1, source_target_pairs={{0,1},{1,0},{2,3},{3,2},{4,5},{5,4},{6,7},{7,6},{8,9},{9,8},{10,11... | collective-permute-start | bytes 884744 | tf_op jit(solution)/shard_map/ppermute | solution.py:610
  27.7 9.9 %collective-permute-start.8 = (f32[4,144,128]{2,1,0:T(8,128)S(1)}, f32[4,144,128]{2,1,0:T(8,128)S(1)}, u32[]{:S(2)}, u32[]{:S(2)}) collective-permute-start(f32[4,144,128]{2,1,0:T(8,128)S(1)} %get-tuple-element.70), channel_id=1, source_target_pairs={{0,7},{1,2},{2,1},{3,4},{4,3},{5,6},{6,5},{7,0},{8,15},{9,10},{10,... | collective-permute-start | bytes 884744 | tf_op jit(solution)/shard_map/ppermute | solution.py:610
  28.7 10.9 %collective-permute-start.9 = (f32[4,144,128]{2,1,0:T(8,128)S(1)}, f32[4,144,128]{2,1,0:T(8,128)S(1)}, u32[]{:S(2)}, u32[]{:S(2)}) collective-permute-start(f32[4,144,128]{2,1,0:T(8,128)S(1)} %get-tuple-element.71), channel_id=1, source_target_pairs={{0,16},{1,17},{2,18},{3,19},{4,20},{5,21},{6,22},{7,23},{8,24},{9,... | collective-permute-start | bytes 884744 | tf_op jit(solution)/shard_map/ppermute | solution.py:610
  31.0 10.6 %collective-permute-start.10 = (f32[4,144,128]{2,1,0:T(8,128)S(1)}, f32[4,144,128]{2,1,0:T(8,128)S(1)}, u32[]{:S(2)}, u32[]{:S(2)}) collective-permute-start(f32[4,144,128]{2,1,0:T(8,128)S(1)} %get-tuple-element.72), channel_id=1, source_target_pairs={{0,48},{1,49},{2,50},{3,51},{4,52},{5,53},{6,54},{7,55},{8,56},{9,... | collective-permute-start | bytes 884744 | tf_op jit(solution)/shard_map/ppermute | solution.py:610
  36.5 6.8 %collective-permute-start.6 = (f32[72,128]{1,0:T(8,128)S(1)}, f32[72,128]{1,0:T(8,128)S(1)}, u32[]{:S(2)}, u32[]{:S(2)}) collective-permute-start(f32[72,128]{1,0:T(8,128)S(1)} %get-tuple-element.67.low), channel_id=1, source_target_pairs={{0,48},{1,49},{2,50},{3,51},{4,52},{5,53},{6,54},{7,55},{8,56},{9,... | collective-permute-start | bytes 110600 | tf_op jit(solution)/shard_map/ppermute | solution.py:610
  37.6 6.0 %collective-permute-start.5 = (f32[72,128]{1,0:T(8,128)S(1)}, f32[72,128]{1,0:T(8,128)S(1)}, u32[]{:S(2)}, u32[]{:S(2)}) collective-permute-start(f32[72,128]{1,0:T(8,128)S(1)} %get-tuple-element.68.high), channel_id=1, source_target_pairs={{0,16},{1,17},{2,18},{3,19},{4,20},{5,21},{6,22},{7,23},{8,24},{9,... | collective-permute-start | bytes 110600 | tf_op jit(solution)/shard_map/ppermute | solution.py:610
  43.5 5.6 %collective-permute-start.11 = (f32[128,128]{1,0:T(8,128)S(1)}, f32[128,128]{1,0:T(8,128)S(1)}, u32[]{:S(2)}, u32[]{:S(2)}) collective-permute-start(f32[128,128]{1,0:T(8,128)S(1)} %get-tuple-element.75.mine), channel_id=1, source_target_pairs={{0,1},{1,0},{2,3},{3,2},{4,5},{5,4},{6,7},{7,6},{8,9},{9,8},{10,11... | collective-permute-start | bytes 196616 | tf_op jit(solution)/shard_map/ppermute | solution.py:610
  51.5 16.4 %collective-permute-start.16 = (f32[4,144,128]{2,1,0:T(8,128)S(1)}, f32[4,144,128]{2,1,0:T(8,128)S(1)}, u32[]{:S(2)}, u32[]{:S(2)}) collective-permute-start(f32[4,144,128]{2,1,0:T(8,128)S(1)} %get-tuple-element.81), channel_id=1, source_target_pairs={{0,1},{1,0},{2,3},{3,2},{4,5},{5,4},{6,7},{7,6},{8,9},{9,8},{10,11... | collective-permute-start | bytes 884744 | tf_op jit(solution)/shard_map/ppermute | solution.py:610
  51.6 16.3 %collective-permute-start.17 = (f32[4,144,128]{2,1,0:T(8,128)S(1)}, f32[4,144,128]{2,1,0:T(8,128)S(1)}, u32[]{:S(2)}, u32[]{:S(2)}) collective-permute-start(f32[4,144,128]{2,1,0:T(8,128)S(1)} %get-tuple-element.82), channel_id=1, source_target_pairs={{0,7},{1,2},{2,1},{3,4},{4,3},{5,6},{6,5},{7,0},{8,15},{9,10},{10,... | collective-permute-start | bytes 884744 | tf_op jit(solution)/shard_map/ppermute | solution.py:610
  53.3 14.6 %collective-permute-start.18 = (f32[4,144,128]{2,1,0:T(8,128)S(1)}, f32[4,144,128]{2,1,0:T(8,128)S(1)}, u32[]{:S(2)}, u32[]{:S(2)}) collective-permute-start(f32[4,144,128]{2,1,0:T(8,128)S(1)} %get-tuple-element.83), channel_id=1, source_target_pairs={{0,16},{1,17},{2,18},{3,19},{4,20},{5,21},{6,22},{7,23},{8,24},{9,... | collective-permute-start | bytes 884744 | tf_op jit(solution)/shard_map/ppermute | solution.py:610
  55.3 12.7 %collective-permute-start.19 = (f32[4,144,128]{2,1,0:T(8,128)S(1)}, f32[4,144,128]{2,1,0:T(8,128)S(1)}, u32[]{:S(2)}, u32[]{:S(2)}) collective-permute-start(f32[4,144,128]{2,1,0:T(8,128)S(1)} %get-tuple-element.84), channel_id=1, source_target_pairs={{0,48},{1,49},{2,50},{3,51},{4,52},{5,53},{6,54},{7,55},{8,56},{9,... | collective-permute-start | bytes 884744 | tf_op jit(solution)/shard_map/ppermute | solution.py:610
  59.3 1.4 %collective-permute-start.12 = (f32[192,128]{1,0:T(8,128)S(1)}, f32[192,128]{1,0:T(8,128)S(1)}, u32[]{:S(2)}, u32[]{:S(2)}) collective-permute-start(f32[192,128]{1,0:T(8,128)S(1)} %table.3), channel_id=1, source_target_pairs={{0,1},{1,0},{2,3},{3,2},{4,5},{5,4},{6,7},{7,6},{8,9},{9,8},{10,11... | collective-permute-start | bytes 294920 | tf_op jit(solution)/shard_map/ppermute | solution.py:610
  60.7 5.2 %collective-permute-start.13 = (f32[128,128]{1,0:T(8,128)S(1)}, f32[128,128]{1,0:T(8,128)S(1)}, u32[]{:S(2)}, u32[]{:S(2)}) collective-permute-start(f32[128,128]{1,0:T(8,128)S(1)} %pair.5.half.mine), channel_id=1, source_target_pairs={{0,7},{1,2},{2,1},{3,4},{4,3},{5,6},{6,5},{7,0},{8,15},{9,10},{10,... | collective-permute-start | bytes 196616 | tf_op jit(solution)/shard_map/ppermute | solution.py:610
  65.8 4.0 %collective-permute-start.15 = (f32[64,128]{1,0:T(8,128)S(1)}, f32[64,128]{1,0:T(8,128)S(1)}, u32[]{:S(2)}, u32[]{:S(2)}) collective-permute-start(f32[64,128]{1,0:T(8,128)S(1)} %get-tuple-element.78.low), channel_id=1, source_target_pairs={{0,48},{1,49},{2,50},{3,51},{4,52},{5,53},{6,54},{7,55},{8,56},{9,... | collective-permute-start | bytes 98312 | tf_op jit(solution)/shard_map/ppermute | solution.py:610
  67.9 5.1 %collective-permute-start.14 = (f32[64,128]{1,0:T(8,128)S(1)}, f32[64,128]{1,0:T(8,128)S(1)}, u32[]{:S(2)}, u32[]{:S(2)}) collective-permute-start(f32[64,128]{1,0:T(8,128)S(1)} %get-tuple-element.79.high), channel_id=1, source_target_pairs={{0,16},{1,17},{2,18},{3,19},{4,20},{5,21},{6,22},{7,23},{8,24},{9,... | collective-permute-start | bytes 98312 | tf_op jit(solution)/shard_map/ppermute | solution.py:610
  73.1 1.3 collective-permute-start.20
  76.9 12.1 %collective-permute-start.25 = (f32[4,144,128]{2,1,0:T(8,128)S(1)}, f32[4,144,128]{2,1,0:T(8,128)S(1)}, u32[]{:S(2)}, u32[]{:S(2)}) collective-permute-start(f32[4,144,128]{2,1,0:T(8,128)S(1)} %get-tuple-element.91), channel_id=1, source_target_pairs={{0,1},{1,0},{2,3},{3,2},{4,5},{5,4},{6,7},{7,6},{8,9},{9,8},{10,11... | collective-permute-start | bytes 884744 | tf_op jit(solution)/shard_map/ppermute | solution.py:610
  77.1 13.9 %collective-permute-start.26 = (f32[4,144,128]{2,1,0:T(8,128)S(1)}, f32[4,144,128]{2,1,0:T(8,128)S(1)}, u32[]{:S(2)}, u32[]{:S(2)}) collective-permute-start(f32[4,144,128]{2,1,0:T(8,128)S(1)} %get-tuple-element.92), channel_id=1, source_target_pairs={{0,7},{1,2},{2,1},{3,4},{4,3},{5,6},{6,5},{7,0},{8,15},{9,10},{10,... | collective-permute-start | bytes 884744 | tf_op jit(solution)/shard_map/ppermute | solution.py:610
  77.1 13.9 %collective-permute-start.27 = (f32[4,144,128]{2,1,0:T(8,128)S(1)}, f32[4,144,128]{2,1,0:T(8,128)S(1)}, u32[]{:S(2)}, u32[]{:S(2)}) collective-permute-start(f32[4,144,128]{2,1,0:T(8,128)S(1)} %get-tuple-element.93), channel_id=1, source_target_pairs={{0,16},{1,17},{2,18},{3,19},{4,20},{5,21},{6,22},{7,23},{8,24},{9,... | collective-permute-start | bytes 884744 | tf_op jit(solution)/shard_map/ppermute | solution.py:610
  77.1 13.8 %collective-permute-start.28 = (f32[4,144,128]{2,1,0:T(8,128)S(1)}, f32[4,144,128]{2,1,0:T(8,128)S(1)}, u32[]{:S(2)}, u32[]{:S(2)}) collective-permute-start(f32[4,144,128]{2,1,0:T(8,128)S(1)} %get-tuple-element.94), channel_id=1, source_target_pairs={{0,48},{1,49},{2,50},{3,51},{4,52},{5,53},{6,54},{7,55},{8,56},{9,... | collective-permute-start | bytes 884744 | tf_op jit(solution)/shard_map/ppermute | solution.py:610
  82.3 1.4 %collective-permute-start.21 = (f32[192,128]{1,0:T(8,128)S(1)}, f32[192,128]{1,0:T(8,128)S(1)}, u32[]{:S(2)}, u32[]{:S(2)}) collective-permute-start(f32[192,128]{1,0:T(8,128)S(1)} %table.4), channel_id=1, source_target_pairs={{0,1},{1,0},{2,3},{3,2},{4,5},{5,4},{6,7},{7,6},{8,9},{9,8},{10,11... | collective-permute-start | bytes 294920 | tf_op jit(solution)/shard_map/ppermute | solution.py:610
  83.7 5.2 %collective-permute-start.22 = (f32[128,128]{1,0:T(8,128)S(1)}, f32[128,128]{1,0:T(8,128)S(1)}, u32[]{:S(2)}, u32[]{:S(2)}) collective-permute-start(f32[128,128]{1,0:T(8,128)S(1)} %pair.6.half.mine), channel_id=1, source_target_pairs={{0,7},{1,2},{2,1},{3,4},{4,3},{5,6},{6,5},{7,0},{8,15},{9,10},{10,... | collective-permute-start | bytes 196616 | tf_op jit(solution)/shard_map/ppermute | solution.py:610
  88.9 4.0 %collective-permute-start.24 = (f32[64,128]{1,0:T(8,128)S(1)}, f32[64,128]{1,0:T(8,128)S(1)}, u32[]{:S(2)}, u32[]{:S(2)}) collective-permute-start(f32[64,128]{1,0:T(8,128)S(1)} %get-tuple-element.89.low), channel_id=1, source_target_pairs={{0,48},{1,49},{2,50},{3,51},{4,52},{5,53},{6,54},{7,55},{8,56},{9,... | collective-permute-start | bytes 98312 | tf_op jit(solution)/shard_map/ppermute | solution.py:610
  89.0 5.2 %collective-permute-start.23 = (f32[64,128]{1,0:T(8,128)S(1)}, f32[64,128]{1,0:T(8,128)S(1)}, u32[]{:S(2)}, u32[]{:S(2)}) collective-permute-start(f32[64,128]{1,0:T(8,128)S(1)} %get-tuple-element.90.high), channel_id=1, source_target_pairs={{0,16},{1,17},{2,18},{3,19},{4,20},{5,21},{6,22},{7,23},{8,24},{9,... | collective-permute-start | bytes 98312 | tf_op jit(solution)/shard_map/ppermute | solution.py:610
  94.2 1.6 %collective-permute-start.29 = (f32[128,128]{1,0:T(8,128)S(1)}, f32[128,128]{1,0:T(8,128)S(1)}, u32[]{:S(2)}, u32[]{:S(2)}) collective-permute-start(f32[128,128]{1,0:T(8,128)S(1)} %get-tuple-element.97.mine), channel_id=1, source_target_pairs={{0,1},{1,0},{2,3},{3,2},{4,5},{5,4},{6,7},{7,6},{8,9},{9,8},{10,11... | collective-permute-start | bytes 196616 | tf_op jit(solution)/shard_map/ppermute | solution.py:610
  98.2 13.1 %collective-permute-start.34 = (f32[4,144,128]{2,1,0:T(8,128)S(1)}, f32[4,144,128]{2,1,0:T(8,128)S(1)}, u32[]{:S(2)}, u32[]{:S(2)}) collective-permute-start(f32[4,144,128]{2,1,0:T(8,128)S(1)} %get-tuple-element.101), channel_id=1, source_target_pairs={{0,1},{1,0},{2,3},{3,2},{4,5},{5,4},{6,7},{7,6},{8,9},{9,8},{10,11... | collective-permute-start | bytes 884744 | tf_op jit(solution)/shard_map/ppermute | solution.py:610
  98.4 14.9 %collective-permute-start.35 = (f32[4,144,128]{2,1,0:T(8,128)S(1)}, f32[4,144,128]{2,1,0:T(8,128)S(1)}, u32[]{:S(2)}, u32[]{:S(2)}) collective-permute-start(f32[4,144,128]{2,1,0:T(8,128)S(1)} %get-tuple-element.102), channel_id=1, source_target_pairs={{0,7},{1,2},{2,1},{3,4},{4,3},{5,6},{6,5},{7,0},{8,15},{9,10},{10,... | collective-permute-start | bytes 884744 | tf_op jit(solution)/shard_map/ppermute | solution.py:610
  99.8 13.5 %collective-permute-start.36 = (f32[4,144,128]{2,1,0:T(8,128)S(1)}, f32[4,144,128]{2,1,0:T(8,128)S(1)}, u32[]{:S(2)}, u32[]{:S(2)}) collective-permute-start(f32[4,144,128]{2,1,0:T(8,128)S(1)} %get-tuple-element.103), channel_id=1, source_target_pairs={{0,16},{1,17},{2,18},{3,19},{4,20},{5,21},{6,22},{7,23},{8,24},{9,... | collective-permute-start | bytes 884744 | tf_op jit(solution)/shard_map/ppermute | solution.py:610
  100.3 13.0 %collective-permute-start.37 = (f32[4,144,128]{2,1,0:T(8,128)S(1)}, f32[4,144,128]{2,1,0:T(8,128)S(1)}, u32[]{:S(2)}, u32[]{:S(2)}) collective-permute-start(f32[4,144,128]{2,1,0:T(8,128)S(1)} %get-tuple-element.104), channel_id=1, source_target_pairs={{0,48},{1,49},{2,50},{3,51},{4,52},{5,53},{6,54},{7,55},{8,56},{9,... | collective-permute-start | bytes 884744 | tf_op jit(solution)/shard_map/ppermute | solution.py:610
  104.9 1.4 %collective-permute-start.30 = (f32[192,128]{1,0:T(8,128)S(1)}, f32[192,128]{1,0:T(8,128)S(1)}, u32[]{:S(2)}, u32[]{:S(2)}) collective-permute-start(f32[192,128]{1,0:T(8,128)S(1)} %table.5), channel_id=1, source_target_pairs={{0,1},{1,0},{2,3},{3,2},{4,5},{5,4},{6,7},{7,6},{8,9},{9,8},{10,11... | collective-permute-start | bytes 294920 | tf_op jit(solution)/shard_map/ppermute | solution.py:610
  106.3 4.8 %collective-permute-start.31 = (f32[128,128]{1,0:T(8,128)S(1)}, f32[128,128]{1,0:T(8,128)S(1)}, u32[]{:S(2)}, u32[]{:S(2)}) collective-permute-start(f32[128,128]{1,0:T(8,128)S(1)} %pair.7.half.mine), channel_id=1, source_target_pairs={{0,7},{1,2},{2,1},{3,4},{4,3},{5,6},{6,5},{7,0},{8,15},{9,10},{10,... | collective-permute-start | bytes 196616 | tf_op jit(solution)/shard_map/ppermute | solution.py:610
  111.2 4.0 %collective-permute-start.33 = (f32[64,128]{1,0:T(8,128)S(1)}, f32[64,128]{1,0:T(8,128)S(1)}, u32[]{:S(2)}, u32[]{:S(2)}) collective-permute-start(f32[64,128]{1,0:T(8,128)S(1)} %get-tuple-element.99.low), channel_id=1, source_target_pairs={{0,48},{1,49},{2,50},{3,51},{4,52},{5,53},{6,54},{7,55},{8,56},{9,... | collective-permute-start | bytes 98312 | tf_op jit(solution)/shard_map/ppermute | solution.py:610
  111.3 5.2 %collective-permute-start.32 = (f32[64,128]{1,0:T(8,128)S(1)}, f32[64,128]{1,0:T(8,128)S(1)}, u32[]{:S(2)}, u32[]{:S(2)}) collective-permute-start(f32[64,128]{1,0:T(8,128)S(1)} %get-tuple-element.100.high), channel_id=1, source_target_pairs={{0,16},{1,17},{2,18},{3,19},{4,20},{5,21},{6,22},{7,23},{8,24},{9,... | collective-permute-start | bytes 98312 | tf_op jit(solution)/shard_map/ppermute | solution.py:610
  116.5 1.3 collective-permute-start.38
  120.6 14.7 %collective-permute-start.39 = (f32[4,8,3072]{2,1,0:T(8,128)S(1)}, f32[4,8,3072]{2,1,0:T(8,128)S(1)}, u32[]{:S(2)}, u32[]{:S(2)}) collective-permute-start(f32[4,8,3072]{2,1,0:T(8,128)S(1)} %get-tuple-element.108), channel_id=1, source_target_pairs={{0,8},{1,9},{2,10},{3,11},{4,12},{5,13},{6,14},{7,15},{8,0},{9,1},... | collective-permute-start | bytes 1179656 | tf_op jit(solution)/shard_map/ppermute | solution.py:610
  123.4 6.2 %collective-permute-start.40 = (f32[2,8,1536]{2,1,0:T(8,128)S(1)}, f32[2,8,1536]{2,1,0:T(8,128)S(1)}, u32[]{:S(2)}, u32[]{:S(2)}) collective-permute-start(f32[2,8,1536]{2,1,0:T(8,128)S(1)} %get-tuple-element.111.here), channel_id=1, source_target_pairs={{0,64},{64,0},{1,65},{65,1},{2,66},{66,2},{3,67},{67,3},{4,68},{68... | collective-permute-start | bytes 294920 | tf_op jit(solution)/shard_map/ppermute | solution.py:829
  129.7 5.7 %collective-permute-start.41 = (f32[8,1536]{1,0:T(8,128)S(1)}, f32[8,1536]{1,0:T(8,128)S(1)}, u32[]{:S(2)}, u32[]{:S(2)}) collective-permute-start(f32[8,1536]{1,0:T(8,128)S(1)} %get-tuple-element.112), channel_id=1, source_target_pairs={{0,8},{1,9},{2,10},{3,11},{4,12},{5,13},{6,14},{7,15},{8,0},{9,1},... | collective-permute-start | bytes 147464 | tf_op jit(solution)/shard_map/ppermute | solution.py:610
  (7 other events, 29.8 us)

commit v5 on v4

--- a/solution.py
+++ b/solution.py
@@ -190,31 +190,27 @@
 
 
 def begin_kernel(
-    place, upper_in, lower_in, weights_in, column_in, shift_in, owner_in, atom_in, raw_in, proj_in, energy_in,
+    weights_in, column_in, shift_in, owner_in, atom_in, raw_in, proj_in, energy_in,
     keep, params, ints, table, note,
-    column, shift, owner, atom, raw, proj, energy, turned, tables, both, placed, partial, near, far, upper_edge, lower_edge, weights, sems,
+    column, shift, owner, atom, raw, proj, energy, turned, tables, both, placed, partial, near, far, weights, sems,
 ):
     pairs = (
         (raw_in, raw), (column_in, column), (shift_in, shift), (owner_in, owner),
-        (atom_in, atom), (upper_in, upper_edge), (lower_in, lower_edge), (weights_in, weights),
+        (atom_in, atom), (weights_in, weights),
         (proj_in, proj), (energy_in, energy),
     )
     copies = [pltpu.make_async_copy(source, target, sems.at[k]) for k, (source, target) in enumerate(pairs)]
     for copy in copies:
         copy.start()
-    for copy in copies[:8]:
+    for copy in copies[:6]:
         copy.wait()
-    side, core = place[0], place[1]
+    here = lax.axis_index("dom")
+    side, core = here // 8 % 2, here % 2
     upper = jnp.full((1, LANES), side, jnp.int32) == 1
     params[0:1] = jnp.full((1, LANES), side, jnp.int32).astype(F32)
     params[1:2] = jnp.full((1, LANES), core, jnp.int32).astype(F32)
-    top = jnp.full((1, LANES), upper_edge[0], F32)
-    bottom = jnp.full((1, LANES), lower_edge[0], F32)
-    half_width = (top - bottom) / 2.0
-    params[2:3] = (top + bottom) / 2.0
-    params[3:4] = 1.0 / half_width
-    params[4:5] = 2.0 / half_width
-    params[5:6] = jnp.full((1, LANES), place[2], jnp.int32).astype(F32)
+    params[2:5] = jnp.zeros((3, LANES), F32)
+    params[5:6] = jnp.full((1, LANES), lax.axis_index("band"), jnp.int32).astype(F32)
     params[6:8] = jnp.zeros((2, LANES), F32)
     for o in range(ORB):
         params[8 + o : 9 + o] = jnp.full((1, LANES), weights[side * ORB + o], F32)
@@ -245,7 +241,7 @@
         keep[o] = turned[o]
 
     each(ORB, turn)
-    for copy in copies[8:]:
+    for copy in copies[6:]:
         copy.wait()
     first_tables(ints, turned, tables, both, proj, placed, partial)
     table[...] = tables[0]
@@ -257,7 +253,13 @@
         note[NOTE + 8 + 4 * k : NOTE + 12 + 4 * k] = numbers[:, k * LANES : (k + 1) * LANES]
 
 
-def start_kernel(params, keep, came, potential, edge, field, pot, xl, xh, inner, outer, near, far):
+def start_kernel(flags, ends, keep, came, potential, edge, params, field, pot, xl, xh, inner, outer, near, far):
+    params[...] = flags[...]
+    top, bottom = ends[0:1], ends[1:2]
+    half_width = (top - bottom) / 2.0
+    params[2:3] = (top + bottom) / 2.0
+    params[3:4] = 1.0 / half_width
+    params[4:5] = 2.0 / half_width
     upper = flag(params, 0)
     here = to_columns(lambda at: potential[0, :, at : at + NZ], near, far)
     there = to_columns(lambda at: came[ORB, :, at : at + NZ], near, far)
@@ -536,7 +538,7 @@
         for spot, pair in from_columns(jnp.where(upper, left, right), near, far):
             sent[o, :, spot : spot + 2 * NZ] = pair
 
-    each(ORB, emit)
+    each(ORB, emit, False)
 
 
 def join_kernel(params, came, b, mine, a, out, density):
@@ -583,7 +585,6 @@
 
 VM = pl.BlockSpec(memory_space=pltpu.VMEM)
 ANY = pl.BlockSpec(memory_space=pl.ANY)
-SM = pl.BlockSpec(memory_space=pltpu.SMEM)
 HB = pl.BlockSpec(memory_space=pltpu.HBM)
 
 
@@ -643,10 +644,8 @@
     ring_w = jnp.asarray(np.stack(two_parts(ring_m)))
     edge_w = jnp.asarray(edge_m.astype(np.float32).astype(jnp.bfloat16))
 
-    here = lax.axis_index("dom")
-    side = (here // 8 % 2).astype(jnp.int32)
-    core = (here % 2).astype(jnp.int32)
-    place = jnp.stack([side, core, lax.axis_index("band").astype(jnp.int32)])
+    row = lax.broadcasted_iota(jnp.int32, (8, LANES), 0)
+    ends = jnp.where(row == 0, upper_edge[0], lower_edge[0])
     packed = (ORB, PACKED, LANES)
     grid = (ORB, NZ, COLS)
     stage = [pltpu.VMEM((LANES, LANES), F32)] * 2
@@ -660,12 +659,13 @@
         [pltpu.SemaphoreType.DMA((2,))],
         flops=10**6,
         name="pick",
+        room=ROOM,
     )
     came = send(message, SWAP)
     line = pltpu.VMEM((1, PIECES), jnp.int32)
     keep, params, ints, own_table, note = call(
         begin_kernel,
-        [SM] + [HB] * 10,
+        [HB] * 8,
         [
             (ORB, NZ, LANES),
             (16, LANES),
@@ -674,7 +674,7 @@
             (NOTE + 24, LANES),
         ],
         (
-            place, upper_edge, lower_edge, occupation, piece_column, piece_shift, piece_owner, piece_atom,
+            occupation, piece_column, piece_shift, piece_owner, piece_atom,
             raw, projectors[0], energies[0],
         ),
         [
@@ -688,10 +688,8 @@
             pltpu.VMEM((NPJ, NZ, OWN), F32),
             pltpu.VMEM((ROWS, OWN), F32),
             *stage,
-            pltpu.SMEM((1,), F32),
-            pltpu.SMEM((1,), F32),
             pltpu.SMEM((2 * ORB,), F32),
-            pltpu.SemaphoreType.DMA((10,)),
+            pltpu.SemaphoreType.DMA((8,)),
         ],
         name="begin",
         room=ROOM,
@@ -699,11 +697,11 @@
     note_came = send(note, SWAP)
     proj = call(gate_kernel, [ANY] * 3, [(NPJ, PIECES, LANES)], (came, note_came, projectors[0]), flops=10**6, name="gate", passed=1)
     proj_came = send(proj[0], SWAP)
-    field, pot, xl, xh, inner, outer = call(
+    params, field, pot, xl, xh, inner, outer = call(
         start_kernel,
-        [VM] * 5,
-        [grid, (NZ, COLS)] + [packed] * 4,
-        (params, keep, came, potential, edge_w),
+        [VM] * 6,
+        [(16, LANES), grid, (NZ, COLS)] + [packed] * 4,
+        (params, ends, keep, came, potential, edge_w),
         stage,
         name="start",
     )

time: 137 us -> 136 us (level)
  starting transfers between devices: 48.3 us -> 50.5 us
  local copies, waits for them, and re-layouts: 2.13 us -> 0.18 us
    ppermute x41, starting transfers between devices: 45.5 us -> 47.7 us  [send(): return lax.ppermute(value, 'dom', pairs)]
    unnamed x27 -> x23, local copies, waits for them, and re-layouts: 2.13 us -> 0.11 us
  transfers between devices with their start and end apart: 42 -> 42, of which waited for: 25 -> 25; matrix products, arithmetic and copies ran while one was open for 1% -> 0% of each run, Pallas kernels for 21% -> 21%
where the time goes in v5:
time: 136 us
  starting transfers between devices  50.5 us (37%)
  waiting for transfers between devices  41.5 us (31%)
  Pallas kernels  40.9 us (30%)
  between operations  2.42 us (2%)
    ppermute x41, starting transfers between devices, send(): return lax.ppermute(value, 'dom', pairs)  47.7 us
    pallas_call x38, Pallas kernels, call(): pl.pallas_call(kernel, out_shape=[jax.ShapeDtypeStruct(*out) for out in o...  40.9 us
    ppermute x41, waiting for transfers between devices, send(): return lax.ppermute(value, 'dom', pairs)  38.2 us
    ppermute x1, waiting for transfers between devices, body(): across_came = lax.ppermute(across, 'band', [(0, 1), (1, 0)])  3.39 us
    ppermute x1, starting transfers between devices, body(): across_came = lax.ppermute(across, 'band', [(0, 1), (1, 0)])  2.81 us
  transfers between devices with their start and end apart: 42, of which 25 were waited for; matrix products, arithmetic and copies ran while one was open for 0% of the time, Pallas kernels for 21%

profile of v5, /device:TPU:0, one launch (start us, length us, event | category | flops | bytes accessed | tf_op | source)
XLA Modules:
  0.0 135.6 jit_solution(14873719062534864806)
XLA Ops:
  0.6 1.9 %pick.1 = f32[5,8,3072]{2,1,0:T(8,128)} custom-call(f32[8,8,3072]{2,1,0:T(8,128)} %bitcast.17, f32[1,8,3072]{2,1,0:T(8,128)} %potential.3), custom_call_target="tpu_custom_call" | custom-call | flops 1000000 | bytes 4000000 | tf_op jit(solution)/shard_map/pick/pallas_call | solution.py:596
  2.5 3.4 %collective-permute-start = (f32[5,8,3072]{2,1,0:T(8,128)}, f32[5,8,3072]{2,1,0:T(8,128)S(1)}, u32[]{:S(2)}, u32[]{:S(2)}) collective-permute-start(f32[5,8,3072]{2,1,0:T(8,128)} %pick.1), channel_id=1, source_target_pairs={{0,8},{1,9},{2,10},{3,11},{4,12},{5,13},{6,14},{7,15},{8,0},{9,1},... | collective-permute-start | bytes 1474568 | tf_op jit(solution)/shard_map/ppermute | solution.py:611
  5.9 6.3 %begin.1 = (f32[4,192,128]{2,1,0:T(8,128)}, f32[16,128]{1,0:T(8,128)}, s32[8,512]{1,0:T(8,128)}, f32[192,128]{1,0:T(8,128)}, f32[216,128]{1,0:T(8,128)}) custom-call(f32[8]{0:T(128)} %weights_in.1, s32[1,448]{1,0:T(1,128)} %column_in.1, s32[1,448]{1,0:T(1,128)} %shift_in.1, s32[1,448]{1,0:T(1,128)} %owner_in.1, s32[1,448]{1,0:T(1,128)} %atom_in.1, ...), custom_call_target="tpu_custom_call" | custom-call | flops 100000000 | bytes 4000000 | tf_op jit(solution)/shard_map/begin/pallas_call | solution.py:596
  12.7 7.0 %collective-permute-done.1.note_came = f32[216,128]{1,0:T(8,128)S(1)} collective-permute-done((f32[216,128]{1,0:T(8,128)}, f32[216,128]{1,0:T(8,128)S(1)}, u32[]{:S(2)}, u32[]{:S(2)}) %collective-permute-start.1) | collective-permute-done | bytes 110624 | tf_op jit(solution)/shard_map/ppermute | solution.py:611
  19.7 3.3 %collective-permute-start.2 = (f32[4,448,128]{2,1,0:T(8,128)S(1)}, f32[4,448,128]{2,1,0:T(8,128)S(1)}, u32[]{:S(2)}, u32[]{:S(2)}) collective-permute-start(f32[4,448,128]{2,1,0:T(8,128)S(1)} %gate.1), channel_id=1, source_target_pairs={{0,8},{1,9},{2,10},{3,11},{4,12},{5,13},{6,14},{7,15},{8,0},{9,1},... | collective-permute-start | bytes 2752520 | tf_op jit(solution)/shard_map/ppermute | solution.py:611
  25.8 1.3 collective-permute-done.3.came
  27.1 1.4 %collective-permute-start.4 = (f32[136,128]{1,0:T(8,128)S(1)}, f32[136,128]{1,0:T(8,128)S(1)}, u32[]{:S(2)}, u32[]{:S(2)}) collective-permute-start(f32[136,128]{1,0:T(8,128)S(1)} %pair.4.half.mine), channel_id=1, source_target_pairs={{0,7},{1,2},{2,1},{3,4},{4,3},{5,6},{6,5},{7,0},{8,15},{9,10},{10,... | collective-permute-start | bytes 208904 | tf_op jit(solution)/shard_map/ppermute | solution.py:611
  29.9 1.9 %collective-permute-start.9 = (f32[4,144,128]{2,1,0:T(8,128)S(1)}, f32[4,144,128]{2,1,0:T(8,128)S(1)}, u32[]{:S(2)}, u32[]{:S(2)}) collective-permute-start(f32[4,144,128]{2,1,0:T(8,128)S(1)} %get-tuple-element.73), channel_id=1, source_target_pairs={{0,16},{1,17},{2,18},{3,19},{4,20},{5,21},{6,22},{7,23},{8,24},{9,... | collective-permute-start | bytes 884744 | tf_op jit(solution)/shard_map/ppermute | solution.py:611
  32.2 4.0 %collective-permute-start.10 = (f32[4,144,128]{2,1,0:T(8,128)S(1)}, f32[4,144,128]{2,1,0:T(8,128)S(1)}, u32[]{:S(2)}, u32[]{:S(2)}) collective-permute-start(f32[4,144,128]{2,1,0:T(8,128)S(1)} %get-tuple-element.74), channel_id=1, source_target_pairs={{0,48},{1,49},{2,50},{3,51},{4,52},{5,53},{6,54},{7,55},{8,56},{9,... | collective-permute-start | bytes 884744 | tf_op jit(solution)/shard_map/ppermute | solution.py:611
  36.2 1.4 %local.4.acc = f32[4,192,256]{2,1,0:T(8,128)S(1)} custom-call(f32[16,128]{1,0:T(8,128)S(1)} %get-tuple-element.62.params, f32[136,128]{1,0:T(8,128)S(1)} %pair.4.half.mine, f32[4,192,256]{2,1,0:T(8,128)S(1)} %get-tuple-element.67.field.before, f32[4,192,256]{2,1,0:T(8,128)S(1)} %get-tuple-element.67.field.before, f32[192,256]{1,0:T(8,128)S(1)} %get-tuple-element.68.pot, ...), custom_call_target="tpu_custom_call" | custom-call | flops 100000000 | bytes 4000000 | tf_op jit(solution)/shard_map/local/pallas_call | solution.py:596
  38.7 1.9 %collective-permute-start.5 = (f32[72,128]{1,0:T(8,128)S(1)}, f32[72,128]{1,0:T(8,128)S(1)}, u32[]{:S(2)}, u32[]{:S(2)}) collective-permute-start(f32[72,128]{1,0:T(8,128)S(1)} %get-tuple-element.70.high), channel_id=1, source_target_pairs={{0,16},{1,17},{2,18},{3,19},{4,20},{5,21},{6,22},{7,23},{8,24},{9,... | collective-permute-start | bytes 110600 | tf_op jit(solution)/shard_map/ppermute | solution.py:611
  40.8 2.0 %collective-permute-done.10.xh = f32[4,144,128]{2,1,0:T(8,128)S(1)} collective-permute-done((f32[4,144,128]{2,1,0:T(8,128)S(1)}, f32[4,144,128]{2,1,0:T(8,128)S(1)}, u32[]{:S(2)}, u32[]{:S(2)}) %collective-permute-start.10) | collective-permute-done | bytes 294944 | tf_op jit(solution)/shard_map/ppermute | solution.py:611
  42.8 1.6 %halo.4.acc = f32[4,192,256]{2,1,0:T(8,128)S(1)} custom-call(f32[16,128]{1,0:T(8,128)S(1)} %get-tuple-element.62.params, f32[4,144,128]{2,1,0:T(8,128)S(1)} %collective-permute-done.7.inner, f32[4,144,128]{2,1,0:T(8,128)S(1)} %collective-permute-done.8.outer, f32[4,144,128]{2,1,0:T(8,128)S(1)} %collective-permute-done.9.xl, ...), custom_call_target="tpu_custom_call" | custom-call | flops 100000000 | bytes 4000000 | tf_op jit(solution)/shard_map/halo/pallas_call | solution.py:596
  47.5 2.4 %update.3 = (f32[4,192,256]{2,1,0:T(8,128)S(1)}, f32[4,144,128]{2,1,0:T(8,128)S(1)}, f32[4,144,128]{2,1,0:T(8,128)S(1)}, f32[4,144,128]{2,1,0:T(8,128)S(1)}, f32[4,144,128]{2,1,0:T(8,128)S(1)}) custom-call(f32[16,128]{1,0:T(8,128)S(1)} %get-tuple-element.62.params, s32[4,896]{1,0:T(4,128)S(1)} %get-tuple-element.65.index, ...), custom_call_target="tpu_custom_call" | custom-call | flops 100000000 | bytes 4000000 | tf_op jit(solution)/shard_map/update/pallas_call | solution.py:596
  50.0 2.6 %collective-permute-start.17 = (f32[4,144,128]{2,1,0:T(8,128)S(1)}, f32[4,144,128]{2,1,0:T(8,128)S(1)}, u32[]{:S(2)}, u32[]{:S(2)}) collective-permute-start(f32[4,144,128]{2,1,0:T(8,128)S(1)} %get-tuple-element.84), channel_id=1, source_target_pairs={{0,7},{1,2},{2,1},{3,4},{4,3},{5,6},{6,5},{7,0},{8,15},{9,10},{10,... | collective-permute-start | bytes 884744 | tf_op jit(solution)/shard_map/ppermute | solution.py:611
  52.6 1.9 %collective-permute-start.18 = (f32[4,144,128]{2,1,0:T(8,128)S(1)}, f32[4,144,128]{2,1,0:T(8,128)S(1)}, u32[]{:S(2)}, u32[]{:S(2)}) collective-permute-start(f32[4,144,128]{2,1,0:T(8,128)S(1)} %get-tuple-element.85), channel_id=1, source_target_pairs={{0,16},{1,17},{2,18},{3,19},{4,20},{5,21},{6,22},{7,23},{8,24},{9,... | collective-permute-start | bytes 884744 | tf_op jit(solution)/shard_map/ppermute | solution.py:611
  54.6 2.1 %collective-permute-start.19 = (f32[4,144,128]{2,1,0:T(8,128)S(1)}, f32[4,144,128]{2,1,0:T(8,128)S(1)}, u32[]{:S(2)}, u32[]{:S(2)}) collective-permute-start(f32[4,144,128]{2,1,0:T(8,128)S(1)} %get-tuple-element.86), channel_id=1, source_target_pairs={{0,48},{1,49},{2,50},{3,51},{4,52},{5,53},{6,54},{7,55},{8,56},{9,... | collective-permute-start | bytes 884744 | tf_op jit(solution)/shard_map/ppermute | solution.py:611
  56.7 1.9 %table.3 = f32[192,128]{1,0:T(8,128)S(1)} custom-call(s32[4,896]{1,0:T(4,128)S(1)} %get-tuple-element.65.index, f32[4,192,256]{2,1,0:T(8,128)S(1)} %get-tuple-element.79.field.before, f32[4,192,384]{2,1,0:T(8,128)S(1)} %own.1.head, f32[4,192,512]{2,1,0:T(8,128)S(1)} %get-tuple-element.78.tail), custom_call_target="tpu_custom_call" | custom-call | flops 100000000 | bytes 4000000 | tf_op jit(solution)/shard_map/table/pallas_call | solution.py:596
  58.7 1.3 collective-permute-done.12.came
  60.4 1.4 %local.5.acc = f32[4,192,256]{2,1,0:T(8,128)S(1)} custom-call(f32[16,128]{1,0:T(8,128)S(1)} %get-tuple-element.62.params, f32[128,128]{1,0:T(8,128)S(1)} %pair.5.half.mine, f32[4,192,256]{2,1,0:T(8,128)S(1)} %get-tuple-element.79.field.before, f32[4,192,256]{2,1,0:T(8,128)S(1)} %get-tuple-element.67.field.before, f32[192,256]{1,0:T(8,128)S(1)} %get-tuple-element.68.pot, ...), custom_call_target="tpu_custom_call" | custom-call | flops 100000000 | bytes 4000000 | tf_op jit(solution)/shard_map/local/pallas_call | solution.py:596
  61.8 2.9 %collective-permute-done.13.came = f32[128,128]{1,0:T(8,128)S(1)} collective-permute-done((f32[128,128]{1,0:T(8,128)S(1)}, f32[128,128]{1,0:T(8,128)S(1)}, u32[]{:S(2)}, u32[]{:S(2)}) %collective-permute-start.13) | collective-permute-done | bytes 65568 | tf_op jit(solution)/shard_map/ppermute | solution.py:611
  64.7 2.1 %collective-permute-start.15 = (f32[64,128]{1,0:T(8,128)S(1)}, f32[64,128]{1,0:T(8,128)S(1)}, u32[]{:S(2)}, u32[]{:S(2)}) collective-permute-start(f32[64,128]{1,0:T(8,128)S(1)} %get-tuple-element.80.low), channel_id=1, source_target_pairs={{0,48},{1,49},{2,50},{3,51},{4,52},{5,53},{6,54},{7,55},{8,56},{9,... | collective-permute-start | bytes 98312 | tf_op jit(solution)/shard_map/ppermute | solution.py:611
  66.8 1.6 %halo.5.acc = f32[4,192,256]{2,1,0:T(8,128)S(1)} custom-call(f32[16,128]{1,0:T(8,128)S(1)} %get-tuple-element.62.params, f32[4,144,128]{2,1,0:T(8,128)S(1)} %collective-permute-done.16.inner, f32[4,144,128]{2,1,0:T(8,128)S(1)} %collective-permute-done.17.outer, f32[4,144,128]{2,1,0:T(8,128)S(1)} %collective-permute-done.18.xl, ...), custom_call_target="tpu_custom_call" | custom-call | flops 100000000 | bytes 4000000 | tf_op jit(solution)/shard_map/halo/pallas_call | solution.py:596
  68.7 3.2 %collective-permute-done.14.below = f32[64,128]{1,0:T(8,128)S(1)} collective-permute-done((f32[64,128]{1,0:T(8,128)S(1)}, f32[64,128]{1,0:T(8,128)S(1)}, u32[]{:S(2)}, u32[]{:S(2)}) %collective-permute-start.14) | collective-permute-done | bytes 32800 | tf_op jit(solution)/shard_map/ppermute | solution.py:611
  73.3 2.4 %update.4 = (f32[4,192,256]{2,1,0:T(8,128)S(1)}, f32[4,144,128]{2,1,0:T(8,128)S(1)}, f32[4,144,128]{2,1,0:T(8,128)S(1)}, f32[4,144,128]{2,1,0:T(8,128)S(1)}, f32[4,144,128]{2,1,0:T(8,128)S(1)}) custom-call(f32[16,128]{1,0:T(8,128)S(1)} %get-tuple-element.62.params, s32[4,896]{1,0:T(4,128)S(1)} %get-tuple-element.65.index, ...), custom_call_target="tpu_custom_call" | custom-call | flops 100000000 | bytes 4000000 | tf_op jit(solution)/shard_map/update/pallas_call | solution.py:596
  76.2 3.2 %collective-permute-start.28 = (f32[4,144,128]{2,1,0:T(8,128)S(1)}, f32[4,144,128]{2,1,0:T(8,128)S(1)}, u32[]{:S(2)}, u32[]{:S(2)}) collective-permute-start(f32[4,144,128]{2,1,0:T(8,128)S(1)} %get-tuple-element.96), channel_id=1, source_target_pairs={{0,48},{1,49},{2,50},{3,51},{4,52},{5,53},{6,54},{7,55},{8,56},{9,... | collective-permute-start | bytes 884744 | tf_op jit(solution)/shard_map/ppermute | solution.py:611
  79.5 1.9 %table.4 = f32[192,128]{1,0:T(8,128)S(1)} custom-call(s32[4,896]{1,0:T(4,128)S(1)} %get-tuple-element.65.index, f32[4,192,256]{2,1,0:T(8,128)S(1)} %get-tuple-element.90.field.before, f32[4,192,384]{2,1,0:T(8,128)S(1)} %own.1.head, f32[4,192,512]{2,1,0:T(8,128)S(1)} %get-tuple-element.78.tail), custom_call_target="tpu_custom_call" | custom-call | flops 100000000 | bytes 4000000 | tf_op jit(solution)/shard_map/table/pallas_call | solution.py:596
  81.5 1.3 collective-permute-done.21.came
  82.8 1.9 %collective-permute-start.22 = (f32[128,128]{1,0:T(8,128)S(1)}, f32[128,128]{1,0:T(8,128)S(1)}, u32[]{:S(2)}, u32[]{:S(2)}) collective-permute-start(f32[128,128]{1,0:T(8,128)S(1)} %pair.6.half.mine), channel_id=1, source_target_pairs={{0,7},{1,2},{2,1},{3,4},{4,3},{5,6},{6,5},{7,0},{8,15},{9,10},{10,... | collective-permute-start | bytes 196616 | tf_op jit(solution)/shard_map/ppermute | solution.py:611
  84.7 1.4 %local.6.acc = f32[4,192,256]{2,1,0:T(8,128)S(1)} custom-call(f32[16,128]{1,0:T(8,128)S(1)} %get-tuple-element.62.params, f32[128,128]{1,0:T(8,128)S(1)} %pair.6.half.mine, f32[4,192,256]{2,1,0:T(8,128)S(1)} %get-tuple-element.90.field.before, f32[4,192,256]{2,1,0:T(8,128)S(1)} %get-tuple-element.79.field.before, f32[192,256]{1,0:T(8,128)S(1)} %get-tuple-element.68.pot, ...), custom_call_target="tpu_custom_call" | custom-call | flops 100000000 | bytes 4000000 | tf_op jit(solution)/shard_map/local/pallas_call | solution.py:596
  86.1 1.6 %collective-permute-done.22.came = f32[128,128]{1,0:T(8,128)S(1)} collective-permute-done((f32[128,128]{1,0:T(8,128)S(1)}, f32[128,128]{1,0:T(8,128)S(1)}, u32[]{:S(2)}, u32[]{:S(2)}) %collective-permute-start.22) | collective-permute-done | bytes 65568 | tf_op jit(solution)/shard_map/ppermute | solution.py:611
  88.0 1.8 %collective-permute-start.23 = (f32[64,128]{1,0:T(8,128)S(1)}, f32[64,128]{1,0:T(8,128)S(1)}, u32[]{:S(2)}, u32[]{:S(2)}) collective-permute-start(f32[64,128]{1,0:T(8,128)S(1)} %get-tuple-element.92.high), channel_id=1, source_target_pairs={{0,16},{1,17},{2,18},{3,19},{4,20},{5,21},{6,22},{7,23},{8,24},{9,... | collective-permute-start | bytes 98312 | tf_op jit(solution)/shard_map/ppermute | solution.py:611
  89.8 1.6 %halo.6.acc = f32[4,192,256]{2,1,0:T(8,128)S(1)} custom-call(f32[16,128]{1,0:T(8,128)S(1)} %get-tuple-element.62.params, f32[4,144,128]{2,1,0:T(8,128)S(1)} %collective-permute-done.25.inner, f32[4,144,128]{2,1,0:T(8,128)S(1)} %collective-permute-done.26.outer, f32[4,144,128]{2,1,0:T(8,128)S(1)} %collective-permute-done.27.xl, ...), custom_call_target="tpu_custom_call" | custom-call | flops 100000000 | bytes 4000000 | tf_op jit(solution)/shard_map/halo/pallas_call | solution.py:596
  91.7 1.4 %collective-permute-done.23.below = f32[64,128]{1,0:T(8,128)S(1)} collective-permute-done((f32[64,128]{1,0:T(8,128)S(1)}, f32[64,128]{1,0:T(8,128)S(1)}, u32[]{:S(2)}, u32[]{:S(2)}) %collective-permute-start.23) | collective-permute-done | bytes 32800 | tf_op jit(solution)/shard_map/ppermute | solution.py:611
  94.7 2.4 %update.5 = (f32[4,192,256]{2,1,0:T(8,128)S(1)}, f32[4,144,128]{2,1,0:T(8,128)S(1)}, f32[4,144,128]{2,1,0:T(8,128)S(1)}, f32[4,144,128]{2,1,0:T(8,128)S(1)}, f32[4,144,128]{2,1,0:T(8,128)S(1)}) custom-call(f32[16,128]{1,0:T(8,128)S(1)} %get-tuple-element.62.params, s32[4,896]{1,0:T(4,128)S(1)} %get-tuple-element.65.index, ...), custom_call_target="tpu_custom_call" | custom-call | flops 100000000 | bytes 4000000 | tf_op jit(solution)/shard_map/update/pallas_call | solution.py:596
  99.0 2.4 %collective-permute-start.37 = (f32[4,144,128]{2,1,0:T(8,128)S(1)}, f32[4,144,128]{2,1,0:T(8,128)S(1)}, u32[]{:S(2)}, u32[]{:S(2)}) collective-permute-start(f32[4,144,128]{2,1,0:T(8,128)S(1)} %get-tuple-element.106), channel_id=1, source_target_pairs={{0,48},{1,49},{2,50},{3,51},{4,52},{5,53},{6,54},{7,55},{8,56},{9,... | collective-permute-start | bytes 884744 | tf_op jit(solution)/shard_map/ppermute | solution.py:611
  101.3 1.9 %table.5 = f32[192,128]{1,0:T(8,128)S(1)} custom-call(s32[4,896]{1,0:T(4,128)S(1)} %get-tuple-element.65.index, f32[4,192,256]{2,1,0:T(8,128)S(1)} %get-tuple-element.100.field, f32[4,192,384]{2,1,0:T(8,128)S(1)} %own.1.head, f32[4,192,512]{2,1,0:T(8,128)S(1)} %get-tuple-element.78.tail), custom_call_target="tpu_custom_call" | custom-call | flops 100000000 | bytes 4000000 | tf_op jit(solution)/shard_map/table/pallas_call | solution.py:596
  104.7 1.4 %collective-permute-start.31 = (f32[128,128]{1,0:T(8,128)S(1)}, f32[128,128]{1,0:T(8,128)S(1)}, u32[]{:S(2)}, u32[]{:S(2)}) collective-permute-start(f32[128,128]{1,0:T(8,128)S(1)} %pair.7.half.mine), channel_id=1, source_target_pairs={{0,7},{1,2},{2,1},{3,4},{4,3},{5,6},{6,5},{7,0},{8,15},{9,10},{10,... | collective-permute-start | bytes 196616 | tf_op jit(solution)/shard_map/ppermute | solution.py:611
  106.1 1.4 %local.7.acc = f32[4,192,256]{2,1,0:T(8,128)S(1)} custom-call(f32[16,128]{1,0:T(8,128)S(1)} %get-tuple-element.62.params, f32[128,128]{1,0:T(8,128)S(1)} %pair.7.half.mine, f32[4,192,256]{2,1,0:T(8,128)S(1)} %get-tuple-element.100.field, f32[4,192,256]{2,1,0:T(8,128)S(1)} %get-tuple-element.90.field.before, f32[192,256]{1,0:T(8,128)S(1)} %get-tuple-element.68.pot, ...), custom_call_target="tpu_custom_call" | custom-call | flops 100000000 | bytes 4000000 | tf_op jit(solution)/shard_map/local/pallas_call | solution.py:596
  107.5 2.2 %collective-permute-done.31.came = f32[128,128]{1,0:T(8,128)S(1)} collective-permute-done((f32[128,128]{1,0:T(8,128)S(1)}, f32[128,128]{1,0:T(8,128)S(1)}, u32[]{:S(2)}, u32[]{:S(2)}) %collective-permute-start.31) | collective-permute-done | bytes 65568 | tf_op jit(solution)/shard_map/ppermute | solution.py:611
  109.8 2.0 %collective-permute-start.32 = (f32[64,128]{1,0:T(8,128)S(1)}, f32[64,128]{1,0:T(8,128)S(1)}, u32[]{:S(2)}, u32[]{:S(2)}) collective-permute-start(f32[64,128]{1,0:T(8,128)S(1)} %get-tuple-element.102.high), channel_id=1, source_target_pairs={{0,16},{1,17},{2,18},{3,19},{4,20},{5,21},{6,22},{7,23},{8,24},{9,... | collective-permute-start | bytes 98312 | tf_op jit(solution)/shard_map/ppermute | solution.py:611
  111.8 1.6 %halo.7.acc = f32[4,192,256]{2,1,0:T(8,128)S(1)} custom-call(f32[16,128]{1,0:T(8,128)S(1)} %get-tuple-element.62.params, f32[4,144,128]{2,1,0:T(8,128)S(1)} %collective-permute-done.34.inner, f32[4,144,128]{2,1,0:T(8,128)S(1)} %collective-permute-done.35.outer, f32[4,144,128]{2,1,0:T(8,128)S(1)} %collective-permute-done.36.xl, ...), custom_call_target="tpu_custom_call" | custom-call | flops 100000000 | bytes 4000000 | tf_op jit(solution)/shard_map/halo/pallas_call | solution.py:596
  113.7 1.3 collective-permute-done.32.below
  116.4 2.2 %finish.1 = (f32[4,8,3072]{2,1,0:T(8,128)S(1)}, f32[4,192,256]{2,1,0:T(8,128)S(1)}) custom-call(f32[16,128]{1,0:T(8,128)S(1)} %get-tuple-element.62.params, s32[4,896]{1,0:T(4,128)S(1)} %get-tuple-element.65.index, f32[4,192,256]{2,1,0:T(8,128)S(1)} %get-tuple-element.108.acc, f32[128,128]{1,0:T(8,128)S(1)} %get-tuple-element.109.mine, ...), custom_call_target="tpu_custom_call" | custom-call | flops 100000000 | bytes 4000000 | tf_op jit(solution)/shard_map/finish/pallas_call | solution.py:596
  118.5 3.7 %collective-permute-start.39 = (f32[4,8,3072]{2,1,0:T(8,128)S(1)}, f32[4,8,3072]{2,1,0:T(8,128)S(1)}, u32[]{:S(2)}, u32[]{:S(2)}) collective-permute-start(f32[4,8,3072]{2,1,0:T(8,128)S(1)} %get-tuple-element.110), channel_id=1, source_target_pairs={{0,8},{1,9},{2,10},{3,11},{4,12},{5,13},{6,14},{7,15},{8,0},{9,1},... | collective-permute-start | bytes 1179656 | tf_op jit(solution)/shard_map/ppermute | solution.py:611
  122.6 2.8 %collective-permute-start.40 = (f32[2,8,1536]{2,1,0:T(8,128)S(1)}, f32[2,8,1536]{2,1,0:T(8,128)S(1)}, u32[]{:S(2)}, u32[]{:S(2)}) collective-permute-start(f32[2,8,1536]{2,1,0:T(8,128)S(1)} %get-tuple-element.113.here), channel_id=1, source_target_pairs={{0,64},{64,0},{1,65},{65,1},{2,66},{66,2},{3,67},{67,3},{4,68},{68... | collective-permute-start | bytes 294920 | tf_op jit(solution)/shard_map/ppermute | solution.py:827
  125.4 3.4 %collective-permute-done.40.came = f32[2,8,1536]{2,1,0:T(8,128)S(1)} collective-permute-done((f32[2,8,1536]{2,1,0:T(8,128)S(1)}, f32[2,8,1536]{2,1,0:T(8,128)S(1)}, u32[]{:S(2)}, u32[]{:S(2)}) %collective-permute-start.40) | collective-permute-done | bytes 98336 | tf_op jit(solution)/shard_map/ppermute | solution.py:827
  129.9 4.5 %collective-permute-done.41.b = f32[8,1536]{1,0:T(8,128)S(1)} collective-permute-done((f32[8,1536]{1,0:T(8,128)S(1)}, f32[8,1536]{1,0:T(8,128)S(1)}, u32[]{:S(2)}, u32[]{:S(2)}) %collective-permute-start.41) | collective-permute-done | bytes 49184 | tf_op jit(solution)/shard_map/ppermute | solution.py:611
  (99 shorter events, 20.1 us)
Async XLA Ops:
  0.6 11.9 %copy-start = (f32[1,4,448,128]{3,2,1,0:T(8,128)S(1)}, f32[1,4,448,128]{3,2,1,0:T(8,128)}, u32[]{:S(2)}) copy-start(f32[1,4,448,128]{3,2,1,0:T(8,128)} %param.18) | copy-start | bytes 2752516
  2.5 17.2 %collective-permute-start = (f32[5,8,3072]{2,1,0:T(8,128)}, f32[5,8,3072]{2,1,0:T(8,128)S(1)}, u32[]{:S(2)}, u32[]{:S(2)}) collective-permute-start(f32[5,8,3072]{2,1,0:T(8,128)} %pick.1), channel_id=1, source_target_pairs={{0,8},{1,9},{2,10},{3,11},{4,12},{5,13},{6,14},{7,15},{8,0},{9,1},... | collective-permute-start | bytes 1474568 | tf_op jit(solution)/shard_map/ppermute | solution.py:611
  12.2 7.5 %collective-permute-start.1 = (f32[216,128]{1,0:T(8,128)}, f32[216,128]{1,0:T(8,128)S(1)}, u32[]{:S(2)}, u32[]{:S(2)}) collective-permute-start(f32[216,128]{1,0:T(8,128)} %get-tuple-element.64), channel_id=1, source_target_pairs={{0,8},{1,9},{2,10},{3,11},{4,12},{5,13},{6,14},{7,15},{8,0},{9,1},... | collective-permute-start | bytes 331784 | tf_op jit(solution)/shard_map/ppermute | solution.py:611
  12.6 11.8 %copy-start.4 = (bf16[256,256]{1,0:T(8,128)(2,1)S(1)}, bf16[256,256]{1,0:T(8,128)(2,1)}, u32[]{:S(2)}) copy-start(bf16[256,256]{1,0:T(8,128)(2,1)} %constant.13.clone.edge.rest_0_) | copy-start | bytes 393220
  12.6 11.8 %copy-start.5 = (f32[4,192,128]{2,1,0:T(8,128)S(1)}, f32[4,192,128]{2,1,0:T(8,128)}, u32[]{:S(2)}) copy-start(f32[4,192,128]{2,1,0:T(8,128)} %get-tuple-element.61.keep) | copy-start | bytes 1179652
  12.7 13.0 %copy-start.7 = (f32[192,128]{1,0:T(8,128)S(1)}, f32[192,128]{1,0:T(8,128)}, u32[]{:S(2)}) copy-start(f32[192,128]{1,0:T(8,128)} %get-tuple-element.66.table) | copy-start | bytes 294916
  19.7 16.5 %copy-start.2 = (bf16[2,256,256]{2,1,0:T(8,128)(2,1)S(1)}, bf16[2,256,256]{2,1,0:T(8,128)(2,1)}, u32[]{:S(2)}) copy-start(bf16[2,256,256]{2,1,0:T(8,128)(2,1)} %constant.10.clone.own_w) | copy-start | bytes 786436
  19.7 16.5 %copy-start.3 = (bf16[2,192,192]{2,1,0:T(8,128)(2,1)S(1)}, bf16[2,192,192]{2,1,0:T(8,128)(2,1)}, u32[]{:S(2)}) copy-start(bf16[2,192,192]{2,1,0:T(8,128)(2,1)} %constant.12.clone.ring_w) | copy-start | bytes 442372
  19.7 26.7 %collective-permute-start.2 = (f32[4,448,128]{2,1,0:T(8,128)S(1)}, f32[4,448,128]{2,1,0:T(8,128)S(1)}, u32[]{:S(2)}, u32[]{:S(2)}) collective-permute-start(f32[4,448,128]{2,1,0:T(8,128)S(1)} %gate.1), channel_id=1, source_target_pairs={{0,8},{1,9},{2,10},{3,11},{4,12},{5,13},{6,14},{7,15},{8,0},{9,1},... | collective-permute-start | bytes 2752520 | tf_op jit(solution)/shard_map/ppermute | solution.py:611
  25.7 1.4 %collective-permute-start.3 = (f32[192,128]{1,0:T(8,128)S(1)}, f32[192,128]{1,0:T(8,128)S(1)}, u32[]{:S(2)}, u32[]{:S(2)}) collective-permute-start(f32[192,128]{1,0:T(8,128)S(1)} %join_table.1.table.note), channel_id=1, source_target_pairs={{0,1},{1,0},{2,3},{3,2},{4,5},{5,4},{6,7},{7,6},{8,9},{9,8},{10,11... | collective-permute-start | bytes 294920 | tf_op jit(solution)/shard_map/ppermute | solution.py:611
  27.1 5.0 %collective-permute-start.4 = (f32[136,128]{1,0:T(8,128)S(1)}, f32[136,128]{1,0:T(8,128)S(1)}, u32[]{:S(2)}, u32[]{:S(2)}) collective-permute-start(f32[136,128]{1,0:T(8,128)S(1)} %pair.4.half.mine), channel_id=1, source_target_pairs={{0,7},{1,2},{2,1},{3,4},{4,3},{5,6},{6,5},{7,0},{8,15},{9,10},{10,... | collective-permute-start | bytes 208904 | tf_op jit(solution)/shard_map/ppermute | solution.py:611
  28.6 9.0 %collective-permute-start.7 = (f32[4,144,128]{2,1,0:T(8,128)S(1)}, f32[4,144,128]{2,1,0:T(8,128)S(1)}, u32[]{:S(2)}, u32[]{:S(2)}) collective-permute-start(f32[4,144,128]{2,1,0:T(8,128)S(1)} %get-tuple-element.71), channel_id=1, source_target_pairs={{0,1},{1,0},{2,3},{3,2},{4,5},{5,4},{6,7},{7,6},{8,9},{9,8},{10,11... | collective-permute-start | bytes 884744 | tf_op jit(solution)/shard_map/ppermute | solution.py:611
  28.8 9.9 %collective-permute-start.8 = (f32[4,144,128]{2,1,0:T(8,128)S(1)}, f32[4,144,128]{2,1,0:T(8,128)S(1)}, u32[]{:S(2)}, u32[]{:S(2)}) collective-permute-start(f32[4,144,128]{2,1,0:T(8,128)S(1)} %get-tuple-element.72), channel_id=1, source_target_pairs={{0,7},{1,2},{2,1},{3,4},{4,3},{5,6},{6,5},{7,0},{8,15},{9,10},{10,... | collective-permute-start | bytes 884744 | tf_op jit(solution)/shard_map/ppermute | solution.py:611
  29.9 10.9 %collective-permute-start.9 = (f32[4,144,128]{2,1,0:T(8,128)S(1)}, f32[4,144,128]{2,1,0:T(8,128)S(1)}, u32[]{:S(2)}, u32[]{:S(2)}) collective-permute-start(f32[4,144,128]{2,1,0:T(8,128)S(1)} %get-tuple-element.73), channel_id=1, source_target_pairs={{0,16},{1,17},{2,18},{3,19},{4,20},{5,21},{6,22},{7,23},{8,24},{9,... | collective-permute-start | bytes 884744 | tf_op jit(solution)/shard_map/ppermute | solution.py:611
  32.2 10.6 %collective-permute-start.10 = (f32[4,144,128]{2,1,0:T(8,128)S(1)}, f32[4,144,128]{2,1,0:T(8,128)S(1)}, u32[]{:S(2)}, u32[]{:S(2)}) collective-permute-start(f32[4,144,128]{2,1,0:T(8,128)S(1)} %get-tuple-element.74), channel_id=1, source_target_pairs={{0,48},{1,49},{2,50},{3,51},{4,52},{5,53},{6,54},{7,55},{8,56},{9,... | collective-permute-start | bytes 884744 | tf_op jit(solution)/shard_map/ppermute | solution.py:611
  37.6 6.8 %collective-permute-start.6 = (f32[72,128]{1,0:T(8,128)S(1)}, f32[72,128]{1,0:T(8,128)S(1)}, u32[]{:S(2)}, u32[]{:S(2)}) collective-permute-start(f32[72,128]{1,0:T(8,128)S(1)} %get-tuple-element.69.low), channel_id=1, source_target_pairs={{0,48},{1,49},{2,50},{3,51},{4,52},{5,53},{6,54},{7,55},{8,56},{9,... | collective-permute-start | bytes 110600 | tf_op jit(solution)/shard_map/ppermute | solution.py:611
  38.7 6.0 %collective-permute-start.5 = (f32[72,128]{1,0:T(8,128)S(1)}, f32[72,128]{1,0:T(8,128)S(1)}, u32[]{:S(2)}, u32[]{:S(2)}) collective-permute-start(f32[72,128]{1,0:T(8,128)S(1)} %get-tuple-element.70.high), channel_id=1, source_target_pairs={{0,16},{1,17},{2,18},{3,19},{4,20},{5,21},{6,22},{7,23},{8,24},{9,... | collective-permute-start | bytes 110600 | tf_op jit(solution)/shard_map/ppermute | solution.py:611
  44.7 2.8 %collective-permute-start.11 = (f32[128,128]{1,0:T(8,128)S(1)}, f32[128,128]{1,0:T(8,128)S(1)}, u32[]{:S(2)}, u32[]{:S(2)}) collective-permute-start(f32[128,128]{1,0:T(8,128)S(1)} %get-tuple-element.77.mine), channel_id=1, source_target_pairs={{0,1},{1,0},{2,3},{3,2},{4,5},{5,4},{6,7},{7,6},{8,9},{9,8},{10,11... | collective-permute-start | bytes 196616 | tf_op jit(solution)/shard_map/ppermute | solution.py:611
  49.9 16.9 %collective-permute-start.16 = (f32[4,144,128]{2,1,0:T(8,128)S(1)}, f32[4,144,128]{2,1,0:T(8,128)S(1)}, u32[]{:S(2)}, u32[]{:S(2)}) collective-permute-start(f32[4,144,128]{2,1,0:T(8,128)S(1)} %get-tuple-element.83), channel_id=1, source_target_pairs={{0,1},{1,0},{2,3},{3,2},{4,5},{5,4},{6,7},{7,6},{8,9},{9,8},{10,11... | collective-permute-start | bytes 884744 | tf_op jit(solution)/shard_map/ppermute | solution.py:611
  50.0 16.8 %collective-permute-start.17 = (f32[4,144,128]{2,1,0:T(8,128)S(1)}, f32[4,144,128]{2,1,0:T(8,128)S(1)}, u32[]{:S(2)}, u32[]{:S(2)}) collective-permute-start(f32[4,144,128]{2,1,0:T(8,128)S(1)} %get-tuple-element.84), channel_id=1, source_target_pairs={{0,7},{1,2},{2,1},{3,4},{4,3},{5,6},{6,5},{7,0},{8,15},{9,10},{10,... | collective-permute-start | bytes 884744 | tf_op jit(solution)/shard_map/ppermute | solution.py:611
  52.6 14.2 %collective-permute-start.18 = (f32[4,144,128]{2,1,0:T(8,128)S(1)}, f32[4,144,128]{2,1,0:T(8,128)S(1)}, u32[]{:S(2)}, u32[]{:S(2)}) collective-permute-start(f32[4,144,128]{2,1,0:T(8,128)S(1)} %get-tuple-element.85), channel_id=1, source_target_pairs={{0,16},{1,17},{2,18},{3,19},{4,20},{5,21},{6,22},{7,23},{8,24},{9,... | collective-permute-start | bytes 884744 | tf_op jit(solution)/shard_map/ppermute | solution.py:611
  54.6 12.3 %collective-permute-start.19 = (f32[4,144,128]{2,1,0:T(8,128)S(1)}, f32[4,144,128]{2,1,0:T(8,128)S(1)}, u32[]{:S(2)}, u32[]{:S(2)}) collective-permute-start(f32[4,144,128]{2,1,0:T(8,128)S(1)} %get-tuple-element.86), channel_id=1, source_target_pairs={{0,48},{1,49},{2,50},{3,51},{4,52},{5,53},{6,54},{7,55},{8,56},{9,... | collective-permute-start | bytes 884744 | tf_op jit(solution)/shard_map/ppermute | solution.py:611
  58.6 1.4 %collective-permute-start.12 = (f32[192,128]{1,0:T(8,128)S(1)}, f32[192,128]{1,0:T(8,128)S(1)}, u32[]{:S(2)}, u32[]{:S(2)}) collective-permute-start(f32[192,128]{1,0:T(8,128)S(1)} %table.3), channel_id=1, source_target_pairs={{0,1},{1,0},{2,3},{3,2},{4,5},{5,4},{6,7},{7,6},{8,9},{9,8},{10,11... | collective-permute-start | bytes 294920 | tf_op jit(solution)/shard_map/ppermute | solution.py:611
  60.0 4.7 %collective-permute-start.13 = (f32[128,128]{1,0:T(8,128)S(1)}, f32[128,128]{1,0:T(8,128)S(1)}, u32[]{:S(2)}, u32[]{:S(2)}) collective-permute-start(f32[128,128]{1,0:T(8,128)S(1)} %pair.5.half.mine), channel_id=1, source_target_pairs={{0,7},{1,2},{2,1},{3,4},{4,3},{5,6},{6,5},{7,0},{8,15},{9,10},{10,... | collective-permute-start | bytes 196616 | tf_op jit(solution)/shard_map/ppermute | solution.py:611
  64.7 4.0 %collective-permute-start.15 = (f32[64,128]{1,0:T(8,128)S(1)}, f32[64,128]{1,0:T(8,128)S(1)}, u32[]{:S(2)}, u32[]{:S(2)}) collective-permute-start(f32[64,128]{1,0:T(8,128)S(1)} %get-tuple-element.80.low), channel_id=1, source_target_pairs={{0,48},{1,49},{2,50},{3,51},{4,52},{5,53},{6,54},{7,55},{8,56},{9,... | collective-permute-start | bytes 98312 | tf_op jit(solution)/shard_map/ppermute | solution.py:611
  66.8 5.1 %collective-permute-start.14 = (f32[64,128]{1,0:T(8,128)S(1)}, f32[64,128]{1,0:T(8,128)S(1)}, u32[]{:S(2)}, u32[]{:S(2)}) collective-permute-start(f32[64,128]{1,0:T(8,128)S(1)} %get-tuple-element.81.high), channel_id=1, source_target_pairs={{0,16},{1,17},{2,18},{3,19},{4,20},{5,21},{6,22},{7,23},{8,24},{9,... | collective-permute-start | bytes 98312 | tf_op jit(solution)/shard_map/ppermute | solution.py:611
  72.0 1.3 collective-permute-start.20
  75.7 12.3 %collective-permute-start.25 = (f32[4,144,128]{2,1,0:T(8,128)S(1)}, f32[4,144,128]{2,1,0:T(8,128)S(1)}, u32[]{:S(2)}, u32[]{:S(2)}) collective-permute-start(f32[4,144,128]{2,1,0:T(8,128)S(1)} %get-tuple-element.93), channel_id=1, source_target_pairs={{0,1},{1,0},{2,3},{3,2},{4,5},{5,4},{6,7},{7,6},{8,9},{9,8},{10,11... | collective-permute-start | bytes 884744 | tf_op jit(solution)/shard_map/ppermute | solution.py:611
  75.9 13.9 %collective-permute-start.26 = (f32[4,144,128]{2,1,0:T(8,128)S(1)}, f32[4,144,128]{2,1,0:T(8,128)S(1)}, u32[]{:S(2)}, u32[]{:S(2)}) collective-permute-start(f32[4,144,128]{2,1,0:T(8,128)S(1)} %get-tuple-element.94), channel_id=1, source_target_pairs={{0,7},{1,2},{2,1},{3,4},{4,3},{5,6},{6,5},{7,0},{8,15},{9,10},{10,... | collective-permute-start | bytes 884744 | tf_op jit(solution)/shard_map/ppermute | solution.py:611
  76.2 13.6 %collective-permute-start.27 = (f32[4,144,128]{2,1,0:T(8,128)S(1)}, f32[4,144,128]{2,1,0:T(8,128)S(1)}, u32[]{:S(2)}, u32[]{:S(2)}) collective-permute-start(f32[4,144,128]{2,1,0:T(8,128)S(1)} %get-tuple-element.95), channel_id=1, source_target_pairs={{0,16},{1,17},{2,18},{3,19},{4,20},{5,21},{6,22},{7,23},{8,24},{9,... | collective-permute-start | bytes 884744 | tf_op jit(solution)/shard_map/ppermute | solution.py:611
  76.2 13.6 %collective-permute-start.28 = (f32[4,144,128]{2,1,0:T(8,128)S(1)}, f32[4,144,128]{2,1,0:T(8,128)S(1)}, u32[]{:S(2)}, u32[]{:S(2)}) collective-permute-start(f32[4,144,128]{2,1,0:T(8,128)S(1)} %get-tuple-element.96), channel_id=1, source_target_pairs={{0,48},{1,49},{2,50},{3,51},{4,52},{5,53},{6,54},{7,55},{8,56},{9,... | collective-permute-start | bytes 884744 | tf_op jit(solution)/shard_map/ppermute | solution.py:611
  81.4 1.4 %collective-permute-start.21 = (f32[192,128]{1,0:T(8,128)S(1)}, f32[192,128]{1,0:T(8,128)S(1)}, u32[]{:S(2)}, u32[]{:S(2)}) collective-permute-start(f32[192,128]{1,0:T(8,128)S(1)} %table.4), channel_id=1, source_target_pairs={{0,1},{1,0},{2,3},{3,2},{4,5},{5,4},{6,7},{7,6},{8,9},{9,8},{10,11... | collective-permute-start | bytes 294920 | tf_op jit(solution)/shard_map/ppermute | solution.py:611
  82.8 4.9 %collective-permute-start.22 = (f32[128,128]{1,0:T(8,128)S(1)}, f32[128,128]{1,0:T(8,128)S(1)}, u32[]{:S(2)}, u32[]{:S(2)}) collective-permute-start(f32[128,128]{1,0:T(8,128)S(1)} %pair.6.half.mine), channel_id=1, source_target_pairs={{0,7},{1,2},{2,1},{3,4},{4,3},{5,6},{6,5},{7,0},{8,15},{9,10},{10,... | collective-permute-start | bytes 196616 | tf_op jit(solution)/shard_map/ppermute | solution.py:611
  87.7 4.0 %collective-permute-start.24 = (f32[64,128]{1,0:T(8,128)S(1)}, f32[64,128]{1,0:T(8,128)S(1)}, u32[]{:S(2)}, u32[]{:S(2)}) collective-permute-start(f32[64,128]{1,0:T(8,128)S(1)} %get-tuple-element.91.low), channel_id=1, source_target_pairs={{0,48},{1,49},{2,50},{3,51},{4,52},{5,53},{6,54},{7,55},{8,56},{9,... | collective-permute-start | bytes 98312 | tf_op jit(solution)/shard_map/ppermute | solution.py:611
  88.0 5.1 %collective-permute-start.23 = (f32[64,128]{1,0:T(8,128)S(1)}, f32[64,128]{1,0:T(8,128)S(1)}, u32[]{:S(2)}, u32[]{:S(2)}) collective-permute-start(f32[64,128]{1,0:T(8,128)S(1)} %get-tuple-element.92.high), channel_id=1, source_target_pairs={{0,16},{1,17},{2,18},{3,19},{4,20},{5,21},{6,22},{7,23},{8,24},{9,... | collective-permute-start | bytes 98312 | tf_op jit(solution)/shard_map/ppermute | solution.py:611
  93.2 1.6 %collective-permute-start.29 = (f32[128,128]{1,0:T(8,128)S(1)}, f32[128,128]{1,0:T(8,128)S(1)}, u32[]{:S(2)}, u32[]{:S(2)}) collective-permute-start(f32[128,128]{1,0:T(8,128)S(1)} %get-tuple-element.99.mine), channel_id=1, source_target_pairs={{0,1},{1,0},{2,3},{3,2},{4,5},{5,4},{6,7},{7,6},{8,9},{9,8},{10,11... | collective-permute-start | bytes 196616 | tf_op jit(solution)/shard_map/ppermute | solution.py:611
  97.1 12.7 %collective-permute-start.34 = (f32[4,144,128]{2,1,0:T(8,128)S(1)}, f32[4,144,128]{2,1,0:T(8,128)S(1)}, u32[]{:S(2)}, u32[]{:S(2)}) collective-permute-start(f32[4,144,128]{2,1,0:T(8,128)S(1)} %get-tuple-element.103), channel_id=1, source_target_pairs={{0,1},{1,0},{2,3},{3,2},{4,5},{5,4},{6,7},{7,6},{8,9},{9,8},{10,11... | collective-permute-start | bytes 884744 | tf_op jit(solution)/shard_map/ppermute | solution.py:611
  97.3 14.5 %collective-permute-start.35 = (f32[4,144,128]{2,1,0:T(8,128)S(1)}, f32[4,144,128]{2,1,0:T(8,128)S(1)}, u32[]{:S(2)}, u32[]{:S(2)}) collective-permute-start(f32[4,144,128]{2,1,0:T(8,128)S(1)} %get-tuple-element.104), channel_id=1, source_target_pairs={{0,7},{1,2},{2,1},{3,4},{4,3},{5,6},{6,5},{7,0},{8,15},{9,10},{10,... | collective-permute-start | bytes 884744 | tf_op jit(solution)/shard_map/ppermute | solution.py:611
  98.1 13.7 %collective-permute-start.36 = (f32[4,144,128]{2,1,0:T(8,128)S(1)}, f32[4,144,128]{2,1,0:T(8,128)S(1)}, u32[]{:S(2)}, u32[]{:S(2)}) collective-permute-start(f32[4,144,128]{2,1,0:T(8,128)S(1)} %get-tuple-element.105), channel_id=1, source_target_pairs={{0,16},{1,17},{2,18},{3,19},{4,20},{5,21},{6,22},{7,23},{8,24},{9,... | collective-permute-start | bytes 884744 | tf_op jit(solution)/shard_map/ppermute | solution.py:611
  99.0 12.9 %collective-permute-start.37 = (f32[4,144,128]{2,1,0:T(8,128)S(1)}, f32[4,144,128]{2,1,0:T(8,128)S(1)}, u32[]{:S(2)}, u32[]{:S(2)}) collective-permute-start(f32[4,144,128]{2,1,0:T(8,128)S(1)} %get-tuple-element.106), channel_id=1, source_target_pairs={{0,48},{1,49},{2,50},{3,51},{4,52},{5,53},{6,54},{7,55},{8,56},{9,... | collective-permute-start | bytes 884744 | tf_op jit(solution)/shard_map/ppermute | solution.py:611
  103.3 1.4 %collective-permute-start.30 = (f32[192,128]{1,0:T(8,128)S(1)}, f32[192,128]{1,0:T(8,128)S(1)}, u32[]{:S(2)}, u32[]{:S(2)}) collective-permute-start(f32[192,128]{1,0:T(8,128)S(1)} %table.5), channel_id=1, source_target_pairs={{0,1},{1,0},{2,3},{3,2},{4,5},{5,4},{6,7},{7,6},{8,9},{9,8},{10,11... | collective-permute-start | bytes 294920 | tf_op jit(solution)/shard_map/ppermute | solution.py:611
  104.7 5.1 %collective-permute-start.31 = (f32[128,128]{1,0:T(8,128)S(1)}, f32[128,128]{1,0:T(8,128)S(1)}, u32[]{:S(2)}, u32[]{:S(2)}) collective-permute-start(f32[128,128]{1,0:T(8,128)S(1)} %pair.7.half.mine), channel_id=1, source_target_pairs={{0,7},{1,2},{2,1},{3,4},{4,3},{5,6},{6,5},{7,0},{8,15},{9,10},{10,... | collective-permute-start | bytes 196616 | tf_op jit(solution)/shard_map/ppermute | solution.py:611
  109.7 4.0 %collective-permute-start.33 = (f32[64,128]{1,0:T(8,128)S(1)}, f32[64,128]{1,0:T(8,128)S(1)}, u32[]{:S(2)}, u32[]{:S(2)}) collective-permute-start(f32[64,128]{1,0:T(8,128)S(1)} %get-tuple-element.101.low), channel_id=1, source_target_pairs={{0,48},{1,49},{2,50},{3,51},{4,52},{5,53},{6,54},{7,55},{8,56},{9,... | collective-permute-start | bytes 98312 | tf_op jit(solution)/shard_map/ppermute | solution.py:611
  109.8 5.2 %collective-permute-start.32 = (f32[64,128]{1,0:T(8,128)S(1)}, f32[64,128]{1,0:T(8,128)S(1)}, u32[]{:S(2)}, u32[]{:S(2)}) collective-permute-start(f32[64,128]{1,0:T(8,128)S(1)} %get-tuple-element.102.high), channel_id=1, source_target_pairs={{0,16},{1,17},{2,18},{3,19},{4,20},{5,21},{6,22},{7,23},{8,24},{9,... | collective-permute-start | bytes 98312 | tf_op jit(solution)/shard_map/ppermute | solution.py:611
  115.0 1.3 collective-permute-start.38
  118.5 15.9 %collective-permute-start.39 = (f32[4,8,3072]{2,1,0:T(8,128)S(1)}, f32[4,8,3072]{2,1,0:T(8,128)S(1)}, u32[]{:S(2)}, u32[]{:S(2)}) collective-permute-start(f32[4,8,3072]{2,1,0:T(8,128)S(1)} %get-tuple-element.110), channel_id=1, source_target_pairs={{0,8},{1,9},{2,10},{3,11},{4,12},{5,13},{6,14},{7,15},{8,0},{9,1},... | collective-permute-start | bytes 1179656 | tf_op jit(solution)/shard_map/ppermute | solution.py:611
  122.6 6.2 %collective-permute-start.40 = (f32[2,8,1536]{2,1,0:T(8,128)S(1)}, f32[2,8,1536]{2,1,0:T(8,128)S(1)}, u32[]{:S(2)}, u32[]{:S(2)}) collective-permute-start(f32[2,8,1536]{2,1,0:T(8,128)S(1)} %get-tuple-element.113.here), channel_id=1, source_target_pairs={{0,64},{64,0},{1,65},{65,1},{2,66},{66,2},{3,67},{67,3},{4,68},{68... | collective-permute-start | bytes 294920 | tf_op jit(solution)/shard_map/ppermute | solution.py:827
  128.8 5.7 %collective-permute-start.41 = (f32[8,1536]{1,0:T(8,128)S(1)}, f32[8,1536]{1,0:T(8,128)S(1)}, u32[]{:S(2)}, u32[]{:S(2)}) collective-permute-start(f32[8,1536]{1,0:T(8,128)S(1)} %get-tuple-element.114), channel_id=1, source_target_pairs={{0,8},{1,9},{2,10},{3,11},{4,12},{5,13},{6,14},{7,15},{8,0},{9,1},... | collective-permute-start | bytes 147464 | tf_op jit(solution)/shard_map/ppermute | solution.py:611
  (5 other events, 39.6 us)

commit v6 on v5

--- a/solution.py
+++ b/solution.py
@@ -549,7 +549,7 @@
         out[o] = jnp.where(upper, came[o], mine[o])
         out[ORB + o] = jnp.where(upper, mine[o], came[o])
 
-    each(ORB, step)
+    each(ORB, step, False)
 
 
 def density_kernel(params, field, mine, across, plane, near, far):

time: 136 us -> 136 us (level)
  no operation moved by 1% of the time
where the time goes in v6:
time: 136 us; the launch traced here: 135 us
  starting transfers between devices  50.5 us (37%)
  waiting for transfers between devices  41.5 us (31%)
  Pallas kernels  40.8 us (30%)
  between operations  2.42 us (2%)
    ppermute x41, starting transfers between devices, send(): return lax.ppermute(value, 'dom', pairs)  47.7 us
    pallas_call x38, Pallas kernels, call(): pl.pallas_call(kernel, out_shape=[jax.ShapeDtypeStruct(*out) for out in o...  40.8 us
    ppermute x41, waiting for transfers between devices, send(): return lax.ppermute(value, 'dom', pairs)  38.2 us
    ppermute x1, waiting for transfers between devices, body(): across_came = lax.ppermute(across, 'band', [(0, 1), (1, 0)])  3.39 us
    ppermute x1, starting transfers between devices, body(): across_came = lax.ppermute(across, 'band', [(0, 1), (1, 0)])  2.81 us
  transfers between devices with their start and end apart: 42, of which 25 were waited for; matrix products, arithmetic and copies ran while one was open for 0% of the time, Pallas kernels for 21%

profile of v6, /device:TPU:0, one launch (start us, length us, event | category | flops | bytes accessed | tf_op | source)
XLA Modules:
  0.0 135.5 jit_solution(8279972650872188058)
XLA Ops:
  0.6 1.9 %pick.1 = f32[5,8,3072]{2,1,0:T(8,128)} custom-call(f32[8,8,3072]{2,1,0:T(8,128)} %bitcast.17, f32[1,8,3072]{2,1,0:T(8,128)} %potential.3), custom_call_target="tpu_custom_call" | custom-call | flops 1000000 | bytes 4000000 | tf_op jit(solution)/shard_map/pick/pallas_call | solution.py:596
  2.5 3.4 %collective-permute-start = (f32[5,8,3072]{2,1,0:T(8,128)}, f32[5,8,3072]{2,1,0:T(8,128)S(1)}, u32[]{:S(2)}, u32[]{:S(2)}) collective-permute-start(f32[5,8,3072]{2,1,0:T(8,128)} %pick.1), channel_id=1, source_target_pairs={{0,8},{1,9},{2,10},{3,11},{4,12},{5,13},{6,14},{7,15},{8,0},{9,1},... | collective-permute-start | bytes 1474568 | tf_op jit(solution)/shard_map/ppermute | solution.py:611
  5.9 6.3 %begin.1 = (f32[4,192,128]{2,1,0:T(8,128)}, f32[16,128]{1,0:T(8,128)}, s32[8,512]{1,0:T(8,128)}, f32[192,128]{1,0:T(8,128)}, f32[216,128]{1,0:T(8,128)}) custom-call(f32[8]{0:T(128)} %weights_in.1, s32[1,448]{1,0:T(1,128)} %column_in.1, s32[1,448]{1,0:T(1,128)} %shift_in.1, s32[1,448]{1,0:T(1,128)} %owner_in.1, s32[1,448]{1,0:T(1,128)} %atom_in.1, ...), custom_call_target="tpu_custom_call" | custom-call | flops 100000000 | bytes 4000000 | tf_op jit(solution)/shard_map/begin/pallas_call | solution.py:596
  12.7 7.0 %collective-permute-done.1.note_came = f32[216,128]{1,0:T(8,128)S(1)} collective-permute-done((f32[216,128]{1,0:T(8,128)}, f32[216,128]{1,0:T(8,128)S(1)}, u32[]{:S(2)}, u32[]{:S(2)}) %collective-permute-start.1) | collective-permute-done | bytes 110624 | tf_op jit(solution)/shard_map/ppermute | solution.py:611
  19.7 3.3 %collective-permute-start.2 = (f32[4,448,128]{2,1,0:T(8,128)S(1)}, f32[4,448,128]{2,1,0:T(8,128)S(1)}, u32[]{:S(2)}, u32[]{:S(2)}) collective-permute-start(f32[4,448,128]{2,1,0:T(8,128)S(1)} %gate.1), channel_id=1, source_target_pairs={{0,8},{1,9},{2,10},{3,11},{4,12},{5,13},{6,14},{7,15},{8,0},{9,1},... | collective-permute-start | bytes 2752520 | tf_op jit(solution)/shard_map/ppermute | solution.py:611
  25.8 1.3 collective-permute-done.3.came
  27.1 1.4 %collective-permute-start.4 = (f32[136,128]{1,0:T(8,128)S(1)}, f32[136,128]{1,0:T(8,128)S(1)}, u32[]{:S(2)}, u32[]{:S(2)}) collective-permute-start(f32[136,128]{1,0:T(8,128)S(1)} %pair.4.half.mine), channel_id=1, source_target_pairs={{0,7},{1,2},{2,1},{3,4},{4,3},{5,6},{6,5},{7,0},{8,15},{9,10},{10,... | collective-permute-start | bytes 208904 | tf_op jit(solution)/shard_map/ppermute | solution.py:611
  29.9 1.9 %collective-permute-start.9 = (f32[4,144,128]{2,1,0:T(8,128)S(1)}, f32[4,144,128]{2,1,0:T(8,128)S(1)}, u32[]{:S(2)}, u32[]{:S(2)}) collective-permute-start(f32[4,144,128]{2,1,0:T(8,128)S(1)} %get-tuple-element.73), channel_id=1, source_target_pairs={{0,16},{1,17},{2,18},{3,19},{4,20},{5,21},{6,22},{7,23},{8,24},{9,... | collective-permute-start | bytes 884744 | tf_op jit(solution)/shard_map/ppermute | solution.py:611
  32.2 4.0 %collective-permute-start.10 = (f32[4,144,128]{2,1,0:T(8,128)S(1)}, f32[4,144,128]{2,1,0:T(8,128)S(1)}, u32[]{:S(2)}, u32[]{:S(2)}) collective-permute-start(f32[4,144,128]{2,1,0:T(8,128)S(1)} %get-tuple-element.74), channel_id=1, source_target_pairs={{0,48},{1,49},{2,50},{3,51},{4,52},{5,53},{6,54},{7,55},{8,56},{9,... | collective-permute-start | bytes 884744 | tf_op jit(solution)/shard_map/ppermute | solution.py:611
  36.2 1.4 %local.4.acc = f32[4,192,256]{2,1,0:T(8,128)S(1)} custom-call(f32[16,128]{1,0:T(8,128)S(1)} %get-tuple-element.62.params, f32[136,128]{1,0:T(8,128)S(1)} %pair.4.half.mine, f32[4,192,256]{2,1,0:T(8,128)S(1)} %get-tuple-element.67.field.before, f32[4,192,256]{2,1,0:T(8,128)S(1)} %get-tuple-element.67.field.before, f32[192,256]{1,0:T(8,128)S(1)} %get-tuple-element.68.pot, ...), custom_call_target="tpu_custom_call" | custom-call | flops 100000000 | bytes 4000000 | tf_op jit(solution)/shard_map/local/pallas_call | solution.py:596
  38.7 1.9 %collective-permute-start.5 = (f32[72,128]{1,0:T(8,128)S(1)}, f32[72,128]{1,0:T(8,128)S(1)}, u32[]{:S(2)}, u32[]{:S(2)}) collective-permute-start(f32[72,128]{1,0:T(8,128)S(1)} %get-tuple-element.70.high), channel_id=1, source_target_pairs={{0,16},{1,17},{2,18},{3,19},{4,20},{5,21},{6,22},{7,23},{8,24},{9,... | collective-permute-start | bytes 110600 | tf_op jit(solution)/shard_map/ppermute | solution.py:611
  40.8 2.0 %collective-permute-done.10.xh = f32[4,144,128]{2,1,0:T(8,128)S(1)} collective-permute-done((f32[4,144,128]{2,1,0:T(8,128)S(1)}, f32[4,144,128]{2,1,0:T(8,128)S(1)}, u32[]{:S(2)}, u32[]{:S(2)}) %collective-permute-start.10) | collective-permute-done | bytes 294944 | tf_op jit(solution)/shard_map/ppermute | solution.py:611
  42.8 1.6 %halo.4.acc = f32[4,192,256]{2,1,0:T(8,128)S(1)} custom-call(f32[16,128]{1,0:T(8,128)S(1)} %get-tuple-element.62.params, f32[4,144,128]{2,1,0:T(8,128)S(1)} %collective-permute-done.7.inner, f32[4,144,128]{2,1,0:T(8,128)S(1)} %collective-permute-done.8.outer, f32[4,144,128]{2,1,0:T(8,128)S(1)} %collective-permute-done.9.xl, ...), custom_call_target="tpu_custom_call" | custom-call | flops 100000000 | bytes 4000000 | tf_op jit(solution)/shard_map/halo/pallas_call | solution.py:596
  47.5 2.4 %update.3 = (f32[4,192,256]{2,1,0:T(8,128)S(1)}, f32[4,144,128]{2,1,0:T(8,128)S(1)}, f32[4,144,128]{2,1,0:T(8,128)S(1)}, f32[4,144,128]{2,1,0:T(8,128)S(1)}, f32[4,144,128]{2,1,0:T(8,128)S(1)}) custom-call(f32[16,128]{1,0:T(8,128)S(1)} %get-tuple-element.62.params, s32[4,896]{1,0:T(4,128)S(1)} %get-tuple-element.65.index, ...), custom_call_target="tpu_custom_call" | custom-call | flops 100000000 | bytes 4000000 | tf_op jit(solution)/shard_map/update/pallas_call | solution.py:596
  50.0 2.6 %collective-permute-start.17 = (f32[4,144,128]{2,1,0:T(8,128)S(1)}, f32[4,144,128]{2,1,0:T(8,128)S(1)}, u32[]{:S(2)}, u32[]{:S(2)}) collective-permute-start(f32[4,144,128]{2,1,0:T(8,128)S(1)} %get-tuple-element.84), channel_id=1, source_target_pairs={{0,7},{1,2},{2,1},{3,4},{4,3},{5,6},{6,5},{7,0},{8,15},{9,10},{10,... | collective-permute-start | bytes 884744 | tf_op jit(solution)/shard_map/ppermute | solution.py:611
  52.6 1.9 %collective-permute-start.18 = (f32[4,144,128]{2,1,0:T(8,128)S(1)}, f32[4,144,128]{2,1,0:T(8,128)S(1)}, u32[]{:S(2)}, u32[]{:S(2)}) collective-permute-start(f32[4,144,128]{2,1,0:T(8,128)S(1)} %get-tuple-element.85), channel_id=1, source_target_pairs={{0,16},{1,17},{2,18},{3,19},{4,20},{5,21},{6,22},{7,23},{8,24},{9,... | collective-permute-start | bytes 884744 | tf_op jit(solution)/shard_map/ppermute | solution.py:611
  54.6 2.1 %collective-permute-start.19 = (f32[4,144,128]{2,1,0:T(8,128)S(1)}, f32[4,144,128]{2,1,0:T(8,128)S(1)}, u32[]{:S(2)}, u32[]{:S(2)}) collective-permute-start(f32[4,144,128]{2,1,0:T(8,128)S(1)} %get-tuple-element.86), channel_id=1, source_target_pairs={{0,48},{1,49},{2,50},{3,51},{4,52},{5,53},{6,54},{7,55},{8,56},{9,... | collective-permute-start | bytes 884744 | tf_op jit(solution)/shard_map/ppermute | solution.py:611
  56.7 1.9 %table.3 = f32[192,128]{1,0:T(8,128)S(1)} custom-call(s32[4,896]{1,0:T(4,128)S(1)} %get-tuple-element.65.index, f32[4,192,256]{2,1,0:T(8,128)S(1)} %get-tuple-element.79.field.before, f32[4,192,384]{2,1,0:T(8,128)S(1)} %own.1.head, f32[4,192,512]{2,1,0:T(8,128)S(1)} %get-tuple-element.78.tail), custom_call_target="tpu_custom_call" | custom-call | flops 100000000 | bytes 4000000 | tf_op jit(solution)/shard_map/table/pallas_call | solution.py:596
  58.7 1.3 collective-permute-done.12.came
  60.4 1.4 %local.5.acc = f32[4,192,256]{2,1,0:T(8,128)S(1)} custom-call(f32[16,128]{1,0:T(8,128)S(1)} %get-tuple-element.62.params, f32[128,128]{1,0:T(8,128)S(1)} %pair.5.half.mine, f32[4,192,256]{2,1,0:T(8,128)S(1)} %get-tuple-element.79.field.before, f32[4,192,256]{2,1,0:T(8,128)S(1)} %get-tuple-element.67.field.before, f32[192,256]{1,0:T(8,128)S(1)} %get-tuple-element.68.pot, ...), custom_call_target="tpu_custom_call" | custom-call | flops 100000000 | bytes 4000000 | tf_op jit(solution)/shard_map/local/pallas_call | solution.py:596
  61.8 2.9 %collective-permute-done.13.came = f32[128,128]{1,0:T(8,128)S(1)} collective-permute-done((f32[128,128]{1,0:T(8,128)S(1)}, f32[128,128]{1,0:T(8,128)S(1)}, u32[]{:S(2)}, u32[]{:S(2)}) %collective-permute-start.13) | collective-permute-done | bytes 65568 | tf_op jit(solution)/shard_map/ppermute | solution.py:611
  64.7 2.1 %collective-permute-start.15 = (f32[64,128]{1,0:T(8,128)S(1)}, f32[64,128]{1,0:T(8,128)S(1)}, u32[]{:S(2)}, u32[]{:S(2)}) collective-permute-start(f32[64,128]{1,0:T(8,128)S(1)} %get-tuple-element.80.low), channel_id=1, source_target_pairs={{0,48},{1,49},{2,50},{3,51},{4,52},{5,53},{6,54},{7,55},{8,56},{9,... | collective-permute-start | bytes 98312 | tf_op jit(solution)/shard_map/ppermute | solution.py:611
  66.8 1.6 %halo.5.acc = f32[4,192,256]{2,1,0:T(8,128)S(1)} custom-call(f32[16,128]{1,0:T(8,128)S(1)} %get-tuple-element.62.params, f32[4,144,128]{2,1,0:T(8,128)S(1)} %collective-permute-done.16.inner, f32[4,144,128]{2,1,0:T(8,128)S(1)} %collective-permute-done.17.outer, f32[4,144,128]{2,1,0:T(8,128)S(1)} %collective-permute-done.18.xl, ...), custom_call_target="tpu_custom_call" | custom-call | flops 100000000 | bytes 4000000 | tf_op jit(solution)/shard_map/halo/pallas_call | solution.py:596
  68.7 3.2 %collective-permute-done.14.below = f32[64,128]{1,0:T(8,128)S(1)} collective-permute-done((f32[64,128]{1,0:T(8,128)S(1)}, f32[64,128]{1,0:T(8,128)S(1)}, u32[]{:S(2)}, u32[]{:S(2)}) %collective-permute-start.14) | collective-permute-done | bytes 32800 | tf_op jit(solution)/shard_map/ppermute | solution.py:611
  73.3 2.4 %update.4 = (f32[4,192,256]{2,1,0:T(8,128)S(1)}, f32[4,144,128]{2,1,0:T(8,128)S(1)}, f32[4,144,128]{2,1,0:T(8,128)S(1)}, f32[4,144,128]{2,1,0:T(8,128)S(1)}, f32[4,144,128]{2,1,0:T(8,128)S(1)}) custom-call(f32[16,128]{1,0:T(8,128)S(1)} %get-tuple-element.62.params, s32[4,896]{1,0:T(4,128)S(1)} %get-tuple-element.65.index, ...), custom_call_target="tpu_custom_call" | custom-call | flops 100000000 | bytes 4000000 | tf_op jit(solution)/shard_map/update/pallas_call | solution.py:596
  76.2 3.2 %collective-permute-start.28 = (f32[4,144,128]{2,1,0:T(8,128)S(1)}, f32[4,144,128]{2,1,0:T(8,128)S(1)}, u32[]{:S(2)}, u32[]{:S(2)}) collective-permute-start(f32[4,144,128]{2,1,0:T(8,128)S(1)} %get-tuple-element.96), channel_id=1, source_target_pairs={{0,48},{1,49},{2,50},{3,51},{4,52},{5,53},{6,54},{7,55},{8,56},{9,... | collective-permute-start | bytes 884744 | tf_op jit(solution)/shard_map/ppermute | solution.py:611
  79.5 1.9 %table.4 = f32[192,128]{1,0:T(8,128)S(1)} custom-call(s32[4,896]{1,0:T(4,128)S(1)} %get-tuple-element.65.index, f32[4,192,256]{2,1,0:T(8,128)S(1)} %get-tuple-element.90.field.before, f32[4,192,384]{2,1,0:T(8,128)S(1)} %own.1.head, f32[4,192,512]{2,1,0:T(8,128)S(1)} %get-tuple-element.78.tail), custom_call_target="tpu_custom_call" | custom-call | flops 100000000 | bytes 4000000 | tf_op jit(solution)/shard_map/table/pallas_call | solution.py:596
  81.5 1.3 collective-permute-done.21.came
  82.8 1.9 %collective-permute-start.22 = (f32[128,128]{1,0:T(8,128)S(1)}, f32[128,128]{1,0:T(8,128)S(1)}, u32[]{:S(2)}, u32[]{:S(2)}) collective-permute-start(f32[128,128]{1,0:T(8,128)S(1)} %pair.6.half.mine), channel_id=1, source_target_pairs={{0,7},{1,2},{2,1},{3,4},{4,3},{5,6},{6,5},{7,0},{8,15},{9,10},{10,... | collective-permute-start | bytes 196616 | tf_op jit(solution)/shard_map/ppermute | solution.py:611
  84.7 1.4 %local.6.acc = f32[4,192,256]{2,1,0:T(8,128)S(1)} custom-call(f32[16,128]{1,0:T(8,128)S(1)} %get-tuple-element.62.params, f32[128,128]{1,0:T(8,128)S(1)} %pair.6.half.mine, f32[4,192,256]{2,1,0:T(8,128)S(1)} %get-tuple-element.90.field.before, f32[4,192,256]{2,1,0:T(8,128)S(1)} %get-tuple-element.79.field.before, f32[192,256]{1,0:T(8,128)S(1)} %get-tuple-element.68.pot, ...), custom_call_target="tpu_custom_call" | custom-call | flops 100000000 | bytes 4000000 | tf_op jit(solution)/shard_map/local/pallas_call | solution.py:596
  86.1 1.6 %collective-permute-done.22.came = f32[128,128]{1,0:T(8,128)S(1)} collective-permute-done((f32[128,128]{1,0:T(8,128)S(1)}, f32[128,128]{1,0:T(8,128)S(1)}, u32[]{:S(2)}, u32[]{:S(2)}) %collective-permute-start.22) | collective-permute-done | bytes 65568 | tf_op jit(solution)/shard_map/ppermute | solution.py:611
  88.0 1.8 %collective-permute-start.23 = (f32[64,128]{1,0:T(8,128)S(1)}, f32[64,128]{1,0:T(8,128)S(1)}, u32[]{:S(2)}, u32[]{:S(2)}) collective-permute-start(f32[64,128]{1,0:T(8,128)S(1)} %get-tuple-element.92.high), channel_id=1, source_target_pairs={{0,16},{1,17},{2,18},{3,19},{4,20},{5,21},{6,22},{7,23},{8,24},{9,... | collective-permute-start | bytes 98312 | tf_op jit(solution)/shard_map/ppermute | solution.py:611
  89.8 1.6 %halo.6.acc = f32[4,192,256]{2,1,0:T(8,128)S(1)} custom-call(f32[16,128]{1,0:T(8,128)S(1)} %get-tuple-element.62.params, f32[4,144,128]{2,1,0:T(8,128)S(1)} %collective-permute-done.25.inner, f32[4,144,128]{2,1,0:T(8,128)S(1)} %collective-permute-done.26.outer, f32[4,144,128]{2,1,0:T(8,128)S(1)} %collective-permute-done.27.xl, ...), custom_call_target="tpu_custom_call" | custom-call | flops 100000000 | bytes 4000000 | tf_op jit(solution)/shard_map/halo/pallas_call | solution.py:596
  91.7 1.4 %collective-permute-done.23.below = f32[64,128]{1,0:T(8,128)S(1)} collective-permute-done((f32[64,128]{1,0:T(8,128)S(1)}, f32[64,128]{1,0:T(8,128)S(1)}, u32[]{:S(2)}, u32[]{:S(2)}) %collective-permute-start.23) | collective-permute-done | bytes 32800 | tf_op jit(solution)/shard_map/ppermute | solution.py:611
  94.7 2.4 %update.5 = (f32[4,192,256]{2,1,0:T(8,128)S(1)}, f32[4,144,128]{2,1,0:T(8,128)S(1)}, f32[4,144,128]{2,1,0:T(8,128)S(1)}, f32[4,144,128]{2,1,0:T(8,128)S(1)}, f32[4,144,128]{2,1,0:T(8,128)S(1)}) custom-call(f32[16,128]{1,0:T(8,128)S(1)} %get-tuple-element.62.params, s32[4,896]{1,0:T(4,128)S(1)} %get-tuple-element.65.index, ...), custom_call_target="tpu_custom_call" | custom-call | flops 100000000 | bytes 4000000 | tf_op jit(solution)/shard_map/update/pallas_call | solution.py:596
  99.0 2.4 %collective-permute-start.37 = (f32[4,144,128]{2,1,0:T(8,128)S(1)}, f32[4,144,128]{2,1,0:T(8,128)S(1)}, u32[]{:S(2)}, u32[]{:S(2)}) collective-permute-start(f32[4,144,128]{2,1,0:T(8,128)S(1)} %get-tuple-element.106), channel_id=1, source_target_pairs={{0,48},{1,49},{2,50},{3,51},{4,52},{5,53},{6,54},{7,55},{8,56},{9,... | collective-permute-start | bytes 884744 | tf_op jit(solution)/shard_map/ppermute | solution.py:611
  101.3 1.9 %table.5 = f32[192,128]{1,0:T(8,128)S(1)} custom-call(s32[4,896]{1,0:T(4,128)S(1)} %get-tuple-element.65.index, f32[4,192,256]{2,1,0:T(8,128)S(1)} %get-tuple-element.100.field, f32[4,192,384]{2,1,0:T(8,128)S(1)} %own.1.head, f32[4,192,512]{2,1,0:T(8,128)S(1)} %get-tuple-element.78.tail), custom_call_target="tpu_custom_call" | custom-call | flops 100000000 | bytes 4000000 | tf_op jit(solution)/shard_map/table/pallas_call | solution.py:596
  104.7 1.4 %collective-permute-start.31 = (f32[128,128]{1,0:T(8,128)S(1)}, f32[128,128]{1,0:T(8,128)S(1)}, u32[]{:S(2)}, u32[]{:S(2)}) collective-permute-start(f32[128,128]{1,0:T(8,128)S(1)} %pair.7.half.mine), channel_id=1, source_target_pairs={{0,7},{1,2},{2,1},{3,4},{4,3},{5,6},{6,5},{7,0},{8,15},{9,10},{10,... | collective-permute-start | bytes 196616 | tf_op jit(solution)/shard_map/ppermute | solution.py:611
  106.1 1.4 %local.7.acc = f32[4,192,256]{2,1,0:T(8,128)S(1)} custom-call(f32[16,128]{1,0:T(8,128)S(1)} %get-tuple-element.62.params, f32[128,128]{1,0:T(8,128)S(1)} %pair.7.half.mine, f32[4,192,256]{2,1,0:T(8,128)S(1)} %get-tuple-element.100.field, f32[4,192,256]{2,1,0:T(8,128)S(1)} %get-tuple-element.90.field.before, f32[192,256]{1,0:T(8,128)S(1)} %get-tuple-element.68.pot, ...), custom_call_target="tpu_custom_call" | custom-call | flops 100000000 | bytes 4000000 | tf_op jit(solution)/shard_map/local/pallas_call | solution.py:596
  107.5 2.2 %collective-permute-done.31.came = f32[128,128]{1,0:T(8,128)S(1)} collective-permute-done((f32[128,128]{1,0:T(8,128)S(1)}, f32[128,128]{1,0:T(8,128)S(1)}, u32[]{:S(2)}, u32[]{:S(2)}) %collective-permute-start.31) | collective-permute-done | bytes 65568 | tf_op jit(solution)/shard_map/ppermute | solution.py:611
  109.8 2.0 %collective-permute-start.32 = (f32[64,128]{1,0:T(8,128)S(1)}, f32[64,128]{1,0:T(8,128)S(1)}, u32[]{:S(2)}, u32[]{:S(2)}) collective-permute-start(f32[64,128]{1,0:T(8,128)S(1)} %get-tuple-element.102.high), channel_id=1, source_target_pairs={{0,16},{1,17},{2,18},{3,19},{4,20},{5,21},{6,22},{7,23},{8,24},{9,... | collective-permute-start | bytes 98312 | tf_op jit(solution)/shard_map/ppermute | solution.py:611
  111.8 1.6 %halo.7.acc = f32[4,192,256]{2,1,0:T(8,128)S(1)} custom-call(f32[16,128]{1,0:T(8,128)S(1)} %get-tuple-element.62.params, f32[4,144,128]{2,1,0:T(8,128)S(1)} %collective-permute-done.34.inner, f32[4,144,128]{2,1,0:T(8,128)S(1)} %collective-permute-done.35.outer, f32[4,144,128]{2,1,0:T(8,128)S(1)} %collective-permute-done.36.xl, ...), custom_call_target="tpu_custom_call" | custom-call | flops 100000000 | bytes 4000000 | tf_op jit(solution)/shard_map/halo/pallas_call | solution.py:596
  113.7 1.3 collective-permute-done.32.below
  116.4 2.2 %finish.1 = (f32[4,8,3072]{2,1,0:T(8,128)S(1)}, f32[4,192,256]{2,1,0:T(8,128)S(1)}) custom-call(f32[16,128]{1,0:T(8,128)S(1)} %get-tuple-element.62.params, s32[4,896]{1,0:T(4,128)S(1)} %get-tuple-element.65.index, f32[4,192,256]{2,1,0:T(8,128)S(1)} %get-tuple-element.108.acc, f32[128,128]{1,0:T(8,128)S(1)} %get-tuple-element.109.mine, ...), custom_call_target="tpu_custom_call" | custom-call | flops 100000000 | bytes 4000000 | tf_op jit(solution)/shard_map/finish/pallas_call | solution.py:596
  118.5 3.7 %collective-permute-start.39 = (f32[4,8,3072]{2,1,0:T(8,128)S(1)}, f32[4,8,3072]{2,1,0:T(8,128)S(1)}, u32[]{:S(2)}, u32[]{:S(2)}) collective-permute-start(f32[4,8,3072]{2,1,0:T(8,128)S(1)} %get-tuple-element.110), channel_id=1, source_target_pairs={{0,8},{1,9},{2,10},{3,11},{4,12},{5,13},{6,14},{7,15},{8,0},{9,1},... | collective-permute-start | bytes 1179656 | tf_op jit(solution)/shard_map/ppermute | solution.py:611
  122.6 2.8 %collective-permute-start.40 = (f32[2,8,1536]{2,1,0:T(8,128)S(1)}, f32[2,8,1536]{2,1,0:T(8,128)S(1)}, u32[]{:S(2)}, u32[]{:S(2)}) collective-permute-start(f32[2,8,1536]{2,1,0:T(8,128)S(1)} %get-tuple-element.113.here), channel_id=1, source_target_pairs={{0,64},{64,0},{1,65},{65,1},{2,66},{66,2},{3,67},{67,3},{4,68},{68... | collective-permute-start | bytes 294920 | tf_op jit(solution)/shard_map/ppermute | solution.py:827
  125.4 3.4 %collective-permute-done.40.came = f32[2,8,1536]{2,1,0:T(8,128)S(1)} collective-permute-done((f32[2,8,1536]{2,1,0:T(8,128)S(1)}, f32[2,8,1536]{2,1,0:T(8,128)S(1)}, u32[]{:S(2)}, u32[]{:S(2)}) %collective-permute-start.40) | collective-permute-done | bytes 98336 | tf_op jit(solution)/shard_map/ppermute | solution.py:827
  129.9 4.5 %collective-permute-done.41.b = f32[8,1536]{1,0:T(8,128)S(1)} collective-permute-done((f32[8,1536]{1,0:T(8,128)S(1)}, f32[8,1536]{1,0:T(8,128)S(1)}, u32[]{:S(2)}, u32[]{:S(2)}) %collective-permute-start.41) | collective-permute-done | bytes 49184 | tf_op jit(solution)/shard_map/ppermute | solution.py:611
  (99 shorter events, 20.0 us)
Async XLA Ops:
  0.6 11.9 %copy-start = (f32[1,4,448,128]{3,2,1,0:T(8,128)S(1)}, f32[1,4,448,128]{3,2,1,0:T(8,128)}, u32[]{:S(2)}) copy-start(f32[1,4,448,128]{3,2,1,0:T(8,128)} %param.18) | copy-start | bytes 2752516
  2.5 17.2 %collective-permute-start = (f32[5,8,3072]{2,1,0:T(8,128)}, f32[5,8,3072]{2,1,0:T(8,128)S(1)}, u32[]{:S(2)}, u32[]{:S(2)}) collective-permute-start(f32[5,8,3072]{2,1,0:T(8,128)} %pick.1), channel_id=1, source_target_pairs={{0,8},{1,9},{2,10},{3,11},{4,12},{5,13},{6,14},{7,15},{8,0},{9,1},... | collective-permute-start | bytes 1474568 | tf_op jit(solution)/shard_map/ppermute | solution.py:611
  12.2 7.5 %collective-permute-start.1 = (f32[216,128]{1,0:T(8,128)}, f32[216,128]{1,0:T(8,128)S(1)}, u32[]{:S(2)}, u32[]{:S(2)}) collective-permute-start(f32[216,128]{1,0:T(8,128)} %get-tuple-element.64), channel_id=1, source_target_pairs={{0,8},{1,9},{2,10},{3,11},{4,12},{5,13},{6,14},{7,15},{8,0},{9,1},... | collective-permute-start | bytes 331784 | tf_op jit(solution)/shard_map/ppermute | solution.py:611
  12.6 11.8 %copy-start.4 = (bf16[256,256]{1,0:T(8,128)(2,1)S(1)}, bf16[256,256]{1,0:T(8,128)(2,1)}, u32[]{:S(2)}) copy-start(bf16[256,256]{1,0:T(8,128)(2,1)} %constant.13.clone.edge.rest_0_) | copy-start | bytes 393220
  12.6 11.8 %copy-start.5 = (f32[4,192,128]{2,1,0:T(8,128)S(1)}, f32[4,192,128]{2,1,0:T(8,128)}, u32[]{:S(2)}) copy-start(f32[4,192,128]{2,1,0:T(8,128)} %get-tuple-element.61.keep) | copy-start | bytes 1179652
  12.7 13.0 %copy-start.7 = (f32[192,128]{1,0:T(8,128)S(1)}, f32[192,128]{1,0:T(8,128)}, u32[]{:S(2)}) copy-start(f32[192,128]{1,0:T(8,128)} %get-tuple-element.66.table) | copy-start | bytes 294916
  19.7 16.5 %copy-start.2 = (bf16[2,256,256]{2,1,0:T(8,128)(2,1)S(1)}, bf16[2,256,256]{2,1,0:T(8,128)(2,1)}, u32[]{:S(2)}) copy-start(bf16[2,256,256]{2,1,0:T(8,128)(2,1)} %constant.10.clone.own_w) | copy-start | bytes 786436
  19.7 16.5 %copy-start.3 = (bf16[2,192,192]{2,1,0:T(8,128)(2,1)S(1)}, bf16[2,192,192]{2,1,0:T(8,128)(2,1)}, u32[]{:S(2)}) copy-start(bf16[2,192,192]{2,1,0:T(8,128)(2,1)} %constant.12.clone.ring_w) | copy-start | bytes 442372
  19.7 26.7 %collective-permute-start.2 = (f32[4,448,128]{2,1,0:T(8,128)S(1)}, f32[4,448,128]{2,1,0:T(8,128)S(1)}, u32[]{:S(2)}, u32[]{:S(2)}) collective-permute-start(f32[4,448,128]{2,1,0:T(8,128)S(1)} %gate.1), channel_id=1, source_target_pairs={{0,8},{1,9},{2,10},{3,11},{4,12},{5,13},{6,14},{7,15},{8,0},{9,1},... | collective-permute-start | bytes 2752520 | tf_op jit(solution)/shard_map/ppermute | solution.py:611
  25.7 1.4 %collective-permute-start.3 = (f32[192,128]{1,0:T(8,128)S(1)}, f32[192,128]{1,0:T(8,128)S(1)}, u32[]{:S(2)}, u32[]{:S(2)}) collective-permute-start(f32[192,128]{1,0:T(8,128)S(1)} %join_table.1.table.note), channel_id=1, source_target_pairs={{0,1},{1,0},{2,3},{3,2},{4,5},{5,4},{6,7},{7,6},{8,9},{9,8},{10,11... | collective-permute-start | bytes 294920 | tf_op jit(solution)/shard_map/ppermute | solution.py:611
  27.1 5.0 %collective-permute-start.4 = (f32[136,128]{1,0:T(8,128)S(1)}, f32[136,128]{1,0:T(8,128)S(1)}, u32[]{:S(2)}, u32[]{:S(2)}) collective-permute-start(f32[136,128]{1,0:T(8,128)S(1)} %pair.4.half.mine), channel_id=1, source_target_pairs={{0,7},{1,2},{2,1},{3,4},{4,3},{5,6},{6,5},{7,0},{8,15},{9,10},{10,... | collective-permute-start | bytes 208904 | tf_op jit(solution)/shard_map/ppermute | solution.py:611
  28.6 9.0 %collective-permute-start.7 = (f32[4,144,128]{2,1,0:T(8,128)S(1)}, f32[4,144,128]{2,1,0:T(8,128)S(1)}, u32[]{:S(2)}, u32[]{:S(2)}) collective-permute-start(f32[4,144,128]{2,1,0:T(8,128)S(1)} %get-tuple-element.71), channel_id=1, source_target_pairs={{0,1},{1,0},{2,3},{3,2},{4,5},{5,4},{6,7},{7,6},{8,9},{9,8},{10,11... | collective-permute-start | bytes 884744 | tf_op jit(solution)/shard_map/ppermute | solution.py:611
  28.8 9.9 %collective-permute-start.8 = (f32[4,144,128]{2,1,0:T(8,128)S(1)}, f32[4,144,128]{2,1,0:T(8,128)S(1)}, u32[]{:S(2)}, u32[]{:S(2)}) collective-permute-start(f32[4,144,128]{2,1,0:T(8,128)S(1)} %get-tuple-element.72), channel_id=1, source_target_pairs={{0,7},{1,2},{2,1},{3,4},{4,3},{5,6},{6,5},{7,0},{8,15},{9,10},{10,... | collective-permute-start | bytes 884744 | tf_op jit(solution)/shard_map/ppermute | solution.py:611
  29.9 10.9 %collective-permute-start.9 = (f32[4,144,128]{2,1,0:T(8,128)S(1)}, f32[4,144,128]{2,1,0:T(8,128)S(1)}, u32[]{:S(2)}, u32[]{:S(2)}) collective-permute-start(f32[4,144,128]{2,1,0:T(8,128)S(1)} %get-tuple-element.73), channel_id=1, source_target_pairs={{0,16},{1,17},{2,18},{3,19},{4,20},{5,21},{6,22},{7,23},{8,24},{9,... | collective-permute-start | bytes 884744 | tf_op jit(solution)/shard_map/ppermute | solution.py:611
  32.2 10.6 %collective-permute-start.10 = (f32[4,144,128]{2,1,0:T(8,128)S(1)}, f32[4,144,128]{2,1,0:T(8,128)S(1)}, u32[]{:S(2)}, u32[]{:S(2)}) collective-permute-start(f32[4,144,128]{2,1,0:T(8,128)S(1)} %get-tuple-element.74), channel_id=1, source_target_pairs={{0,48},{1,49},{2,50},{3,51},{4,52},{5,53},{6,54},{7,55},{8,56},{9,... | collective-permute-start | bytes 884744 | tf_op jit(solution)/shard_map/ppermute | solution.py:611
  37.6 6.8 %collective-permute-start.6 = (f32[72,128]{1,0:T(8,128)S(1)}, f32[72,128]{1,0:T(8,128)S(1)}, u32[]{:S(2)}, u32[]{:S(2)}) collective-permute-start(f32[72,128]{1,0:T(8,128)S(1)} %get-tuple-element.69.low), channel_id=1, source_target_pairs={{0,48},{1,49},{2,50},{3,51},{4,52},{5,53},{6,54},{7,55},{8,56},{9,... | collective-permute-start | bytes 110600 | tf_op jit(solution)/shard_map/ppermute | solution.py:611
  38.7 6.0 %collective-permute-start.5 = (f32[72,128]{1,0:T(8,128)S(1)}, f32[72,128]{1,0:T(8,128)S(1)}, u32[]{:S(2)}, u32[]{:S(2)}) collective-permute-start(f32[72,128]{1,0:T(8,128)S(1)} %get-tuple-element.70.high), channel_id=1, source_target_pairs={{0,16},{1,17},{2,18},{3,19},{4,20},{5,21},{6,22},{7,23},{8,24},{9,... | collective-permute-start | bytes 110600 | tf_op jit(solution)/shard_map/ppermute | solution.py:611
  44.7 2.8 %collective-permute-start.11 = (f32[128,128]{1,0:T(8,128)S(1)}, f32[128,128]{1,0:T(8,128)S(1)}, u32[]{:S(2)}, u32[]{:S(2)}) collective-permute-start(f32[128,128]{1,0:T(8,128)S(1)} %get-tuple-element.77.mine), channel_id=1, source_target_pairs={{0,1},{1,0},{2,3},{3,2},{4,5},{5,4},{6,7},{7,6},{8,9},{9,8},{10,11... | collective-permute-start | bytes 196616 | tf_op jit(solution)/shard_map/ppermute | solution.py:611
  49.9 16.9 %collective-permute-start.16 = (f32[4,144,128]{2,1,0:T(8,128)S(1)}, f32[4,144,128]{2,1,0:T(8,128)S(1)}, u32[]{:S(2)}, u32[]{:S(2)}) collective-permute-start(f32[4,144,128]{2,1,0:T(8,128)S(1)} %get-tuple-element.83), channel_id=1, source_target_pairs={{0,1},{1,0},{2,3},{3,2},{4,5},{5,4},{6,7},{7,6},{8,9},{9,8},{10,11... | collective-permute-start | bytes 884744 | tf_op jit(solution)/shard_map/ppermute | solution.py:611
  50.0 16.8 %collective-permute-start.17 = (f32[4,144,128]{2,1,0:T(8,128)S(1)}, f32[4,144,128]{2,1,0:T(8,128)S(1)}, u32[]{:S(2)}, u32[]{:S(2)}) collective-permute-start(f32[4,144,128]{2,1,0:T(8,128)S(1)} %get-tuple-element.84), channel_id=1, source_target_pairs={{0,7},{1,2},{2,1},{3,4},{4,3},{5,6},{6,5},{7,0},{8,15},{9,10},{10,... | collective-permute-start | bytes 884744 | tf_op jit(solution)/shard_map/ppermute | solution.py:611
  52.6 14.2 %collective-permute-start.18 = (f32[4,144,128]{2,1,0:T(8,128)S(1)}, f32[4,144,128]{2,1,0:T(8,128)S(1)}, u32[]{:S(2)}, u32[]{:S(2)}) collective-permute-start(f32[4,144,128]{2,1,0:T(8,128)S(1)} %get-tuple-element.85), channel_id=1, source_target_pairs={{0,16},{1,17},{2,18},{3,19},{4,20},{5,21},{6,22},{7,23},{8,24},{9,... | collective-permute-start | bytes 884744 | tf_op jit(solution)/shard_map/ppermute | solution.py:611
  54.6 12.3 %collective-permute-start.19 = (f32[4,144,128]{2,1,0:T(8,128)S(1)}, f32[4,144,128]{2,1,0:T(8,128)S(1)}, u32[]{:S(2)}, u32[]{:S(2)}) collective-permute-start(f32[4,144,128]{2,1,0:T(8,128)S(1)} %get-tuple-element.86), channel_id=1, source_target_pairs={{0,48},{1,49},{2,50},{3,51},{4,52},{5,53},{6,54},{7,55},{8,56},{9,... | collective-permute-start | bytes 884744 | tf_op jit(solution)/shard_map/ppermute | solution.py:611
  58.6 1.4 %collective-permute-start.12 = (f32[192,128]{1,0:T(8,128)S(1)}, f32[192,128]{1,0:T(8,128)S(1)}, u32[]{:S(2)}, u32[]{:S(2)}) collective-permute-start(f32[192,128]{1,0:T(8,128)S(1)} %table.3), channel_id=1, source_target_pairs={{0,1},{1,0},{2,3},{3,2},{4,5},{5,4},{6,7},{7,6},{8,9},{9,8},{10,11... | collective-permute-start | bytes 294920 | tf_op jit(solution)/shard_map/ppermute | solution.py:611
  60.0 4.7 %collective-permute-start.13 = (f32[128,128]{1,0:T(8,128)S(1)}, f32[128,128]{1,0:T(8,128)S(1)}, u32[]{:S(2)}, u32[]{:S(2)}) collective-permute-start(f32[128,128]{1,0:T(8,128)S(1)} %pair.5.half.mine), channel_id=1, source_target_pairs={{0,7},{1,2},{2,1},{3,4},{4,3},{5,6},{6,5},{7,0},{8,15},{9,10},{10,... | collective-permute-start | bytes 196616 | tf_op jit(solution)/shard_map/ppermute | solution.py:611
  64.7 4.0 %collective-permute-start.15 = (f32[64,128]{1,0:T(8,128)S(1)}, f32[64,128]{1,0:T(8,128)S(1)}, u32[]{:S(2)}, u32[]{:S(2)}) collective-permute-start(f32[64,128]{1,0:T(8,128)S(1)} %get-tuple-element.80.low), channel_id=1, source_target_pairs={{0,48},{1,49},{2,50},{3,51},{4,52},{5,53},{6,54},{7,55},{8,56},{9,... | collective-permute-start | bytes 98312 | tf_op jit(solution)/shard_map/ppermute | solution.py:611
  66.8 5.1 %collective-permute-start.14 = (f32[64,128]{1,0:T(8,128)S(1)}, f32[64,128]{1,0:T(8,128)S(1)}, u32[]{:S(2)}, u32[]{:S(2)}) collective-permute-start(f32[64,128]{1,0:T(8,128)S(1)} %get-tuple-element.81.high), channel_id=1, source_target_pairs={{0,16},{1,17},{2,18},{3,19},{4,20},{5,21},{6,22},{7,23},{8,24},{9,... | collective-permute-start | bytes 98312 | tf_op jit(solution)/shard_map/ppermute | solution.py:611
  72.0 1.3 collective-permute-start.20
  75.7 12.3 %collective-permute-start.25 = (f32[4,144,128]{2,1,0:T(8,128)S(1)}, f32[4,144,128]{2,1,0:T(8,128)S(1)}, u32[]{:S(2)}, u32[]{:S(2)}) collective-permute-start(f32[4,144,128]{2,1,0:T(8,128)S(1)} %get-tuple-element.93), channel_id=1, source_target_pairs={{0,1},{1,0},{2,3},{3,2},{4,5},{5,4},{6,7},{7,6},{8,9},{9,8},{10,11... | collective-permute-start | bytes 884744 | tf_op jit(solution)/shard_map/ppermute | solution.py:611
  75.9 13.9 %collective-permute-start.26 = (f32[4,144,128]{2,1,0:T(8,128)S(1)}, f32[4,144,128]{2,1,0:T(8,128)S(1)}, u32[]{:S(2)}, u32[]{:S(2)}) collective-permute-start(f32[4,144,128]{2,1,0:T(8,128)S(1)} %get-tuple-element.94), channel_id=1, source_target_pairs={{0,7},{1,2},{2,1},{3,4},{4,3},{5,6},{6,5},{7,0},{8,15},{9,10},{10,... | collective-permute-start | bytes 884744 | tf_op jit(solution)/shard_map/ppermute | solution.py:611
  76.2 13.6 %collective-permute-start.27 = (f32[4,144,128]{2,1,0:T(8,128)S(1)}, f32[4,144,128]{2,1,0:T(8,128)S(1)}, u32[]{:S(2)}, u32[]{:S(2)}) collective-permute-start(f32[4,144,128]{2,1,0:T(8,128)S(1)} %get-tuple-element.95), channel_id=1, source_target_pairs={{0,16},{1,17},{2,18},{3,19},{4,20},{5,21},{6,22},{7,23},{8,24},{9,... | collective-permute-start | bytes 884744 | tf_op jit(solution)/shard_map/ppermute | solution.py:611
  76.2 13.6 %collective-permute-start.28 = (f32[4,144,128]{2,1,0:T(8,128)S(1)}, f32[4,144,128]{2,1,0:T(8,128)S(1)}, u32[]{:S(2)}, u32[]{:S(2)}) collective-permute-start(f32[4,144,128]{2,1,0:T(8,128)S(1)} %get-tuple-element.96), channel_id=1, source_target_pairs={{0,48},{1,49},{2,50},{3,51},{4,52},{5,53},{6,54},{7,55},{8,56},{9,... | collective-permute-start | bytes 884744 | tf_op jit(solution)/shard_map/ppermute | solution.py:611
  81.4 1.4 %collective-permute-start.21 = (f32[192,128]{1,0:T(8,128)S(1)}, f32[192,128]{1,0:T(8,128)S(1)}, u32[]{:S(2)}, u32[]{:S(2)}) collective-permute-start(f32[192,128]{1,0:T(8,128)S(1)} %table.4), channel_id=1, source_target_pairs={{0,1},{1,0},{2,3},{3,2},{4,5},{5,4},{6,7},{7,6},{8,9},{9,8},{10,11... | collective-permute-start | bytes 294920 | tf_op jit(solution)/shard_map/ppermute | solution.py:611
  82.8 4.9 %collective-permute-start.22 = (f32[128,128]{1,0:T(8,128)S(1)}, f32[128,128]{1,0:T(8,128)S(1)}, u32[]{:S(2)}, u32[]{:S(2)}) collective-permute-start(f32[128,128]{1,0:T(8,128)S(1)} %pair.6.half.mine), channel_id=1, source_target_pairs={{0,7},{1,2},{2,1},{3,4},{4,3},{5,6},{6,5},{7,0},{8,15},{9,10},{10,... | collective-permute-start | bytes 196616 | tf_op jit(solution)/shard_map/ppermute | solution.py:611
  87.7 4.0 %collective-permute-start.24 = (f32[64,128]{1,0:T(8,128)S(1)}, f32[64,128]{1,0:T(8,128)S(1)}, u32[]{:S(2)}, u32[]{:S(2)}) collective-permute-start(f32[64,128]{1,0:T(8,128)S(1)} %get-tuple-element.91.low), channel_id=1, source_target_pairs={{0,48},{1,49},{2,50},{3,51},{4,52},{5,53},{6,54},{7,55},{8,56},{9,... | collective-permute-start | bytes 98312 | tf_op jit(solution)/shard_map/ppermute | solution.py:611
  88.0 5.1 %collective-permute-start.23 = (f32[64,128]{1,0:T(8,128)S(1)}, f32[64,128]{1,0:T(8,128)S(1)}, u32[]{:S(2)}, u32[]{:S(2)}) collective-permute-start(f32[64,128]{1,0:T(8,128)S(1)} %get-tuple-element.92.high), channel_id=1, source_target_pairs={{0,16},{1,17},{2,18},{3,19},{4,20},{5,21},{6,22},{7,23},{8,24},{9,... | collective-permute-start | bytes 98312 | tf_op jit(solution)/shard_map/ppermute | solution.py:611
  93.2 1.6 %collective-permute-start.29 = (f32[128,128]{1,0:T(8,128)S(1)}, f32[128,128]{1,0:T(8,128)S(1)}, u32[]{:S(2)}, u32[]{:S(2)}) collective-permute-start(f32[128,128]{1,0:T(8,128)S(1)} %get-tuple-element.99.mine), channel_id=1, source_target_pairs={{0,1},{1,0},{2,3},{3,2},{4,5},{5,4},{6,7},{7,6},{8,9},{9,8},{10,11... | collective-permute-start | bytes 196616 | tf_op jit(solution)/shard_map/ppermute | solution.py:611
  97.1 12.7 %collective-permute-start.34 = (f32[4,144,128]{2,1,0:T(8,128)S(1)}, f32[4,144,128]{2,1,0:T(8,128)S(1)}, u32[]{:S(2)}, u32[]{:S(2)}) collective-permute-start(f32[4,144,128]{2,1,0:T(8,128)S(1)} %get-tuple-element.103), channel_id=1, source_target_pairs={{0,1},{1,0},{2,3},{3,2},{4,5},{5,4},{6,7},{7,6},{8,9},{9,8},{10,11... | collective-permute-start | bytes 884744 | tf_op jit(solution)/shard_map/ppermute | solution.py:611
  97.3 14.5 %collective-permute-start.35 = (f32[4,144,128]{2,1,0:T(8,128)S(1)}, f32[4,144,128]{2,1,0:T(8,128)S(1)}, u32[]{:S(2)}, u32[]{:S(2)}) collective-permute-start(f32[4,144,128]{2,1,0:T(8,128)S(1)} %get-tuple-element.104), channel_id=1, source_target_pairs={{0,7},{1,2},{2,1},{3,4},{4,3},{5,6},{6,5},{7,0},{8,15},{9,10},{10,... | collective-permute-start | bytes 884744 | tf_op jit(solution)/shard_map/ppermute | solution.py:611
  98.1 13.7 %collective-permute-start.36 = (f32[4,144,128]{2,1,0:T(8,128)S(1)}, f32[4,144,128]{2,1,0:T(8,128)S(1)}, u32[]{:S(2)}, u32[]{:S(2)}) collective-permute-start(f32[4,144,128]{2,1,0:T(8,128)S(1)} %get-tuple-element.105), channel_id=1, source_target_pairs={{0,16},{1,17},{2,18},{3,19},{4,20},{5,21},{6,22},{7,23},{8,24},{9,... | collective-permute-start | bytes 884744 | tf_op jit(solution)/shard_map/ppermute | solution.py:611
  99.0 12.9 %collective-permute-start.37 = (f32[4,144,128]{2,1,0:T(8,128)S(1)}, f32[4,144,128]{2,1,0:T(8,128)S(1)}, u32[]{:S(2)}, u32[]{:S(2)}) collective-permute-start(f32[4,144,128]{2,1,0:T(8,128)S(1)} %get-tuple-element.106), channel_id=1, source_target_pairs={{0,48},{1,49},{2,50},{3,51},{4,52},{5,53},{6,54},{7,55},{8,56},{9,... | collective-permute-start | bytes 884744 | tf_op jit(solution)/shard_map/ppermute | solution.py:611
  103.3 1.4 %collective-permute-start.30 = (f32[192,128]{1,0:T(8,128)S(1)}, f32[192,128]{1,0:T(8,128)S(1)}, u32[]{:S(2)}, u32[]{:S(2)}) collective-permute-start(f32[192,128]{1,0:T(8,128)S(1)} %table.5), channel_id=1, source_target_pairs={{0,1},{1,0},{2,3},{3,2},{4,5},{5,4},{6,7},{7,6},{8,9},{9,8},{10,11... | collective-permute-start | bytes 294920 | tf_op jit(solution)/shard_map/ppermute | solution.py:611
  104.7 5.1 %collective-permute-start.31 = (f32[128,128]{1,0:T(8,128)S(1)}, f32[128,128]{1,0:T(8,128)S(1)}, u32[]{:S(2)}, u32[]{:S(2)}) collective-permute-start(f32[128,128]{1,0:T(8,128)S(1)} %pair.7.half.mine), channel_id=1, source_target_pairs={{0,7},{1,2},{2,1},{3,4},{4,3},{5,6},{6,5},{7,0},{8,15},{9,10},{10,... | collective-permute-start | bytes 196616 | tf_op jit(solution)/shard_map/ppermute | solution.py:611
  109.7 4.0 %collective-permute-start.33 = (f32[64,128]{1,0:T(8,128)S(1)}, f32[64,128]{1,0:T(8,128)S(1)}, u32[]{:S(2)}, u32[]{:S(2)}) collective-permute-start(f32[64,128]{1,0:T(8,128)S(1)} %get-tuple-element.101.low), channel_id=1, source_target_pairs={{0,48},{1,49},{2,50},{3,51},{4,52},{5,53},{6,54},{7,55},{8,56},{9,... | collective-permute-start | bytes 98312 | tf_op jit(solution)/shard_map/ppermute | solution.py:611
  109.8 5.2 %collective-permute-start.32 = (f32[64,128]{1,0:T(8,128)S(1)}, f32[64,128]{1,0:T(8,128)S(1)}, u32[]{:S(2)}, u32[]{:S(2)}) collective-permute-start(f32[64,128]{1,0:T(8,128)S(1)} %get-tuple-element.102.high), channel_id=1, source_target_pairs={{0,16},{1,17},{2,18},{3,19},{4,20},{5,21},{6,22},{7,23},{8,24},{9,... | collective-permute-start | bytes 98312 | tf_op jit(solution)/shard_map/ppermute | solution.py:611
  115.0 1.3 collective-permute-start.38
  118.5 15.9 %collective-permute-start.39 = (f32[4,8,3072]{2,1,0:T(8,128)S(1)}, f32[4,8,3072]{2,1,0:T(8,128)S(1)}, u32[]{:S(2)}, u32[]{:S(2)}) collective-permute-start(f32[4,8,3072]{2,1,0:T(8,128)S(1)} %get-tuple-element.110), channel_id=1, source_target_pairs={{0,8},{1,9},{2,10},{3,11},{4,12},{5,13},{6,14},{7,15},{8,0},{9,1},... | collective-permute-start | bytes 1179656 | tf_op jit(solution)/shard_map/ppermute | solution.py:611
  122.6 6.2 %collective-permute-start.40 = (f32[2,8,1536]{2,1,0:T(8,128)S(1)}, f32[2,8,1536]{2,1,0:T(8,128)S(1)}, u32[]{:S(2)}, u32[]{:S(2)}) collective-permute-start(f32[2,8,1536]{2,1,0:T(8,128)S(1)} %get-tuple-element.113.here), channel_id=1, source_target_pairs={{0,64},{64,0},{1,65},{65,1},{2,66},{66,2},{3,67},{67,3},{4,68},{68... | collective-permute-start | bytes 294920 | tf_op jit(solution)/shard_map/ppermute | solution.py:827
  128.8 5.7 %collective-permute-start.41 = (f32[8,1536]{1,0:T(8,128)S(1)}, f32[8,1536]{1,0:T(8,128)S(1)}, u32[]{:S(2)}, u32[]{:S(2)}) collective-permute-start(f32[8,1536]{1,0:T(8,128)S(1)} %get-tuple-element.114), channel_id=1, source_target_pairs={{0,8},{1,9},{2,10},{3,11},{4,12},{5,13},{6,14},{7,15},{8,0},{9,1},... | collective-permute-start | bytes 147464 | tf_op jit(solution)/shard_map/ppermute | solution.py:611
  (5 other events, 39.6 us)
